TPU v7x, 32 devices: a whole 2x2x4 slice. The times are simulated.
32 devices in a mesh: dp: 8 (over z, core), mp: 4 (over y, x).
Axes of the slice: x: 2, y: 2, z: 4, core: 2. Of those that a mesh axis runs over, the one named last changes fastest.
Arguments:
- grad: bfloat16 [8, 4096, 7168], P('dp', 'mp')
- error: bfloat16 [8, 4096, 7168], P('dp', 'mp'), may hold values from -3 to 3
- init_factor: bfloat16 [7168, 128], replicated, may hold values from -0.0625 to 0.0625
Outputs:
- new_error: bfloat16 [8, 4096, 7168], P('dp', 'mp')
- right_factor: bfloat16 [7168, 128], P('mp')
All inputs are finite; a program needn't handle non-finite values.
Results may differ from a plain program's by a relative error of at most 0.009.
Values may be sent and summed in bfloat16 or wider, within the bound.
No kernel may reach another device: no remote copies, remote signals or barrier semaphores. Data moves between devices by JAX's collectives and lax.ppermute only.
A program may use at most 128 MiB of HBM per device.

v0:
```python
import jax
import jax.numpy as jnp
from jax import lax
from jax.sharding import PartitionSpec as P


def triangular_basis(cholesky_factor, row_block):
    return jax.scipy.linalg.solve_triangular(cholesky_factor, row_block.T, lower=True).T


def orthonormal(partial_value):
    summed = lax.psum(partial_value, "dp")
    gram_part = jnp.dot(
        summed.T, summed, precision=lax.Precision.HIGHEST, preferred_element_type=jnp.float32
    )
    gram_matrix = lax.psum(gram_part, "mp")
    cholesky_factor = jnp.linalg.cholesky(gram_matrix)
    return triangular_basis(cholesky_factor, summed).astype(jnp.bfloat16)


def reduce_factor(compensated, ortho_basis):
    replicas = lax.axis_size("dp")
    own_rows = lax.psum_scatter(
        lax.dot_general(
            compensated, ortho_basis, (((0,), (0,)), ((), ())), preferred_element_type=jnp.float32
        ),
        ("dp", "mp"),
        scatter_dimension=0,
        tiled=True,
    )
    return (own_rows / replicas).astype(jnp.bfloat16)


def on_device(grad, error, init_factor):
    compensated = (grad[0].astype(jnp.float32) + error[0].astype(jnp.float32)).astype(jnp.bfloat16)
    partial_value = jnp.dot(compensated, init_factor, preferred_element_type=jnp.float32)
    ortho_basis = orthonormal(partial_value)
    factor_rows = reduce_factor(compensated, ortho_basis)
    full_factor = lax.all_gather(factor_rows, ("dp", "mp"), axis=0, tiled=True)
    decompressed = lax.dot_general(
        ortho_basis, full_factor, (((1,), (1,)), ((), ())), preferred_element_type=jnp.float32
    )
    mp_rows = full_factor.shape[0] // lax.axis_size("mp")
    right_factor = lax.dynamic_slice_in_dim(full_factor, lax.axis_index("mp") * mp_rows, mp_rows, 0)
    new_error = (compensated.astype(jnp.float32) - decompressed).astype(jnp.bfloat16)
    return (new_error[None], right_factor)


def solution(mesh):
    return jax.shard_map(
        on_device,
        mesh=mesh,
        in_specs=(P("dp", "mp", None), P("dp", "mp", None), P()),
        out_specs=(P("dp", "mp", None), P("mp", None)),
        check_vma=False,
    )
```

profile of v0, /device:TPU:1, one launch (start us, length us, event | category | flops | bytes accessed | tf_op | source)
XLA Modules:
  0.0 391.2 jit_solution(17219335235409300268)
XLA Ops:
  7.2 0.0 copy-start
  7.2 0.0 all-reduce.3.cloned.1.call-start
  7.2 1.4 copy-done
  8.7 12.2 %fusion.7 = f32[1024,128]{1,0:T(8,128)} fusion(bf16[7168,128]{1,0:T(8,128)(2,1)S(1)} %copy-done, bf16[1,1024,7168]{2,1,0:T(8,128)(2,1)} %param.4, bf16[1,1024,7168]{2,1,0:T(8,128)(2,1)} %param.3), kind=kOutput, calls=%fused_computation.17 | convolution fusion | flops 1908408320 | bytes 31719424 | tf_op jit(solution)/shard_map/dot_general | solution.py:36
  20.9 0.0 all-reduce.3.cloned.1.call-update
  20.9 0.0 all-reduce.5.cloned.1.call-start
  21.0 56.6 %all-reduce.3.cloned.1.call-done = f32[1024,128]{1,0:T(8,128)} async-done(((f32[1024,128]{1,0:T(8,128)}), f32[1024,128]{1,0:T(8,128)}) %all-reduce.3.cloned.1.call-update) | async-done | bytes 524304 | tf_op jit(solution)/shard_map/psum | solution.py:12
  77.5 2.8 fusion.9
  80.3 0.0 all-reduce.5.cloned.1.call-update
  80.4 0.2 reduce-scatter.2.cloned.1.call-start
  80.6 42.5 %all-reduce.5.cloned.1.call-done = f32[128,128]{0,1:T(8,128)} async-done(((f32[128,128]{0,1:T(8,128)}), f32[128,128]{0,1:T(8,128)}) %all-reduce.5.cloned.1.call-update) | async-done | bytes 65552 | tf_op jit(solution)/shard_map/psum | solution.py:16
  123.1 0.9 copy.6
  124.0 0.9 fusion.4
  124.9 11.7 %cholesky.16 = f32[128,128]{1,0:T(8,128)S(1)} custom-call(f32[128,128]{1,0:T(8,128)S(1)} %fusion.4), custom_call_target="Cholesky" | custom-call | tf_op jit(solution)/shard_map/jit(cholesky)/cholesky | solution.py:17
  136.6 0.6 compare_reduce_fusion
  137.3 0.7 fusion.2
  137.9 9.8 %custom-call.7 = f32[1,128,128]{1,2,0:T(8,128)S(1)} custom-call(f32[1,128,128]{2,1,0:T(8,128)S(1)} %fusion.2), custom_call_target="InvertDiagBlocksLowerTriangular" | custom-call | tf_op jit(solution)/shard_map/jit(_solve_triangular)/triangular_solve | solution.py:8
  147.8 1.6 convolution_convert_fusion
  149.4 17.7 %fusion.5 = f32[7168,128]{1,0:T(8,128)} fusion(bf16[1024,128]{1,0:T(8,128)(2,1)S(1)} %convolution_convert_fusion, bf16[1,1024,7168]{2,1,0:T(8,128)(2,1)} %param.4, bf16[1,1024,7168]{2,1,0:T(8,128)(2,1)} %param.3), kind=kOutput, calls=%fused_computation.16 | convolution fusion | flops 1908408320 | bytes 33292288 | tf_op jit(solution)/shard_map/dot_general | solution.py:24
  167.1 0.0 reduce-scatter.2.cloned.1.call-update
  167.1 0.0 all-gather.2.cloned.1.call-start
  167.1 136.6 %reduce-scatter.2.cloned.1.call-done = f32[224,128]{1,0:T(8,128)} async-done(((f32[7168,128]{1,0:T(8,128)}), f32[224,128]{1,0:T(8,128)}) %reduce-scatter.2.cloned.1.call-update) | async-done | bytes 114704 | tf_op jit(solution)/shard_map/reduce_scatter | solution.py:23
  303.7 1.5 multiply_convert_fusion
  305.3 0.0 all-gather.2.cloned.1.call-update
  305.3 60.0 %all-gather.2.cloned.1.call-done = bf16[7168,128]{1,0:T(8,128)(2,1)} async-done(((bf16[224,128]{1,0:T(8,128)(2,1)}), bf16[7168,128]{1,0:T(8,128)(2,1)}) %all-gather.2.cloned.1.call-update) | async-done | bytes 1835024 | tf_op jit(solution)/shard_map/all_gather | solution.py:39
  365.3 17.5 %fusion.1 = bf16[1,1024,7168]{2,1,0:T(8,128)(2,1)} fusion(bf16[1024,128]{1,0:T(8,128)(2,1)S(1)} %convolution_convert_fusion, bf16[7168,128]{1,0:T(8,128)(2,1)} %all-gather.2.cloned.1.call-done, bf16[1,1024,7168]{2,1,0:T(8,128)(2,1)} %param.4, bf16[1,1024,7168]{2,1,0:T(8,128)(2,1)} %param.3), kind=kOutput, calls=%fused_computation.3 | convolution fusion | flops 1930428416 | bytes 46137344 | tf_op jit(solution)/shard_map/dot_general | solution.py:40
  382.9 1.8 constant_dynamic-slice_fusion
  (1 shorter events, 0.0 us)
Async XLA Ops:
  7.2 1.5 copy-start
  7.2 70.3 %all-reduce.3.cloned.1.call-start = ((), (), s32[]{:S(2)}) async-start(), calls=%async_computation.1 | async-start | bytes 1048576 | tf_op jit(solution)/shard_map/psum | solution.py:12
  20.9 102.2 %all-reduce.5.cloned.1.call-start = ((), (), s32[]{:S(2)}) async-start(), calls=%async_computation.2 | async-start | bytes 131072 | tf_op jit(solution)/shard_map/psum | solution.py:16
  80.4 223.4 %reduce-scatter.2.cloned.1.call-start = ((), (), s32[]{:S(2)}) async-start(), calls=%async_computation.3 | async-start | bytes 3784704 | tf_op jit(solution)/shard_map/reduce_scatter | solution.py:23
  167.1 198.2 %all-gather.2.cloned.1.call-start = ((), (), s32[]{:S(2)}) async-start(), calls=%async_computation.4 | async-start | bytes 1892352 | tf_op jit(solution)/shard_map/all_gather | solution.py:39
Sparse Core Ops, SparseCore 0:
  21.0 56.4 all-reduce.2
  81.2 41.8 all-reduce.4
  167.2 136.4 reduce-scatter.1
  307.5 57.8 all-gather.1
where the time goes:
time: 392 us; the launch traced here: 391 us
  waiting for transfers between devices  296 us (76%)
  matrix products  51.9 us (13%)
  other arithmetic  25.2 us (6%)
  between operations  13.8 us (4%)
  local copies, waits for them, and re-layouts  4.19 us (1%)
    reduce_scatter x1, waiting for transfers between devices, reduce_factor(): lax.psum_scatter(lax.dot_general(compensated, ortho_basis, (((0,), (0,)),...  137 us
    all_gather x1, waiting for transfers between devices, on_device(): full_factor = lax.all_gather(factor_rows, ('dp', 'mp'), axis=0, tiled=True)  60 us
    psum x1, waiting for transfers between devices, orthonormal(): summed = lax.psum(partial_value, 'dp')  56.6 us
    psum x1, waiting for transfers between devices, orthonormal(): gram_matrix = lax.psum(gram_part, 'mp')  42.5 us
    dot_general x1, matrix products, reduce_factor(): lax.dot_general(compensated, ortho_basis, (((0,), (0,)), ((), ())), prefe...  17.7 us
    dot_general x1, matrix products, on_device(): lax.dot_general(ortho_basis, full_factor, (((1,), (1,)), ((), ())), prefe...  17.5 us
    another operation x3, other arithmetic, orthonormal(): cholesky_factor = jnp.linalg.cholesky(gram_matrix)  12.4 us
    dot_general x1, matrix products, on_device(): jnp.dot(compensated, init_factor, preferred_element_type=jnp.float32)  12.2 us
  transfers between devices with their start and end apart: 4, of which 4 were waited for; matrix products, arithmetic and copies ran while one was open for 0% of the time, Pallas kernels for 0%

commit v1 on v0

v1 whole, which is shorter than its diff:
```python
import functools

import jax
import jax.numpy as jnp
from jax import lax
from jax.experimental import pallas as pl
from jax.experimental.pallas import tpu as pltpu
from jax.sharding import PartitionSpec as P

F32 = jnp.float32
BF16 = jnp.bfloat16
LANES = 128
MIB = 1024 * 1024
AXES = ("dp", "mp")


def as_bf16(x):
    rounded = lax.reduce_precision(x, 8, 7)
    return rounded.astype(BF16), rounded


def left_kernel(half_ref, grad_ref, error_ref, init_ref, comp_ref, left_ref):
    del half_ref
    tile = grad_ref.shape[0]
    total = (grad_ref[...].astype(F32) + error_ref[...].astype(F32)).astype(BF16)
    comp_ref[pl.ds(pl.multiple_of(pl.program_id(0) * tile, tile), tile), :] = total
    left_ref[...] = jnp.dot(total, init_ref[...], preferred_element_type=F32)


def left_product(half, grad, error, init):
    rows, cols = grad.shape
    rank = init.shape[1]
    count = rows // 2
    tile = min(128, count)
    steps = count // tile
    return pl.pallas_call(
        left_kernel,
        grid_spec=pltpu.PrefetchScalarGridSpec(
            num_scalar_prefetch=1,
            grid=(steps,),
            in_specs=[
                pl.BlockSpec((tile, cols), lambda i, half: (half[0] * steps + i, 0)),
                pl.BlockSpec((tile, cols), lambda i, half: (half[0] * steps + i, 0)),
                pl.BlockSpec((cols, rank), lambda i, half: (0, 0)),
            ],
            out_specs=[
                pl.BlockSpec(memory_space=pltpu.VMEM),
                pl.BlockSpec((tile, rank), lambda i, half: (i, 0)),
            ],
        ),
        out_shape=[pltpu.VMEM((count, cols), BF16), jax.ShapeDtypeStruct((count, rank), F32)],
        compiler_params=pltpu.CompilerParams(vmem_limit_bytes=24 * MIB),
        cost_estimate=pl.CostEstimate(
            flops=2 * count * cols * rank, bytes_accessed=4 * count * cols, transcendentals=0
        ),
        name="left_product",
    )(half, grad, error, init)


def right_kernel(order_ref, near_ref, far_ref, left_near_ref, left_far_ref, out_ref, lhs_ref):
    units = out_ref.shape[0] // order_ref.shape[0]
    count = near_ref.shape[0]
    lhs_ref[:, :count] = left_near_ref[...].T.astype(BF16)
    lhs_ref[:, count:] = left_far_ref[...].T.astype(BF16)

    @pl.loop(0, order_ref.shape[0])
    def _(block):
        start = order_ref[block] * (units * LANES)
        for first in range(0, units, 2):
            width = min(2, units - first)
            cols = pl.ds(pl.multiple_of(start + first * LANES, LANES), width * LANES)
            product = jnp.dot(lhs_ref[:, :count], near_ref[:, cols], preferred_element_type=F32)
            product += jnp.dot(lhs_ref[:, count:], far_ref[:, cols], preferred_element_type=F32)
            for unit in range(width):
                out_ref[block * units + first + unit] = product[
                    :, unit * LANES : (unit + 1) * LANES
                ].astype(out_ref.dtype)


def right_product(order, near, far, left_near, left_far, units, dtype):
    count, cols = near.shape
    rank = left_near.shape[1]
    vmem = pl.BlockSpec(memory_space=pltpu.VMEM)
    total = order.shape[0] * units
    return pl.pallas_call(
        right_kernel,
        grid_spec=pltpu.PrefetchScalarGridSpec(
            num_scalar_prefetch=1,
            grid=(),
            in_specs=[vmem] * 4,
            out_specs=vmem,
            scratch_shapes=[pltpu.VMEM((rank, 2 * count), BF16)],
        ),
        out_shape=jax.ShapeDtypeStruct((total, rank, LANES), dtype),
        compiler_params=pltpu.CompilerParams(vmem_limit_bytes=24 * MIB),
        cost_estimate=pl.CostEstimate(
            flops=4 * count * total * LANES * rank, bytes_accessed=4 * MIB, transcendentals=0
        ),
        name="right_product",
    )(order, in_vmem(near), in_vmem(far), left_near, left_far)


def in_vmem(x):
    return pltpu.with_memory_space_constraint(x, pltpu.VMEM)


def error_kernel(order_ref, halves_ref, near_ref, far_ref, base_near_ref, base_far_ref, right_ref, *rest):
    del halves_ref
    out_ref = rest[-1]
    units = right_ref.shape[0]
    start = order_ref[pl.program_id(0)] * (units * LANES)

    def write(comp_ref, base_ref):
        for first in range(0, units, 2):
            width = min(2, units - first)
            right = right_ref[first]
            if width == 2:
                right = jnp.concatenate([right, right_ref[first + 1]], axis=1)
            cols = pl.ds(pl.multiple_of(start + first * LANES, LANES), width * LANES)
            product = jnp.dot(base_ref[...], right, preferred_element_type=F32)
            out_ref[:, first * LANES : (first + width) * LANES] = (
                comp_ref[:, cols].astype(F32) - product
            ).astype(BF16)

    @pl.when(pl.program_id(1) == 0)
    def _():
        write(near_ref, base_near_ref)

    @pl.when(pl.program_id(1) == 1)
    def _():
        write(far_ref, base_far_ref)


def new_error(order, halves, near, far, base_near, base_far, right, units, held=None):
    count, cols = near.shape
    rank = base_near.shape[1]
    vmem = pl.BlockSpec(memory_space=pltpu.VMEM)
    blocks = order.shape[0]
    extra = [] if held is None else [held]
    return pl.pallas_call(
        error_kernel,
        grid_spec=pltpu.PrefetchScalarGridSpec(
            num_scalar_prefetch=2,
            grid=(blocks, 2),
            in_specs=[vmem] * 4
            + [pl.BlockSpec((units, rank, LANES), lambda j, h, order, halves: (j, 0, 0))]
            + [pl.BlockSpec(memory_space=pl.ANY)] * len(extra),
            out_specs=pl.BlockSpec(
                (count, units * LANES), lambda j, h, order, halves: (halves[h], order[j])
            ),
        ),
        out_shape=jax.ShapeDtypeStruct((2 * count, cols), BF16),
        input_output_aliases={7: 0} if extra else {},
        compiler_params=pltpu.CompilerParams(vmem_limit_bytes=24 * MIB),
        cost_estimate=pl.CostEstimate(
            flops=4 * count * blocks * units * LANES * rank,
            bytes_accessed=4 * count * blocks * units * LANES,
            transcendentals=0,
        ),
        name="new_error",
    )(order, halves, in_vmem(near), in_vmem(far), base_near, base_far, right, *extra)


class Exchange:
    def __init__(self, dp, mp):
        self.dp, self.mp = dp, mp
        mp_bits = [("mp", 1 << k) for k in range(mp.bit_length() - 1)]
        z_bits = [("dp", 2 << k) for k in range(dp.bit_length() - 2)]
        low, high = mp_bits[0], mp_bits[len(mp_bits) // 2]
        other = [bit for bit in mp_bits if bit not in (low, high)]
        self.scatter = [(low, high), (high, low)]
        rest = other + z_bits
        self.rest = list(zip(rest, rest[::-1]))
        self.replicas = list(zip(z_bits, z_bits[::-1]))
        self.other = other
        self.low, self.high = low[1], high[1]

    def send(self, x, step):
        pairs = []
        for d in range(self.dp):
            for m in range(self.mp):
                axis, bit = step[d % 2]
                to = (d ^ bit) * self.mp + m if axis == "dp" else d * self.mp + (m ^ bit)
                pairs.append((d * self.mp + m, to))
        return lax.ppermute(x, AXES, pairs)

    def core(self, x):
        return self.send(x, (("dp", 1), ("dp", 1)))

    def both_sum(self, x, step):
        sent, own = as_bf16(x)
        return own + self.send(sent, step).astype(F32)


def split3(x):
    high = lax.reduce_precision(x, 8, 7)
    mid = lax.reduce_precision(x - high, 8, 7)
    low = x - high - mid
    return jnp.stack([high, mid, low]).astype(BF16)


def join3(parts):
    parts = parts.astype(F32)
    return parts[0] + (parts[1] + parts[2])


def gram_of(block):
    return lax.dot_general(
        block, block, (((0,), (0,)), ((), ())), precision=lax.Precision.HIGHEST, preferred_element_type=F32
    )


def on_device(dp, mp, grad, error, init):
    grad, error = grad[0], error[0]
    rows, cols = grad.shape
    rank = init.shape[1]
    net = Exchange(dp, mp)
    units = cols // 8 // LANES

    d = lax.axis_index("dp").astype(jnp.int32)
    m = lax.axis_index("mp").astype(jnp.int32)
    core = d % 2
    low = (m & net.low) // net.low
    high = (m & net.high) // net.high

    def blocks_of(which_core):
        out = []
        for a in range(2):
            for b in range(2):
                flip_low = jnp.where(which_core == 0, a, b)
                flip_high = jnp.where(which_core == 0, b, a)
                out.append((high ^ flip_high) * 4 + (low ^ flip_low) * 2 + which_core)
        return jnp.stack(out).astype(jnp.int32)

    order_near, order_far = blocks_of(core), blocks_of(1 - core)
    halves = jnp.stack([core, 1 - core])

    comp_far, left_far = left_product(halves[1:], grad, error, init)
    arrived = net.core(left_far)
    comp_near, left_near = left_product(halves[:1], grad, error, init)
    left_near = left_near + arrived
    for step in net.replicas:
        left_near = net.both_sum(left_near, step)
    left_far = net.core(left_near)

    gram = gram_of(left_near) + gram_of(left_far)

    part_far = right_product(order_far, comp_near, comp_far, left_near, left_far, units, BF16)
    arrived = net.core(part_far)
    part = right_product(order_near, comp_near, comp_far, left_near, left_far, units, F32)
    part = part + arrived.astype(F32)

    for step in net.scatter:
        kept = part.shape[0] // 2
        sent = jnp.concatenate([part[kept:].astype(BF16), split3(gram)], axis=0)
        arrived = net.send(sent, step)
        part = part[:kept] + arrived[:kept].astype(F32)
        gram = gram + join3(arrived[kept:])
    for bit in net.other:
        gram = gram + net.send(gram, (bit, bit))

    lower = jnp.linalg.cholesky(gram)
    inverse = jax.scipy.linalg.solve_triangular(lower, jnp.eye(rank, dtype=F32), lower=True)

    first, later = net.rest[0], net.rest[1:]
    d_bit = jnp.where(core == 0, d & first[0][1] if first[0][0] == "dp" else m & first[0][1],
                      d & first[1][1] if first[1][0] == "dp" else m & first[1][1])
    upper = d_bit != 0
    top, bottom = part[:, : rank // 2], part[:, rank // 2 :]
    arrived = net.send(jnp.where(upper, top, bottom).astype(BF16), first)
    part = jnp.where(upper, bottom, top) + arrived.astype(F32)
    for step in later:
        part = net.both_sum(part, step)
    sent, own = as_bf16(part)
    arrived = net.send(sent, first)
    summed = jnp.where(
        upper, jnp.concatenate([arrived, sent], axis=1), jnp.concatenate([sent, arrived], axis=1)
    ).astype(F32)

    right = lax.dot_general(
        summed, inverse, (((1,), (1,)), ((), ())), precision=lax.Precision.HIGHEST, preferred_element_type=F32
    )
    right = (jnp.swapaxes(right, 1, 2) / dp).astype(BF16)

    def base_of(left):
        return lax.dot_general(
            left, inverse, (((1,), (1,)), ((), ())), precision=lax.Precision.HIGHEST, preferred_element_type=F32
        ).astype(BF16)

    base_near, base_far = base_of(left_near), base_of(left_far)

    for step in net.scatter[::-1]:
        right = jnp.concatenate([right, net.send(right, step)], axis=0)
    right_far = net.core(right)
    write = functools.partial(new_error, halves=halves, near=comp_near, far=comp_far,
                              base_near=base_near, base_far=base_far, units=units)
    out = write(order_near, right=right)
    out = write(order_far, right=right_far, held=out)

    share = cols // mp
    width = units * LANES
    covered = max(share, width)
    everything = jnp.concatenate([right, right_far], axis=0)
    names = jnp.concatenate([order_near, order_far])
    first_block = m * share // width
    picks = [
        lax.dynamic_slice_in_dim(everything, jnp.argmax(names == first_block + k) * units, units, 0)
        for k in range(covered // width)
    ]
    chosen = jnp.swapaxes(jnp.concatenate(picks, axis=0), 1, 2).reshape(covered, rank)
    right_factor = lax.dynamic_slice_in_dim(chosen, m * share - first_block * width, share, 0)
    return (out[None], right_factor)


def solution(mesh):
    return jax.shard_map(
        functools.partial(on_device, mesh.shape["dp"], mesh.shape["mp"]),
        mesh=mesh,
        in_specs=(P("dp", "mp", None), P("dp", "mp", None), P()),
        out_specs=(P("dp", "mp", None), P("mp", None)),
        check_vma=False,
    )
```

time: 392 us -> 169 us (0.43)
  waiting for transfers between devices: 296 us -> 41.4 us
  matrix products: 51.9 us -> 2.73 us
  local copies, waits for them, and re-layouts: 4.19 us -> 41 us
  Pallas kernels: 0 us -> 29.5 us
  starting transfers between devices: 0.34 us -> 23.4 us
  between operations: 13.8 us -> 2.25 us
    reduce_scatter x1 -> x0, waiting for transfers between devices: 137 us -> none  [reduce_factor(): lax.psum_scatter(lax.dot_general(compensated, ortho_basis, (((0,), (0,)),...]
    psum x2 -> x0, waiting for transfers between devices: 99.1 us -> none  [the longest x1 56.6 us: orthonormal(): summed = lax.psum(partial_value, 'dp')]
    all_gather x1 -> x0, waiting for transfers between devices: 60 us -> none  [on_device(): full_factor = lax.all_gather(factor_rows, ('dp', 'mp'), axis=0, tiled=True)]
    dot_general x4 -> x5, matrix products: 50.3 us -> 2.49 us  [the longest x2 1.18 us: gram_of(): lax.dot_general(block, block, (((0,), (0,)), ((), ())), precision=lax.Pre...]
    ppermute x0 -> x13, waiting for transfers between devices: none -> 41.4 us  [send(): return lax.ppermute(x, AXES, pairs)]
    unnamed x2 -> x26, local copies, waits for them, and re-layouts: 1.45 us -> 37.3 us
    pallas_call x0 -> x6, Pallas kernels: none -> 29.5 us  [the longest x2 12.6 us: new_error(): pl.pallas_call(error_kernel, grid_spec=pltpu.PrefetchScalarGridSpec(num_s...]
    ppermute x0 -> x13, starting transfers between devices: none -> 23.4 us  [send(): return lax.ppermute(x, AXES, pairs)]
  transfers between devices with their start and end apart: 4 -> 13, of which waited for: 4 -> 9; matrix products, arithmetic and copies ran while one was open for 0% -> 10% of each run, Pallas kernels for 0% -> 9%
where the time goes in v1:
time: 169 us; the launch traced here: 168 us
  waiting for transfers between devices  41.4 us (24%)
  local copies, waits for them, and re-layouts  41 us (24%)
  Pallas kernels  29.5 us (17%)
  other arithmetic  27.9 us (17%)
  starting transfers between devices  23.4 us (14%)
  matrix products  2.73 us (2%)
  between operations  2.25 us (1%)
    ppermute x13, waiting for transfers between devices, send(): return lax.ppermute(x, AXES, pairs)  41.4 us
    unnamed x26, local copies, waits for them, and re-layouts  37.3 us
    ppermute x13, starting transfers between devices, send(): return lax.ppermute(x, AXES, pairs)  23.4 us
    pallas_call x2, Pallas kernels, new_error(): pl.pallas_call(error_kernel, grid_spec=pltpu.PrefetchScalarGridSpec(num_s...  12.6 us
    another operation x3, other arithmetic, on_device(): lower = jnp.linalg.cholesky(gram)  12.4 us
    pallas_call x2, Pallas kernels, left_product(): pl.pallas_call(left_kernel, grid_spec=pltpu.PrefetchScalarGridSpec(num_sc...  11.7 us
    another operation x2, other arithmetic, on_device(): jax.scipy.linalg.solve_triangular(lower, jnp.eye(rank, dtype=F32), lower=...  10.5 us
    pallas_call x2, Pallas kernels, right_product(): pl.pallas_call(right_kernel, grid_spec=pltpu.PrefetchScalarGridSpec(num_s...  5.24 us
  transfers between devices with their start and end apart: 13, of which 9 were waited for; matrix products, arithmetic and copies ran while one was open for 10% of the time, Pallas kernels for 9%

profile of v1, /device:TPU:1, one launch (start us, length us, event | category | flops | bytes accessed | tf_op | source)
XLA Modules:
  0.0 168.2 jit_solution(10648281471738949835)
XLA Ops:
  0.7 5.2 %copy-done.10 = bf16[1,1024,7168]{2,1,0:T(8,128)(2,1)S(1)} copy-done((bf16[1,1024,7168]{2,1,0:T(8,128)(2,1)S(1)}, bf16[1,1024,7168]{2,1,0:T(8,128)(2,1)}, u32[]{:S(2)}) %copy-start.10) | copy-done | bytes 14680088
  5.8 1.5 copy-done.12
  7.3 6.0 %left_product.3 = (bf16[512,7168]{1,0:T(8,128)(2,1)S(1)}, f32[512,128]{1,0:T(8,128)S(1)}) custom-call(s32[1]{0:T(128)} %bitcast.5.half_ref, bf16[1024,7168]{1,0:T(8,128)(2,1)S(1)} %bitcast.59, bf16[1024,7168]{1,0:T(8,128)(2,1)} %bitcast.62, bf16[7168,128]{1,0:T(8,128)(2,1)S(1)} %copy-done.12), custom_call_target="tpu_custom_call" | custom-call | flops 939524096 | bytes 14680064 | tf_op jit(solution)/shard_map/left_product/pallas_call | solution.py:36
  13.4 3.0 %copy-done = bf16[512,7168]{1,0:T(8,128)(2,1)} copy-done((bf16[512,7168]{1,0:T(8,128)(2,1)}, bf16[512,7168]{1,0:T(8,128)(2,1)S(1)}, u32[]{:S(2)}) %copy-start) | copy-done | bytes 7340056
  16.4 5.7 %left_product.2 = (bf16[512,7168]{1,0:T(8,128)(2,1)S(1)}, f32[512,128]{1,0:T(8,128)S(1)}) custom-call(s32[1]{0:T(128)} %bitcast.4.half_ref, bf16[1024,7168]{1,0:T(8,128)(2,1)S(1)} %bitcast.60, bf16[1024,7168]{1,0:T(8,128)(2,1)} %bitcast.63, bf16[7168,128]{1,0:T(8,128)(2,1)S(1)} %copy-done.12), custom_call_target="tpu_custom_call" | custom-call | flops 939524096 | bytes 14680064 | tf_op jit(solution)/shard_map/left_product/pallas_call | solution.py:36
  22.1 2.9 %copy-done.5 = bf16[512,7168]{1,0:T(8,128)(2,1)} copy-done((bf16[512,7168]{1,0:T(8,128)(2,1)}, bf16[512,7168]{1,0:T(8,128)(2,1)S(1)}, u32[]{:S(2)}) %copy-start.5) | copy-done | bytes 7340056
  25.1 3.8 %collective-permute-start.1 = (bf16[512,128]{1,0:T(8,128)(2,1)S(1)}, bf16[512,128]{1,0:T(8,128)(2,1)S(1)}, u32[]{:S(2)}, u32[]{:S(2)}) collective-permute-start(bf16[512,128]{1,0:T(8,128)(2,1)S(1)} %fusion.30), channel_id=1, source_target_pairs={{0,8},{1,9},{2,10},{3,11},{4,20},{5,21},{6,22},{7,23},{8,0},{9,1},... | collective-permute-start | bytes 393224 | tf_op jit(solution)/shard_map/ppermute | solution.py:185
  28.9 3.3 %collective-permute-done.1 = bf16[512,128]{1,0:T(8,128)(2,1)S(1)} collective-permute-done((bf16[512,128]{1,0:T(8,128)(2,1)S(1)}, bf16[512,128]{1,0:T(8,128)(2,1)S(1)}, u32[]{:S(2)}, u32[]{:S(2)}) %collective-permute-start.1) | collective-permute-done | bytes 131104 | tf_op jit(solution)/shard_map/ppermute | solution.py:185
  32.3 1.4 collective-permute-start.2
  33.7 2.8 %collective-permute-done.2 = bf16[512,128]{1,0:T(8,128)(2,1)S(1)} collective-permute-done((bf16[512,128]{1,0:T(8,128)(2,1)S(1)}, bf16[512,128]{1,0:T(8,128)(2,1)S(1)}, u32[]{:S(2)}, u32[]{:S(2)}) %collective-permute-start.2) | collective-permute-done | bytes 131104 | tf_op jit(solution)/shard_map/ppermute | solution.py:185
  36.5 0.1 convert_add_fusion.1.left_near_ref
  36.6 2.1 %collective-permute-start.3 = (f32[512,128]{1,0:T(8,128)S(1)}, f32[512,128]{1,0:T(8,128)S(1)}, u32[]{:S(2)}, u32[]{:S(2)}) collective-permute-start(f32[512,128]{1,0:T(8,128)S(1)} %convert_add_fusion.1.left_near_ref), channel_id=1, source_target_pairs={{0,4},{1,5},{2,6},{3,7},{4,0},{5,1},{6,2},{7,3},{8,12},{9,13},{10,... | collective-permute-start | bytes 786440 | tf_op jit(solution)/shard_map/ppermute | solution.py:185
  38.7 1.1 collective-permute-done.3.left_far_ref
  39.8 3.1 %copy-done.1 = bf16[512,7168]{1,0:T(8,128)(2,1)S(1)} copy-done((bf16[512,7168]{1,0:T(8,128)(2,1)S(1)}, bf16[512,7168]{1,0:T(8,128)(2,1)}, u32[]{:S(2)}) %copy-start.1) | copy-done | bytes 7340056
  42.9 3.1 %copy-done.6 = bf16[512,7168]{1,0:T(8,128)(2,1)S(1)} copy-done((bf16[512,7168]{1,0:T(8,128)(2,1)S(1)}, bf16[512,7168]{1,0:T(8,128)(2,1)}, u32[]{:S(2)}) %copy-start.6) | copy-done | bytes 7340056
  46.0 2.6 %right_product.3 = bf16[28,128,128]{2,1,0:T(8,128)(2,1)S(1)} custom-call(s32[4]{0:T(128)S(1)} %pad_add_fusion.order_ref, bf16[512,7168]{1,0:T(8,128)(2,1)S(1)} %copy-done.6, bf16[512,7168]{1,0:T(8,128)(2,1)S(1)} %copy-done.1, f32[512,128]{1,0:T(8,128)S(1)} %convert_add_fusion.1.left_near_ref, f32[512,128]{1,0:T(8,128)S(1)} %collective-permute-done.3.left_far_ref), custom_call_target="tpu_custom_call" | custom-call | flops 939524096 | bytes 4194304 | tf_op jit(solution)/shard_map/right_product/pallas_call | solution.py:85
  48.6 0.7 copy.14
  49.3 0.5 collective-permute-start.4
  49.8 3.1 %copy-done.2 = bf16[512,7168]{1,0:T(8,128)(2,1)S(1)} copy-done((bf16[512,7168]{1,0:T(8,128)(2,1)S(1)}, bf16[512,7168]{1,0:T(8,128)(2,1)}, u32[]{:S(2)}) %copy-start.2) | copy-done | bytes 7340056
  52.9 3.1 %copy-done.7 = bf16[512,7168]{1,0:T(8,128)(2,1)S(1)} copy-done((bf16[512,7168]{1,0:T(8,128)(2,1)S(1)}, bf16[512,7168]{1,0:T(8,128)(2,1)}, u32[]{:S(2)}) %copy-start.7) | copy-done | bytes 7340056
  56.0 2.6 %right_product.2 = f32[28,128,128]{2,1,0:T(8,128)S(1)} custom-call(s32[4]{0:T(128)S(1)} %pad_add_fusion.2.order_ref, bf16[512,7168]{1,0:T(8,128)(2,1)S(1)} %copy-done.7, bf16[512,7168]{1,0:T(8,128)(2,1)S(1)} %copy-done.2, f32[512,128]{1,0:T(8,128)S(1)} %convert_add_fusion.1.left_near_ref, f32[512,128]{1,0:T(8,128)S(1)} %collective-permute-done.3.left_far_ref), custom_call_target="tpu_custom_call" | custom-call | flops 939524096 | bytes 4194304 | tf_op jit(solution)/shard_map/right_product/pallas_call | solution.py:85
  58.6 1.7 %copy.15 = f32[28,128,128]{1,2,0:T(8,128)} copy(f32[28,128,128]{2,1,0:T(8,128)S(1)} %right_product.2) | data formatting | bytes 3670016 | tf_op jit(solution)/shard_map/right_product/pallas_call | solution.py:85
  60.3 0.6 fusion.32
  60.9 0.6 convolution_add_fusion
  61.5 1.9 %convert_add_fusion = f32[28,128,128]{1,2,0:T(8,128)S(1)} fusion(f32[28,128,128]{1,2,0:T(8,128)} %copy.15, bf16[28,128,128]{1,2,0:T(8,128)(2,1)} %collective-permute-done.4), kind=kLoop, calls=%fused_computation.1 | loop fusion | flops 917504 | bytes 4587520 | tf_op jit(solution)/shard_map/add | solution.py:251
  63.6 0.1 pad_maximum_fusion.2
  63.7 2.7 %collective-permute-start.5 = (bf16[17,128,128]{1,2,0:T(8,128)(2,1)S(1)}, bf16[17,128,128]{1,2,0:T(8,128)(2,1)S(1)}, u32[]{:S(2)}, u32[]{:S(2)}) collective-permute-start(bf16[17,128,128]{1,2,0:T(8,128)(2,1)S(1)} %pad_maximum_fusion.2), channel_id=1, source_target_pairs={{0,1},{1,0},{2,3},{3,2},{4,6},{5,7},{6,4},{7,5},{8,9},{9,8},{10,11... | collective-permute-start | bytes 1671176 | tf_op jit(solution)/shard_map/ppermute | solution.py:185
  66.4 7.2 %collective-permute-done.5 = bf16[17,128,128]{1,2,0:T(8,128)(2,1)S(1)} collective-permute-done((bf16[17,128,128]{1,2,0:T(8,128)(2,1)S(1)}, bf16[17,128,128]{1,2,0:T(8,128)(2,1)S(1)}, u32[]{:S(2)}, u32[]{:S(2)}) %collective-permute-start.5) | collective-permute-done | bytes 557088 | tf_op jit(solution)/shard_map/ppermute | solution.py:185
  73.7 0.1 slice_add_fusion
  73.9 1.5 collective-permute-start.6
  75.4 4.8 %collective-permute-done.6 = bf16[10,128,128]{1,2,0:T(8,128)(2,1)S(1)} collective-permute-done((bf16[10,128,128]{1,2,0:T(8,128)(2,1)S(1)}, bf16[10,128,128]{1,2,0:T(8,128)(2,1)S(1)}, u32[]{:S(2)}, u32[]{:S(2)}) %collective-permute-start.6) | collective-permute-done | bytes 327712 | tf_op jit(solution)/shard_map/ppermute | solution.py:185
  80.2 0.1 copy.16
  80.4 11.7 %cholesky.17 = f32[128,128]{1,0:T(8,128)S(1)} custom-call(f32[128,128]{1,0:T(8,128)S(1)} %fusion.21), custom_call_target="Cholesky" | custom-call | tf_op jit(solution)/shard_map/jit(cholesky)/cholesky | solution.py:262
  92.1 0.1 select_convert_fusion
  92.3 1.2 collective-permute-start.7
  93.5 0.6 compare_reduce_fusion.2
  94.1 6.4 %collective-permute-done.7 = bf16[7,64,128]{1,2,0:T(8,128)(2,1)S(1)} collective-permute-done((bf16[7,64,128]{1,2,0:T(8,128)(2,1)S(1)}, bf16[7,64,128]{1,2,0:T(8,128)(2,1)S(1)}, u32[]{:S(2)}, u32[]{:S(2)}) %collective-permute-start.7) | collective-permute-done | bytes 114720 | tf_op jit(solution)/shard_map/ppermute | solution.py:185
  100.6 0.2 fusion.29
  100.8 0.7 fusion.9
  101.5 9.8 %custom-call.7 = f32[1,128,128]{1,2,0:T(8,128)S(1)} custom-call(f32[1,128,128]{2,1,0:T(8,128)S(1)} %fusion.9), custom_call_target="InvertDiagBlocksLowerTriangular" | custom-call | tf_op jit(solution)/shard_map/jit(_solve_triangular)/triangular_solve | solution.py:263
  111.3 0.2 reduce-precision_convert_fusion
  111.5 2.5 %collective-permute-start.9 = (bf16[7,64,128]{1,2,0:T(8,128)(2,1)S(1)}, bf16[7,64,128]{1,2,0:T(8,128)(2,1)S(1)}, u32[]{:S(2)}, u32[]{:S(2)}) collective-permute-start(bf16[7,64,128]{1,2,0:T(8,128)(2,1)S(1)} %reduce-precision_convert_fusion), channel_id=1, source_target_pairs={{0,8},{1,9},{2,10},{3,11},{4,20},{5,21},{6,22},{7,23},{8,0},{9,1},... | collective-permute-start | bytes 344072 | tf_op jit(solution)/shard_map/ppermute | solution.py:185
  114.0 0.2 fusion.19
  114.2 5.7 %collective-permute-done.9 = bf16[7,64,128]{1,2,0:T(8,128)(2,1)S(1)} collective-permute-done((bf16[7,64,128]{1,2,0:T(8,128)(2,1)S(1)}, bf16[7,64,128]{1,2,0:T(8,128)(2,1)S(1)}, u32[]{:S(2)}, u32[]{:S(2)}) %collective-permute-start.9) | collective-permute-done | bytes 114720 | tf_op jit(solution)/shard_map/ppermute | solution.py:185
  120.0 0.6 fusion.1
  120.5 1.5 collective-permute-start.10
  122.1 3.4 %collective-permute-done.10 = bf16[7,128,128]{2,1,0:T(8,128)(2,1)S(1)} collective-permute-done((bf16[7,128,128]{2,1,0:T(8,128)(2,1)S(1)}, bf16[7,128,128]{2,1,0:T(8,128)(2,1)S(1)}, u32[]{:S(2)}, u32[]{:S(2)}) %collective-permute-start.10) | collective-permute-done | bytes 229408 | tf_op jit(solution)/shard_map/ppermute | solution.py:185
  125.5 1.6 collective-permute-start.11
  127.1 0.1 concatenate.39
  127.2 6.6 %collective-permute-done.11 = bf16[14,128,128]{2,1,0:T(8,128)(2,1)S(1)} collective-permute-done((bf16[14,128,128]{2,1,0:T(8,128)(2,1)S(1)}, bf16[14,128,128]{2,1,0:T(8,128)(2,1)S(1)}, u32[]{:S(2)}, u32[]{:S(2)}) %collective-permute-start.11) | collective-permute-done | bytes 458784 | tf_op jit(solution)/shard_map/ppermute | solution.py:185
  133.8 0.1 pad_maximum_fusion.1.right_ref
  133.9 4.6 %collective-permute-start.12 = (bf16[28,128,128]{2,1,0:T(8,128)(2,1)S(1)}, bf16[28,128,128]{2,1,0:T(8,128)(2,1)S(1)}, u32[]{:S(2)}, u32[]{:S(2)}) collective-permute-start(bf16[28,128,128]{2,1,0:T(8,128)(2,1)S(1)} %pad_maximum_fusion.1.right_ref), channel_id=1, source_target_pairs={{0,4},{1,5},{2,6},{3,7},{4,0},{5,1},{6,2},{7,3},{8,12},{9,13},{10,... | collective-permute-start | bytes 2752520 | tf_op jit(solution)/shard_map/ppermute | solution.py:185
  138.5 0.7 compare_reduce_fusion
  139.8 0.7 compare_reduce_fusion.1
  141.3 0.4 convolution_convert_fusion.1.base_near_ref
  141.7 0.4 convolution_convert_fusion.base_far_ref
  142.0 3.1 %copy-done.3 = bf16[512,7168]{1,0:T(8,128)(2,1)S(1)} copy-done((bf16[512,7168]{1,0:T(8,128)(2,1)S(1)}, bf16[512,7168]{1,0:T(8,128)(2,1)}, u32[]{:S(2)}) %copy-start.3) | copy-done | bytes 7340056
  145.1 3.1 %copy-done.8 = bf16[512,7168]{1,0:T(8,128)(2,1)S(1)} copy-done((bf16[512,7168]{1,0:T(8,128)(2,1)S(1)}, bf16[512,7168]{1,0:T(8,128)(2,1)}, u32[]{:S(2)}) %copy-start.8) | copy-done | bytes 7340056
  148.2 6.3 %new_error.2.rest_0_ = bf16[1024,7168]{1,0:T(8,128)(2,1)} custom-call(s32[4]{0:T(128)S(1)} %pad_add_fusion.2.order_ref, s32[2]{0:T(128)S(1)} %pad_add_fusion.1.halves_ref, bf16[512,7168]{1,0:T(8,128)(2,1)S(1)} %copy-done.8, bf16[512,7168]{1,0:T(8,128)(2,1)S(1)} %copy-done.3, bf16[512,128]{1,0:T(8,128)(2,1)S(1)} %convolution_convert_fusion.1.base_near_ref, ...), custom_call_target="tpu_custom_call" | custom-call | flops 939524096 | bytes 7340032 | tf_op jit(solution)/shard_map/new_error/pallas_call | solution.py:140
  154.5 0.2 pad_maximum_fusion
  154.8 1.0 copy.18
  155.8 3.1 %copy-done.4 = bf16[512,7168]{1,0:T(8,128)(2,1)S(1)} copy-done((bf16[512,7168]{1,0:T(8,128)(2,1)S(1)}, bf16[512,7168]{1,0:T(8,128)(2,1)}, u32[]{:S(2)}) %copy-start.4) | copy-done | bytes 7340056
  158.9 3.1 %copy-done.9 = bf16[512,7168]{1,0:T(8,128)(2,1)S(1)} copy-done((bf16[512,7168]{1,0:T(8,128)(2,1)S(1)}, bf16[512,7168]{1,0:T(8,128)(2,1)}, u32[]{:S(2)}) %copy-start.9) | copy-done | bytes 7340056
  161.9 6.3 %new_error.3 = bf16[1024,7168]{1,0:T(8,128)(2,1)} custom-call(s32[4]{0:T(128)S(1)} %pad_add_fusion.order_ref, s32[2]{0:T(128)S(1)} %pad_add_fusion.1.halves_ref, bf16[512,7168]{1,0:T(8,128)(2,1)S(1)} %copy-done.9, bf16[512,7168]{1,0:T(8,128)(2,1)S(1)} %copy-done.4, ...), custom_call_target="tpu_custom_call", output_to_operand_aliasing={{}: (7, {})} | custom-call | flops 939524096 | bytes 7340032 | tf_op jit(solution)/shard_map/new_error/pallas_call | solution.py:140
  (40 shorter events, 1.0 us)
Async XLA Ops:
  0.6 5.2 %copy-start.10 = (bf16[1,1024,7168]{2,1,0:T(8,128)(2,1)S(1)}, bf16[1,1024,7168]{2,1,0:T(8,128)(2,1)}, u32[]{:S(2)}) copy-start(bf16[1,1024,7168]{2,1,0:T(8,128)(2,1)} %param.3) | copy-start | bytes 44040196
  5.8 1.5 copy-start.12
  7.3 9.1 %copy-start.11 = (bf16[1,1024,7168]{2,1,0:T(8,128)(2,1)S(1)}, bf16[1,1024,7168]{2,1,0:T(8,128)(2,1)}, u32[]{:S(2)}) copy-start(bf16[1,1024,7168]{2,1,0:T(8,128)(2,1)} %param.3) | copy-start | bytes 44040196
  13.4 3.0 %copy-start = (bf16[512,7168]{1,0:T(8,128)(2,1)}, bf16[512,7168]{1,0:T(8,128)(2,1)S(1)}, u32[]{:S(2)}) copy-start(bf16[512,7168]{1,0:T(8,128)(2,1)S(1)} %get-tuple-element.9.far_ref) | copy-start | bytes 22020100
  16.4 8.7 %collective-permute-start = (f32[512,128]{1,0:T(8,128)S(1)}, f32[512,128]{1,0:T(8,128)S(1)}, u32[]{:S(2)}, u32[]{:S(2)}) collective-permute-start(f32[512,128]{1,0:T(8,128)S(1)} %get-tuple-element.11), channel_id=1, source_target_pairs={{0,4},{1,5},{2,6},{3,7},{4,0},{5,1},{6,2},{7,3},{8,12},{9,13},{10,... | collective-permute-start | bytes 786440 | tf_op jit(solution)/shard_map/ppermute | solution.py:185
  22.1 2.9 %copy-start.5 = (bf16[512,7168]{1,0:T(8,128)(2,1)}, bf16[512,7168]{1,0:T(8,128)(2,1)S(1)}, u32[]{:S(2)}) copy-start(bf16[512,7168]{1,0:T(8,128)(2,1)S(1)} %get-tuple-element.8.near_ref) | copy-start | bytes 22020100
  25.1 7.1 %collective-permute-start.1 = (bf16[512,128]{1,0:T(8,128)(2,1)S(1)}, bf16[512,128]{1,0:T(8,128)(2,1)S(1)}, u32[]{:S(2)}, u32[]{:S(2)}) collective-permute-start(bf16[512,128]{1,0:T(8,128)(2,1)S(1)} %fusion.30), channel_id=1, source_target_pairs={{0,8},{1,9},{2,10},{3,11},{4,20},{5,21},{6,22},{7,23},{8,0},{9,1},... | collective-permute-start | bytes 393224 | tf_op jit(solution)/shard_map/ppermute | solution.py:185
  32.3 4.2 %collective-permute-start.2 = (bf16[512,128]{1,0:T(8,128)(2,1)S(1)}, bf16[512,128]{1,0:T(8,128)(2,1)S(1)}, u32[]{:S(2)}, u32[]{:S(2)}) collective-permute-start(bf16[512,128]{1,0:T(8,128)(2,1)S(1)} %fusion.8), channel_id=1, source_target_pairs={{0,16},{1,17},{2,18},{3,19},{4,12},{5,13},{6,14},{7,15},{8,24},{9,... | collective-permute-start | bytes 393224 | tf_op jit(solution)/shard_map/ppermute | solution.py:185
  36.6 3.2 %collective-permute-start.3 = (f32[512,128]{1,0:T(8,128)S(1)}, f32[512,128]{1,0:T(8,128)S(1)}, u32[]{:S(2)}, u32[]{:S(2)}) collective-permute-start(f32[512,128]{1,0:T(8,128)S(1)} %convert_add_fusion.1.left_near_ref), channel_id=1, source_target_pairs={{0,4},{1,5},{2,6},{3,7},{4,0},{5,1},{6,2},{7,3},{8,12},{9,13},{10,... | collective-permute-start | bytes 786440 | tf_op jit(solution)/shard_map/ppermute | solution.py:185
  39.8 3.1 %copy-start.1 = (bf16[512,7168]{1,0:T(8,128)(2,1)S(1)}, bf16[512,7168]{1,0:T(8,128)(2,1)}, u32[]{:S(2)}) copy-start(bf16[512,7168]{1,0:T(8,128)(2,1)} %copy-done) | copy-start | bytes 22020100
  42.9 3.1 %copy-start.6 = (bf16[512,7168]{1,0:T(8,128)(2,1)S(1)}, bf16[512,7168]{1,0:T(8,128)(2,1)}, u32[]{:S(2)}) copy-start(bf16[512,7168]{1,0:T(8,128)(2,1)} %copy-done.5) | copy-start | bytes 22020100
  49.3 12.2 %collective-permute-start.4 = (bf16[28,128,128]{1,2,0:T(8,128)(2,1)S(1)}, bf16[28,128,128]{1,2,0:T(8,128)(2,1)}, u32[]{:S(2)}, u32[]{:S(2)}) collective-permute-start(bf16[28,128,128]{1,2,0:T(8,128)(2,1)S(1)} %copy.14), channel_id=1, source_target_pairs={{0,4},{1,5},{2,6},{3,7},{4,0},{5,1},{6,2},{7,3},{8,12},{9,13},{10,... | collective-permute-start | bytes 2752520 | tf_op jit(solution)/shard_map/ppermute | solution.py:185
  49.8 3.1 %copy-start.2 = (bf16[512,7168]{1,0:T(8,128)(2,1)S(1)}, bf16[512,7168]{1,0:T(8,128)(2,1)}, u32[]{:S(2)}) copy-start(bf16[512,7168]{1,0:T(8,128)(2,1)} %copy-done) | copy-start | bytes 22020100
  52.9 3.1 %copy-start.7 = (bf16[512,7168]{1,0:T(8,128)(2,1)S(1)}, bf16[512,7168]{1,0:T(8,128)(2,1)}, u32[]{:S(2)}) copy-start(bf16[512,7168]{1,0:T(8,128)(2,1)} %copy-done.5) | copy-start | bytes 22020100
  63.7 9.9 %collective-permute-start.5 = (bf16[17,128,128]{1,2,0:T(8,128)(2,1)S(1)}, bf16[17,128,128]{1,2,0:T(8,128)(2,1)S(1)}, u32[]{:S(2)}, u32[]{:S(2)}) collective-permute-start(bf16[17,128,128]{1,2,0:T(8,128)(2,1)S(1)} %pad_maximum_fusion.2), channel_id=1, source_target_pairs={{0,1},{1,0},{2,3},{3,2},{4,6},{5,7},{6,4},{7,5},{8,9},{9,8},{10,11... | collective-permute-start | bytes 1671176 | tf_op jit(solution)/shard_map/ppermute | solution.py:185
  73.9 6.3 %collective-permute-start.6 = (bf16[10,128,128]{1,2,0:T(8,128)(2,1)S(1)}, bf16[10,128,128]{1,2,0:T(8,128)(2,1)S(1)}, u32[]{:S(2)}, u32[]{:S(2)}) collective-permute-start(bf16[10,128,128]{1,2,0:T(8,128)(2,1)S(1)} %pad_maximum_fusion.4), channel_id=1, source_target_pairs={{0,2},{1,3},{2,0},{3,1},{4,5},{5,4},{6,7},{7,6},{8,10},{9,11},{10,... | collective-permute-start | bytes 983048 | tf_op jit(solution)/shard_map/ppermute | solution.py:185
  92.3 8.3 %collective-permute-start.7 = (bf16[7,64,128]{1,2,0:T(8,128)(2,1)S(1)}, bf16[7,64,128]{1,2,0:T(8,128)(2,1)S(1)}, u32[]{:S(2)}, u32[]{:S(2)}) collective-permute-start(bf16[7,64,128]{1,2,0:T(8,128)(2,1)S(1)} %select_convert_fusion), channel_id=1, source_target_pairs={{0,8},{1,9},{2,10},{3,11},{4,20},{5,21},{6,22},{7,23},{8,0},{9,1},... | collective-permute-start | bytes 344072 | tf_op jit(solution)/shard_map/ppermute | solution.py:185
  100.8 10.6 %collective-permute-start.8 = (bf16[7,64,128]{1,2,0:T(8,128)(2,1)S(1)}, bf16[7,64,128]{1,2,0:T(8,128)(2,1)S(1)}, u32[]{:S(2)}, u32[]{:S(2)}) collective-permute-start(bf16[7,64,128]{1,2,0:T(8,128)(2,1)S(1)} %fusion.29), channel_id=1, source_target_pairs={{0,16},{1,17},{2,18},{3,19},{4,12},{5,13},{6,14},{7,15},{8,24},{9,... | collective-permute-start | bytes 344072 | tf_op jit(solution)/shard_map/ppermute | solution.py:185
  111.5 8.4 %collective-permute-start.9 = (bf16[7,64,128]{1,2,0:T(8,128)(2,1)S(1)}, bf16[7,64,128]{1,2,0:T(8,128)(2,1)S(1)}, u32[]{:S(2)}, u32[]{:S(2)}) collective-permute-start(bf16[7,64,128]{1,2,0:T(8,128)(2,1)S(1)} %reduce-precision_convert_fusion), channel_id=1, source_target_pairs={{0,8},{1,9},{2,10},{3,11},{4,20},{5,21},{6,22},{7,23},{8,0},{9,1},... | collective-permute-start | bytes 344072 | tf_op jit(solution)/shard_map/ppermute | solution.py:185
  120.5 5.0 %collective-permute-start.10 = (bf16[7,128,128]{2,1,0:T(8,128)(2,1)S(1)}, bf16[7,128,128]{2,1,0:T(8,128)(2,1)S(1)}, u32[]{:S(2)}, u32[]{:S(2)}) collective-permute-start(bf16[7,128,128]{2,1,0:T(8,128)(2,1)S(1)} %fusion.1), channel_id=1, source_target_pairs={{0,2},{1,3},{2,0},{3,1},{4,5},{5,4},{6,7},{7,6},{8,10},{9,11},{10,... | collective-permute-start | bytes 688136 | tf_op jit(solution)/shard_map/ppermute | solution.py:185
  125.5 8.3 %collective-permute-start.11 = (bf16[14,128,128]{2,1,0:T(8,128)(2,1)S(1)}, bf16[14,128,128]{2,1,0:T(8,128)(2,1)S(1)}, u32[]{:S(2)}, u32[]{:S(2)}) collective-permute-start(bf16[14,128,128]{2,1,0:T(8,128)(2,1)S(1)} %pad_maximum_fusion.3), channel_id=1, source_target_pairs={{0,1},{1,0},{2,3},{3,2},{4,6},{5,7},{6,4},{7,5},{8,9},{9,8},{10,11... | collective-permute-start | bytes 1376264 | tf_op jit(solution)/shard_map/ppermute | solution.py:185
  133.9 20.6 %collective-permute-start.12 = (bf16[28,128,128]{2,1,0:T(8,128)(2,1)S(1)}, bf16[28,128,128]{2,1,0:T(8,128)(2,1)S(1)}, u32[]{:S(2)}, u32[]{:S(2)}) collective-permute-start(bf16[28,128,128]{2,1,0:T(8,128)(2,1)S(1)} %pad_maximum_fusion.1.right_ref), channel_id=1, source_target_pairs={{0,4},{1,5},{2,6},{3,7},{4,0},{5,1},{6,2},{7,3},{8,12},{9,13},{10,... | collective-permute-start | bytes 2752520 | tf_op jit(solution)/shard_map/ppermute | solution.py:185
  142.0 3.1 %copy-start.3 = (bf16[512,7168]{1,0:T(8,128)(2,1)S(1)}, bf16[512,7168]{1,0:T(8,128)(2,1)}, u32[]{:S(2)}) copy-start(bf16[512,7168]{1,0:T(8,128)(2,1)} %copy-done) | copy-start | bytes 22020100
  145.1 3.1 %copy-start.8 = (bf16[512,7168]{1,0:T(8,128)(2,1)S(1)}, bf16[512,7168]{1,0:T(8,128)(2,1)}, u32[]{:S(2)}) copy-start(bf16[512,7168]{1,0:T(8,128)(2,1)} %copy-done.5) | copy-start | bytes 22020100
  155.8 3.1 %copy-start.4 = (bf16[512,7168]{1,0:T(8,128)(2,1)S(1)}, bf16[512,7168]{1,0:T(8,128)(2,1)}, u32[]{:S(2)}) copy-start(bf16[512,7168]{1,0:T(8,128)(2,1)} %copy-done) | copy-start | bytes 22020100
  158.9 3.1 %copy-start.9 = (bf16[512,7168]{1,0:T(8,128)(2,1)S(1)}, bf16[512,7168]{1,0:T(8,128)(2,1)}, u32[]{:S(2)}) copy-start(bf16[512,7168]{1,0:T(8,128)(2,1)} %copy-done.5) | copy-start | bytes 22020100

commit v2 on v0

v2 whole, which is shorter than its diff:
```python
import functools

import jax
import jax.numpy as jnp
import numpy as np
from jax import lax
from jax.experimental import pallas as pl
from jax.experimental.pallas import tpu as pltpu
from jax.sharding import PartitionSpec as P

F32 = jnp.float32
BF16 = jnp.bfloat16
LANES = 128
MIB = 1024 * 1024
AXES = ("dp", "mp")
PIECES = 14
LEAF = 8

VMEM = pl.BlockSpec(memory_space=pltpu.VMEM)
HBM = pl.BlockSpec(memory_space=pltpu.HBM)
SMEM = pl.BlockSpec(memory_space=pltpu.SMEM)

HALF, NEAR, FAR, UPPER, WIDTH = 0, 2, 6, 10, 16


def call(kernel, name, outs, ins, vmem_mib, micros, **more):
    return pl.pallas_call(
        kernel,
        out_shape=outs,
        in_specs=ins,
        compiler_params=pltpu.CompilerParams(vmem_limit_bytes=vmem_mib * MIB),
        cost_estimate=pl.CostEstimate(flops=0, bytes_accessed=int(micros * 3.5e6), transcendentals=0),
        name=name,
        **more,
    )


def shaped(shape, dtype):
    return jax.ShapeDtypeStruct(shape, dtype)


def in_hbm(x):
    return pltpu.with_memory_space_constraint(x, pltpu.HBM)


def in_vmem(x):
    return pltpu.with_memory_space_constraint(x, pltpu.VMEM)


def left_kernel(pieces, table, grad, error, init, comp, near, far, error_v, init_v, sems):
    rows, cols = comp.shape
    count, width = rows // 2, cols // pieces

    def copies(i):
        at = pl.ds(i * width, width)
        out = [pltpu.make_async_copy(init.at[at], init_v.at[at], sems.at[4, i])]
        for half in range(2):
            source = pl.ds(pl.multiple_of(table[HALF + half] * count, count), count)
            target = pl.ds(half * count, count)
            out.append(pltpu.make_async_copy(grad.at[source, at], comp.at[target, at], sems.at[half, i]))
            out.append(pltpu.make_async_copy(error.at[source, at], error_v.at[target, at], sems.at[2 + half, i]))
        return out

    for i in range(pieces):
        for copy in copies(i):
            copy.start()
    for i in range(pieces):
        for copy in copies(i):
            copy.wait()
        at = pl.ds(i * width, width)
        total = (comp[:, at].astype(F32) + error_v[:, at].astype(F32)).astype(BF16)
        comp[:, at] = total
        part = lax.dot_general(init_v[at].T, total, (((1,), (1,)), ((), ())), preferred_element_type=F32)
        if i == 0:
            near[...] = part[:, :count]
            far[...] = part[:, count:]
        else:
            near[...] += part[:, :count]
            far[...] += part[:, count:]


def left_product(table, grad, error, init):
    rows, cols = grad.shape
    rank = init.shape[1]
    return call(
        functools.partial(left_kernel, PIECES),
        "left_product",
        [pltpu.VMEM((rows, cols), BF16), shaped((rank, rows // 2), F32), shaped((rank, rows // 2), F32)],
        [SMEM, HBM, HBM, HBM],
        26,
        12,
        out_specs=[VMEM] * 3,
        scratch_shapes=[
            pltpu.VMEM((rows, cols), BF16),
            pltpu.VMEM((cols, rank), BF16),
            pltpu.SemaphoreType.DMA((5, PIECES)),
        ],
    )(table, in_hbm(grad), in_hbm(error), in_hbm(init))


def right_kernel(units, first, table, comp, near, far, out):
    rows = comp.shape[0]
    count = rows // 2

    @pl.loop(0, out.shape[0] // units)
    def _(block):
        start = table[first + block] * (units * LANES)
        for unit in range(0, units, 2):
            wide = min(2, units - unit)
            at = pl.ds(pl.multiple_of(start + unit * LANES, LANES), wide * LANES)
            product = jnp.dot(near[...], comp[:count, at], preferred_element_type=F32)
            product += jnp.dot(far[...], comp[count:, at], preferred_element_type=F32)
            for k in range(wide):
                out[block * units + unit + k] = product[:, k * LANES : (k + 1) * LANES].astype(out.dtype)


def right_product(table, first, blocks, units, comp, near, far, dtype):
    rank = near.shape[0]
    return call(
        functools.partial(right_kernel, units, first),
        "right_product",
        shaped((blocks * units, rank, LANES), dtype),
        [SMEM, VMEM, VMEM, VMEM],
        4,
        0.7 * blocks,
        out_specs=VMEM,
    )(table, in_vmem(comp), near, far)


def new_error_kernel(units, blocks, table, comp, near, far, *rest):
    arrays = rest[: 1 + max(which for _, which, _ in blocks)]
    out, buf, sems = rest[-3:]
    count = comp.shape[0] // 2
    width = units * LANES
    copies = []
    for j, (entry, which, place) in enumerate(blocks):
        right = arrays[which]
        start = pl.multiple_of(table[entry] * width, LANES)
        for half, base in enumerate((near, far)):
            for unit in range(0, units, 2):
                wide = min(2, units - unit)
                factor = [right[place * units + unit + k] for k in range(wide)]
                factor = jnp.concatenate(factor, axis=1) if wide > 1 else factor[0]
                product = jnp.dot(base[...], factor, preferred_element_type=F32)
                at = pl.ds(pl.multiple_of(start + unit * LANES, LANES), wide * LANES)
                kept = comp[half * count : (half + 1) * count, at].astype(F32)
                buf[half, j, :, unit * LANES : (unit + wide) * LANES] = (kept - product).astype(BF16)
            rows = pl.ds(pl.multiple_of(table[HALF + half] * count, count), count)
            copy = pltpu.make_async_copy(buf.at[half, j], out.at[rows, pl.ds(start, width)], sems.at[half, j])
            copy.start()
            copies.append(copy)
    for copy in copies:
        copy.wait()


def new_error(table, blocks, arrays, units, comp, near, far, held=None):
    rows, cols = comp.shape
    extra = [] if held is None else [in_hbm(held)]
    return call(
        functools.partial(new_error_kernel, units, blocks),
        "new_error",
        shaped((rows, cols), BF16),
        [SMEM] + [VMEM] * (3 + len(arrays)) + [HBM] * len(extra),
        12,
        1 + 0.7 * len(blocks),
        out_specs=HBM,
        scratch_shapes=[
            pltpu.VMEM((2, len(blocks), rows // 2, units * LANES), BF16),
            pltpu.SemaphoreType.DMA((2, len(blocks))),
        ],
        input_output_aliases={4 + len(arrays): 0} if extra else {},
    )(table, in_vmem(comp), near, far, *arrays, *extra)


def leaf_steps(state, leaf):
    n, b = state.shape[0], LEAF
    base = leaf * b

    def splat(v):
        return jnp.broadcast_to(v, (b, n))

    def column(tile, j):
        return splat(state[b * tile : b * tile + b, base + j : base + j + 1])

    here = [column(leaf, j) for j in range(b)]
    a = [[splat(here[j][i : i + 1]) if j <= i else None for j in range(b)] for i in range(b)]
    mult = [[None] * b for _ in range(b)]
    unit = [[None] * b for _ in range(b)]
    recip, scale = [], []
    for k in range(b):
        recip.append(1.0 / a[k][k])
        scale.append(lax.rsqrt(a[k][k]))
        for i in range(k + 1, b):
            mult[i][k] = a[i][k] * recip[k]
        for i in range(k + 1, b):
            for j in range(k + 1, i + 1):
                a[i][j] = a[i][j] - mult[i][k] * a[j][k]
    for j in range(b):
        for i in range(j + 1, b):
            total = mult[i][j]
            for k in range(j + 1, i):
                total = total + mult[i][k] * unit[k][j]
            unit[i][j] = -total
    rows_x = [splat(state[base + j : base + j + 1, n:]) for j in range(b)]
    if leaf + 1 < n // b:
        rows_g = [splat(state[base + j : base + j + 1, :n]) for j in range(b)]

        def term(k, j):
            return recip[k] if j == k else recip[k] * unit[k][j]

        inverse = [[None] * b for _ in range(b)]
        for i in range(b):
            for j in range(i + 1):
                total = term(i, j)
                for k in range(i + 1, b):
                    total = total + unit[k][i] * term(k, j)
                inverse[i][j] = inverse[j][i] = total

        def mixed(rows):
            out = []
            for k in range(b):
                total = inverse[k][0] * rows[0]
                for j in range(1, b):
                    total = total + inverse[k][j] * rows[j]
                out.append(total)
            return out

        mixed_g, mixed_x = mixed(rows_g), mixed(rows_x)
        for tile in range(leaf + 1, n // b):
            at = slice(b * tile, b * tile + b)
            columns = [column(tile, j) for j in range(b)]
            g, x = state[at, :n], state[at, n:]
            for k in range(b):
                g = g - columns[k] * mixed_g[k]
                x = x - columns[k] * mixed_x[k]
            state[at, :n] = g
            state[at, n:] = x
    for i in range(b):
        total = rows_x[i]
        for j in range(i):
            total = total + unit[i][j] * rows_x[j]
        state[base + i : base + i + 1, n:] = (total * scale[i])[:1]


def leaves_kernel(leaves, source, state):
    n = state.shape[0]
    if source.shape == state.shape:
        state[...] = source[...]
    else:
        state[:, :n] = source[...]
        row = lax.broadcasted_iota(jnp.int32, (n, n), 0)
        state[:, n:] = (row == lax.broadcasted_iota(jnp.int32, (n, n), 1)).astype(F32)
    for leaf in leaves:
        leaf_steps(state, leaf)


def inverse_part(source, leaves):
    n = source.shape[0]
    return call(
        functools.partial(leaves_kernel, leaves),
        "inverse_part",
        shaped((n, 2 * n), F32),
        [VMEM],
        4,
        1.5,
        out_specs=VMEM,
    )(source)


def split2(x):
    high = x.astype(BF16)
    return high, (x - high.astype(F32)).astype(BF16)


def put3(ref, at, x):
    high, rest = split2(x)
    ref[at] = high
    rest = x - high.astype(F32)
    mid, low = split2(rest)
    ref[at + 1] = mid
    ref[at + 2] = low


def get3(ref, at):
    return ref[at].astype(F32) + (ref[at + 1].astype(F32) + ref[at + 2].astype(F32))


def first_kernel(part, arrived, near, far, out, gram):
    count = part.shape[0]
    contract = (((1,), (1,)), ((), ()))
    total = lax.dot_general(near[...], near[...], contract, preferred_element_type=F32)
    total += lax.dot_general(far[...], far[...], contract, preferred_element_type=F32)
    gram[...] = total
    put3(out, count, total)

    @pl.loop(0, count)
    def _(i):
        out[i] = (part[i] + arrived[i].astype(F32)).astype(BF16)


def second_kernel(part, across, arrived, gram_in, out, kept, gram):
    units = kept.shape[0]
    total = gram_in[...] + get3(arrived, 2 * units)
    gram[...] = total
    put3(out, units, total)

    @pl.loop(0, units)
    def _(i):
        j = i + units
        out[i] = (part[j] + across[j].astype(F32) + arrived[j].astype(F32)).astype(BF16)
        kept[i] = part[i] + across[i].astype(F32) + arrived[i].astype(F32)


def third_kernel(table, part, arrived, gram_in, out, kept, gram, held):
    units, rank = part.shape[:2]
    half = rank // 2
    gram[...] = gram_in[...] + get3(arrived, units)
    mine = pl.multiple_of(table[UPPER] * half, half)

    @pl.loop(0, units)
    def _(i):
        held[...] = part[i] + arrived[i].astype(F32)
        out[i] = held[pl.ds(half - mine, half), :].astype(BF16)
        kept[i] = held[pl.ds(mine, half), :]


def add_kernel(kept, arrived, out):
    @pl.loop(0, kept.shape[0])
    def _(i):
        out[i] = (kept[i].astype(F32) + arrived[i].astype(F32)).astype(BF16)


def factor_kernel(replicas, table, own, arrived, state, out, held):
    units, half = own.shape[:2]
    rank = 2 * half
    mine = pl.multiple_of(table[UPPER] * half, half)
    lhs = jnp.concatenate(split2(state[:, rank:]), axis=0)
    for i in range(units):
        at = slice(i * LANES, (i + 1) * LANES)
        held[pl.ds(mine, half), at] = own[i]
        held[pl.ds(half - mine, half), at] = arrived[i]
    for i in range(0, units, 2):
        wide = min(2, units - i)
        product = jnp.dot(lhs, held[:, i * LANES : (i + wide) * LANES], preferred_element_type=F32)
        product = (product[:rank] + product[rank:]) / replicas
        for k in range(wide):
            out[i + k] = product[:, k * LANES : (k + 1) * LANES].astype(BF16)


def base_kernel(near, far, state, near_out, far_out):
    rank = near.shape[0]
    lhs = jnp.concatenate(split2(state[:, rank:]), axis=0)
    for source, out in ((near, near_out), (far, far_out)):
        product = jnp.dot(lhs, source[...], preferred_element_type=F32)
        out[...] = (product[:rank] + product[rank:]).T.astype(BF16)


def rows_kernel(units, table, own, other, out):
    for half, source in enumerate((own, other)):
        start = table[HALF + half] * (units * LANES)

        @pl.loop(0, units)
        def _(i):
            out[pl.ds(pl.multiple_of(start + i * LANES, LANES), LANES), :] = source[i].T


class Exchange:
    def __init__(self, dp, mp):
        self.dp, self.mp = dp, mp
        mp_bits = [("mp", 1 << k) for k in range(mp.bit_length() - 1)]
        z_bits = [("dp", 2 << k) for k in range(dp.bit_length() - 2)]
        low, high = mp_bits[0], mp_bits[len(mp_bits) // 2]
        self.other = [bit for bit in mp_bits if bit not in (low, high)]
        self.scatter = [(low, high), (high, low)]
        rest = self.other + z_bits
        self.rest = list(zip(rest, rest[::-1]))
        self.replicas = list(zip(z_bits, z_bits[::-1]))
        self.low, self.high = low[1], high[1]

    def send(self, x, step):
        pairs = []
        for d in range(self.dp):
            for m in range(self.mp):
                axis, bit = step[d % 2]
                to = (d ^ bit) * self.mp + m if axis == "dp" else d * self.mp + (m ^ bit)
                pairs.append((d * self.mp + m, to))
        return lax.ppermute(x, AXES, pairs)

    def core(self, x):
        return self.send(x, (("dp", 1), ("dp", 1)))

    def tables(self):
        table = np.zeros((self.dp, self.mp, WIDTH), np.int32)
        for d in range(self.dp):
            for m in range(self.mp):
                core = d % 2
                table[d, m, HALF : HALF + 2] = core, 1 - core
                for entry, which in ((NEAR, core), (FAR, 1 - core)):
                    for k in range(4):
                        first, second = self.scatter[0][which][1], self.scatter[1][which][1]
                        at = m ^ (first * (k // 2)) ^ (second * (k % 2))
                        low, high = int(at & self.low != 0), int(at & self.high != 0)
                        table[d, m, entry + k] = high * 4 + low * 2 + which
                axis, bit = self.rest[0][core]
                table[d, m, UPPER] = int((d if axis == "dp" else m) & bit != 0)
        return table


def on_device(dp, mp, grad, error, init, table):
    grad, error, table = grad[0], error[0], table.reshape(-1)
    rows, cols = grad.shape
    rank = init.shape[1]
    half = rank // 2
    net = Exchange(dp, mp)
    units = cols // 8 // LANES
    square = (rank, LANES)

    comp, near, far = left_product(table, grad, error, init)
    near = near + net.core(far)
    for step in net.replicas:
        sent = lax.reduce_precision(near, 8, 7)
        near = sent + net.send(sent.astype(BF16), step).astype(F32)
    near = near.astype(BF16)
    far = net.core(near)

    def right(first, dtype):
        return right_product(table, first, 2, units, comp, near, far, dtype)

    across = net.core(right(FAR + 2, BF16))
    part = right(NEAR + 2, F32)
    sent, gram = call(
        first_kernel, "first_sum",
        [shaped((2 * units + 3, *square), BF16), shaped((rank, rank), F32)],
        [VMEM] * 4, 4, 0.5, out_specs=[VMEM] * 2,
    )(part, across, near, far)
    arrived = net.send(sent, net.scatter[0])
    across = net.core(right(FAR, BF16))
    part = right(NEAR, F32)
    sent, kept, gram = call(
        second_kernel, "second_sum",
        [shaped((units + 3, *square), BF16), shaped((units, *square), F32), shaped((rank, rank), F32)],
        [VMEM] * 4, 4, 0.5, out_specs=[VMEM] * 3,
    )(part, across, arrived, gram)
    arrived = net.send(sent, net.scatter[1])
    sent, kept, gram = call(
        third_kernel, "third_sum",
        [shaped((units, half, LANES), BF16), shaped((units, half, LANES), F32), shaped((rank, rank), F32)],
        [SMEM] + [VMEM] * 3, 4, 0.5, out_specs=[VMEM] * 3,
        scratch_shapes=[pltpu.VMEM(square, F32)],
    )(table, kept, arrived, gram)
    for bit in net.other:
        gram = gram + net.send(gram, (bit, bit))

    leaves = list(range(rank // LEAF))
    state = gram
    for k in range(3):
        state = inverse_part(state, leaves[len(leaves) * k // 3 : len(leaves) * (k + 1) // 3])
    for step in net.rest:
        kept = call(
            add_kernel, "pair_sum", shaped((units, half, LANES), BF16), [VMEM] * 2, 2, 0.3, out_specs=VMEM
        )(kept, net.send(sent, step))
        sent = kept
    own = call(
        functools.partial(factor_kernel, dp), "factor", shaped((units, *square), BF16),
        [SMEM] + [VMEM] * 3, 4, 0.7, out_specs=VMEM,
        scratch_shapes=[pltpu.VMEM((rank, units * LANES), BF16)],
    )(table, sent, net.send(sent, net.rest[0]), state)
    base_near, base_far = call(
        base_kernel, "base", [shaped((rows // 2, rank), BF16)] * 2, [VMEM] * 3, 4, 0.7, out_specs=[VMEM] * 2
    )(near, far, state)

    write = functools.partial(new_error, table, units=units, comp=comp, near=base_near, far=base_far)
    own = jnp.concatenate([own, net.send(own, net.scatter[1])], axis=0)
    arrived = net.send(own, net.scatter[0])
    other = net.core(own)
    out = write([(NEAR, 0, 0), (NEAR + 1, 0, 1)], [own])
    crossed = net.core(arrived)
    out = write(
        [(FAR, 0, 0), (FAR + 1, 0, 1), (NEAR + 2, 1, 0), (NEAR + 3, 1, 1)], [other, arrived], held=out
    )
    out = write([(FAR + 2, 0, 0), (FAR + 3, 0, 1)], [crossed], held=out)

    share, width = cols // mp, units * LANES
    if share == 2 * width:
        right_factor = call(
            functools.partial(rows_kernel, units), "factor_rows", shaped((share, rank), BF16),
            [SMEM, VMEM, VMEM], 4, 1, out_specs=VMEM,
        )(table, own, other)
    else:
        everything = jnp.concatenate([own, arrived, other, crossed], axis=0)
        block = lax.axis_index("mp") * share // width
        place = jnp.argmax(table[NEAR : NEAR + 8] == block)
        chosen = lax.dynamic_slice_in_dim(everything, place * units, units, 0)
        chosen = jnp.swapaxes(chosen, 1, 2).reshape(width, rank)
        right_factor = lax.dynamic_slice_in_dim(chosen, lax.axis_index("mp") * share - block * width, share, 0)
    return (out[None], right_factor)


def solution(mesh):
    dp, mp = mesh.shape["dp"], mesh.shape["mp"]
    table = Exchange(dp, mp).tables()
    run = jax.shard_map(
        functools.partial(on_device, dp, mp),
        mesh=mesh,
        in_specs=(P("dp", "mp", None), P("dp", "mp", None), P(), P("dp", "mp", None)),
        out_specs=(P("dp", "mp", None), P("mp", None)),
        check_vma=False,
    )

    def whole(grad, error, init_factor):
        return run(grad, error, init_factor, jnp.asarray(table))

    return whole
```

time: 392 us -> 105 us (0.27)
  waiting for transfers between devices: 296 us -> 27.4 us
  matrix products: 51.9 us -> 0 us
  Pallas kernels: 0 us -> 36.8 us
  starting transfers between devices: 0.34 us -> 35.4 us
  other arithmetic: 25.2 us -> 0.21 us
  between operations: 13.8 us -> 0.96 us
    reduce_scatter x1 -> x0, waiting for transfers between devices: 137 us -> none  [reduce_factor(): lax.psum_scatter(lax.dot_general(compensated, ortho_basis, (((0,), (0,)),...]
    psum x2 -> x0, waiting for transfers between devices: 99.1 us -> none  [the longest x1 56.6 us: orthonormal(): summed = lax.psum(partial_value, 'dp')]
    all_gather x1 -> x0, waiting for transfers between devices: 60 us -> none  [on_device(): full_factor = lax.all_gather(factor_rows, ('dp', 'mp'), axis=0, tiled=True)]
    dot_general x4 -> x0, matrix products: 50.3 us -> none  [the longest x1 17.7 us: reduce_factor(): lax.dot_general(compensated, ortho_basis, (((0,), (0,)), ((), ())), prefe...]
    pallas_call x0 -> x19, Pallas kernels: none -> 36.8 us  [the longest x1 11.8 us: left_product(): call(functools.partial(left_kernel, PIECES), 'left_product', [pltpu.VMEM(...]
    ppermute x0 -> x15, starting transfers between devices: none -> 35.4 us  [send(): return lax.ppermute(x, AXES, pairs)]
    ppermute x0 -> x15, waiting for transfers between devices: none -> 27.4 us  [send(): return lax.ppermute(x, AXES, pairs)]
    another operation x5 -> x0, other arithmetic: 22.9 us -> none  [the longest x3 12.4 us: orthonormal(): cholesky_factor = jnp.linalg.cholesky(gram_matrix)]
  transfers between devices with their start and end apart: 4 -> 15, of which waited for: 4 -> 10; matrix products, arithmetic and copies ran while one was open for 0% -> 0% of each run, Pallas kernels for 0% -> 17%
where the time goes in v2:
time: 105 us
  Pallas kernels  36.8 us (35%)
  starting transfers between devices  35.4 us (34%)
  waiting for transfers between devices  27.4 us (26%)
  local copies, waits for them, and re-layouts  4.46 us (4%)
    ppermute x15, starting transfers between devices, send(): return lax.ppermute(x, AXES, pairs)  35.4 us
    ppermute x15, waiting for transfers between devices, send(): return lax.ppermute(x, AXES, pairs)  27.4 us
    pallas_call x1, Pallas kernels, left_product(): call(functools.partial(left_kernel, PIECES), 'left_product', [pltpu.VMEM(...  11.8 us
    pallas_call x3, Pallas kernels, new_error(): call(functools.partial(new_error_kernel, units, blocks), 'new_error', sha...  9.69 us
    pallas_call x4, Pallas kernels, right_product(): call(functools.partial(right_kernel, units, first), 'right_product', shap...  6.23 us
    pallas_call x3, Pallas kernels, inverse_part(): call(functools.partial(leaves_kernel, leaves), 'inverse_part', shaped((n,...  4.23 us
    unnamed x2, local copies, waits for them, and re-layouts  2.48 us
    pallas_call x1, Pallas kernels, on_device(): call(functools.partial(rows_kernel, units), 'factor_rows', shaped((share,...  2.3 us
  transfers between devices with their start and end apart: 15, of which 10 were waited for; matrix products, arithmetic and copies ran while one was open for 0% of the time, Pallas kernels for 17%

profile of v2, /device:TPU:1, one launch (start us, length us, event | category | flops | bytes accessed | tf_op | source)
XLA Modules:
  0.0 105.2 jit_solution(17370193621687552683)
XLA Ops:
  0.6 1.2 %dynamic-slice = s32[1]{0:T(128)} dynamic-slice(s32[32]{0:T(128)} %constant.6, u32[]{:T(128)S(6)} %partition-id.1), dynamic_slice_sizes={1} | dynamic-slice | bytes 12
  1.9 1.2 %dynamic-slice.1 = s32[1]{0:T(128)} dynamic-slice(s32[32]{0:T(128)} %constant.7, u32[]{:T(128)S(6)} %partition-id.1), dynamic_slice_sizes={1} | dynamic-slice | bytes 12
  3.1 2.0 %dynamic-slice_bitcast_fusion.table = s32[16]{0:T(128)S(1)} fusion(s32[8,4,16]{2,1,0:T(4,128)} %constant.5, s32[]{:T(128)} %bitcast, s32[]{:T(128)} %bitcast.1), kind=kLoop, calls=%fused_computation.5 | loop fusion | bytes 136 | tf_op jit(solution)/shard_map/reshape | solution.py:410
  5.1 11.8 %left_product.1 = (bf16[1024,7168]{1,0:T(8,128)(2,1)S(1)}, f32[128,512]{1,0:T(8,128)S(1)}, f32[128,512]{1,0:T(8,128)S(1)}) custom-call(s32[16]{0:T(128)S(1)} %dynamic-slice_bitcast_fusion.table, bf16[1024,7168]{1,0:T(8,128)(2,1)} %bitcast.8, bf16[1024,7168]{1,0:T(8,128)(2,1)} %bitcast.9, bf16[7168,128]{1,0:T(8,128)(2,1)} %init.1), custom_call_target="tpu_custom_call" | custom-call | bytes 42000000 | tf_op jit(solution)/shard_map/left_product/pallas_call | solution.py:85
  16.9 0.1 collective-permute-start
  17.0 1.5 %collective-permute-done = f32[128,512]{1,0:T(8,128)S(1)} collective-permute-done((f32[128,512]{1,0:T(8,128)S(1)}, f32[128,512]{1,0:T(8,128)S(1)}, u32[]{:S(2)}, u32[]{:S(2)}) %collective-permute-start) | collective-permute-done | bytes 262176 | tf_op jit(solution)/shard_map/ppermute | solution.py:387
  18.5 3.5 %collective-permute-start.1 = (bf16[128,512]{1,0:T(8,128)(2,1)S(1)}, bf16[128,512]{1,0:T(8,128)(2,1)S(1)}, u32[]{:S(2)}, u32[]{:S(2)}) collective-permute-start(bf16[128,512]{1,0:T(8,128)(2,1)S(1)} %fusion.1), channel_id=1, source_target_pairs={{0,8},{1,9},{2,10},{3,11},{4,20},{5,21},{6,22},{7,23},{8,0},{9,1},... | collective-permute-start | bytes 393224 | tf_op jit(solution)/shard_map/ppermute | solution.py:387
  22.0 3.7 %collective-permute-done.1 = bf16[128,512]{1,0:T(8,128)(2,1)S(1)} collective-permute-done((bf16[128,512]{1,0:T(8,128)(2,1)S(1)}, bf16[128,512]{1,0:T(8,128)(2,1)S(1)}, u32[]{:S(2)}, u32[]{:S(2)}) %collective-permute-start.1) | collective-permute-done | bytes 131104 | tf_op jit(solution)/shard_map/ppermute | solution.py:387
  25.7 0.1 fusion
  25.8 0.7 collective-permute-start.2
  26.5 3.4 %collective-permute-done.2 = bf16[128,512]{1,0:T(8,128)(2,1)S(1)} collective-permute-done((bf16[128,512]{1,0:T(8,128)(2,1)S(1)}, bf16[128,512]{1,0:T(8,128)(2,1)S(1)}, u32[]{:S(2)}, u32[]{:S(2)}) %collective-permute-start.2) | collective-permute-done | bytes 131104 | tf_op jit(solution)/shard_map/ppermute | solution.py:387
  30.0 0.1 add_convert_fusion.near
  30.1 1.9 %collective-permute-start.3 = (bf16[128,512]{1,0:T(8,128)(2,1)S(1)}, bf16[128,512]{1,0:T(8,128)(2,1)S(1)}, u32[]{:S(2)}, u32[]{:S(2)}) collective-permute-start(bf16[128,512]{1,0:T(8,128)(2,1)S(1)} %add_convert_fusion.near), channel_id=1, source_target_pairs={{0,4},{1,5},{2,6},{3,7},{4,0},{5,1},{6,2},{7,3},{8,12},{9,13},{10,... | collective-permute-start | bytes 393224 | tf_op jit(solution)/shard_map/ppermute | solution.py:387
  31.9 1.0 collective-permute-done.3.far
  32.9 1.7 %right_product.7 = bf16[14,128,128]{2,1,0:T(8,128)(2,1)S(1)} custom-call(s32[16]{0:T(128)S(1)} %dynamic-slice_bitcast_fusion.table, bf16[1024,7168]{1,0:T(8,128)(2,1)S(1)} %get-tuple-element.15.comp, bf16[128,512]{1,0:T(8,128)(2,1)S(1)} %add_convert_fusion.near, bf16[128,512]{1,0:T(8,128)(2,1)S(1)} %collective-permute-done.3.far), custom_call_target="tpu_custom_call" | custom-call | bytes 4900000 | tf_op jit(solution)/shard_map/right_product/pallas_call | solution.py:119
  34.6 0.5 collective-permute-start.5
  35.0 1.5 %right_product.6.part = f32[14,128,128]{2,1,0:T(8,128)S(1)} custom-call(s32[16]{0:T(128)S(1)} %dynamic-slice_bitcast_fusion.table, bf16[1024,7168]{1,0:T(8,128)(2,1)S(1)} %get-tuple-element.15.comp, bf16[128,512]{1,0:T(8,128)(2,1)S(1)} %add_convert_fusion.near, bf16[128,512]{1,0:T(8,128)(2,1)S(1)} %collective-permute-done.3.far), custom_call_target="tpu_custom_call" | custom-call | bytes 4900000 | tf_op jit(solution)/shard_map/right_product/pallas_call | solution.py:119
  36.6 0.0 collective-permute-done.5.arrived
  36.6 0.4 first_sum.1
  37.0 2.4 %collective-permute-start.6 = (bf16[17,128,128]{2,1,0:T(8,128)(2,1)S(1)}, bf16[17,128,128]{2,1,0:T(8,128)(2,1)S(1)}, u32[]{:S(2)}, u32[]{:S(2)}) collective-permute-start(bf16[17,128,128]{2,1,0:T(8,128)(2,1)S(1)} %get-tuple-element.18), channel_id=1, source_target_pairs={{0,1},{1,0},{2,3},{3,2},{4,6},{5,7},{6,4},{7,5},{8,9},{9,8},{10,11... | collective-permute-start | bytes 1671176 | tf_op jit(solution)/shard_map/ppermute | solution.py:387
  39.4 1.5 %right_product.5 = bf16[14,128,128]{2,1,0:T(8,128)(2,1)S(1)} custom-call(s32[16]{0:T(128)S(1)} %dynamic-slice_bitcast_fusion.table, bf16[1024,7168]{1,0:T(8,128)(2,1)S(1)} %get-tuple-element.15.comp, bf16[128,512]{1,0:T(8,128)(2,1)S(1)} %add_convert_fusion.near, bf16[128,512]{1,0:T(8,128)(2,1)S(1)} %collective-permute-done.3.far), custom_call_target="tpu_custom_call" | custom-call | bytes 4900000 | tf_op jit(solution)/shard_map/right_product/pallas_call | solution.py:119
  40.9 0.6 collective-permute-start.4
  41.6 1.5 %right_product.4.part = f32[14,128,128]{2,1,0:T(8,128)S(1)} custom-call(s32[16]{0:T(128)S(1)} %dynamic-slice_bitcast_fusion.table, bf16[1024,7168]{1,0:T(8,128)(2,1)S(1)} %get-tuple-element.15.comp, bf16[128,512]{1,0:T(8,128)(2,1)S(1)} %add_convert_fusion.near, bf16[128,512]{1,0:T(8,128)(2,1)S(1)} %collective-permute-done.3.far), custom_call_target="tpu_custom_call" | custom-call | bytes 4900000 | tf_op jit(solution)/shard_map/right_product/pallas_call | solution.py:119
  43.1 0.0 collective-permute-done.4.across
  43.1 3.5 %collective-permute-done.6.arrived = bf16[17,128,128]{2,1,0:T(8,128)(2,1)S(1)} collective-permute-done((bf16[17,128,128]{2,1,0:T(8,128)(2,1)S(1)}, bf16[17,128,128]{2,1,0:T(8,128)(2,1)S(1)}, u32[]{:S(2)}, u32[]{:S(2)}) %collective-permute-start.6) | collective-permute-done | bytes 557088 | tf_op jit(solution)/shard_map/ppermute | solution.py:387
  46.6 0.2 second_sum.1
  46.8 1.5 %collective-permute-start.7 = (bf16[10,128,128]{2,1,0:T(8,128)(2,1)S(1)}, bf16[10,128,128]{2,1,0:T(8,128)(2,1)S(1)}, u32[]{:S(2)}, u32[]{:S(2)}) collective-permute-start(bf16[10,128,128]{2,1,0:T(8,128)(2,1)S(1)} %get-tuple-element.21), channel_id=1, source_target_pairs={{0,2},{1,3},{2,0},{3,1},{4,5},{5,4},{6,7},{7,6},{8,10},{9,11},{10,... | collective-permute-start | bytes 983048 | tf_op jit(solution)/shard_map/ppermute | solution.py:387
  48.4 4.8 %collective-permute-done.7.arrived = bf16[10,128,128]{2,1,0:T(8,128)(2,1)S(1)} collective-permute-done((bf16[10,128,128]{2,1,0:T(8,128)(2,1)S(1)}, bf16[10,128,128]{2,1,0:T(8,128)(2,1)S(1)}, u32[]{:S(2)}, u32[]{:S(2)}) %collective-permute-start.7) | collective-permute-done | bytes 327712 | tf_op jit(solution)/shard_map/ppermute | solution.py:387
  53.1 0.7 third_sum.1
  53.8 1.3 %collective-permute-start.8 = (bf16[7,64,128]{2,1,0:T(8,128)(2,1)S(1)}, bf16[7,64,128]{2,1,0:T(8,128)(2,1)S(1)}, u32[]{:S(2)}, u32[]{:S(2)}) collective-permute-start(bf16[7,64,128]{2,1,0:T(8,128)(2,1)S(1)} %get-tuple-element.27), channel_id=1, source_target_pairs={{0,8},{1,9},{2,10},{3,11},{4,20},{5,21},{6,22},{7,23},{8,0},{9,1},... | collective-permute-start | bytes 344072 | tf_op jit(solution)/shard_map/ppermute | solution.py:387
  55.1 3.4 %collective-permute-done.8.arrived = bf16[7,64,128]{2,1,0:T(8,128)(2,1)S(1)} collective-permute-done((bf16[7,64,128]{2,1,0:T(8,128)(2,1)S(1)}, bf16[7,64,128]{2,1,0:T(8,128)(2,1)S(1)}, u32[]{:S(2)}, u32[]{:S(2)}) %collective-permute-start.8) | collective-permute-done | bytes 114720 | tf_op jit(solution)/shard_map/ppermute | solution.py:387
  58.4 0.1 pair_sum.2.kept
  58.5 1.6 %collective-permute-start.9 = (bf16[7,64,128]{2,1,0:T(8,128)(2,1)S(1)}, bf16[7,64,128]{2,1,0:T(8,128)(2,1)S(1)}, u32[]{:S(2)}, u32[]{:S(2)}) collective-permute-start(bf16[7,64,128]{2,1,0:T(8,128)(2,1)S(1)} %pair_sum.2.kept), channel_id=1, source_target_pairs={{0,16},{1,17},{2,18},{3,19},{4,12},{5,13},{6,14},{7,15},{8,24},{9,... | collective-permute-start | bytes 344072 | tf_op jit(solution)/shard_map/ppermute | solution.py:387
  60.1 2.2 %collective-permute-done.9.arrived = bf16[7,64,128]{2,1,0:T(8,128)(2,1)S(1)} collective-permute-done((bf16[7,64,128]{2,1,0:T(8,128)(2,1)S(1)}, bf16[7,64,128]{2,1,0:T(8,128)(2,1)S(1)}, u32[]{:S(2)}, u32[]{:S(2)}) %collective-permute-start.9) | collective-permute-done | bytes 114720 | tf_op jit(solution)/shard_map/ppermute | solution.py:387
  62.3 2.3 %collective-permute-start.10 = (bf16[7,64,128]{2,1,0:T(8,128)(2,1)S(1)}, bf16[7,64,128]{2,1,0:T(8,128)(2,1)S(1)}, u32[]{:S(2)}, u32[]{:S(2)}) collective-permute-start(bf16[7,64,128]{2,1,0:T(8,128)(2,1)S(1)} %pair_sum.3.own), channel_id=1, source_target_pairs={{0,8},{1,9},{2,10},{3,11},{4,20},{5,21},{6,22},{7,23},{8,0},{9,1},... | collective-permute-start | bytes 344072 | tf_op jit(solution)/shard_map/ppermute | solution.py:387
  64.6 1.4 %inverse_part.3.source = f32[128,256]{1,0:T(8,128)S(1)} custom-call(f32[128,128]{1,0:T(8,128)S(1)} %get-tuple-element.23.source), custom_call_target="tpu_custom_call" | custom-call | bytes 5250000 | tf_op jit(solution)/shard_map/inverse_part/pallas_call | solution.py:259
  65.9 1.3 %inverse_part.4.source = f32[128,256]{1,0:T(8,128)S(1)} custom-call(f32[128,256]{1,0:T(8,128)S(1)} %inverse_part.3.source), custom_call_target="tpu_custom_call" | custom-call | bytes 5250000 | tf_op jit(solution)/shard_map/inverse_part/pallas_call | solution.py:259
  67.3 1.5 %inverse_part.5.state = f32[128,256]{1,0:T(8,128)S(1)} custom-call(f32[128,256]{1,0:T(8,128)S(1)} %inverse_part.4.source), custom_call_target="tpu_custom_call" | custom-call | bytes 5250000 | tf_op jit(solution)/shard_map/inverse_part/pallas_call | solution.py:259
  68.8 0.5 collective-permute-done.10.arrived
  69.4 0.8 factor.1
  70.2 1.9 %collective-permute-start.11 = (bf16[7,128,128]{2,1,0:T(8,128)(2,1)S(1)}, bf16[7,128,128]{2,1,0:T(8,128)(2,1)S(1)}, u32[]{:S(2)}, u32[]{:S(2)}) collective-permute-start(bf16[7,128,128]{2,1,0:T(8,128)(2,1)S(1)} %factor.1), channel_id=1, source_target_pairs={{0,2},{1,3},{2,0},{3,1},{4,5},{5,4},{6,7},{7,6},{8,10},{9,11},{10,... | collective-permute-start | bytes 688136 | tf_op jit(solution)/shard_map/ppermute | solution.py:387
  72.1 3.4 %collective-permute-done.11 = bf16[7,128,128]{2,1,0:T(8,128)(2,1)S(1)} collective-permute-done((bf16[7,128,128]{2,1,0:T(8,128)(2,1)S(1)}, bf16[7,128,128]{2,1,0:T(8,128)(2,1)S(1)}, u32[]{:S(2)}, u32[]{:S(2)}) %collective-permute-start.11) | collective-permute-done | bytes 229408 | tf_op jit(solution)/shard_map/ppermute | solution.py:387
  75.5 1.5 %collective-permute-start.12 = (bf16[14,128,128]{2,1,0:T(8,128)(2,1)S(1)}, bf16[14,128,128]{2,1,0:T(8,128)(2,1)S(1)}, u32[]{:S(2)}, u32[]{:S(2)}) collective-permute-start(bf16[14,128,128]{2,1,0:T(8,128)(2,1)S(1)} %pad_maximum_fusion.rest_0_.own), channel_id=1, source_target_pairs={{0,1},{1,0},{2,3},{3,2},{4,6},{5,7},{6,4},{7,5},{8,9},{9,8},{10,11... | collective-permute-start | bytes 1376264 | tf_op jit(solution)/shard_map/ppermute | solution.py:387
  77.0 8.7 %collective-permute-start.14 = (bf16[14,128,128]{2,1,0:T(8,128)(2,1)S(1)}, bf16[14,128,128]{2,1,0:T(8,128)(2,1)S(1)}, u32[]{:S(2)}, u32[]{:S(2)}) collective-permute-start(bf16[14,128,128]{2,1,0:T(8,128)(2,1)S(1)} %pad_maximum_fusion.rest_0_.own), channel_id=1, source_target_pairs={{0,4},{1,5},{2,6},{3,7},{4,0},{5,1},{6,2},{7,3},{8,12},{9,13},{10,... | collective-permute-start | bytes 1376264 | tf_op jit(solution)/shard_map/ppermute | solution.py:387
  85.8 0.0 collective-permute-done.12.rest_1_
  85.8 6.9 %collective-permute-start.13 = (bf16[14,128,128]{2,1,0:T(8,128)(2,1)S(1)}, bf16[14,128,128]{2,1,0:T(8,128)(2,1)S(1)}, u32[]{:S(2)}, u32[]{:S(2)}) collective-permute-start(bf16[14,128,128]{2,1,0:T(8,128)(2,1)S(1)} %collective-permute-done.12.rest_1_), channel_id=1, source_target_pairs={{0,4},{1,5},{2,6},{3,7},{4,0},{5,1},{6,2},{7,3},{8,12},{9,13},{10,... | collective-permute-start | bytes 1376264 | tf_op jit(solution)/shard_map/ppermute | solution.py:387
  92.7 0.3 base.1
  93.0 2.8 %new_error.3.rest_2_ = bf16[1024,7168]{1,0:T(8,128)(2,1)} custom-call(s32[16]{0:T(128)S(1)} %dynamic-slice_bitcast_fusion.table, bf16[1024,7168]{1,0:T(8,128)(2,1)S(1)} %get-tuple-element.15.comp, bf16[512,128]{1,0:T(8,128)(2,1)S(1)} %get-tuple-element.24.near, bf16[512,128]{1,0:T(8,128)(2,1)S(1)} %get-tuple-element.25.far, ...), custom_call_target="tpu_custom_call" | custom-call | bytes 8400000 | tf_op jit(solution)/shard_map/new_error/pallas_call | solution.py:159
  95.9 0.0 collective-permute-done.14.rest_0_.other
  95.9 2.3 %factor_rows.1 = bf16[1792,128]{1,0:T(8,128)(2,1)} custom-call(s32[16]{0:T(128)S(1)} %dynamic-slice_bitcast_fusion.table, bf16[14,128,128]{2,1,0:T(8,128)(2,1)S(1)} %pad_maximum_fusion.rest_0_.own, bf16[14,128,128]{2,1,0:T(8,128)(2,1)S(1)} %collective-permute-done.14.rest_0_.other), custom_call_target="tpu_custom_call" | custom-call | bytes 3500000 | tf_op jit(solution)/shard_map/factor_rows/pallas_call | solution.py:485
  98.2 4.0 %new_error.4.rest_1_ = bf16[1024,7168]{1,0:T(8,128)(2,1)} custom-call(s32[16]{0:T(128)S(1)} %dynamic-slice_bitcast_fusion.table, bf16[1024,7168]{1,0:T(8,128)(2,1)S(1)} %get-tuple-element.15.comp, bf16[512,128]{1,0:T(8,128)(2,1)S(1)} %get-tuple-element.24.near, bf16[512,128]{1,0:T(8,128)(2,1)S(1)} %get-tuple-element.25.far, ...), custom_call_target="tpu_custom_call", output_to_operand_aliasing={{}: (6, {})} | custom-call | bytes 13300000 | tf_op jit(solution)/shard_map/new_error/pallas_call | solution.py:159
  102.2 0.0 collective-permute-done.13.rest_0_
  102.2 2.8 %new_error.5 = bf16[1024,7168]{1,0:T(8,128)(2,1)} custom-call(s32[16]{0:T(128)S(1)} %dynamic-slice_bitcast_fusion.table, bf16[1024,7168]{1,0:T(8,128)(2,1)S(1)} %get-tuple-element.15.comp, bf16[512,128]{1,0:T(8,128)(2,1)S(1)} %get-tuple-element.24.near, bf16[512,128]{1,0:T(8,128)(2,1)S(1)} %get-tuple-element.25.far, ...), custom_call_target="tpu_custom_call", output_to_operand_aliasing={{}: (5, {})} | custom-call | bytes 8400000 | tf_op jit(solution)/shard_map/new_error/pallas_call | solution.py:159
  (3 shorter events, 0.1 us)
Async XLA Ops:
  16.9 1.6 %collective-permute-start = (f32[128,512]{1,0:T(8,128)S(1)}, f32[128,512]{1,0:T(8,128)S(1)}, u32[]{:S(2)}, u32[]{:S(2)}) collective-permute-start(f32[128,512]{1,0:T(8,128)S(1)} %get-tuple-element.17), channel_id=1, source_target_pairs={{0,4},{1,5},{2,6},{3,7},{4,0},{5,1},{6,2},{7,3},{8,12},{9,13},{10,... | collective-permute-start | bytes 786440 | tf_op jit(solution)/shard_map/ppermute | solution.py:387
  18.5 7.2 %collective-permute-start.1 = (bf16[128,512]{1,0:T(8,128)(2,1)S(1)}, bf16[128,512]{1,0:T(8,128)(2,1)S(1)}, u32[]{:S(2)}, u32[]{:S(2)}) collective-permute-start(bf16[128,512]{1,0:T(8,128)(2,1)S(1)} %fusion.1), channel_id=1, source_target_pairs={{0,8},{1,9},{2,10},{3,11},{4,20},{5,21},{6,22},{7,23},{8,0},{9,1},... | collective-permute-start | bytes 393224 | tf_op jit(solution)/shard_map/ppermute | solution.py:387
  25.8 4.2 %collective-permute-start.2 = (bf16[128,512]{1,0:T(8,128)(2,1)S(1)}, bf16[128,512]{1,0:T(8,128)(2,1)S(1)}, u32[]{:S(2)}, u32[]{:S(2)}) collective-permute-start(bf16[128,512]{1,0:T(8,128)(2,1)S(1)} %fusion), channel_id=1, source_target_pairs={{0,16},{1,17},{2,18},{3,19},{4,12},{5,13},{6,14},{7,15},{8,24},{9,... | collective-permute-start | bytes 393224 | tf_op jit(solution)/shard_map/ppermute | solution.py:387
  30.1 2.8 %collective-permute-start.3 = (bf16[128,512]{1,0:T(8,128)(2,1)S(1)}, bf16[128,512]{1,0:T(8,128)(2,1)S(1)}, u32[]{:S(2)}, u32[]{:S(2)}) collective-permute-start(bf16[128,512]{1,0:T(8,128)(2,1)S(1)} %add_convert_fusion.near), channel_id=1, source_target_pairs={{0,4},{1,5},{2,6},{3,7},{4,0},{5,1},{6,2},{7,3},{8,12},{9,13},{10,... | collective-permute-start | bytes 393224 | tf_op jit(solution)/shard_map/ppermute | solution.py:387
  34.6 2.0 %collective-permute-start.5 = (bf16[14,128,128]{2,1,0:T(8,128)(2,1)S(1)}, bf16[14,128,128]{2,1,0:T(8,128)(2,1)S(1)}, u32[]{:S(2)}, u32[]{:S(2)}) collective-permute-start(bf16[14,128,128]{2,1,0:T(8,128)(2,1)S(1)} %right_product.7), channel_id=1, source_target_pairs={{0,4},{1,5},{2,6},{3,7},{4,0},{5,1},{6,2},{7,3},{8,12},{9,13},{10,... | collective-permute-start | bytes 1376264 | tf_op jit(solution)/shard_map/ppermute | solution.py:387
  37.0 9.7 %collective-permute-start.6 = (bf16[17,128,128]{2,1,0:T(8,128)(2,1)S(1)}, bf16[17,128,128]{2,1,0:T(8,128)(2,1)S(1)}, u32[]{:S(2)}, u32[]{:S(2)}) collective-permute-start(bf16[17,128,128]{2,1,0:T(8,128)(2,1)S(1)} %get-tuple-element.18), channel_id=1, source_target_pairs={{0,1},{1,0},{2,3},{3,2},{4,6},{5,7},{6,4},{7,5},{8,9},{9,8},{10,11... | collective-permute-start | bytes 1671176 | tf_op jit(solution)/shard_map/ppermute | solution.py:387
  40.9 2.1 %collective-permute-start.4 = (bf16[14,128,128]{2,1,0:T(8,128)(2,1)S(1)}, bf16[14,128,128]{2,1,0:T(8,128)(2,1)S(1)}, u32[]{:S(2)}, u32[]{:S(2)}) collective-permute-start(bf16[14,128,128]{2,1,0:T(8,128)(2,1)S(1)} %right_product.5), channel_id=1, source_target_pairs={{0,4},{1,5},{2,6},{3,7},{4,0},{5,1},{6,2},{7,3},{8,12},{9,13},{10,... | collective-permute-start | bytes 1376264 | tf_op jit(solution)/shard_map/ppermute | solution.py:387
  46.8 6.3 %collective-permute-start.7 = (bf16[10,128,128]{2,1,0:T(8,128)(2,1)S(1)}, bf16[10,128,128]{2,1,0:T(8,128)(2,1)S(1)}, u32[]{:S(2)}, u32[]{:S(2)}) collective-permute-start(bf16[10,128,128]{2,1,0:T(8,128)(2,1)S(1)} %get-tuple-element.21), channel_id=1, source_target_pairs={{0,2},{1,3},{2,0},{3,1},{4,5},{5,4},{6,7},{7,6},{8,10},{9,11},{10,... | collective-permute-start | bytes 983048 | tf_op jit(solution)/shard_map/ppermute | solution.py:387
  53.8 4.6 %collective-permute-start.8 = (bf16[7,64,128]{2,1,0:T(8,128)(2,1)S(1)}, bf16[7,64,128]{2,1,0:T(8,128)(2,1)S(1)}, u32[]{:S(2)}, u32[]{:S(2)}) collective-permute-start(bf16[7,64,128]{2,1,0:T(8,128)(2,1)S(1)} %get-tuple-element.27), channel_id=1, source_target_pairs={{0,8},{1,9},{2,10},{3,11},{4,20},{5,21},{6,22},{7,23},{8,0},{9,1},... | collective-permute-start | bytes 344072 | tf_op jit(solution)/shard_map/ppermute | solution.py:387
  58.5 3.7 %collective-permute-start.9 = (bf16[7,64,128]{2,1,0:T(8,128)(2,1)S(1)}, bf16[7,64,128]{2,1,0:T(8,128)(2,1)S(1)}, u32[]{:S(2)}, u32[]{:S(2)}) collective-permute-start(bf16[7,64,128]{2,1,0:T(8,128)(2,1)S(1)} %pair_sum.2.kept), channel_id=1, source_target_pairs={{0,16},{1,17},{2,18},{3,19},{4,12},{5,13},{6,14},{7,15},{8,24},{9,... | collective-permute-start | bytes 344072 | tf_op jit(solution)/shard_map/ppermute | solution.py:387
  62.3 7.1 %collective-permute-start.10 = (bf16[7,64,128]{2,1,0:T(8,128)(2,1)S(1)}, bf16[7,64,128]{2,1,0:T(8,128)(2,1)S(1)}, u32[]{:S(2)}, u32[]{:S(2)}) collective-permute-start(bf16[7,64,128]{2,1,0:T(8,128)(2,1)S(1)} %pair_sum.3.own), channel_id=1, source_target_pairs={{0,8},{1,9},{2,10},{3,11},{4,20},{5,21},{6,22},{7,23},{8,0},{9,1},... | collective-permute-start | bytes 344072 | tf_op jit(solution)/shard_map/ppermute | solution.py:387
  70.2 5.3 %collective-permute-start.11 = (bf16[7,128,128]{2,1,0:T(8,128)(2,1)S(1)}, bf16[7,128,128]{2,1,0:T(8,128)(2,1)S(1)}, u32[]{:S(2)}, u32[]{:S(2)}) collective-permute-start(bf16[7,128,128]{2,1,0:T(8,128)(2,1)S(1)} %factor.1), channel_id=1, source_target_pairs={{0,2},{1,3},{2,0},{3,1},{4,5},{5,4},{6,7},{7,6},{8,10},{9,11},{10,... | collective-permute-start | bytes 688136 | tf_op jit(solution)/shard_map/ppermute | solution.py:387
  75.5 10.2 %collective-permute-start.12 = (bf16[14,128,128]{2,1,0:T(8,128)(2,1)S(1)}, bf16[14,128,128]{2,1,0:T(8,128)(2,1)S(1)}, u32[]{:S(2)}, u32[]{:S(2)}) collective-permute-start(bf16[14,128,128]{2,1,0:T(8,128)(2,1)S(1)} %pad_maximum_fusion.rest_0_.own), channel_id=1, source_target_pairs={{0,1},{1,0},{2,3},{3,2},{4,6},{5,7},{6,4},{7,5},{8,9},{9,8},{10,11... | collective-permute-start | bytes 1376264 | tf_op jit(solution)/shard_map/ppermute | solution.py:387
  77.0 18.8 %collective-permute-start.14 = (bf16[14,128,128]{2,1,0:T(8,128)(2,1)S(1)}, bf16[14,128,128]{2,1,0:T(8,128)(2,1)S(1)}, u32[]{:S(2)}, u32[]{:S(2)}) collective-permute-start(bf16[14,128,128]{2,1,0:T(8,128)(2,1)S(1)} %pad_maximum_fusion.rest_0_.own), channel_id=1, source_target_pairs={{0,4},{1,5},{2,6},{3,7},{4,0},{5,1},{6,2},{7,3},{8,12},{9,13},{10,... | collective-permute-start | bytes 1376264 | tf_op jit(solution)/shard_map/ppermute | solution.py:387
  85.8 16.5 %collective-permute-start.13 = (bf16[14,128,128]{2,1,0:T(8,128)(2,1)S(1)}, bf16[14,128,128]{2,1,0:T(8,128)(2,1)S(1)}, u32[]{:S(2)}, u32[]{:S(2)}) collective-permute-start(bf16[14,128,128]{2,1,0:T(8,128)(2,1)S(1)} %collective-permute-done.12.rest_1_), channel_id=1, source_target_pairs={{0,4},{1,5},{2,6},{3,7},{4,0},{5,1},{6,2},{7,3},{8,12},{9,13},{10,... | collective-permute-start | bytes 1376264 | tf_op jit(solution)/shard_map/ppermute | solution.py:387

commit v3 on v2

v3 whole, which is shorter than its diff:
```python
import functools

import jax
import jax.numpy as jnp
from jax import lax
from jax.experimental import pallas as pl
from jax.experimental.pallas import tpu as pltpu
from jax.sharding import PartitionSpec as P

F32 = jnp.float32
BF16 = jnp.bfloat16
LANES = 128
MIB = 1024 * 1024
AXES = ("dp", "mp")
PIECES = 14
LEAF = 8

VMEM = pl.BlockSpec(memory_space=pltpu.VMEM)
HBM = pl.BlockSpec(memory_space=pltpu.HBM)
SMEM = pl.BlockSpec(memory_space=pltpu.SMEM)

NEAR, FAR = 0, 1


class Place:
    def __init__(self, net, place):
        self.net = net
        self.dp, self.mp = place[0][0], place[1][0]
        self.core = self.dp & 1

    def half(self, side):
        return self.core if side == NEAR else 1 - self.core

    def bit(self, name):
        axis, value = name
        return ((self.dp if axis == "dp" else self.mp) >> (value.bit_length() - 1)) & 1

    def block(self, side, k):
        core = self.half(side)
        a, b = k // 2, k % 2
        low = self.bit(self.net.low) ^ (a + (b - a) * core)
        high = self.bit(self.net.high) ^ (b + (a - b) * core)
        return high * 4 + low * 2 + core

    def upper(self):
        first, second = (self.bit(name) for name in self.net.rest[0])
        return first + (second - first) * self.core


def call(kernel, name, outs, ins, vmem_mib, micros, **more):
    return pl.pallas_call(
        kernel,
        out_shape=outs,
        in_specs=ins,
        compiler_params=pltpu.CompilerParams(vmem_limit_bytes=vmem_mib * MIB),
        cost_estimate=pl.CostEstimate(flops=0, bytes_accessed=int(micros * 3.5e6), transcendentals=0),
        name=name,
        **more,
    )


def shaped(shape, dtype):
    return jax.ShapeDtypeStruct(shape, dtype)


def in_hbm(x):
    return pltpu.with_memory_space_constraint(x, pltpu.HBM)


def in_vmem(x):
    return pltpu.with_memory_space_constraint(x, pltpu.VMEM)


def left_kernel(net, pieces, dp, mp, grad, error, init, comp, near, far, error_v, init_v, sems):
    place = Place(net, (dp, mp))
    rows, cols = comp.shape
    count, width = rows // 2, cols // pieces

    def copies(i):
        at = pl.ds(i * width, width)
        out = [pltpu.make_async_copy(init.at[at], init_v.at[at], sems.at[4, i])]
        for half in range(2):
            source = pl.ds(pl.multiple_of(place.half(half) * count, count), count)
            target = pl.ds(half * count, count)
            out.append(pltpu.make_async_copy(grad.at[source, at], comp.at[target, at], sems.at[half, i]))
            out.append(pltpu.make_async_copy(error.at[source, at], error_v.at[target, at], sems.at[2 + half, i]))
        return out

    for i in range(pieces):
        for copy in copies(i):
            copy.start()
    for i in range(pieces):
        for copy in copies(i):
            copy.wait()
        at = pl.ds(i * width, width)
        total = (comp[:, at].astype(F32) + error_v[:, at].astype(F32)).astype(BF16)
        comp[:, at] = total
        part = lax.dot_general(init_v[at].T, total, (((1,), (1,)), ((), ())), preferred_element_type=F32)
        if i == 0:
            near[...] = part[:, :count]
            far[...] = part[:, count:]
        else:
            near[...] += part[:, :count]
            far[...] += part[:, count:]


def left_product(net, place, grad, error, init):
    rows, cols = grad.shape
    rank = init.shape[1]
    return call(
        functools.partial(left_kernel, net, PIECES),
        "left_product",
        [pltpu.VMEM((rows, cols), BF16), shaped((rank, rows // 2), F32), shaped((rank, rows // 2), F32)],
        [SMEM, SMEM, HBM, HBM, HBM],
        26,
        12,
        out_specs=[VMEM] * 3,
        scratch_shapes=[
            pltpu.VMEM((rows, cols), BF16),
            pltpu.VMEM((cols, rank), BF16),
            pltpu.SemaphoreType.DMA((5, PIECES)),
        ],
    )(*place, in_hbm(grad), in_hbm(error), in_hbm(init))


def right_kernel(net, units, side, places, dp, mp, comp, near, far, out):
    place = Place(net, (dp, mp))
    rows = comp.shape[0]
    count = rows // 2
    for block, k in enumerate(places):
        start = place.block(side, k) * (units * LANES)
        for unit in range(0, units, 2):
            wide = min(2, units - unit)
            at = pl.ds(pl.multiple_of(start + unit * LANES, LANES), wide * LANES)
            product = jnp.dot(near[...], comp[:count, at], preferred_element_type=F32)
            product += jnp.dot(far[...], comp[count:, at], preferred_element_type=F32)
            for k in range(wide):
                out[block * units + unit + k] = product[:, k * LANES : (k + 1) * LANES].astype(out.dtype)


def right_product(net, place, side, places, units, comp, near, far, dtype):
    rank = near.shape[0]
    return call(
        functools.partial(right_kernel, net, units, side, places),
        "right_product",
        shaped((len(places) * units, rank, LANES), dtype),
        [SMEM, SMEM, VMEM, VMEM, VMEM],
        4,
        0.7 * len(places),
        out_specs=VMEM,
    )(*place, in_vmem(comp), near, far)


def new_error_kernel(net, units, side, places, dp, mp, comp, near, far, right, *rest):
    place = Place(net, (dp, mp))
    out, buf, sems = rest[-3:]
    count = comp.shape[0] // 2
    width = units * LANES
    copies = []
    for j, k in enumerate(places):
        start = pl.multiple_of(place.block(side, k) * width, LANES)
        for half, base in enumerate((near, far)):
            for unit in range(0, units, 2):
                wide = min(2, units - unit)
                factor = [right[j * units + unit + i] for i in range(wide)]
                factor = jnp.concatenate(factor, axis=1) if wide > 1 else factor[0]
                product = jnp.dot(base[...], factor, preferred_element_type=F32)
                at = pl.ds(pl.multiple_of(start + unit * LANES, LANES), wide * LANES)
                kept = comp[half * count : (half + 1) * count, at].astype(F32)
                buf[half, j, :, unit * LANES : (unit + wide) * LANES] = (kept - product).astype(BF16)
            rows = pl.ds(pl.multiple_of(place.half(half) * count, count), count)
            copy = pltpu.make_async_copy(buf.at[half, j], out.at[rows, pl.ds(start, width)], sems.at[half, j])
            copy.start()
            copies.append(copy)
    for copy in copies:
        copy.wait()


def new_error(net, place, side, places, right, units, comp, near, far, held=None):
    rows, cols = comp.shape
    extra = [] if held is None else [in_hbm(held)]
    return call(
        functools.partial(new_error_kernel, net, units, side, places),
        "new_error",
        shaped((rows, cols), BF16),
        [SMEM] * 2 + [VMEM] * 4 + [HBM] * len(extra),
        12,
        1 + 0.7 * len(places),
        out_specs=HBM,
        scratch_shapes=[
            pltpu.VMEM((2, len(places), rows // 2, units * LANES), BF16),
            pltpu.SemaphoreType.DMA((2, len(places))),
        ],
        input_output_aliases={6: 0} if extra else {},
    )(*place, in_vmem(comp), near, far, right, *extra)


def leaf_steps(state, leaf):
    n, b = state.shape[0], LEAF
    base = leaf * b

    def splat(v):
        return jnp.broadcast_to(v, (b, n))

    def column(tile, j):
        return splat(state[b * tile : b * tile + b, base + j : base + j + 1])

    here = [column(leaf, j) for j in range(b)]
    a = [[splat(here[j][i : i + 1]) if j <= i else None for j in range(b)] for i in range(b)]
    mult = [[None] * b for _ in range(b)]
    unit = [[None] * b for _ in range(b)]
    recip, scale = [], []
    for k in range(b):
        recip.append(1.0 / a[k][k])
        scale.append(lax.rsqrt(a[k][k]))
        for i in range(k + 1, b):
            mult[i][k] = a[i][k] * recip[k]
        for i in range(k + 1, b):
            for j in range(k + 1, i + 1):
                a[i][j] = a[i][j] - mult[i][k] * a[j][k]
    for j in range(b):
        for i in range(j + 1, b):
            total = mult[i][j]
            for k in range(j + 1, i):
                total = total + mult[i][k] * unit[k][j]
            unit[i][j] = -total
    rows_x = [splat(state[base + j : base + j + 1, n:]) for j in range(b)]
    if leaf + 1 < n // b:
        rows_g = [splat(state[base + j : base + j + 1, :n]) for j in range(b)]

        def term(k, j):
            return recip[k] if j == k else recip[k] * unit[k][j]

        inverse = [[None] * b for _ in range(b)]
        for i in range(b):
            for j in range(i + 1):
                total = term(i, j)
                for k in range(i + 1, b):
                    total = total + unit[k][i] * term(k, j)
                inverse[i][j] = inverse[j][i] = total

        def mixed(rows):
            out = []
            for k in range(b):
                total = inverse[k][0] * rows[0]
                for j in range(1, b):
                    total = total + inverse[k][j] * rows[j]
                out.append(total)
            return out

        mixed_g, mixed_x = mixed(rows_g), mixed(rows_x)
        for tile in range(leaf + 1, n // b):
            at = slice(b * tile, b * tile + b)
            columns = [column(tile, j) for j in range(b)]
            g, x = state[at, :n], state[at, n:]
            for k in range(b):
                g = g - columns[k] * mixed_g[k]
                x = x - columns[k] * mixed_x[k]
            state[at, :n] = g
            state[at, n:] = x
    for i in range(b):
        total = rows_x[i]
        for j in range(i):
            total = total + unit[i][j] * rows_x[j]
        state[base + i : base + i + 1, n:] = (total * scale[i])[:1]


def leaves_kernel(leaves, source, state):
    n = state.shape[0]
    if source.shape == state.shape:
        state[...] = source[...]
    else:
        state[:, :n] = source[...]
        row = lax.broadcasted_iota(jnp.int32, (n, n), 0)
        state[:, n:] = (row == lax.broadcasted_iota(jnp.int32, (n, n), 1)).astype(F32)
    for leaf in leaves:
        leaf_steps(state, leaf)


def inverse_part(source, leaves):
    n = source.shape[0]
    return call(
        functools.partial(leaves_kernel, leaves),
        "inverse_part",
        shaped((n, 2 * n), F32),
        [VMEM],
        4,
        1.5,
        out_specs=VMEM,
    )(source)


def split2(x):
    high = x.astype(BF16)
    return high, (x - high.astype(F32)).astype(BF16)


def put2(ref, at, x):
    ref[at], ref[at + 1] = split2(x)


def get2(ref, at):
    return ref[at].astype(F32) + ref[at + 1].astype(F32)


def first_kernel(part, arrived, near, far, out, gram):
    count = part.shape[0]
    contract = (((1,), (1,)), ((), ()))
    total = lax.dot_general(near[...], near[...], contract, preferred_element_type=F32)
    total += lax.dot_general(far[...], far[...], contract, preferred_element_type=F32)
    gram[...] = total
    put2(out, count, total)

    @pl.loop(0, count)
    def _(i):
        out[i] = (part[i] + arrived[i].astype(F32)).astype(BF16)


def second_kernel(part, across, arrived, gram_in, out, kept, gram):
    units = kept.shape[0]
    total = gram_in[...] + get2(arrived, 2 * units)
    gram[...] = total
    put2(out, units, total)

    @pl.loop(0, units)
    def _(i):
        j = i + units
        out[i] = (part[j] + across[j].astype(F32) + arrived[j].astype(F32)).astype(BF16)
        kept[i] = part[i] + across[i].astype(F32) + arrived[i].astype(F32)


def third_kernel(net, dp, mp, part, arrived, gram_in, out, kept, gram, held):
    units, rank = part.shape[:2]
    half = rank // 2
    gram[...] = gram_in[...] + get2(arrived, units)
    mine = pl.multiple_of(Place(net, (dp, mp)).upper() * half, half)

    @pl.loop(0, units)
    def _(i):
        held[...] = part[i] + arrived[i].astype(F32)
        out[i] = held[pl.ds(half - mine, half), :].astype(BF16)
        kept[i] = held[pl.ds(mine, half), :]


def add_kernel(kept, arrived, out):
    @pl.loop(0, kept.shape[0])
    def _(i):
        out[i] = (kept[i].astype(F32) + arrived[i].astype(F32)).astype(BF16)


def factor_kernel(net, dp, mp, own, arrived, state, out, held):
    units, half = own.shape[:2]
    rank = 2 * half
    mine = pl.multiple_of(Place(net, (dp, mp)).upper() * half, half)
    lhs = jnp.concatenate(split2(state[:, rank:]), axis=0)
    for i in range(units):
        at = slice(i * LANES, (i + 1) * LANES)
        held[pl.ds(mine, half), at] = own[i]
        held[pl.ds(half - mine, half), at] = arrived[i]
    for i in range(0, units, 2):
        wide = min(2, units - i)
        product = jnp.dot(lhs, held[:, i * LANES : (i + wide) * LANES], preferred_element_type=F32)
        product = (product[:rank] + product[rank:]) / net.dp
        for k in range(wide):
            out[i + k] = product[:, k * LANES : (k + 1) * LANES].astype(BF16)


def base_kernel(near, far, state, near_out, far_out):
    rank = near.shape[0]
    lhs = jnp.concatenate(split2(state[:, rank:]), axis=0)
    for source, out in ((near, near_out), (far, far_out)):
        product = jnp.dot(lhs, source[...], preferred_element_type=F32)
        out[...] = (product[:rank] + product[rank:]).T.astype(BF16)


def rows_kernel(net, units, dp, mp, own, other, out):
    place = Place(net, (dp, mp))
    for side, source in ((NEAR, own), (FAR, other)):
        start = place.half(side) * (units * LANES)
        for i in range(units):
            out[pl.ds(pl.multiple_of(start + i * LANES, LANES), LANES), :] = source[i].T


class Exchange:
    def __init__(self, dp, mp):
        self.dp, self.mp = dp, mp
        mp_bits = [("mp", 1 << k) for k in range(mp.bit_length() - 1)]
        z_bits = [("dp", 2 << k) for k in range(dp.bit_length() - 2)]
        low, high = mp_bits[0], mp_bits[len(mp_bits) // 2]
        self.other = [bit for bit in mp_bits if bit not in (low, high)]
        self.scatter = [(low, high), (high, low)]
        rest = self.other + z_bits
        self.rest = list(zip(rest, rest[::-1]))
        self.replicas = list(zip(z_bits, z_bits[::-1]))
        self.low, self.high = low, high

    def send(self, x, step):
        pairs = []
        for d in range(self.dp):
            for m in range(self.mp):
                axis, bit = step[d % 2]
                to = (d ^ bit) * self.mp + m if axis == "dp" else d * self.mp + (m ^ bit)
                pairs.append((d * self.mp + m, to))
        return lax.ppermute(x, AXES, pairs)

    def core(self, x):
        return self.send(x, (("dp", 1), ("dp", 1)))


def on_device(dp, mp, grad, error, init):
    grad, error = grad[0], error[0]
    rows, cols = grad.shape
    rank = init.shape[1]
    half = rank // 2
    net = Exchange(dp, mp)
    place = [lax.axis_index(axis).astype(jnp.int32).reshape(1) for axis in AXES]
    units = cols // 8 // LANES
    square = (rank, LANES)

    comp, near, far = left_product(net, place, grad, error, init)
    near = near + net.core(far)
    for step in net.replicas:
        sent = lax.reduce_precision(near, 8, 7)
        near = sent + net.send(sent.astype(BF16), step).astype(F32)
    near = near.astype(BF16)
    far = net.core(near)

    def right(side, places, dtype):
        return right_product(net, place, side, places, units, comp, near, far, dtype)

    across = net.core(right(FAR, (2, 3), BF16))
    part = right(NEAR, (2, 3), F32)
    sent, gram = call(
        first_kernel, "first_sum",
        [shaped((2 * units + 2, *square), BF16), shaped((rank, rank), F32)],
        [VMEM] * 4, 4, 0.5, out_specs=[VMEM] * 2,
    )(part, across, near, far)
    arrived = net.send(sent, net.scatter[0])
    across = net.core(right(FAR, (0, 1), BF16))
    part = right(NEAR, (0, 1), F32)
    sent, kept, gram = call(
        second_kernel, "second_sum",
        [shaped((units + 2, *square), BF16), shaped((units, *square), F32), shaped((rank, rank), F32)],
        [VMEM] * 4, 4, 0.5, out_specs=[VMEM] * 3,
    )(part, across, arrived, gram)
    arrived = net.send(sent, net.scatter[1])
    sent, kept, gram = call(
        functools.partial(third_kernel, net), "third_sum",
        [shaped((units, half, LANES), BF16), shaped((units, half, LANES), F32), shaped((rank, rank), F32)],
        [SMEM] * 2 + [VMEM] * 3, 4, 0.5, out_specs=[VMEM] * 3,
        scratch_shapes=[pltpu.VMEM(square, F32)],
    )(*place, kept, arrived, gram)
    for bit in net.other:
        gram = gram + net.send(gram, (bit, bit))

    leaves = list(range(rank // LEAF))
    steps = len(net.rest) + 1
    state = gram
    for k in range(steps):
        share = leaves[len(leaves) * k // steps : len(leaves) * (k + 1) // steps]
        arrived = net.send(sent, net.rest[k] if k < len(net.rest) else net.rest[0])
        state = inverse_part(state, share)
        arrived, state = lax.optimization_barrier((arrived, state))
        if k < len(net.rest):
            sent = call(
                add_kernel, "pair_sum", shaped((units, half, LANES), BF16), [VMEM] * 2, 2, 0.3, out_specs=VMEM
            )(kept, arrived)
            kept = sent
    own = call(
        functools.partial(factor_kernel, net), "factor", shaped((units, *square), BF16),
        [SMEM] * 2 + [VMEM] * 3, 4, 0.7, out_specs=VMEM,
        scratch_shapes=[pltpu.VMEM((rank, units * LANES), BF16)],
    )(*place, sent, arrived, state)

    arrived = net.send(own, net.scatter[1])
    base_near, base_far = call(
        base_kernel, "base", [shaped((rows // 2, rank), BF16)] * 2, [VMEM] * 3, 4, 0.7, out_specs=[VMEM] * 2
    )(near, far, state)
    arrived, base_near, base_far = lax.optimization_barrier((arrived, base_near, base_far))
    write = functools.partial(new_error, net, place, units=units, comp=comp, near=base_near, far=base_far)
    own = jnp.concatenate([own, arrived], axis=0)
    arrived = net.send(own, net.scatter[0])
    other = net.core(own)
    out = write(NEAR, (0, 1), own)
    out = write(FAR, (0, 1), other, held=out)
    share, width = cols // mp, units * LANES
    if share == 2 * width:
        right_factor = call(
            functools.partial(rows_kernel, net, units), "factor_rows", shaped((share, rank), BF16),
            [SMEM, SMEM, VMEM, VMEM], 4, 1, out_specs=VMEM,
        )(*place, own, other)
        arrived, out, right_factor = lax.optimization_barrier((arrived, out, right_factor))
    else:
        arrived, out = lax.optimization_barrier((arrived, out))
    crossed = net.core(arrived)
    out = write(NEAR, (2, 3), arrived, held=out)
    out = write(FAR, (2, 3), crossed, held=out)
    if share != 2 * width:
        everything = jnp.concatenate([own, arrived, other, crossed], axis=0)
        here = Place(net, place)
        names = jnp.stack([here.block(side, k) for side in (NEAR, FAR) for k in range(4)])
        block = here.mp * share // width
        chosen = lax.dynamic_slice_in_dim(everything, jnp.argmax(names == block) * units, units, 0)
        chosen = jnp.swapaxes(chosen, 1, 2).reshape(width, rank)
        right_factor = lax.dynamic_slice_in_dim(chosen, here.mp * share - block * width, share, 0)
    return (out[None], right_factor)


def solution(mesh):
    return jax.shard_map(
        functools.partial(on_device, mesh.shape["dp"], mesh.shape["mp"]),
        mesh=mesh,
        in_specs=(P("dp", "mp", None), P("dp", "mp", None), P()),
        out_specs=(P("dp", "mp", None), P("mp", None)),
        check_vma=False,
    )
```

time: 105 us -> 87.2 us (0.83)
  starting transfers between devices: 35.4 us -> 26.5 us
  Pallas kernels: 36.8 us -> 30.4 us
  local copies, waits for them, and re-layouts: 4.46 us -> 0 us
  waiting for transfers between devices: 27.4 us -> 29 us
    ppermute x15, starting transfers between devices: 35.4 us -> 26.5 us  [send(): return lax.ppermute(x, AXES, pairs)]
    pallas_call x13 -> x14, Pallas kernels: 32.1 us -> 25.8 us  [the longest x1 11.2 us: left_product(): call(functools.partial(left_kernel, net, PIECES), 'left_product', [pltpu....]
    unnamed x2 -> x0, local copies, waits for them, and re-layouts: 2.48 us -> none
    reshape x1 -> x0, local copies, waits for them, and re-layouts: 1.98 us -> none  [on_device(): grad, error, table = (grad[0], error[0], table.reshape(-1))]
    ppermute x15, waiting for transfers between devices: 27.4 us -> 29 us  [send(): return lax.ppermute(x, AXES, pairs)]
  transfers between devices with their start and end apart: 15 -> 15, of which waited for: 10 -> 13; matrix products, arithmetic and copies ran while one was open for 0% -> 0% of each run, Pallas kernels for 17% -> 17%
where the time goes in v3:
time: 87.2 us; the launch traced here: 87.1 us
  Pallas kernels  30.4 us (35%)
  waiting for transfers between devices  29 us (33%)
  starting transfers between devices  26.5 us (30%)
  between operations  0.95 us (1%)
    ppermute x15, waiting for transfers between devices, send(): return lax.ppermute(x, AXES, pairs)  29 us
    ppermute x15, starting transfers between devices, send(): return lax.ppermute(x, AXES, pairs)  26.5 us
    pallas_call x1, Pallas kernels, left_product(): call(functools.partial(left_kernel, net, PIECES), 'left_product', [pltpu....  11.2 us
    pallas_call x4, Pallas kernels, new_error(): call(functools.partial(new_error_kernel, net, units, side, places), 'new_...  9.19 us
    pallas_call x3, Pallas kernels, inverse_part(): call(functools.partial(leaves_kernel, leaves), 'inverse_part', shaped((n,...  4.23 us
    pallas_call x4, Pallas kernels, right_product(): call(functools.partial(right_kernel, net, units, side, places), 'right_pr...  3.14 us
  transfers between devices with their start and end apart: 15, of which 13 were waited for; matrix products, arithmetic and copies ran while one was open for 0% of the time, Pallas kernels for 17%

profile of v3, /device:TPU:1, one launch (start us, length us, event | category | flops | bytes accessed | tf_op | source)
XLA Modules:
  0.0 87.1 jit_solution(2318941214500301156)
XLA Ops:
  0.6 11.2 %left_product.1 = (bf16[1024,7168]{1,0:T(8,128)(2,1)S(1)}, f32[128,512]{1,0:T(8,128)S(1)}, f32[128,512]{1,0:T(8,128)S(1)}) custom-call(s32[1]{0:T(128)} %bitcast.dp, s32[1]{0:T(128)} %bitcast.1.mp, bf16[1024,7168]{1,0:T(8,128)(2,1)} %bitcast.6, bf16[1024,7168]{1,0:T(8,128)(2,1)} %bitcast.7, bf16[7168,128]{1,0:T(8,128)(2,1)} %init.1), custom_call_target="tpu_custom_call" | custom-call | bytes 42000000 | tf_op jit(solution)/shard_map/left_product/pallas_call | solution.py:110
  11.9 0.1 collective-permute-start
  12.0 1.5 %collective-permute-done = f32[128,512]{1,0:T(8,128)S(1)} collective-permute-done((f32[128,512]{1,0:T(8,128)S(1)}, f32[128,512]{1,0:T(8,128)S(1)}, u32[]{:S(2)}, u32[]{:S(2)}) %collective-permute-start) | collective-permute-done | bytes 262176 | tf_op jit(solution)/shard_map/ppermute | solution.py:404
  13.5 3.5 %collective-permute-start.1 = (bf16[128,512]{1,0:T(8,128)(2,1)S(1)}, bf16[128,512]{1,0:T(8,128)(2,1)S(1)}, u32[]{:S(2)}, u32[]{:S(2)}) collective-permute-start(bf16[128,512]{1,0:T(8,128)(2,1)S(1)} %fusion.1), channel_id=1, source_target_pairs={{0,8},{1,9},{2,10},{3,11},{4,20},{5,21},{6,22},{7,23},{8,0},{9,1},... | collective-permute-start | bytes 393224 | tf_op jit(solution)/shard_map/ppermute | solution.py:404
  17.0 3.7 %collective-permute-done.1 = bf16[128,512]{1,0:T(8,128)(2,1)S(1)} collective-permute-done((bf16[128,512]{1,0:T(8,128)(2,1)S(1)}, bf16[128,512]{1,0:T(8,128)(2,1)S(1)}, u32[]{:S(2)}, u32[]{:S(2)}) %collective-permute-start.1) | collective-permute-done | bytes 131104 | tf_op jit(solution)/shard_map/ppermute | solution.py:404
  20.7 0.1 fusion
  20.8 0.7 collective-permute-start.2
  21.5 3.4 %collective-permute-done.2 = bf16[128,512]{1,0:T(8,128)(2,1)S(1)} collective-permute-done((bf16[128,512]{1,0:T(8,128)(2,1)S(1)}, bf16[128,512]{1,0:T(8,128)(2,1)S(1)}, u32[]{:S(2)}, u32[]{:S(2)}) %collective-permute-start.2) | collective-permute-done | bytes 131104 | tf_op jit(solution)/shard_map/ppermute | solution.py:404
  25.0 0.1 add_convert_fusion.near
  25.1 1.9 %collective-permute-start.3 = (bf16[128,512]{1,0:T(8,128)(2,1)S(1)}, bf16[128,512]{1,0:T(8,128)(2,1)S(1)}, u32[]{:S(2)}, u32[]{:S(2)}) collective-permute-start(bf16[128,512]{1,0:T(8,128)(2,1)S(1)} %add_convert_fusion.near), channel_id=1, source_target_pairs={{0,4},{1,5},{2,6},{3,7},{4,0},{5,1},{6,2},{7,3},{8,12},{9,13},{10,... | collective-permute-start | bytes 393224 | tf_op jit(solution)/shard_map/ppermute | solution.py:404
  26.9 1.0 %collective-permute-done.3.far = bf16[128,512]{1,0:T(8,128)(2,1)S(1)} collective-permute-done((bf16[128,512]{1,0:T(8,128)(2,1)S(1)}, bf16[128,512]{1,0:T(8,128)(2,1)S(1)}, u32[]{:S(2)}, u32[]{:S(2)}) %collective-permute-start.3) | collective-permute-done | bytes 131104 | tf_op jit(solution)/shard_map/ppermute | solution.py:404
  27.9 0.8 right_product.7
  28.7 0.4 collective-permute-start.5
  29.2 0.8 right_product.6.part
  29.9 0.6 collective-permute-done.5.arrived
  30.6 0.6 first_sum.1
  31.2 2.4 %collective-permute-start.6 = (bf16[16,128,128]{2,1,0:T(8,128)(2,1)S(1)}, bf16[16,128,128]{2,1,0:T(8,128)(2,1)S(1)}, u32[]{:S(2)}, u32[]{:S(2)}) collective-permute-start(bf16[16,128,128]{2,1,0:T(8,128)(2,1)S(1)} %get-tuple-element.30), channel_id=1, source_target_pairs={{0,1},{1,0},{2,3},{3,2},{4,6},{5,7},{6,4},{7,5},{8,9},{9,8},{10,11... | collective-permute-start | bytes 1572872 | tf_op jit(solution)/shard_map/ppermute | solution.py:404
  33.6 0.8 right_product.5
  34.4 0.7 collective-permute-start.4
  35.1 0.8 right_product.4.part
  35.9 0.6 collective-permute-done.4.across
  36.5 3.9 %collective-permute-done.6.arrived = bf16[16,128,128]{2,1,0:T(8,128)(2,1)S(1)} collective-permute-done((bf16[16,128,128]{2,1,0:T(8,128)(2,1)S(1)}, bf16[16,128,128]{2,1,0:T(8,128)(2,1)S(1)}, u32[]{:S(2)}, u32[]{:S(2)}) %collective-permute-start.6) | collective-permute-done | bytes 524320 | tf_op jit(solution)/shard_map/ppermute | solution.py:404
  40.5 0.2 second_sum.1
  40.7 1.5 %collective-permute-start.7 = (bf16[9,128,128]{2,1,0:T(8,128)(2,1)S(1)}, bf16[9,128,128]{2,1,0:T(8,128)(2,1)S(1)}, u32[]{:S(2)}, u32[]{:S(2)}) collective-permute-start(bf16[9,128,128]{2,1,0:T(8,128)(2,1)S(1)} %get-tuple-element.33), channel_id=1, source_target_pairs={{0,2},{1,3},{2,0},{3,1},{4,5},{5,4},{6,7},{7,6},{8,10},{9,11},{10,... | collective-permute-start | bytes 884744 | tf_op jit(solution)/shard_map/ppermute | solution.py:404
  42.2 4.4 %collective-permute-done.7.arrived = bf16[9,128,128]{2,1,0:T(8,128)(2,1)S(1)} collective-permute-done((bf16[9,128,128]{2,1,0:T(8,128)(2,1)S(1)}, bf16[9,128,128]{2,1,0:T(8,128)(2,1)S(1)}, u32[]{:S(2)}, u32[]{:S(2)}) %collective-permute-start.7) | collective-permute-done | bytes 294944 | tf_op jit(solution)/shard_map/ppermute | solution.py:404
  46.6 0.1 third_sum.1
  46.8 1.2 %collective-permute-start.8 = (bf16[7,64,128]{2,1,0:T(8,128)(2,1)S(1)}, bf16[7,64,128]{2,1,0:T(8,128)(2,1)S(1)}, u32[]{:S(2)}, u32[]{:S(2)}) collective-permute-start(bf16[7,64,128]{2,1,0:T(8,128)(2,1)S(1)} %get-tuple-element.36), channel_id=1, source_target_pairs={{0,8},{1,9},{2,10},{3,11},{4,20},{5,21},{6,22},{7,23},{8,0},{9,1},... | collective-permute-start | bytes 344072 | tf_op jit(solution)/shard_map/ppermute | solution.py:404
  48.0 1.4 %inverse_part.3.source = f32[128,256]{1,0:T(8,128)S(1)} custom-call(f32[128,128]{1,0:T(8,128)S(1)} %get-tuple-element.37.source), custom_call_target="tpu_custom_call" | custom-call | bytes 5250000 | tf_op jit(solution)/shard_map/inverse_part/pallas_call | solution.py:282
  49.4 2.0 %collective-permute-done.8.arrived = bf16[7,64,128]{2,1,0:T(8,128)(2,1)S(1)} collective-permute-done((bf16[7,64,128]{2,1,0:T(8,128)(2,1)S(1)}, bf16[7,64,128]{2,1,0:T(8,128)(2,1)S(1)}, u32[]{:S(2)}, u32[]{:S(2)}) %collective-permute-start.8) | collective-permute-done | bytes 114720 | tf_op jit(solution)/shard_map/ppermute | solution.py:404
  51.4 0.1 pair_sum.2.kept
  51.4 1.6 %collective-permute-start.9 = (bf16[7,64,128]{2,1,0:T(8,128)(2,1)S(1)}, bf16[7,64,128]{2,1,0:T(8,128)(2,1)S(1)}, u32[]{:S(2)}, u32[]{:S(2)}) collective-permute-start(bf16[7,64,128]{2,1,0:T(8,128)(2,1)S(1)} %pair_sum.2.kept), channel_id=1, source_target_pairs={{0,16},{1,17},{2,18},{3,19},{4,12},{5,13},{6,14},{7,15},{8,24},{9,... | collective-permute-start | bytes 344072 | tf_op jit(solution)/shard_map/ppermute | solution.py:404
  53.0 1.3 %inverse_part.4.source = f32[128,256]{1,0:T(8,128)S(1)} custom-call(f32[128,256]{1,0:T(8,128)S(1)} %inverse_part.3.source), custom_call_target="tpu_custom_call" | custom-call | bytes 5250000 | tf_op jit(solution)/shard_map/inverse_part/pallas_call | solution.py:282
  54.3 0.8 collective-permute-done.9.arrived
  55.2 2.3 %collective-permute-start.10 = (bf16[7,64,128]{2,1,0:T(8,128)(2,1)S(1)}, bf16[7,64,128]{2,1,0:T(8,128)(2,1)S(1)}, u32[]{:S(2)}, u32[]{:S(2)}) collective-permute-start(bf16[7,64,128]{2,1,0:T(8,128)(2,1)S(1)} %pair_sum.3.own), channel_id=1, source_target_pairs={{0,8},{1,9},{2,10},{3,11},{4,20},{5,21},{6,22},{7,23},{8,0},{9,1},... | collective-permute-start | bytes 344072 | tf_op jit(solution)/shard_map/ppermute | solution.py:404
  57.5 1.5 %inverse_part.5.state = f32[128,256]{1,0:T(8,128)S(1)} custom-call(f32[128,256]{1,0:T(8,128)S(1)} %inverse_part.4.source), custom_call_target="tpu_custom_call" | custom-call | bytes 5250000 | tf_op jit(solution)/shard_map/inverse_part/pallas_call | solution.py:282
  59.1 3.2 %collective-permute-done.10.arrived = bf16[7,64,128]{2,1,0:T(8,128)(2,1)S(1)} collective-permute-done((bf16[7,64,128]{2,1,0:T(8,128)(2,1)S(1)}, bf16[7,64,128]{2,1,0:T(8,128)(2,1)S(1)}, u32[]{:S(2)}, u32[]{:S(2)}) %collective-permute-start.10) | collective-permute-done | bytes 114720 | tf_op jit(solution)/shard_map/ppermute | solution.py:404
  62.3 0.3 factor.1
  62.6 1.9 %collective-permute-start.11 = (bf16[7,128,128]{2,1,0:T(8,128)(2,1)S(1)}, bf16[7,128,128]{2,1,0:T(8,128)(2,1)S(1)}, u32[]{:S(2)}, u32[]{:S(2)}) collective-permute-start(bf16[7,128,128]{2,1,0:T(8,128)(2,1)S(1)} %factor.1), channel_id=1, source_target_pairs={{0,2},{1,3},{2,0},{3,1},{4,5},{5,4},{6,7},{7,6},{8,10},{9,11},{10,... | collective-permute-start | bytes 688136 | tf_op jit(solution)/shard_map/ppermute | solution.py:404
  64.6 0.3 base.1
  64.9 3.1 %collective-permute-done.11 = bf16[7,128,128]{2,1,0:T(8,128)(2,1)S(1)} collective-permute-done((bf16[7,128,128]{2,1,0:T(8,128)(2,1)S(1)}, bf16[7,128,128]{2,1,0:T(8,128)(2,1)S(1)}, u32[]{:S(2)}, u32[]{:S(2)}) %collective-permute-start.11) | collective-permute-done | bytes 229408 | tf_op jit(solution)/shard_map/ppermute | solution.py:404
  68.0 5.7 %collective-permute-start.13 = (bf16[14,128,128]{2,1,0:T(8,128)(2,1)S(1)}, bf16[14,128,128]{2,1,0:T(8,128)(2,1)S(1)}, u32[]{:S(2)}, u32[]{:S(2)}) collective-permute-start(bf16[14,128,128]{2,1,0:T(8,128)(2,1)S(1)} %pad_maximum_fusion.right.own), channel_id=1, source_target_pairs={{0,4},{1,5},{2,6},{3,7},{4,0},{5,1},{6,2},{7,3},{8,12},{9,13},{10,... | collective-permute-start | bytes 1376264 | tf_op jit(solution)/shard_map/ppermute | solution.py:404
  73.8 1.7 %collective-permute-start.12 = (bf16[14,128,128]{2,1,0:T(8,128)(2,1)S(1)}, bf16[14,128,128]{2,1,0:T(8,128)(2,1)S(1)}, u32[]{:S(2)}, u32[]{:S(2)}) collective-permute-start(bf16[14,128,128]{2,1,0:T(8,128)(2,1)S(1)} %pad_maximum_fusion.right.own), channel_id=1, source_target_pairs={{0,1},{1,0},{2,3},{3,2},{4,6},{5,7},{6,4},{7,5},{8,9},{9,8},{10,11... | collective-permute-start | bytes 1376264 | tf_op jit(solution)/shard_map/ppermute | solution.py:404
  75.5 2.3 %new_error.4.rest_0_ = bf16[1024,7168]{1,0:T(8,128)(2,1)} custom-call(s32[1]{0:T(128)} %bitcast.dp, s32[1]{0:T(128)} %bitcast.1.mp, bf16[1024,7168]{1,0:T(8,128)(2,1)S(1)} %get-tuple-element.27.comp, bf16[512,128]{1,0:T(8,128)(2,1)S(1)} %get-tuple-element.46.near, bf16[512,128]{1,0:T(8,128)(2,1)S(1)} %get-tuple-element.47.far, ...), custom_call_target="tpu_custom_call" | custom-call | bytes 8400000 | tf_op jit(solution)/shard_map/new_error/pallas_call | solution.py:182
  77.8 0.0 collective-permute-done.13.right.other
  77.8 0.9 %factor_rows.1 = bf16[1792,128]{1,0:T(8,128)(2,1)} custom-call(s32[1]{0:T(128)} %bitcast.dp, s32[1]{0:T(128)} %bitcast.1.mp, bf16[14,128,128]{2,1,0:T(8,128)(2,1)S(1)} %pad_maximum_fusion.right.own, bf16[14,128,128]{2,1,0:T(8,128)(2,1)S(1)} %collective-permute-done.13.right.other), custom_call_target="tpu_custom_call" | custom-call | bytes 3500000 | tf_op jit(solution)/shard_map/factor_rows/pallas_call | solution.py:488
  78.8 2.3 %new_error.5.rest_0_ = bf16[1024,7168]{1,0:T(8,128)(2,1)} custom-call(s32[1]{0:T(128)} %bitcast.dp, s32[1]{0:T(128)} %bitcast.1.mp, bf16[1024,7168]{1,0:T(8,128)(2,1)S(1)} %get-tuple-element.27.comp, bf16[512,128]{1,0:T(8,128)(2,1)S(1)} %get-tuple-element.46.near, bf16[512,128]{1,0:T(8,128)(2,1)S(1)} %get-tuple-element.47.far, ...), custom_call_target="tpu_custom_call", output_to_operand_aliasing={{}: (6, {})} | custom-call | bytes 8400000 | tf_op jit(solution)/shard_map/new_error/pallas_call | solution.py:182
  81.1 0.6 collective-permute-done.12.right
  81.7 0.7 collective-permute-start.14
  82.3 2.3 %new_error.6.rest_0_ = bf16[1024,7168]{1,0:T(8,128)(2,1)} custom-call(s32[1]{0:T(128)} %bitcast.dp, s32[1]{0:T(128)} %bitcast.1.mp, bf16[1024,7168]{1,0:T(8,128)(2,1)S(1)} %get-tuple-element.27.comp, bf16[512,128]{1,0:T(8,128)(2,1)S(1)} %get-tuple-element.46.near, bf16[512,128]{1,0:T(8,128)(2,1)S(1)} %get-tuple-element.47.far, ...), custom_call_target="tpu_custom_call", output_to_operand_aliasing={{}: (6, {})} | custom-call | bytes 8400000 | tf_op jit(solution)/shard_map/new_error/pallas_call | solution.py:182
  84.6 0.0 collective-permute-done.14.right
  84.6 2.3 %new_error.7 = bf16[1024,7168]{1,0:T(8,128)(2,1)} custom-call(s32[1]{0:T(128)} %bitcast.dp, s32[1]{0:T(128)} %bitcast.1.mp, bf16[1024,7168]{1,0:T(8,128)(2,1)S(1)} %get-tuple-element.27.comp, bf16[512,128]{1,0:T(8,128)(2,1)S(1)} %get-tuple-element.46.near, bf16[512,128]{1,0:T(8,128)(2,1)S(1)} %get-tuple-element.47.far, ...), custom_call_target="tpu_custom_call", output_to_operand_aliasing={{}: (6, {})} | custom-call | bytes 8400000 | tf_op jit(solution)/shard_map/new_error/pallas_call | solution.py:182
  (3 shorter events, 0.1 us)
Async XLA Ops:
  11.9 1.6 %collective-permute-start = (f32[128,512]{1,0:T(8,128)S(1)}, f32[128,512]{1,0:T(8,128)S(1)}, u32[]{:S(2)}, u32[]{:S(2)}) collective-permute-start(f32[128,512]{1,0:T(8,128)S(1)} %get-tuple-element.29), channel_id=1, source_target_pairs={{0,4},{1,5},{2,6},{3,7},{4,0},{5,1},{6,2},{7,3},{8,12},{9,13},{10,... | collective-permute-start | bytes 786440 | tf_op jit(solution)/shard_map/ppermute | solution.py:404
  13.5 7.2 %collective-permute-start.1 = (bf16[128,512]{1,0:T(8,128)(2,1)S(1)}, bf16[128,512]{1,0:T(8,128)(2,1)S(1)}, u32[]{:S(2)}, u32[]{:S(2)}) collective-permute-start(bf16[128,512]{1,0:T(8,128)(2,1)S(1)} %fusion.1), channel_id=1, source_target_pairs={{0,8},{1,9},{2,10},{3,11},{4,20},{5,21},{6,22},{7,23},{8,0},{9,1},... | collective-permute-start | bytes 393224 | tf_op jit(solution)/shard_map/ppermute | solution.py:404
  20.8 4.2 %collective-permute-start.2 = (bf16[128,512]{1,0:T(8,128)(2,1)S(1)}, bf16[128,512]{1,0:T(8,128)(2,1)S(1)}, u32[]{:S(2)}, u32[]{:S(2)}) collective-permute-start(bf16[128,512]{1,0:T(8,128)(2,1)S(1)} %fusion), channel_id=1, source_target_pairs={{0,16},{1,17},{2,18},{3,19},{4,12},{5,13},{6,14},{7,15},{8,24},{9,... | collective-permute-start | bytes 393224 | tf_op jit(solution)/shard_map/ppermute | solution.py:404
  25.1 2.8 %collective-permute-start.3 = (bf16[128,512]{1,0:T(8,128)(2,1)S(1)}, bf16[128,512]{1,0:T(8,128)(2,1)S(1)}, u32[]{:S(2)}, u32[]{:S(2)}) collective-permute-start(bf16[128,512]{1,0:T(8,128)(2,1)S(1)} %add_convert_fusion.near), channel_id=1, source_target_pairs={{0,4},{1,5},{2,6},{3,7},{4,0},{5,1},{6,2},{7,3},{8,12},{9,13},{10,... | collective-permute-start | bytes 393224 | tf_op jit(solution)/shard_map/ppermute | solution.py:404
  28.7 1.9 %collective-permute-start.5 = (bf16[14,128,128]{2,1,0:T(8,128)(2,1)S(1)}, bf16[14,128,128]{2,1,0:T(8,128)(2,1)S(1)}, u32[]{:S(2)}, u32[]{:S(2)}) collective-permute-start(bf16[14,128,128]{2,1,0:T(8,128)(2,1)S(1)} %right_product.7), channel_id=1, source_target_pairs={{0,4},{1,5},{2,6},{3,7},{4,0},{5,1},{6,2},{7,3},{8,12},{9,13},{10,... | collective-permute-start | bytes 1376264 | tf_op jit(solution)/shard_map/ppermute | solution.py:404
  31.2 9.3 %collective-permute-start.6 = (bf16[16,128,128]{2,1,0:T(8,128)(2,1)S(1)}, bf16[16,128,128]{2,1,0:T(8,128)(2,1)S(1)}, u32[]{:S(2)}, u32[]{:S(2)}) collective-permute-start(bf16[16,128,128]{2,1,0:T(8,128)(2,1)S(1)} %get-tuple-element.30), channel_id=1, source_target_pairs={{0,1},{1,0},{2,3},{3,2},{4,6},{5,7},{6,4},{7,5},{8,9},{9,8},{10,11... | collective-permute-start | bytes 1572872 | tf_op jit(solution)/shard_map/ppermute | solution.py:404
  34.4 2.1 %collective-permute-start.4 = (bf16[14,128,128]{2,1,0:T(8,128)(2,1)S(1)}, bf16[14,128,128]{2,1,0:T(8,128)(2,1)S(1)}, u32[]{:S(2)}, u32[]{:S(2)}) collective-permute-start(bf16[14,128,128]{2,1,0:T(8,128)(2,1)S(1)} %right_product.5), channel_id=1, source_target_pairs={{0,4},{1,5},{2,6},{3,7},{4,0},{5,1},{6,2},{7,3},{8,12},{9,13},{10,... | collective-permute-start | bytes 1376264 | tf_op jit(solution)/shard_map/ppermute | solution.py:404
  40.7 5.9 %collective-permute-start.7 = (bf16[9,128,128]{2,1,0:T(8,128)(2,1)S(1)}, bf16[9,128,128]{2,1,0:T(8,128)(2,1)S(1)}, u32[]{:S(2)}, u32[]{:S(2)}) collective-permute-start(bf16[9,128,128]{2,1,0:T(8,128)(2,1)S(1)} %get-tuple-element.33), channel_id=1, source_target_pairs={{0,2},{1,3},{2,0},{3,1},{4,5},{5,4},{6,7},{7,6},{8,10},{9,11},{10,... | collective-permute-start | bytes 884744 | tf_op jit(solution)/shard_map/ppermute | solution.py:404
  46.8 4.6 %collective-permute-start.8 = (bf16[7,64,128]{2,1,0:T(8,128)(2,1)S(1)}, bf16[7,64,128]{2,1,0:T(8,128)(2,1)S(1)}, u32[]{:S(2)}, u32[]{:S(2)}) collective-permute-start(bf16[7,64,128]{2,1,0:T(8,128)(2,1)S(1)} %get-tuple-element.36), channel_id=1, source_target_pairs={{0,8},{1,9},{2,10},{3,11},{4,20},{5,21},{6,22},{7,23},{8,0},{9,1},... | collective-permute-start | bytes 344072 | tf_op jit(solution)/shard_map/ppermute | solution.py:404
  51.4 3.7 %collective-permute-start.9 = (bf16[7,64,128]{2,1,0:T(8,128)(2,1)S(1)}, bf16[7,64,128]{2,1,0:T(8,128)(2,1)S(1)}, u32[]{:S(2)}, u32[]{:S(2)}) collective-permute-start(bf16[7,64,128]{2,1,0:T(8,128)(2,1)S(1)} %pair_sum.2.kept), channel_id=1, source_target_pairs={{0,16},{1,17},{2,18},{3,19},{4,12},{5,13},{6,14},{7,15},{8,24},{9,... | collective-permute-start | bytes 344072 | tf_op jit(solution)/shard_map/ppermute | solution.py:404
  55.2 7.1 %collective-permute-start.10 = (bf16[7,64,128]{2,1,0:T(8,128)(2,1)S(1)}, bf16[7,64,128]{2,1,0:T(8,128)(2,1)S(1)}, u32[]{:S(2)}, u32[]{:S(2)}) collective-permute-start(bf16[7,64,128]{2,1,0:T(8,128)(2,1)S(1)} %pair_sum.3.own), channel_id=1, source_target_pairs={{0,8},{1,9},{2,10},{3,11},{4,20},{5,21},{6,22},{7,23},{8,0},{9,1},... | collective-permute-start | bytes 344072 | tf_op jit(solution)/shard_map/ppermute | solution.py:404
  62.6 5.3 %collective-permute-start.11 = (bf16[7,128,128]{2,1,0:T(8,128)(2,1)S(1)}, bf16[7,128,128]{2,1,0:T(8,128)(2,1)S(1)}, u32[]{:S(2)}, u32[]{:S(2)}) collective-permute-start(bf16[7,128,128]{2,1,0:T(8,128)(2,1)S(1)} %factor.1), channel_id=1, source_target_pairs={{0,2},{1,3},{2,0},{3,1},{4,5},{5,4},{6,7},{7,6},{8,10},{9,11},{10,... | collective-permute-start | bytes 688136 | tf_op jit(solution)/shard_map/ppermute | solution.py:404
  68.0 9.8 %collective-permute-start.13 = (bf16[14,128,128]{2,1,0:T(8,128)(2,1)S(1)}, bf16[14,128,128]{2,1,0:T(8,128)(2,1)S(1)}, u32[]{:S(2)}, u32[]{:S(2)}) collective-permute-start(bf16[14,128,128]{2,1,0:T(8,128)(2,1)S(1)} %pad_maximum_fusion.right.own), channel_id=1, source_target_pairs={{0,4},{1,5},{2,6},{3,7},{4,0},{5,1},{6,2},{7,3},{8,12},{9,13},{10,... | collective-permute-start | bytes 1376264 | tf_op jit(solution)/shard_map/ppermute | solution.py:404
  73.8 7.9 %collective-permute-start.12 = (bf16[14,128,128]{2,1,0:T(8,128)(2,1)S(1)}, bf16[14,128,128]{2,1,0:T(8,128)(2,1)S(1)}, u32[]{:S(2)}, u32[]{:S(2)}) collective-permute-start(bf16[14,128,128]{2,1,0:T(8,128)(2,1)S(1)} %pad_maximum_fusion.right.own), channel_id=1, source_target_pairs={{0,1},{1,0},{2,3},{3,2},{4,6},{5,7},{6,4},{7,5},{8,9},{9,8},{10,11... | collective-permute-start | bytes 1376264 | tf_op jit(solution)/shard_map/ppermute | solution.py:404
  81.7 3.0 %collective-permute-start.14 = (bf16[14,128,128]{2,1,0:T(8,128)(2,1)S(1)}, bf16[14,128,128]{2,1,0:T(8,128)(2,1)S(1)}, u32[]{:S(2)}, u32[]{:S(2)}) collective-permute-start(bf16[14,128,128]{2,1,0:T(8,128)(2,1)S(1)} %collective-permute-done.12.right), channel_id=1, source_target_pairs={{0,4},{1,5},{2,6},{3,7},{4,0},{5,1},{6,2},{7,3},{8,12},{9,13},{10,... | collective-permute-start | bytes 1376264 | tf_op jit(solution)/shard_map/ppermute | solution.py:404

commit v4 on v3

--- a/solution.py
+++ b/solution.py
@@ -41,10 +41,6 @@
         low = self.bit(self.net.low) ^ (a + (b - a) * core)
         high = self.bit(self.net.high) ^ (b + (a - b) * core)
         return high * 4 + low * 2 + core
-
-    def upper(self):
-        first, second = (self.bit(name) for name in self.net.rest[0])
-        return first + (second - first) * self.core
 
 
 def call(kernel, name, outs, ins, vmem_mib, micros, **more):
@@ -167,11 +163,14 @@
                 product = jnp.dot(base[...], factor, preferred_element_type=F32)
                 at = pl.ds(pl.multiple_of(start + unit * LANES, LANES), wide * LANES)
                 kept = comp[half * count : (half + 1) * count, at].astype(F32)
-                buf[half, j, :, unit * LANES : (unit + wide) * LANES] = (kept - product).astype(BF16)
-            rows = pl.ds(pl.multiple_of(place.half(half) * count, count), count)
-            copy = pltpu.make_async_copy(buf.at[half, j], out.at[rows, pl.ds(start, width)], sems.at[half, j])
-            copy.start()
-            copies.append(copy)
+                here = pl.ds(unit * LANES, wide * LANES)
+                buf[half, j, :, here] = (kept - product).astype(BF16)
+                rows = pl.ds(pl.multiple_of(place.half(half) * count, count), count)
+                copy = pltpu.make_async_copy(
+                    buf.at[half, j, :, here], out.at[rows, at], sems.at[half, j, unit // 2]
+                )
+                copy.start()
+                copies.append(copy)
     for copy in copies:
         copy.wait()
 
@@ -189,7 +188,7 @@
         out_specs=HBM,
         scratch_shapes=[
             pltpu.VMEM((2, len(places), rows // 2, units * LANES), BF16),
-            pltpu.SemaphoreType.DMA((2, len(places))),
+            pltpu.SemaphoreType.DMA((2, len(places), (units + 1) // 2)),
         ],
         input_output_aliases={6: 0} if extra else {},
     )(*place, in_vmem(comp), near, far, right, *extra)
@@ -311,8 +310,7 @@
     gram[...] = total
     put2(out, count, total)
 
-    @pl.loop(0, count)
-    def _(i):
+    for i in range(count):
         out[i] = (part[i] + arrived[i].astype(F32)).astype(BF16)
 
 
@@ -322,47 +320,35 @@
     gram[...] = total
     put2(out, units, total)
 
-    @pl.loop(0, units)
-    def _(i):
+    for i in range(units):
         j = i + units
         out[i] = (part[j] + across[j].astype(F32) + arrived[j].astype(F32)).astype(BF16)
         kept[i] = part[i] + across[i].astype(F32) + arrived[i].astype(F32)
 
 
-def third_kernel(net, dp, mp, part, arrived, gram_in, out, kept, gram, held):
-    units, rank = part.shape[:2]
-    half = rank // 2
+def third_kernel(part, arrived, gram_in, out, gram):
+    units = part.shape[0]
     gram[...] = gram_in[...] + get2(arrived, units)
-    mine = pl.multiple_of(Place(net, (dp, mp)).upper() * half, half)
-
-    @pl.loop(0, units)
-    def _(i):
-        held[...] = part[i] + arrived[i].astype(F32)
-        out[i] = held[pl.ds(half - mine, half), :].astype(BF16)
-        kept[i] = held[pl.ds(mine, half), :]
+    for i in range(units):
+        out[i] = (part[i] + arrived[i].astype(F32)).astype(BF16)
 
 
 def add_kernel(kept, arrived, out):
-    @pl.loop(0, kept.shape[0])
-    def _(i):
+    for i in range(kept.shape[0]):
         out[i] = (kept[i].astype(F32) + arrived[i].astype(F32)).astype(BF16)
 
 
-def factor_kernel(net, dp, mp, own, arrived, state, out, held):
-    units, half = own.shape[:2]
-    rank = 2 * half
-    mine = pl.multiple_of(Place(net, (dp, mp)).upper() * half, half)
+def factor_kernel(replicas, own, arrived, state, out):
+    units, rank = own.shape[:2]
     lhs = jnp.concatenate(split2(state[:, rank:]), axis=0)
-    for i in range(units):
-        at = slice(i * LANES, (i + 1) * LANES)
-        held[pl.ds(mine, half), at] = own[i]
-        held[pl.ds(half - mine, half), at] = arrived[i]
     for i in range(0, units, 2):
-        wide = min(2, units - i)
-        product = jnp.dot(lhs, held[:, i * LANES : (i + wide) * LANES], preferred_element_type=F32)
-        product = (product[:rank] + product[rank:]) / net.dp
-        for k in range(wide):
-            out[i + k] = product[:, k * LANES : (k + 1) * LANES].astype(BF16)
+        some = range(i, min(i + 2, units))
+        summed = [(own[k].astype(F32) + arrived[k].astype(F32)).astype(BF16) for k in some]
+        summed = jnp.concatenate(summed, axis=1) if len(summed) > 1 else summed[0]
+        product = jnp.dot(lhs, summed, preferred_element_type=F32)
+        product = (product[:rank] + product[rank:]) / replicas
+        for k in some:
+            out[k] = product[:, (k - i) * LANES : (k - i + 1) * LANES].astype(BF16)
 
 
 def base_kernel(near, far, state, near_out, far_out):
@@ -411,7 +397,6 @@
     grad, error = grad[0], error[0]
     rows, cols = grad.shape
     rank = init.shape[1]
-    half = rank // 2
     net = Exchange(dp, mp)
     place = [lax.axis_index(axis).astype(jnp.int32).reshape(1) for axis in AXES]
     units = cols // 8 // LANES
@@ -444,33 +429,29 @@
         [VMEM] * 4, 4, 0.5, out_specs=[VMEM] * 3,
     )(part, across, arrived, gram)
     arrived = net.send(sent, net.scatter[1])
-    sent, kept, gram = call(
-        functools.partial(third_kernel, net), "third_sum",
-        [shaped((units, half, LANES), BF16), shaped((units, half, LANES), F32), shaped((rank, rank), F32)],
-        [SMEM] * 2 + [VMEM] * 3, 4, 0.5, out_specs=[VMEM] * 3,
-        scratch_shapes=[pltpu.VMEM(square, F32)],
-    )(*place, kept, arrived, gram)
+    sent, gram = call(
+        third_kernel, "third_sum",
+        [shaped((units, *square), BF16), shaped((rank, rank), F32)],
+        [VMEM] * 3, 4, 0.5, out_specs=[VMEM] * 2,
+    )(kept, arrived, gram)
     for bit in net.other:
         gram = gram + net.send(gram, (bit, bit))
 
     leaves = list(range(rank // LEAF))
-    steps = len(net.rest) + 1
+    steps = len(net.rest)
     state = gram
-    for k in range(steps):
-        share = leaves[len(leaves) * k // steps : len(leaves) * (k + 1) // steps]
-        arrived = net.send(sent, net.rest[k] if k < len(net.rest) else net.rest[0])
-        state = inverse_part(state, share)
+    for k, step in enumerate(net.rest):
+        arrived = net.send(sent, step)
+        state = inverse_part(state, leaves[len(leaves) * k // steps : len(leaves) * (k + 1) // steps])
         arrived, state = lax.optimization_barrier((arrived, state))
-        if k < len(net.rest):
+        if k < steps - 1:
             sent = call(
-                add_kernel, "pair_sum", shaped((units, half, LANES), BF16), [VMEM] * 2, 2, 0.3, out_specs=VMEM
-            )(kept, arrived)
-            kept = sent
+                add_kernel, "pair_sum", shaped((units, *square), BF16), [VMEM] * 2, 2, 0.3, out_specs=VMEM
+            )(sent, arrived)
     own = call(
-        functools.partial(factor_kernel, net), "factor", shaped((units, *square), BF16),
-        [SMEM] * 2 + [VMEM] * 3, 4, 0.7, out_specs=VMEM,
-        scratch_shapes=[pltpu.VMEM((rank, units * LANES), BF16)],
-    )(*place, sent, arrived, state)
+        functools.partial(factor_kernel, dp), "factor", shaped((units, *square), BF16),
+        [VMEM] * 3, 4, 0.7, out_specs=VMEM,
+    )(sent, arrived, state)
 
     arrived = net.send(own, net.scatter[1])
     base_near, base_far = call(

time: 87.2 us -> 85.1 us (0.976)
  starting transfers between devices: 26.5 us -> 19.7 us
  waiting for transfers between devices: 29 us -> 34 us
    ppermute x15 -> x14, starting transfers between devices: 26.5 us -> 19.7 us  [send(): return lax.ppermute(x, AXES, pairs)]
    ppermute x15 -> x14, waiting for transfers between devices: 29 us -> 34 us  [send(): return lax.ppermute(x, AXES, pairs)]
    pallas_call x3 -> x2, Pallas kernels: 4.23 us -> 4.49 us  [inverse_part(): call(functools.partial(leaves_kernel, leaves), 'inverse_part', shaped((n,...]
  transfers between devices with their start and end apart: 15 -> 14, of which waited for: 13 -> 12; matrix products, arithmetic and copies ran while one was open for 0% -> 0% of each run, Pallas kernels for 17% -> 18%
where the time goes in v4:
time: 85.1 us; the launch traced here: 85 us
  waiting for transfers between devices  34 us (40%)
  Pallas kernels  30.2 us (35%)
  starting transfers between devices  19.7 us (23%)
  between operations  0.95 us (1%)
    ppermute x14, waiting for transfers between devices, send(): return lax.ppermute(x, AXES, pairs)  34 us
    ppermute x14, starting transfers between devices, send(): return lax.ppermute(x, AXES, pairs)  19.7 us
    pallas_call x1, Pallas kernels, left_product(): call(functools.partial(left_kernel, net, PIECES), 'left_product', [pltpu....  11.2 us
    pallas_call x4, Pallas kernels, new_error(): call(functools.partial(new_error_kernel, net, units, side, places), 'new_...  9.24 us
    pallas_call x2, Pallas kernels, inverse_part(): call(functools.partial(leaves_kernel, leaves), 'inverse_part', shaped((n,...  4.49 us
    pallas_call x4, Pallas kernels, right_product(): call(functools.partial(right_kernel, net, units, side, places), 'right_pr...  3.14 us
  transfers between devices with their start and end apart: 14, of which 12 were waited for; matrix products, arithmetic and copies ran while one was open for 0% of the time, Pallas kernels for 18%

profile of v4, /device:TPU:1, one launch (start us, length us, event | category | flops | bytes accessed | tf_op | source)
XLA Modules:
  0.0 85.0 jit_solution(11788111159386990399)
XLA Ops:
  0.6 11.2 %left_product.1 = (bf16[1024,7168]{1,0:T(8,128)(2,1)S(1)}, f32[128,512]{1,0:T(8,128)S(1)}, f32[128,512]{1,0:T(8,128)S(1)}) custom-call(s32[1]{0:T(128)} %bitcast.dp, s32[1]{0:T(128)} %bitcast.1.mp, bf16[1024,7168]{1,0:T(8,128)(2,1)} %bitcast.6, bf16[1024,7168]{1,0:T(8,128)(2,1)} %bitcast.7, bf16[7168,128]{1,0:T(8,128)(2,1)} %init.1), custom_call_target="tpu_custom_call" | custom-call | bytes 42000000 | tf_op jit(solution)/shard_map/left_product/pallas_call | solution.py:106
  11.9 0.1 collective-permute-start
  12.0 1.5 %collective-permute-done = f32[128,512]{1,0:T(8,128)S(1)} collective-permute-done((f32[128,512]{1,0:T(8,128)S(1)}, f32[128,512]{1,0:T(8,128)S(1)}, u32[]{:S(2)}, u32[]{:S(2)}) %collective-permute-start) | collective-permute-done | bytes 262176 | tf_op jit(solution)/shard_map/ppermute | solution.py:390
  13.5 3.5 %collective-permute-start.1 = (bf16[128,512]{1,0:T(8,128)(2,1)S(1)}, bf16[128,512]{1,0:T(8,128)(2,1)S(1)}, u32[]{:S(2)}, u32[]{:S(2)}) collective-permute-start(bf16[128,512]{1,0:T(8,128)(2,1)S(1)} %fusion.1), channel_id=1, source_target_pairs={{0,8},{1,9},{2,10},{3,11},{4,20},{5,21},{6,22},{7,23},{8,0},{9,1},... | collective-permute-start | bytes 393224 | tf_op jit(solution)/shard_map/ppermute | solution.py:390
  17.0 3.7 %collective-permute-done.1 = bf16[128,512]{1,0:T(8,128)(2,1)S(1)} collective-permute-done((bf16[128,512]{1,0:T(8,128)(2,1)S(1)}, bf16[128,512]{1,0:T(8,128)(2,1)S(1)}, u32[]{:S(2)}, u32[]{:S(2)}) %collective-permute-start.1) | collective-permute-done | bytes 131104 | tf_op jit(solution)/shard_map/ppermute | solution.py:390
  20.7 0.1 fusion
  20.8 0.7 collective-permute-start.2
  21.5 3.4 %collective-permute-done.2 = bf16[128,512]{1,0:T(8,128)(2,1)S(1)} collective-permute-done((bf16[128,512]{1,0:T(8,128)(2,1)S(1)}, bf16[128,512]{1,0:T(8,128)(2,1)S(1)}, u32[]{:S(2)}, u32[]{:S(2)}) %collective-permute-start.2) | collective-permute-done | bytes 131104 | tf_op jit(solution)/shard_map/ppermute | solution.py:390
  25.0 0.1 add_convert_fusion.near
  25.1 1.9 %collective-permute-start.3 = (bf16[128,512]{1,0:T(8,128)(2,1)S(1)}, bf16[128,512]{1,0:T(8,128)(2,1)S(1)}, u32[]{:S(2)}, u32[]{:S(2)}) collective-permute-start(bf16[128,512]{1,0:T(8,128)(2,1)S(1)} %add_convert_fusion.near), channel_id=1, source_target_pairs={{0,4},{1,5},{2,6},{3,7},{4,0},{5,1},{6,2},{7,3},{8,12},{9,13},{10,... | collective-permute-start | bytes 393224 | tf_op jit(solution)/shard_map/ppermute | solution.py:390
  26.9 1.0 %collective-permute-done.3.far = bf16[128,512]{1,0:T(8,128)(2,1)S(1)} collective-permute-done((bf16[128,512]{1,0:T(8,128)(2,1)S(1)}, bf16[128,512]{1,0:T(8,128)(2,1)S(1)}, u32[]{:S(2)}, u32[]{:S(2)}) %collective-permute-start.3) | collective-permute-done | bytes 131104 | tf_op jit(solution)/shard_map/ppermute | solution.py:390
  27.9 0.8 right_product.7
  28.7 0.4 collective-permute-start.5
  29.2 0.8 right_product.6.part
  29.9 0.6 collective-permute-done.5.arrived
  30.6 0.2 first_sum.1
  30.8 2.4 %collective-permute-start.6 = (bf16[16,128,128]{2,1,0:T(8,128)(2,1)S(1)}, bf16[16,128,128]{2,1,0:T(8,128)(2,1)S(1)}, u32[]{:S(2)}, u32[]{:S(2)}) collective-permute-start(bf16[16,128,128]{2,1,0:T(8,128)(2,1)S(1)} %get-tuple-element.27), channel_id=1, source_target_pairs={{0,1},{1,0},{2,3},{3,2},{4,6},{5,7},{6,4},{7,5},{8,9},{9,8},{10,11... | collective-permute-start | bytes 1572872 | tf_op jit(solution)/shard_map/ppermute | solution.py:390
  33.3 0.8 right_product.5
  34.1 0.7 collective-permute-start.4
  34.8 0.8 right_product.4.part
  35.6 0.6 collective-permute-done.4.across
  36.2 3.9 %collective-permute-done.6.arrived = bf16[16,128,128]{2,1,0:T(8,128)(2,1)S(1)} collective-permute-done((bf16[16,128,128]{2,1,0:T(8,128)(2,1)S(1)}, bf16[16,128,128]{2,1,0:T(8,128)(2,1)S(1)}, u32[]{:S(2)}, u32[]{:S(2)}) %collective-permute-start.6) | collective-permute-done | bytes 524320 | tf_op jit(solution)/shard_map/ppermute | solution.py:390
  40.1 0.2 second_sum.1
  40.3 1.5 %collective-permute-start.7 = (bf16[9,128,128]{2,1,0:T(8,128)(2,1)S(1)}, bf16[9,128,128]{2,1,0:T(8,128)(2,1)S(1)}, u32[]{:S(2)}, u32[]{:S(2)}) collective-permute-start(bf16[9,128,128]{2,1,0:T(8,128)(2,1)S(1)} %get-tuple-element.30), channel_id=1, source_target_pairs={{0,2},{1,3},{2,0},{3,1},{4,5},{5,4},{6,7},{7,6},{8,10},{9,11},{10,... | collective-permute-start | bytes 884744 | tf_op jit(solution)/shard_map/ppermute | solution.py:390
  41.8 4.4 %collective-permute-done.7.arrived = bf16[9,128,128]{2,1,0:T(8,128)(2,1)S(1)} collective-permute-done((bf16[9,128,128]{2,1,0:T(8,128)(2,1)S(1)}, bf16[9,128,128]{2,1,0:T(8,128)(2,1)S(1)}, u32[]{:S(2)}, u32[]{:S(2)}) %collective-permute-start.7) | collective-permute-done | bytes 294944 | tf_op jit(solution)/shard_map/ppermute | solution.py:390
  46.3 1.3 %collective-permute-start.8 = (bf16[7,128,128]{2,1,0:T(8,128)(2,1)S(1)}, bf16[7,128,128]{2,1,0:T(8,128)(2,1)S(1)}, u32[]{:S(2)}, u32[]{:S(2)}) collective-permute-start(bf16[7,128,128]{2,1,0:T(8,128)(2,1)S(1)} %get-tuple-element.32.kept), channel_id=1, source_target_pairs={{0,8},{1,9},{2,10},{3,11},{4,20},{5,21},{6,22},{7,23},{8,0},{9,1},... | collective-permute-start | bytes 688136 | tf_op jit(solution)/shard_map/ppermute | solution.py:390
  47.6 2.2 %inverse_part.2.source = f32[128,256]{1,0:T(8,128)S(1)} custom-call(f32[128,128]{1,0:T(8,128)S(1)} %get-tuple-element.33.source), custom_call_target="tpu_custom_call" | custom-call | bytes 5250000 | tf_op jit(solution)/shard_map/inverse_part/pallas_call | solution.py:281
  49.7 5.0 %collective-permute-done.8.arrived = bf16[7,128,128]{2,1,0:T(8,128)(2,1)S(1)} collective-permute-done((bf16[7,128,128]{2,1,0:T(8,128)(2,1)S(1)}, bf16[7,128,128]{2,1,0:T(8,128)(2,1)S(1)}, u32[]{:S(2)}, u32[]{:S(2)}) %collective-permute-start.8) | collective-permute-done | bytes 229408 | tf_op jit(solution)/shard_map/ppermute | solution.py:390
  54.7 0.1 pair_sum.1.own
  54.8 0.1 collective-permute-start.9
  54.8 2.3 %inverse_part.3.state = f32[128,256]{1,0:T(8,128)S(1)} custom-call(f32[128,256]{1,0:T(8,128)S(1)} %inverse_part.2.source), custom_call_target="tpu_custom_call" | custom-call | bytes 5250000 | tf_op jit(solution)/shard_map/inverse_part/pallas_call | solution.py:281
  57.2 4.6 %collective-permute-done.9.arrived = bf16[7,128,128]{2,1,0:T(8,128)(2,1)S(1)} collective-permute-done((bf16[7,128,128]{2,1,0:T(8,128)(2,1)S(1)}, bf16[7,128,128]{2,1,0:T(8,128)(2,1)S(1)}, u32[]{:S(2)}, u32[]{:S(2)}) %collective-permute-start.9) | collective-permute-done | bytes 229408 | tf_op jit(solution)/shard_map/ppermute | solution.py:390
  61.8 0.3 factor.1
  62.1 0.1 collective-permute-start.10
  62.2 0.3 base.1
  62.5 4.5 %collective-permute-done.10 = bf16[7,128,128]{2,1,0:T(8,128)(2,1)S(1)} collective-permute-done((bf16[7,128,128]{2,1,0:T(8,128)(2,1)S(1)}, bf16[7,128,128]{2,1,0:T(8,128)(2,1)S(1)}, u32[]{:S(2)}, u32[]{:S(2)}) %collective-permute-start.10) | collective-permute-done | bytes 229408 | tf_op jit(solution)/shard_map/ppermute | solution.py:390
  67.1 4.5 %collective-permute-start.12 = (bf16[14,128,128]{2,1,0:T(8,128)(2,1)S(1)}, bf16[14,128,128]{2,1,0:T(8,128)(2,1)S(1)}, u32[]{:S(2)}, u32[]{:S(2)}) collective-permute-start(bf16[14,128,128]{2,1,0:T(8,128)(2,1)S(1)} %pad_maximum_fusion.right.own), channel_id=1, source_target_pairs={{0,4},{1,5},{2,6},{3,7},{4,0},{5,1},{6,2},{7,3},{8,12},{9,13},{10,... | collective-permute-start | bytes 1376264 | tf_op jit(solution)/shard_map/ppermute | solution.py:390
  71.6 1.7 %collective-permute-start.11 = (bf16[14,128,128]{2,1,0:T(8,128)(2,1)S(1)}, bf16[14,128,128]{2,1,0:T(8,128)(2,1)S(1)}, u32[]{:S(2)}, u32[]{:S(2)}) collective-permute-start(bf16[14,128,128]{2,1,0:T(8,128)(2,1)S(1)} %pad_maximum_fusion.right.own), channel_id=1, source_target_pairs={{0,1},{1,0},{2,3},{3,2},{4,6},{5,7},{6,4},{7,5},{8,9},{9,8},{10,11... | collective-permute-start | bytes 1376264 | tf_op jit(solution)/shard_map/ppermute | solution.py:390
  73.4 2.3 %new_error.4.rest_0_ = bf16[1024,7168]{1,0:T(8,128)(2,1)} custom-call(s32[1]{0:T(128)} %bitcast.dp, s32[1]{0:T(128)} %bitcast.1.mp, bf16[1024,7168]{1,0:T(8,128)(2,1)S(1)} %get-tuple-element.24.comp, bf16[512,128]{1,0:T(8,128)(2,1)S(1)} %get-tuple-element.40.near, bf16[512,128]{1,0:T(8,128)(2,1)S(1)} %get-tuple-element.41.far, ...), custom_call_target="tpu_custom_call" | custom-call | bytes 8400000 | tf_op jit(solution)/shard_map/new_error/pallas_call | solution.py:181
  75.7 0.0 collective-permute-done.12.right.other
  75.7 0.9 %factor_rows.1 = bf16[1792,128]{1,0:T(8,128)(2,1)} custom-call(s32[1]{0:T(128)} %bitcast.dp, s32[1]{0:T(128)} %bitcast.1.mp, bf16[14,128,128]{2,1,0:T(8,128)(2,1)S(1)} %pad_maximum_fusion.right.own, bf16[14,128,128]{2,1,0:T(8,128)(2,1)S(1)} %collective-permute-done.12.right.other), custom_call_target="tpu_custom_call" | custom-call | bytes 3500000 | tf_op jit(solution)/shard_map/factor_rows/pallas_call | solution.py:469
  76.7 2.3 %new_error.5.rest_0_ = bf16[1024,7168]{1,0:T(8,128)(2,1)} custom-call(s32[1]{0:T(128)} %bitcast.dp, s32[1]{0:T(128)} %bitcast.1.mp, bf16[1024,7168]{1,0:T(8,128)(2,1)S(1)} %get-tuple-element.24.comp, bf16[512,128]{1,0:T(8,128)(2,1)S(1)} %get-tuple-element.40.near, bf16[512,128]{1,0:T(8,128)(2,1)S(1)} %get-tuple-element.41.far, ...), custom_call_target="tpu_custom_call", output_to_operand_aliasing={{}: (6, {})} | custom-call | bytes 8400000 | tf_op jit(solution)/shard_map/new_error/pallas_call | solution.py:181
  79.0 0.6 collective-permute-done.11.right
  79.5 0.7 collective-permute-start.13
  80.2 2.3 %new_error.6.rest_0_ = bf16[1024,7168]{1,0:T(8,128)(2,1)} custom-call(s32[1]{0:T(128)} %bitcast.dp, s32[1]{0:T(128)} %bitcast.1.mp, bf16[1024,7168]{1,0:T(8,128)(2,1)S(1)} %get-tuple-element.24.comp, bf16[512,128]{1,0:T(8,128)(2,1)S(1)} %get-tuple-element.40.near, bf16[512,128]{1,0:T(8,128)(2,1)S(1)} %get-tuple-element.41.far, ...), custom_call_target="tpu_custom_call", output_to_operand_aliasing={{}: (6, {})} | custom-call | bytes 8400000 | tf_op jit(solution)/shard_map/new_error/pallas_call | solution.py:181
  82.5 0.0 collective-permute-done.13.right
  82.5 2.3 %new_error.7 = bf16[1024,7168]{1,0:T(8,128)(2,1)} custom-call(s32[1]{0:T(128)} %bitcast.dp, s32[1]{0:T(128)} %bitcast.1.mp, bf16[1024,7168]{1,0:T(8,128)(2,1)S(1)} %get-tuple-element.24.comp, bf16[512,128]{1,0:T(8,128)(2,1)S(1)} %get-tuple-element.40.near, bf16[512,128]{1,0:T(8,128)(2,1)S(1)} %get-tuple-element.41.far, ...), custom_call_target="tpu_custom_call", output_to_operand_aliasing={{}: (6, {})} | custom-call | bytes 8400000 | tf_op jit(solution)/shard_map/new_error/pallas_call | solution.py:181
  (3 shorter events, 0.1 us)
Async XLA Ops:
  11.9 1.6 %collective-permute-start = (f32[128,512]{1,0:T(8,128)S(1)}, f32[128,512]{1,0:T(8,128)S(1)}, u32[]{:S(2)}, u32[]{:S(2)}) collective-permute-start(f32[128,512]{1,0:T(8,128)S(1)} %get-tuple-element.26), channel_id=1, source_target_pairs={{0,4},{1,5},{2,6},{3,7},{4,0},{5,1},{6,2},{7,3},{8,12},{9,13},{10,... | collective-permute-start | bytes 786440 | tf_op jit(solution)/shard_map/ppermute | solution.py:390
  13.5 7.2 %collective-permute-start.1 = (bf16[128,512]{1,0:T(8,128)(2,1)S(1)}, bf16[128,512]{1,0:T(8,128)(2,1)S(1)}, u32[]{:S(2)}, u32[]{:S(2)}) collective-permute-start(bf16[128,512]{1,0:T(8,128)(2,1)S(1)} %fusion.1), channel_id=1, source_target_pairs={{0,8},{1,9},{2,10},{3,11},{4,20},{5,21},{6,22},{7,23},{8,0},{9,1},... | collective-permute-start | bytes 393224 | tf_op jit(solution)/shard_map/ppermute | solution.py:390
  20.8 4.2 %collective-permute-start.2 = (bf16[128,512]{1,0:T(8,128)(2,1)S(1)}, bf16[128,512]{1,0:T(8,128)(2,1)S(1)}, u32[]{:S(2)}, u32[]{:S(2)}) collective-permute-start(bf16[128,512]{1,0:T(8,128)(2,1)S(1)} %fusion), channel_id=1, source_target_pairs={{0,16},{1,17},{2,18},{3,19},{4,12},{5,13},{6,14},{7,15},{8,24},{9,... | collective-permute-start | bytes 393224 | tf_op jit(solution)/shard_map/ppermute | solution.py:390
  25.1 2.8 %collective-permute-start.3 = (bf16[128,512]{1,0:T(8,128)(2,1)S(1)}, bf16[128,512]{1,0:T(8,128)(2,1)S(1)}, u32[]{:S(2)}, u32[]{:S(2)}) collective-permute-start(bf16[128,512]{1,0:T(8,128)(2,1)S(1)} %add_convert_fusion.near), channel_id=1, source_target_pairs={{0,4},{1,5},{2,6},{3,7},{4,0},{5,1},{6,2},{7,3},{8,12},{9,13},{10,... | collective-permute-start | bytes 393224 | tf_op jit(solution)/shard_map/ppermute | solution.py:390
  28.7 1.9 %collective-permute-start.5 = (bf16[14,128,128]{2,1,0:T(8,128)(2,1)S(1)}, bf16[14,128,128]{2,1,0:T(8,128)(2,1)S(1)}, u32[]{:S(2)}, u32[]{:S(2)}) collective-permute-start(bf16[14,128,128]{2,1,0:T(8,128)(2,1)S(1)} %right_product.7), channel_id=1, source_target_pairs={{0,4},{1,5},{2,6},{3,7},{4,0},{5,1},{6,2},{7,3},{8,12},{9,13},{10,... | collective-permute-start | bytes 1376264 | tf_op jit(solution)/shard_map/ppermute | solution.py:390
  30.8 9.3 %collective-permute-start.6 = (bf16[16,128,128]{2,1,0:T(8,128)(2,1)S(1)}, bf16[16,128,128]{2,1,0:T(8,128)(2,1)S(1)}, u32[]{:S(2)}, u32[]{:S(2)}) collective-permute-start(bf16[16,128,128]{2,1,0:T(8,128)(2,1)S(1)} %get-tuple-element.27), channel_id=1, source_target_pairs={{0,1},{1,0},{2,3},{3,2},{4,6},{5,7},{6,4},{7,5},{8,9},{9,8},{10,11... | collective-permute-start | bytes 1572872 | tf_op jit(solution)/shard_map/ppermute | solution.py:390
  34.1 2.1 %collective-permute-start.4 = (bf16[14,128,128]{2,1,0:T(8,128)(2,1)S(1)}, bf16[14,128,128]{2,1,0:T(8,128)(2,1)S(1)}, u32[]{:S(2)}, u32[]{:S(2)}) collective-permute-start(bf16[14,128,128]{2,1,0:T(8,128)(2,1)S(1)} %right_product.5), channel_id=1, source_target_pairs={{0,4},{1,5},{2,6},{3,7},{4,0},{5,1},{6,2},{7,3},{8,12},{9,13},{10,... | collective-permute-start | bytes 1376264 | tf_op jit(solution)/shard_map/ppermute | solution.py:390
  40.3 5.9 %collective-permute-start.7 = (bf16[9,128,128]{2,1,0:T(8,128)(2,1)S(1)}, bf16[9,128,128]{2,1,0:T(8,128)(2,1)S(1)}, u32[]{:S(2)}, u32[]{:S(2)}) collective-permute-start(bf16[9,128,128]{2,1,0:T(8,128)(2,1)S(1)} %get-tuple-element.30), channel_id=1, source_target_pairs={{0,2},{1,3},{2,0},{3,1},{4,5},{5,4},{6,7},{7,6},{8,10},{9,11},{10,... | collective-permute-start | bytes 884744 | tf_op jit(solution)/shard_map/ppermute | solution.py:390
  46.3 8.4 %collective-permute-start.8 = (bf16[7,128,128]{2,1,0:T(8,128)(2,1)S(1)}, bf16[7,128,128]{2,1,0:T(8,128)(2,1)S(1)}, u32[]{:S(2)}, u32[]{:S(2)}) collective-permute-start(bf16[7,128,128]{2,1,0:T(8,128)(2,1)S(1)} %get-tuple-element.32.kept), channel_id=1, source_target_pairs={{0,8},{1,9},{2,10},{3,11},{4,20},{5,21},{6,22},{7,23},{8,0},{9,1},... | collective-permute-start | bytes 688136 | tf_op jit(solution)/shard_map/ppermute | solution.py:390
  54.8 7.1 %collective-permute-start.9 = (bf16[7,128,128]{2,1,0:T(8,128)(2,1)S(1)}, bf16[7,128,128]{2,1,0:T(8,128)(2,1)S(1)}, u32[]{:S(2)}, u32[]{:S(2)}) collective-permute-start(bf16[7,128,128]{2,1,0:T(8,128)(2,1)S(1)} %pair_sum.1.own), channel_id=1, source_target_pairs={{0,16},{1,17},{2,18},{3,19},{4,12},{5,13},{6,14},{7,15},{8,24},{9,... | collective-permute-start | bytes 688136 | tf_op jit(solution)/shard_map/ppermute | solution.py:390
  62.1 4.9 %collective-permute-start.10 = (bf16[7,128,128]{2,1,0:T(8,128)(2,1)S(1)}, bf16[7,128,128]{2,1,0:T(8,128)(2,1)S(1)}, u32[]{:S(2)}, u32[]{:S(2)}) collective-permute-start(bf16[7,128,128]{2,1,0:T(8,128)(2,1)S(1)} %factor.1), channel_id=1, source_target_pairs={{0,2},{1,3},{2,0},{3,1},{4,5},{5,4},{6,7},{7,6},{8,10},{9,11},{10,... | collective-permute-start | bytes 688136 | tf_op jit(solution)/shard_map/ppermute | solution.py:390
  67.1 8.6 %collective-permute-start.12 = (bf16[14,128,128]{2,1,0:T(8,128)(2,1)S(1)}, bf16[14,128,128]{2,1,0:T(8,128)(2,1)S(1)}, u32[]{:S(2)}, u32[]{:S(2)}) collective-permute-start(bf16[14,128,128]{2,1,0:T(8,128)(2,1)S(1)} %pad_maximum_fusion.right.own), channel_id=1, source_target_pairs={{0,4},{1,5},{2,6},{3,7},{4,0},{5,1},{6,2},{7,3},{8,12},{9,13},{10,... | collective-permute-start | bytes 1376264 | tf_op jit(solution)/shard_map/ppermute | solution.py:390
  71.6 7.9 %collective-permute-start.11 = (bf16[14,128,128]{2,1,0:T(8,128)(2,1)S(1)}, bf16[14,128,128]{2,1,0:T(8,128)(2,1)S(1)}, u32[]{:S(2)}, u32[]{:S(2)}) collective-permute-start(bf16[14,128,128]{2,1,0:T(8,128)(2,1)S(1)} %pad_maximum_fusion.right.own), channel_id=1, source_target_pairs={{0,1},{1,0},{2,3},{3,2},{4,6},{5,7},{6,4},{7,5},{8,9},{9,8},{10,11... | collective-permute-start | bytes 1376264 | tf_op jit(solution)/shard_map/ppermute | solution.py:390
  79.5 3.0 %collective-permute-start.13 = (bf16[14,128,128]{2,1,0:T(8,128)(2,1)S(1)}, bf16[14,128,128]{2,1,0:T(8,128)(2,1)S(1)}, u32[]{:S(2)}, u32[]{:S(2)}) collective-permute-start(bf16[14,128,128]{2,1,0:T(8,128)(2,1)S(1)} %collective-permute-done.11.right), channel_id=1, source_target_pairs={{0,4},{1,5},{2,6},{3,7},{4,0},{5,1},{6,2},{7,3},{8,12},{9,13},{10,... | collective-permute-start | bytes 1376264 | tf_op jit(solution)/shard_map/ppermute | solution.py:390

commit v5 on v4

--- a/solution.py
+++ b/solution.py
@@ -147,25 +147,24 @@
     )(*place, in_vmem(comp), near, far)
 
 
-def new_error_kernel(net, units, side, places, dp, mp, comp, near, far, right, *rest):
+def new_error_kernel(net, units, blocks, dp, mp, comp, near, far, *rest):
     place = Place(net, (dp, mp))
-    out, buf, sems = rest[-3:]
+    rights, (out, buf, sems) = rest[: len(blocks)], rest[-3:]
     count = comp.shape[0] // 2
-    width = units * LANES
     copies = []
-    for j, k in enumerate(places):
-        start = pl.multiple_of(place.block(side, k) * width, LANES)
+    for j, ((side, k), right) in enumerate(zip(blocks, rights)):
+        start = place.block(side, k) * (units * LANES)
         for half, base in enumerate((near, far)):
+            rows = pl.ds(pl.multiple_of(place.half(half) * count, count), count)
             for unit in range(0, units, 2):
                 wide = min(2, units - unit)
-                factor = [right[j * units + unit + i] for i in range(wide)]
+                factor = [right[unit + i] for i in range(wide)]
                 factor = jnp.concatenate(factor, axis=1) if wide > 1 else factor[0]
                 product = jnp.dot(base[...], factor, preferred_element_type=F32)
                 at = pl.ds(pl.multiple_of(start + unit * LANES, LANES), wide * LANES)
                 kept = comp[half * count : (half + 1) * count, at].astype(F32)
                 here = pl.ds(unit * LANES, wide * LANES)
                 buf[half, j, :, here] = (kept - product).astype(BF16)
-                rows = pl.ds(pl.multiple_of(place.half(half) * count, count), count)
                 copy = pltpu.make_async_copy(
                     buf.at[half, j, :, here], out.at[rows, at], sems.at[half, j, unit // 2]
                 )
@@ -175,23 +174,23 @@
         copy.wait()
 
 
-def new_error(net, place, side, places, right, units, comp, near, far, held=None):
+def new_error(net, place, blocks, rights, units, comp, near, far, held=None):
     rows, cols = comp.shape
     extra = [] if held is None else [in_hbm(held)]
     return call(
-        functools.partial(new_error_kernel, net, units, side, places),
+        functools.partial(new_error_kernel, net, units, blocks),
         "new_error",
         shaped((rows, cols), BF16),
-        [SMEM] * 2 + [VMEM] * 4 + [HBM] * len(extra),
+        [SMEM] * 2 + [VMEM] * (3 + len(blocks)) + [HBM] * len(extra),
         12,
-        1 + 0.7 * len(places),
+        0.6 + 0.8 * len(blocks),
         out_specs=HBM,
         scratch_shapes=[
-            pltpu.VMEM((2, len(places), rows // 2, units * LANES), BF16),
-            pltpu.SemaphoreType.DMA((2, len(places), (units + 1) // 2)),
+            pltpu.VMEM((2, len(blocks), rows // 2, units * LANES), BF16),
+            pltpu.SemaphoreType.DMA((2, len(blocks), (units + 1) // 2)),
         ],
-        input_output_aliases={6: 0} if extra else {},
-    )(*place, in_vmem(comp), near, far, right, *extra)
+        input_output_aliases={5 + len(blocks): 0} if extra else {},
+    )(*place, in_vmem(comp), near, far, *rights, *extra)
 
 
 def leaf_steps(state, leaf):
@@ -294,48 +293,32 @@
     return high, (x - high.astype(F32)).astype(BF16)
 
 
-def put2(ref, at, x):
-    ref[at], ref[at + 1] = split2(x)
-
-
-def get2(ref, at):
-    return ref[at].astype(F32) + ref[at + 1].astype(F32)
-
-
-def first_kernel(part, arrived, near, far, out, gram):
-    count = part.shape[0]
+def first_kernel(part, across, near, far, out, gram):
+    units = part.shape[0]
     contract = (((1,), (1,)), ((), ()))
     total = lax.dot_general(near[...], near[...], contract, preferred_element_type=F32)
     total += lax.dot_general(far[...], far[...], contract, preferred_element_type=F32)
-    gram[...] = total
-    put2(out, count, total)
-
-    for i in range(count):
-        out[i] = (part[i] + arrived[i].astype(F32)).astype(BF16)
-
-
-def second_kernel(part, across, arrived, gram_in, out, kept, gram):
-    units = kept.shape[0]
-    total = gram_in[...] + get2(arrived, 2 * units)
-    gram[...] = total
-    put2(out, units, total)
-
+    out[units], out[units + 1] = split2(total)
+    gram[...] = out[units].astype(F32) + out[units + 1].astype(F32)
     for i in range(units):
-        j = i + units
-        out[i] = (part[j] + across[j].astype(F32) + arrived[j].astype(F32)).astype(BF16)
-        kept[i] = part[i] + across[i].astype(F32) + arrived[i].astype(F32)
-
-
-def third_kernel(part, arrived, gram_in, out, gram):
-    units = part.shape[0]
-    gram[...] = gram_in[...] + get2(arrived, units)
+        out[i] = (part[i] + across[i].astype(F32)).astype(BF16)
+
+
+def second_kernel(part, across, arrived, out):
+    for i in range(out.shape[0]):
+        out[i] = (part[i] + across[i].astype(F32) + arrived[i].astype(F32)).astype(BF16)
+
+
+def kept_kernel(part, across, arrived, gram_in, out, gram):
+    units = out.shape[0]
+    gram[...] = gram_in[...] + (arrived[units].astype(F32) + arrived[units + 1].astype(F32))
     for i in range(units):
-        out[i] = (part[i] + arrived[i].astype(F32)).astype(BF16)
-
-
-def add_kernel(kept, arrived, out):
-    for i in range(kept.shape[0]):
-        out[i] = (kept[i].astype(F32) + arrived[i].astype(F32)).astype(BF16)
+        out[i] = part[i] + across[i].astype(F32) + arrived[i].astype(F32)
+
+
+def add_kernel(one, other, out):
+    for i in range(one.shape[0]):
+        out[i] = (one[i].astype(F32) + other[i].astype(F32)).astype(BF16)
 
 
 def factor_kernel(replicas, own, arrived, state, out):
@@ -413,29 +396,35 @@
     def right(side, places, dtype):
         return right_product(net, place, side, places, units, comp, near, far, dtype)
 
-    across = net.core(right(FAR, (2, 3), BF16))
-    part = right(NEAR, (2, 3), F32)
-    sent, gram = call(
-        first_kernel, "first_sum",
-        [shaped((2 * units + 2, *square), BF16), shaped((rank, rank), F32)],
-        [VMEM] * 4, 4, 0.5, out_specs=[VMEM] * 2,
-    )(part, across, near, far)
-    arrived = net.send(sent, net.scatter[0])
-    across = net.core(right(FAR, (0, 1), BF16))
-    part = right(NEAR, (0, 1), F32)
-    sent, kept, gram = call(
-        second_kernel, "second_sum",
-        [shaped((units + 2, *square), BF16), shaped((units, *square), F32), shaped((rank, rank), F32)],
-        [VMEM] * 4, 4, 0.5, out_specs=[VMEM] * 3,
-    )(part, across, arrived, gram)
+    def small(kernel, name, outs, *ins):
+        return call(kernel, name, outs, [VMEM] * len(ins), 4, 0.3, out_specs=jax.tree.map(lambda _: VMEM, outs))(*ins)
+
+    block, square_f32 = shaped((units, *square), BF16), shaped((rank, rank), F32)
+    across_3 = net.core(right(FAR, (3,), BF16))
+    across_2 = net.core(right(FAR, (2,), BF16))
+    sent = small(add_kernel, "first_sum", block, right(NEAR, (3,), F32), across_3)
+    near, far, sent = lax.optimization_barrier((near, far, sent))
+    arrived_1 = net.send(sent, net.scatter[0])
+    sent, gram = small(
+        first_kernel, "first_sum", [shaped((units + 2, *square), BF16), square_f32],
+        right(NEAR, (2,), F32), across_2, near, far,
+    )
+    near, far, sent = lax.optimization_barrier((near, far, sent))
+    arrived_0 = net.send(sent, net.scatter[0])
+    across = net.core(right(FAR, (1,), BF16))
+    part = right(NEAR, (1,), F32)
+    near, far, arrived_1 = lax.optimization_barrier((near, far, arrived_1))
+    sent = small(second_kernel, "second_sum", block, part, across, arrived_1)
+    across = net.core(right(FAR, (0,), BF16))
+    part = right(NEAR, (0,), F32)
     arrived = net.send(sent, net.scatter[1])
-    sent, gram = call(
-        third_kernel, "third_sum",
-        [shaped((units, *square), BF16), shaped((rank, rank), F32)],
-        [VMEM] * 3, 4, 0.5, out_specs=[VMEM] * 2,
-    )(kept, arrived, gram)
+    kept, gram = small(
+        kept_kernel, "second_sum", [shaped((units, *square), F32), square_f32], part, across, arrived_0, gram
+    )
+    gram = gram + net.send(gram, net.scatter[1])
     for bit in net.other:
         gram = gram + net.send(gram, (bit, bit))
+    sent = small(add_kernel, "third_sum", block, kept, arrived)
 
     leaves = list(range(rank // LEAF))
     steps = len(net.rest)
@@ -445,39 +434,33 @@
         state = inverse_part(state, leaves[len(leaves) * k // steps : len(leaves) * (k + 1) // steps])
         arrived, state = lax.optimization_barrier((arrived, state))
         if k < steps - 1:
-            sent = call(
-                add_kernel, "pair_sum", shaped((units, *square), BF16), [VMEM] * 2, 2, 0.3, out_specs=VMEM
-            )(sent, arrived)
-    own = call(
-        functools.partial(factor_kernel, dp), "factor", shaped((units, *square), BF16),
-        [VMEM] * 3, 4, 0.7, out_specs=VMEM,
-    )(sent, arrived, state)
-
-    arrived = net.send(own, net.scatter[1])
-    base_near, base_far = call(
-        base_kernel, "base", [shaped((rows // 2, rank), BF16)] * 2, [VMEM] * 3, 4, 0.7, out_specs=[VMEM] * 2
-    )(near, far, state)
-    arrived, base_near, base_far = lax.optimization_barrier((arrived, base_near, base_far))
+            sent = small(add_kernel, "pair_sum", block, sent, arrived)
+    own = small(functools.partial(factor_kernel, dp), "factor", block, sent, arrived, state)
+
+    blocks = [own, net.send(own, net.scatter[1]), net.send(own, net.scatter[0]), None]
+    base_near, base_far = small(
+        base_kernel, "base", [shaped((rows // 2, rank), BF16)] * 2, near, far, state
+    )
+    own, base_near, base_far = lax.optimization_barrier((own, base_near, base_far))
+    others = [net.core(own)]
     write = functools.partial(new_error, net, place, units=units, comp=comp, near=base_near, far=base_far)
-    own = jnp.concatenate([own, arrived], axis=0)
-    arrived = net.send(own, net.scatter[0])
-    other = net.core(own)
-    out = write(NEAR, (0, 1), own)
-    out = write(FAR, (0, 1), other, held=out)
+    out = write([(NEAR, 0)], [own])
     share, width = cols // mp, units * LANES
+    right_factor = None
     if share == 2 * width:
         right_factor = call(
             functools.partial(rows_kernel, net, units), "factor_rows", shaped((share, rank), BF16),
             [SMEM, SMEM, VMEM, VMEM], 4, 1, out_specs=VMEM,
-        )(*place, own, other)
-        arrived, out, right_factor = lax.optimization_barrier((arrived, out, right_factor))
-    else:
-        arrived, out = lax.optimization_barrier((arrived, out))
-    crossed = net.core(arrived)
-    out = write(NEAR, (2, 3), arrived, held=out)
-    out = write(FAR, (2, 3), crossed, held=out)
-    if share != 2 * width:
-        everything = jnp.concatenate([own, arrived, other, crossed], axis=0)
+        )(*place, own, others[0])
+    for k in range(1, 4):
+        blocks[k], out, right_factor = lax.optimization_barrier((blocks[k], out, right_factor))
+        if k == 1:
+            blocks[3] = net.send(blocks[1], net.scatter[0])
+        others.append(net.core(blocks[k]))
+        out = write([(FAR, k - 1), (NEAR, k)], [others[k - 1], blocks[k]], held=out)
+    out = write([(FAR, 3)], [others[3]], held=out)
+    if right_factor is None:
+        everything = jnp.concatenate(blocks + others, axis=0)
         here = Place(net, place)
         names = jnp.stack([here.block(side, k) for side in (NEAR, FAR) for k in range(4)])
         block = here.mp * share // width

time: 85.1 us -> 82 us (0.964)
  waiting for transfers between devices: 34 us -> 18 us
  starting transfers between devices: 19.7 us -> 30.4 us
  Pallas kernels: 30.2 us -> 31.9 us
    ppermute x14 -> x21, waiting for transfers between devices: 34 us -> 18 us  [send(): return lax.ppermute(x, AXES, pairs)]
    ppermute x14 -> x21, starting transfers between devices: 19.7 us -> 30.4 us  [send(): return lax.ppermute(x, AXES, pairs)]
    pallas_call x10 -> x13, Pallas kernels: 10.4 us -> 11.3 us  [the longest x5 10.2 us: new_error(): call(functools.partial(new_error_kernel, net, units, blocks), 'new_error'...]
    pallas_call x4 -> x8, Pallas kernels: 3.14 us -> 3.86 us  [right_product(): call(functools.partial(right_kernel, net, units, side, places), 'right_pr...]
  transfers between devices with their start and end apart: 14 -> 21, of which waited for: 12 -> 10; matrix products, arithmetic and copies ran while one was open for 0% -> 0% of each run, Pallas kernels for 18% -> 22%
where the time goes in v5:
time: 82 us; the launch traced here: 81.4 us
  Pallas kernels  31.9 us (39%)
  starting transfers between devices  30.4 us (37%)
  waiting for transfers between devices  18 us (22%)
  between operations  1.02 us (1%)
    ppermute x21, starting transfers between devices, send(): return lax.ppermute(x, AXES, pairs)  30.4 us
    ppermute x21, waiting for transfers between devices, send(): return lax.ppermute(x, AXES, pairs)  18 us
    pallas_call x1, Pallas kernels, left_product(): call(functools.partial(left_kernel, net, PIECES), 'left_product', [pltpu....  11.2 us
    pallas_call x5, Pallas kernels, new_error(): call(functools.partial(new_error_kernel, net, units, blocks), 'new_error'...  10.2 us
    pallas_call x2, Pallas kernels, inverse_part(): call(functools.partial(leaves_kernel, leaves), 'inverse_part', shaped((n,...  4.49 us
    pallas_call x8, Pallas kernels, right_product(): call(functools.partial(right_kernel, net, units, side, places), 'right_pr...  3.86 us
  transfers between devices with their start and end apart: 21, of which 10 were waited for; matrix products, arithmetic and copies ran while one was open for 0% of the time, Pallas kernels for 22%

profile of v5, /device:TPU:1, one launch (start us, length us, event | category | flops | bytes accessed | tf_op | source)
XLA Modules:
  0.0 81.4 jit_solution(8222429650410491756)
XLA Ops:
  0.6 11.2 %left_product.1 = (bf16[1024,7168]{1,0:T(8,128)(2,1)S(1)}, f32[128,512]{1,0:T(8,128)S(1)}, f32[128,512]{1,0:T(8,128)S(1)}) custom-call(s32[1]{0:T(128)} %bitcast.dp, s32[1]{0:T(128)} %bitcast.1.mp, bf16[1024,7168]{1,0:T(8,128)(2,1)} %bitcast.6, bf16[1024,7168]{1,0:T(8,128)(2,1)} %bitcast.7, bf16[7168,128]{1,0:T(8,128)(2,1)} %init.1), custom_call_target="tpu_custom_call" | custom-call | bytes 42000000 | tf_op jit(solution)/shard_map/left_product/pallas_call | solution.py:106
  11.9 0.1 collective-permute-start
  12.0 1.5 %collective-permute-done = f32[128,512]{1,0:T(8,128)S(1)} collective-permute-done((f32[128,512]{1,0:T(8,128)S(1)}, f32[128,512]{1,0:T(8,128)S(1)}, u32[]{:S(2)}, u32[]{:S(2)}) %collective-permute-start) | collective-permute-done | bytes 262176 | tf_op jit(solution)/shard_map/ppermute | solution.py:373
  13.5 3.5 %collective-permute-start.1 = (bf16[128,512]{1,0:T(8,128)(2,1)S(1)}, bf16[128,512]{1,0:T(8,128)(2,1)S(1)}, u32[]{:S(2)}, u32[]{:S(2)}) collective-permute-start(bf16[128,512]{1,0:T(8,128)(2,1)S(1)} %fusion.1), channel_id=1, source_target_pairs={{0,8},{1,9},{2,10},{3,11},{4,20},{5,21},{6,22},{7,23},{8,0},{9,1},... | collective-permute-start | bytes 393224 | tf_op jit(solution)/shard_map/ppermute | solution.py:373
  17.0 3.7 %collective-permute-done.1 = bf16[128,512]{1,0:T(8,128)(2,1)S(1)} collective-permute-done((bf16[128,512]{1,0:T(8,128)(2,1)S(1)}, bf16[128,512]{1,0:T(8,128)(2,1)S(1)}, u32[]{:S(2)}, u32[]{:S(2)}) %collective-permute-start.1) | collective-permute-done | bytes 131104 | tf_op jit(solution)/shard_map/ppermute | solution.py:373
  20.7 0.1 fusion
  20.8 0.7 collective-permute-start.2
  21.5 3.4 %collective-permute-done.2 = bf16[128,512]{1,0:T(8,128)(2,1)S(1)} collective-permute-done((bf16[128,512]{1,0:T(8,128)(2,1)S(1)}, bf16[128,512]{1,0:T(8,128)(2,1)S(1)}, u32[]{:S(2)}, u32[]{:S(2)}) %collective-permute-start.2) | collective-permute-done | bytes 131104 | tf_op jit(solution)/shard_map/ppermute | solution.py:373
  25.0 0.1 add_convert_fusion.near
  25.1 1.9 %collective-permute-start.3 = (bf16[128,512]{1,0:T(8,128)(2,1)S(1)}, bf16[128,512]{1,0:T(8,128)(2,1)S(1)}, u32[]{:S(2)}, u32[]{:S(2)}) collective-permute-start(bf16[128,512]{1,0:T(8,128)(2,1)S(1)} %add_convert_fusion.near), channel_id=1, source_target_pairs={{0,4},{1,5},{2,6},{3,7},{4,0},{5,1},{6,2},{7,3},{8,12},{9,13},{10,... | collective-permute-start | bytes 393224 | tf_op jit(solution)/shard_map/ppermute | solution.py:373
  26.9 1.0 %collective-permute-done.3.far = bf16[128,512]{1,0:T(8,128)(2,1)S(1)} collective-permute-done((bf16[128,512]{1,0:T(8,128)(2,1)S(1)}, bf16[128,512]{1,0:T(8,128)(2,1)S(1)}, u32[]{:S(2)}, u32[]{:S(2)}) %collective-permute-start.3) | collective-permute-done | bytes 131104 | tf_op jit(solution)/shard_map/ppermute | solution.py:373
  27.9 0.5 right_product.9
  28.4 0.4 collective-permute-start.4
  28.9 0.5 right_product.11
  29.3 0.2 collective-permute-start.5
  29.5 0.5 right_product.8.one
  30.0 0.0 collective-permute-done.4.other
  30.0 0.1 first_sum.2
  30.1 2.4 %collective-permute-start.6 = (bf16[7,128,128]{2,1,0:T(8,128)(2,1)S(1)}, bf16[7,128,128]{2,1,0:T(8,128)(2,1)S(1)}, u32[]{:S(2)}, u32[]{:S(2)}) collective-permute-start(bf16[7,128,128]{2,1,0:T(8,128)(2,1)S(1)} %first_sum.2), channel_id=1, source_target_pairs={{0,1},{1,0},{2,3},{3,2},{4,6},{5,7},{6,4},{7,5},{8,9},{9,8},{10,11... | collective-permute-start | bytes 688136 | tf_op jit(solution)/shard_map/ppermute | solution.py:373
  32.6 0.5 right_product.10.part
  33.0 0.0 collective-permute-done.5.across
  33.0 0.2 first_sum.3
  33.3 0.5 right_product.15
  33.8 0.7 collective-permute-start.9
  34.5 1.2 %collective-permute-start.8 = (bf16[9,128,128]{2,1,0:T(8,128)(2,1)S(1)}, bf16[9,128,128]{2,1,0:T(8,128)(2,1)S(1)}, u32[]{:S(2)}, u32[]{:S(2)}) collective-permute-start(bf16[9,128,128]{2,1,0:T(8,128)(2,1)S(1)} %get-tuple-element.47), channel_id=1, source_target_pairs={{0,1},{1,0},{2,3},{3,2},{4,6},{5,7},{6,4},{7,5},{8,9},{9,8},{10,11... | collective-permute-start | bytes 884744 | tf_op jit(solution)/shard_map/ppermute | solution.py:373
  35.7 0.5 right_product.14.part
  36.2 0.0 collective-permute-done.6.arrived
  36.3 0.5 right_product.13
  36.8 1.0 %collective-permute-start.7 = (bf16[7,128,128]{2,1,0:T(8,128)(2,1)S(1)}, bf16[7,128,128]{2,1,0:T(8,128)(2,1)S(1)}, u32[]{:S(2)}, u32[]{:S(2)}) collective-permute-start(bf16[7,128,128]{2,1,0:T(8,128)(2,1)S(1)} %right_product.13), channel_id=1, source_target_pairs={{0,4},{1,5},{2,6},{3,7},{4,0},{5,1},{6,2},{7,3},{8,12},{9,13},{10,... | collective-permute-start | bytes 688136 | tf_op jit(solution)/shard_map/ppermute | solution.py:373
  37.7 0.0 collective-permute-done.9.across
  37.7 0.1 second_sum.3
  37.8 1.8 %collective-permute-start.10 = (bf16[7,128,128]{2,1,0:T(8,128)(2,1)S(1)}, bf16[7,128,128]{2,1,0:T(8,128)(2,1)S(1)}, u32[]{:S(2)}, u32[]{:S(2)}) collective-permute-start(bf16[7,128,128]{2,1,0:T(8,128)(2,1)S(1)} %second_sum.3), channel_id=1, source_target_pairs={{0,2},{1,3},{2,0},{3,1},{4,5},{5,4},{6,7},{7,6},{8,10},{9,11},{10,... | collective-permute-start | bytes 688136 | tf_op jit(solution)/shard_map/ppermute | solution.py:373
  39.6 0.5 right_product.12.part
  40.1 0.2 collective-permute-done.8.arrived
  40.3 0.0 collective-permute-done.7.across
  40.3 0.1 second_sum.2
  40.4 2.9 %collective-permute-done.10.other = bf16[7,128,128]{2,1,0:T(8,128)(2,1)S(1)} collective-permute-done((bf16[7,128,128]{2,1,0:T(8,128)(2,1)S(1)}, bf16[7,128,128]{2,1,0:T(8,128)(2,1)S(1)}, u32[]{:S(2)}, u32[]{:S(2)}) %collective-permute-start.10) | collective-permute-done | bytes 229408 | tf_op jit(solution)/shard_map/ppermute | solution.py:373
  43.4 1.3 %collective-permute-start.11 = (bf16[7,128,128]{2,1,0:T(8,128)(2,1)S(1)}, bf16[7,128,128]{2,1,0:T(8,128)(2,1)S(1)}, u32[]{:S(2)}, u32[]{:S(2)}) collective-permute-start(bf16[7,128,128]{2,1,0:T(8,128)(2,1)S(1)} %third_sum.1.one), channel_id=1, source_target_pairs={{0,8},{1,9},{2,10},{3,11},{4,20},{5,21},{6,22},{7,23},{8,0},{9,1},... | collective-permute-start | bytes 688136 | tf_op jit(solution)/shard_map/ppermute | solution.py:373
  44.7 1.2 %collective-permute-start.12 = (f32[128,128]{1,0:T(8,128)S(1)}, f32[128,128]{1,0:T(8,128)S(1)}, u32[]{:S(2)}, u32[]{:S(2)}) collective-permute-start(f32[128,128]{1,0:T(8,128)S(1)} %get-tuple-element.51), channel_id=1, source_target_pairs={{0,2},{1,3},{2,0},{3,1},{4,5},{5,4},{6,7},{7,6},{8,10},{9,11},{10,... | collective-permute-start | bytes 196616 | tf_op jit(solution)/shard_map/ppermute | solution.py:373
  45.9 2.2 %collective-permute-done.12 = f32[128,128]{1,0:T(8,128)S(1)} collective-permute-done((f32[128,128]{1,0:T(8,128)S(1)}, f32[128,128]{1,0:T(8,128)S(1)}, u32[]{:S(2)}, u32[]{:S(2)}) %collective-permute-start.12) | collective-permute-done | bytes 65568 | tf_op jit(solution)/shard_map/ppermute | solution.py:373
  48.1 2.2 %inverse_part.2.source = f32[128,256]{1,0:T(8,128)S(1)} custom-call(f32[128,128]{1,0:T(8,128)S(1)} %add.15.source), custom_call_target="tpu_custom_call" | custom-call | bytes 5250000 | tf_op jit(solution)/shard_map/inverse_part/pallas_call | solution.py:280
  50.3 1.2 %collective-permute-done.11.other = bf16[7,128,128]{2,1,0:T(8,128)(2,1)S(1)} collective-permute-done((bf16[7,128,128]{2,1,0:T(8,128)(2,1)S(1)}, bf16[7,128,128]{2,1,0:T(8,128)(2,1)S(1)}, u32[]{:S(2)}, u32[]{:S(2)}) %collective-permute-start.11) | collective-permute-done | bytes 229408 | tf_op jit(solution)/shard_map/ppermute | solution.py:373
  51.4 0.1 pair_sum.1.own
  51.5 1.4 %collective-permute-start.13 = (bf16[7,128,128]{2,1,0:T(8,128)(2,1)S(1)}, bf16[7,128,128]{2,1,0:T(8,128)(2,1)S(1)}, u32[]{:S(2)}, u32[]{:S(2)}) collective-permute-start(bf16[7,128,128]{2,1,0:T(8,128)(2,1)S(1)} %pair_sum.1.own), channel_id=1, source_target_pairs={{0,16},{1,17},{2,18},{3,19},{4,12},{5,13},{6,14},{7,15},{8,24},{9,... | collective-permute-start | bytes 688136 | tf_op jit(solution)/shard_map/ppermute | solution.py:373
  52.9 2.3 %inverse_part.3.state = f32[128,256]{1,0:T(8,128)S(1)} custom-call(f32[128,256]{1,0:T(8,128)S(1)} %inverse_part.2.source), custom_call_target="tpu_custom_call" | custom-call | bytes 5250000 | tf_op jit(solution)/shard_map/inverse_part/pallas_call | solution.py:280
  55.3 1.5 %collective-permute-done.13.arrived = bf16[7,128,128]{2,1,0:T(8,128)(2,1)S(1)} collective-permute-done((bf16[7,128,128]{2,1,0:T(8,128)(2,1)S(1)}, bf16[7,128,128]{2,1,0:T(8,128)(2,1)S(1)}, u32[]{:S(2)}, u32[]{:S(2)}) %collective-permute-start.13) | collective-permute-done | bytes 229408 | tf_op jit(solution)/shard_map/ppermute | solution.py:373
  56.7 0.3 base.1
  57.1 0.3 factor.1.rest_0_.own
  57.4 5.3 %collective-permute-start.15 = (bf16[7,128,128]{2,1,0:T(8,128)(2,1)S(1)}, bf16[7,128,128]{2,1,0:T(8,128)(2,1)S(1)}, u32[]{:S(2)}, u32[]{:S(2)}) collective-permute-start(bf16[7,128,128]{2,1,0:T(8,128)(2,1)S(1)} %factor.1.rest_0_.own), channel_id=1, source_target_pairs={{0,4},{1,5},{2,6},{3,7},{4,0},{5,1},{6,2},{7,3},{8,12},{9,13},{10,... | collective-permute-start | bytes 688136 | tf_op jit(solution)/shard_map/ppermute | solution.py:373
  62.7 1.3 %collective-permute-start.14 = (bf16[7,128,128]{2,1,0:T(8,128)(2,1)S(1)}, bf16[7,128,128]{2,1,0:T(8,128)(2,1)S(1)}, u32[]{:S(2)}, u32[]{:S(2)}) collective-permute-start(bf16[7,128,128]{2,1,0:T(8,128)(2,1)S(1)} %factor.1.rest_0_.own), channel_id=1, source_target_pairs={{0,2},{1,3},{2,0},{3,1},{4,5},{5,4},{6,7},{7,6},{8,10},{9,11},{10,... | collective-permute-start | bytes 688136 | tf_op jit(solution)/shard_map/ppermute | solution.py:373
  64.0 1.2 %collective-permute-start.18 = (bf16[7,128,128]{2,1,0:T(8,128)(2,1)S(1)}, bf16[7,128,128]{2,1,0:T(8,128)(2,1)S(1)}, u32[]{:S(2)}, u32[]{:S(2)}) collective-permute-start(bf16[7,128,128]{2,1,0:T(8,128)(2,1)S(1)} %factor.1.rest_0_.own), channel_id=1, source_target_pairs={{0,1},{1,0},{2,3},{3,2},{4,6},{5,7},{6,4},{7,5},{8,9},{9,8},{10,11... | collective-permute-start | bytes 688136 | tf_op jit(solution)/shard_map/ppermute | solution.py:373
  65.3 1.6 %new_error.5.rest_2_ = bf16[1024,7168]{1,0:T(8,128)(2,1)} custom-call(s32[1]{0:T(128)} %bitcast.dp, s32[1]{0:T(128)} %bitcast.1.mp, bf16[1024,7168]{1,0:T(8,128)(2,1)S(1)} %get-tuple-element.36.comp, bf16[512,128]{1,0:T(8,128)(2,1)S(1)} %get-tuple-element.58.near, bf16[512,128]{1,0:T(8,128)(2,1)S(1)} %get-tuple-element.59.far, ...), custom_call_target="tpu_custom_call" | custom-call | bytes 4900000 | tf_op jit(solution)/shard_map/new_error/pallas_call | solution.py:180
  66.9 0.9 %factor_rows.1 = bf16[1792,128]{1,0:T(8,128)(2,1)} custom-call(s32[1]{0:T(128)} %bitcast.dp, s32[1]{0:T(128)} %bitcast.1.mp, bf16[7,128,128]{2,1,0:T(8,128)(2,1)S(1)} %factor.1.rest_0_.own, bf16[7,128,128]{2,1,0:T(8,128)(2,1)S(1)} %collective-permute-done.15.other.rest_0_), custom_call_target="tpu_custom_call" | custom-call | bytes 3500000 | tf_op jit(solution)/shard_map/factor_rows/pallas_call | solution.py:451
  67.8 0.3 collective-permute-done.14.rest_1_
  68.1 2.4 %collective-permute-start.17 = (bf16[7,128,128]{2,1,0:T(8,128)(2,1)S(1)}, bf16[7,128,128]{2,1,0:T(8,128)(2,1)S(1)}, u32[]{:S(2)}, u32[]{:S(2)}) collective-permute-start(bf16[7,128,128]{2,1,0:T(8,128)(2,1)S(1)} %collective-permute-done.14.rest_1_), channel_id=1, source_target_pairs={{0,4},{1,5},{2,6},{3,7},{4,0},{5,1},{6,2},{7,3},{8,12},{9,13},{10,... | collective-permute-start | bytes 688136 | tf_op jit(solution)/shard_map/ppermute | solution.py:373
  70.5 1.4 %collective-permute-start.16 = (bf16[7,128,128]{2,1,0:T(8,128)(2,1)S(1)}, bf16[7,128,128]{2,1,0:T(8,128)(2,1)S(1)}, u32[]{:S(2)}, u32[]{:S(2)}) collective-permute-start(bf16[7,128,128]{2,1,0:T(8,128)(2,1)S(1)} %collective-permute-done.14.rest_1_), channel_id=1, source_target_pairs={{0,1},{1,0},{2,3},{3,2},{4,6},{5,7},{6,4},{7,5},{8,9},{9,8},{10,11... | collective-permute-start | bytes 688136 | tf_op jit(solution)/shard_map/ppermute | solution.py:373
  72.0 2.3 %new_error.6.rest_2_ = bf16[1024,7168]{1,0:T(8,128)(2,1)} custom-call(s32[1]{0:T(128)} %bitcast.dp, s32[1]{0:T(128)} %bitcast.1.mp, bf16[1024,7168]{1,0:T(8,128)(2,1)S(1)} %get-tuple-element.36.comp, bf16[512,128]{1,0:T(8,128)(2,1)S(1)} %get-tuple-element.58.near, bf16[512,128]{1,0:T(8,128)(2,1)S(1)} %get-tuple-element.59.far, ...), custom_call_target="tpu_custom_call", output_to_operand_aliasing={{}: (7, {})} | custom-call | bytes 7700000 | tf_op jit(solution)/shard_map/new_error/pallas_call | solution.py:180
  74.3 0.0 collective-permute-done.18.rest_1_
  74.3 0.6 collective-permute-start.20
  74.9 2.3 %new_error.7.rest_2_ = bf16[1024,7168]{1,0:T(8,128)(2,1)} custom-call(s32[1]{0:T(128)} %bitcast.dp, s32[1]{0:T(128)} %bitcast.1.mp, bf16[1024,7168]{1,0:T(8,128)(2,1)S(1)} %get-tuple-element.36.comp, bf16[512,128]{1,0:T(8,128)(2,1)S(1)} %get-tuple-element.58.near, bf16[512,128]{1,0:T(8,128)(2,1)S(1)} %get-tuple-element.59.far, ...), custom_call_target="tpu_custom_call", output_to_operand_aliasing={{}: (7, {})} | custom-call | bytes 7700000 | tf_op jit(solution)/shard_map/new_error/pallas_call | solution.py:180
  77.2 0.0 collective-permute-done.16.rest_1_
  77.2 0.1 collective-permute-start.19
  77.3 2.3 %new_error.8.rest_1_ = bf16[1024,7168]{1,0:T(8,128)(2,1)} custom-call(s32[1]{0:T(128)} %bitcast.dp, s32[1]{0:T(128)} %bitcast.1.mp, bf16[1024,7168]{1,0:T(8,128)(2,1)S(1)} %get-tuple-element.36.comp, bf16[512,128]{1,0:T(8,128)(2,1)S(1)} %get-tuple-element.58.near, bf16[512,128]{1,0:T(8,128)(2,1)S(1)} %get-tuple-element.59.far, ...), custom_call_target="tpu_custom_call", output_to_operand_aliasing={{}: (7, {})} | custom-call | bytes 7700000 | tf_op jit(solution)/shard_map/new_error/pallas_call | solution.py:180
  79.6 1.6 %new_error.9 = bf16[1024,7168]{1,0:T(8,128)(2,1)} custom-call(s32[1]{0:T(128)} %bitcast.dp, s32[1]{0:T(128)} %bitcast.1.mp, bf16[1024,7168]{1,0:T(8,128)(2,1)S(1)} %get-tuple-element.36.comp, bf16[512,128]{1,0:T(8,128)(2,1)S(1)} %get-tuple-element.58.near, bf16[512,128]{1,0:T(8,128)(2,1)S(1)} %get-tuple-element.59.far, ...), custom_call_target="tpu_custom_call", output_to_operand_aliasing={{}: (6, {})} | custom-call | bytes 4900000 | tf_op jit(solution)/shard_map/new_error/pallas_call | solution.py:180
  (7 shorter events, 0.1 us)
Async XLA Ops:
  11.9 1.6 %collective-permute-start = (f32[128,512]{1,0:T(8,128)S(1)}, f32[128,512]{1,0:T(8,128)S(1)}, u32[]{:S(2)}, u32[]{:S(2)}) collective-permute-start(f32[128,512]{1,0:T(8,128)S(1)} %get-tuple-element.38), channel_id=1, source_target_pairs={{0,4},{1,5},{2,6},{3,7},{4,0},{5,1},{6,2},{7,3},{8,12},{9,13},{10,... | collective-permute-start | bytes 786440 | tf_op jit(solution)/shard_map/ppermute | solution.py:373
  13.5 7.2 %collective-permute-start.1 = (bf16[128,512]{1,0:T(8,128)(2,1)S(1)}, bf16[128,512]{1,0:T(8,128)(2,1)S(1)}, u32[]{:S(2)}, u32[]{:S(2)}) collective-permute-start(bf16[128,512]{1,0:T(8,128)(2,1)S(1)} %fusion.1), channel_id=1, source_target_pairs={{0,8},{1,9},{2,10},{3,11},{4,20},{5,21},{6,22},{7,23},{8,0},{9,1},... | collective-permute-start | bytes 393224 | tf_op jit(solution)/shard_map/ppermute | solution.py:373
  20.8 4.2 %collective-permute-start.2 = (bf16[128,512]{1,0:T(8,128)(2,1)S(1)}, bf16[128,512]{1,0:T(8,128)(2,1)S(1)}, u32[]{:S(2)}, u32[]{:S(2)}) collective-permute-start(bf16[128,512]{1,0:T(8,128)(2,1)S(1)} %fusion), channel_id=1, source_target_pairs={{0,16},{1,17},{2,18},{3,19},{4,12},{5,13},{6,14},{7,15},{8,24},{9,... | collective-permute-start | bytes 393224 | tf_op jit(solution)/shard_map/ppermute | solution.py:373
  25.1 2.8 %collective-permute-start.3 = (bf16[128,512]{1,0:T(8,128)(2,1)S(1)}, bf16[128,512]{1,0:T(8,128)(2,1)S(1)}, u32[]{:S(2)}, u32[]{:S(2)}) collective-permute-start(bf16[128,512]{1,0:T(8,128)(2,1)S(1)} %add_convert_fusion.near), channel_id=1, source_target_pairs={{0,4},{1,5},{2,6},{3,7},{4,0},{5,1},{6,2},{7,3},{8,12},{9,13},{10,... | collective-permute-start | bytes 393224 | tf_op jit(solution)/shard_map/ppermute | solution.py:373
  28.4 1.6 %collective-permute-start.4 = (bf16[7,128,128]{2,1,0:T(8,128)(2,1)S(1)}, bf16[7,128,128]{2,1,0:T(8,128)(2,1)S(1)}, u32[]{:S(2)}, u32[]{:S(2)}) collective-permute-start(bf16[7,128,128]{2,1,0:T(8,128)(2,1)S(1)} %right_product.9), channel_id=1, source_target_pairs={{0,4},{1,5},{2,6},{3,7},{4,0},{5,1},{6,2},{7,3},{8,12},{9,13},{10,... | collective-permute-start | bytes 688136 | tf_op jit(solution)/shard_map/ppermute | solution.py:373
  29.3 3.7 %collective-permute-start.5 = (bf16[7,128,128]{2,1,0:T(8,128)(2,1)S(1)}, bf16[7,128,128]{2,1,0:T(8,128)(2,1)S(1)}, u32[]{:S(2)}, u32[]{:S(2)}) collective-permute-start(bf16[7,128,128]{2,1,0:T(8,128)(2,1)S(1)} %right_product.11), channel_id=1, source_target_pairs={{0,4},{1,5},{2,6},{3,7},{4,0},{5,1},{6,2},{7,3},{8,12},{9,13},{10,... | collective-permute-start | bytes 688136 | tf_op jit(solution)/shard_map/ppermute | solution.py:373
  30.1 6.2 %collective-permute-start.6 = (bf16[7,128,128]{2,1,0:T(8,128)(2,1)S(1)}, bf16[7,128,128]{2,1,0:T(8,128)(2,1)S(1)}, u32[]{:S(2)}, u32[]{:S(2)}) collective-permute-start(bf16[7,128,128]{2,1,0:T(8,128)(2,1)S(1)} %first_sum.2), channel_id=1, source_target_pairs={{0,1},{1,0},{2,3},{3,2},{4,6},{5,7},{6,4},{7,5},{8,9},{9,8},{10,11... | collective-permute-start | bytes 688136 | tf_op jit(solution)/shard_map/ppermute | solution.py:373
  33.8 3.9 %collective-permute-start.9 = (bf16[7,128,128]{2,1,0:T(8,128)(2,1)S(1)}, bf16[7,128,128]{2,1,0:T(8,128)(2,1)S(1)}, u32[]{:S(2)}, u32[]{:S(2)}) collective-permute-start(bf16[7,128,128]{2,1,0:T(8,128)(2,1)S(1)} %right_product.15), channel_id=1, source_target_pairs={{0,4},{1,5},{2,6},{3,7},{4,0},{5,1},{6,2},{7,3},{8,12},{9,13},{10,... | collective-permute-start | bytes 688136 | tf_op jit(solution)/shard_map/ppermute | solution.py:373
  34.5 5.9 %collective-permute-start.8 = (bf16[9,128,128]{2,1,0:T(8,128)(2,1)S(1)}, bf16[9,128,128]{2,1,0:T(8,128)(2,1)S(1)}, u32[]{:S(2)}, u32[]{:S(2)}) collective-permute-start(bf16[9,128,128]{2,1,0:T(8,128)(2,1)S(1)} %get-tuple-element.47), channel_id=1, source_target_pairs={{0,1},{1,0},{2,3},{3,2},{4,6},{5,7},{6,4},{7,5},{8,9},{9,8},{10,11... | collective-permute-start | bytes 884744 | tf_op jit(solution)/shard_map/ppermute | solution.py:373
  36.8 3.6 %collective-permute-start.7 = (bf16[7,128,128]{2,1,0:T(8,128)(2,1)S(1)}, bf16[7,128,128]{2,1,0:T(8,128)(2,1)S(1)}, u32[]{:S(2)}, u32[]{:S(2)}) collective-permute-start(bf16[7,128,128]{2,1,0:T(8,128)(2,1)S(1)} %right_product.13), channel_id=1, source_target_pairs={{0,4},{1,5},{2,6},{3,7},{4,0},{5,1},{6,2},{7,3},{8,12},{9,13},{10,... | collective-permute-start | bytes 688136 | tf_op jit(solution)/shard_map/ppermute | solution.py:373
  37.8 5.5 %collective-permute-start.10 = (bf16[7,128,128]{2,1,0:T(8,128)(2,1)S(1)}, bf16[7,128,128]{2,1,0:T(8,128)(2,1)S(1)}, u32[]{:S(2)}, u32[]{:S(2)}) collective-permute-start(bf16[7,128,128]{2,1,0:T(8,128)(2,1)S(1)} %second_sum.3), channel_id=1, source_target_pairs={{0,2},{1,3},{2,0},{3,1},{4,5},{5,4},{6,7},{7,6},{8,10},{9,11},{10,... | collective-permute-start | bytes 688136 | tf_op jit(solution)/shard_map/ppermute | solution.py:373
  43.4 8.1 %collective-permute-start.11 = (bf16[7,128,128]{2,1,0:T(8,128)(2,1)S(1)}, bf16[7,128,128]{2,1,0:T(8,128)(2,1)S(1)}, u32[]{:S(2)}, u32[]{:S(2)}) collective-permute-start(bf16[7,128,128]{2,1,0:T(8,128)(2,1)S(1)} %third_sum.1.one), channel_id=1, source_target_pairs={{0,8},{1,9},{2,10},{3,11},{4,20},{5,21},{6,22},{7,23},{8,0},{9,1},... | collective-permute-start | bytes 688136 | tf_op jit(solution)/shard_map/ppermute | solution.py:373
  44.7 3.4 %collective-permute-start.12 = (f32[128,128]{1,0:T(8,128)S(1)}, f32[128,128]{1,0:T(8,128)S(1)}, u32[]{:S(2)}, u32[]{:S(2)}) collective-permute-start(f32[128,128]{1,0:T(8,128)S(1)} %get-tuple-element.51), channel_id=1, source_target_pairs={{0,2},{1,3},{2,0},{3,1},{4,5},{5,4},{6,7},{7,6},{8,10},{9,11},{10,... | collective-permute-start | bytes 196616 | tf_op jit(solution)/shard_map/ppermute | solution.py:373
  51.5 5.2 %collective-permute-start.13 = (bf16[7,128,128]{2,1,0:T(8,128)(2,1)S(1)}, bf16[7,128,128]{2,1,0:T(8,128)(2,1)S(1)}, u32[]{:S(2)}, u32[]{:S(2)}) collective-permute-start(bf16[7,128,128]{2,1,0:T(8,128)(2,1)S(1)} %pair_sum.1.own), channel_id=1, source_target_pairs={{0,16},{1,17},{2,18},{3,19},{4,12},{5,13},{6,14},{7,15},{8,24},{9,... | collective-permute-start | bytes 688136 | tf_op jit(solution)/shard_map/ppermute | solution.py:373
  57.4 9.5 %collective-permute-start.15 = (bf16[7,128,128]{2,1,0:T(8,128)(2,1)S(1)}, bf16[7,128,128]{2,1,0:T(8,128)(2,1)S(1)}, u32[]{:S(2)}, u32[]{:S(2)}) collective-permute-start(bf16[7,128,128]{2,1,0:T(8,128)(2,1)S(1)} %factor.1.rest_0_.own), channel_id=1, source_target_pairs={{0,4},{1,5},{2,6},{3,7},{4,0},{5,1},{6,2},{7,3},{8,12},{9,13},{10,... | collective-permute-start | bytes 688136 | tf_op jit(solution)/shard_map/ppermute | solution.py:373
  62.7 5.4 %collective-permute-start.14 = (bf16[7,128,128]{2,1,0:T(8,128)(2,1)S(1)}, bf16[7,128,128]{2,1,0:T(8,128)(2,1)S(1)}, u32[]{:S(2)}, u32[]{:S(2)}) collective-permute-start(bf16[7,128,128]{2,1,0:T(8,128)(2,1)S(1)} %factor.1.rest_0_.own), channel_id=1, source_target_pairs={{0,2},{1,3},{2,0},{3,1},{4,5},{5,4},{6,7},{7,6},{8,10},{9,11},{10,... | collective-permute-start | bytes 688136 | tf_op jit(solution)/shard_map/ppermute | solution.py:373
  64.0 10.3 %collective-permute-start.18 = (bf16[7,128,128]{2,1,0:T(8,128)(2,1)S(1)}, bf16[7,128,128]{2,1,0:T(8,128)(2,1)S(1)}, u32[]{:S(2)}, u32[]{:S(2)}) collective-permute-start(bf16[7,128,128]{2,1,0:T(8,128)(2,1)S(1)} %factor.1.rest_0_.own), channel_id=1, source_target_pairs={{0,1},{1,0},{2,3},{3,2},{4,6},{5,7},{6,4},{7,5},{8,9},{9,8},{10,11... | collective-permute-start | bytes 688136 | tf_op jit(solution)/shard_map/ppermute | solution.py:373
  68.1 6.8 %collective-permute-start.17 = (bf16[7,128,128]{2,1,0:T(8,128)(2,1)S(1)}, bf16[7,128,128]{2,1,0:T(8,128)(2,1)S(1)}, u32[]{:S(2)}, u32[]{:S(2)}) collective-permute-start(bf16[7,128,128]{2,1,0:T(8,128)(2,1)S(1)} %collective-permute-done.14.rest_1_), channel_id=1, source_target_pairs={{0,4},{1,5},{2,6},{3,7},{4,0},{5,1},{6,2},{7,3},{8,12},{9,13},{10,... | collective-permute-start | bytes 688136 | tf_op jit(solution)/shard_map/ppermute | solution.py:373
  70.5 6.7 %collective-permute-start.16 = (bf16[7,128,128]{2,1,0:T(8,128)(2,1)S(1)}, bf16[7,128,128]{2,1,0:T(8,128)(2,1)S(1)}, u32[]{:S(2)}, u32[]{:S(2)}) collective-permute-start(bf16[7,128,128]{2,1,0:T(8,128)(2,1)S(1)} %collective-permute-done.14.rest_1_), channel_id=1, source_target_pairs={{0,1},{1,0},{2,3},{3,2},{4,6},{5,7},{6,4},{7,5},{8,9},{9,8},{10,11... | collective-permute-start | bytes 688136 | tf_op jit(solution)/shard_map/ppermute | solution.py:373
  74.3 3.0 %collective-permute-start.20 = (bf16[7,128,128]{2,1,0:T(8,128)(2,1)S(1)}, bf16[7,128,128]{2,1,0:T(8,128)(2,1)S(1)}, u32[]{:S(2)}, u32[]{:S(2)}) collective-permute-start(bf16[7,128,128]{2,1,0:T(8,128)(2,1)S(1)} %collective-permute-done.18.rest_1_), channel_id=1, source_target_pairs={{0,4},{1,5},{2,6},{3,7},{4,0},{5,1},{6,2},{7,3},{8,12},{9,13},{10,... | collective-permute-start | bytes 688136 | tf_op jit(solution)/shard_map/ppermute | solution.py:373
  77.2 2.4 %collective-permute-start.19 = (bf16[7,128,128]{2,1,0:T(8,128)(2,1)S(1)}, bf16[7,128,128]{2,1,0:T(8,128)(2,1)S(1)}, u32[]{:S(2)}, u32[]{:S(2)}) collective-permute-start(bf16[7,128,128]{2,1,0:T(8,128)(2,1)S(1)} %collective-permute-done.16.rest_1_), channel_id=1, source_target_pairs={{0,4},{1,5},{2,6},{3,7},{4,0},{5,1},{6,2},{7,3},{8,12},{9,13},{10,... | collective-permute-start | bytes 688136 | tf_op jit(solution)/shard_map/ppermute | solution.py:373

commit v6 on v5

--- a/solution.py
+++ b/solution.py
@@ -263,29 +263,18 @@
         state[base + i : base + i + 1, n:] = (total * scale[i])[:1]
 
 
-def leaves_kernel(leaves, source, state):
+def inverse_kernel(gram, state):
     n = state.shape[0]
-    if source.shape == state.shape:
-        state[...] = source[...]
-    else:
-        state[:, :n] = source[...]
-        row = lax.broadcasted_iota(jnp.int32, (n, n), 0)
-        state[:, n:] = (row == lax.broadcasted_iota(jnp.int32, (n, n), 1)).astype(F32)
-    for leaf in leaves:
+    state[:, :n] = gram[...]
+    row = lax.broadcasted_iota(jnp.int32, (n, n), 0)
+    state[:, n:] = (row == lax.broadcasted_iota(jnp.int32, (n, n), 1)).astype(F32)
+    for leaf in range(n // LEAF):
         leaf_steps(state, leaf)
 
 
-def inverse_part(source, leaves):
-    n = source.shape[0]
-    return call(
-        functools.partial(leaves_kernel, leaves),
-        "inverse_part",
-        shaped((n, 2 * n), F32),
-        [VMEM],
-        4,
-        1.5,
-        out_specs=VMEM,
-    )(source)
+def inverse_of(gram):
+    n = gram.shape[0]
+    return call(inverse_kernel, "inverse", shaped((n, 2 * n), F32), [VMEM], 4, 4.5, out_specs=VMEM)(gram)
 
 
 def split2(x):
@@ -334,7 +323,8 @@
             out[k] = product[:, (k - i) * LANES : (k - i + 1) * LANES].astype(BF16)
 
 
-def base_kernel(near, far, state, near_out, far_out):
+def base_kernel(near, far, state, after, near_out, far_out):
+    del after
     rank = near.shape[0]
     lhs = jnp.concatenate(split2(state[:, rank:]), axis=0)
     for source, out in ((near, near_out), (far, far_out)):
@@ -426,25 +416,22 @@
         gram = gram + net.send(gram, (bit, bit))
     sent = small(add_kernel, "third_sum", block, kept, arrived)
 
-    leaves = list(range(rank // LEAF))
-    steps = len(net.rest)
-    state = gram
-    for k, step in enumerate(net.rest):
-        arrived = net.send(sent, step)
-        state = inverse_part(state, leaves[len(leaves) * k // steps : len(leaves) * (k + 1) // steps])
-        arrived, state = lax.optimization_barrier((arrived, state))
-        if k < steps - 1:
-            sent = small(add_kernel, "pair_sum", block, sent, arrived)
+    for step in net.rest[:-1]:
+        arrived, gram = lax.optimization_barrier((net.send(sent, step), gram))
+        sent = small(add_kernel, "pair_sum", block, sent, arrived)
+    arrived = net.send(sent, net.rest[-1])
+    sent, gram = lax.optimization_barrier((sent, gram))
+    arrived, state = lax.optimization_barrier((arrived, inverse_of(gram)))
     own = small(functools.partial(factor_kernel, dp), "factor", block, sent, arrived, state)
 
     blocks = [own, net.send(own, net.scatter[1]), net.send(own, net.scatter[0]), None]
     base_near, base_far = small(
-        base_kernel, "base", [shaped((rows // 2, rank), BF16)] * 2, near, far, state
+        base_kernel, "base", [shaped((rows // 2, rank), BF16)] * 2, near, far, state, own
     )
-    own, base_near, base_far = lax.optimization_barrier((own, base_near, base_far))
-    others = [net.core(own)]
     write = functools.partial(new_error, net, place, units=units, comp=comp, near=base_near, far=base_far)
     out = write([(NEAR, 0)], [own])
+    own, out = lax.optimization_barrier((own, out))
+    others = [net.core(own)]
     share, width = cols // mp, units * LANES
     right_factor = None
     if share == 2 * width:
@@ -452,13 +439,16 @@
             functools.partial(rows_kernel, net, units), "factor_rows", shaped((share, rank), BF16),
             [SMEM, SMEM, VMEM, VMEM], 4, 1, out_specs=VMEM,
         )(*place, own, others[0])
-    for k in range(1, 4):
-        blocks[k], out, right_factor = lax.optimization_barrier((blocks[k], out, right_factor))
-        if k == 1:
-            blocks[3] = net.send(blocks[1], net.scatter[0])
-        others.append(net.core(blocks[k]))
-        out = write([(FAR, k - 1), (NEAR, k)], [others[k - 1], blocks[k]], held=out)
-    out = write([(FAR, 3)], [others[3]], held=out)
+    blocks[1], out = lax.optimization_barrier((blocks[1], out))
+    blocks[3] = net.send(blocks[1], net.scatter[0])
+    others.append(net.core(blocks[1]))
+    blocks[2], out = lax.optimization_barrier((blocks[2], out))
+    others.append(net.core(blocks[2]))
+    out = write([(FAR, 0), (NEAR, 1), (FAR, 1)], [others[0], blocks[1], others[1]], held=out)
+    blocks[3], out, right_factor = lax.optimization_barrier((blocks[3], out, right_factor))
+    others.append(net.core(blocks[3]))
+    out = write([(NEAR, 2), (FAR, 2)], [blocks[2], others[2]], held=out)
+    out = write([(NEAR, 3), (FAR, 3)], [blocks[3], others[3]], held=out)
     if right_factor is None:
         everything = jnp.concatenate(blocks + others, axis=0)
         here = Place(net, place)

time: 82 us -> 79.8 us (0.973)
  starting transfers between devices: 30.4 us -> 27.6 us
  waiting for transfers between devices: 18 us -> 19.2 us
    ppermute x21, starting transfers between devices: 30.4 us -> 27.6 us  [send(): return lax.ppermute(x, AXES, pairs)]
    ppermute x21, waiting for transfers between devices: 18 us -> 19.2 us  [send(): return lax.ppermute(x, AXES, pairs)]
    pallas_call x5 -> x4, Pallas kernels: 10.2 us -> 9.27 us  [new_error(): call(functools.partial(new_error_kernel, net, units, blocks), 'new_error'...]
    pallas_call x2 -> x1, Pallas kernels: 4.49 us -> 4.86 us  [inverse_of(): call(inverse_kernel, 'inverse', shaped((n, 2 * n), F32), [VMEM], 4, 4.5,...]
  transfers between devices with their start and end apart: 21 -> 21, of which waited for: 10 -> 9; matrix products, arithmetic and copies ran while one was open for 0% -> 0% of each run, Pallas kernels for 22% -> 21%
where the time goes in v6:
time: 79.8 us; the launch traced here: 79.3 us
  Pallas kernels  31.4 us (39%)
  starting transfers between devices  27.6 us (35%)
  waiting for transfers between devices  19.2 us (24%)
  between operations  1 us (1%)
    ppermute x21, starting transfers between devices, send(): return lax.ppermute(x, AXES, pairs)  27.6 us
    ppermute x21, waiting for transfers between devices, send(): return lax.ppermute(x, AXES, pairs)  19.2 us
    pallas_call x1, Pallas kernels, left_product(): call(functools.partial(left_kernel, net, PIECES), 'left_product', [pltpu....  11.2 us
    pallas_call x4, Pallas kernels, new_error(): call(functools.partial(new_error_kernel, net, units, blocks), 'new_error'...  9.27 us
    pallas_call x1, Pallas kernels, inverse_of(): call(inverse_kernel, 'inverse', shaped((n, 2 * n), F32), [VMEM], 4, 4.5,...  4.86 us
    pallas_call x8, Pallas kernels, right_product(): call(functools.partial(right_kernel, net, units, side, places), 'right_pr...  3.86 us
  transfers between devices with their start and end apart: 21, of which 9 were waited for; matrix products, arithmetic and copies ran while one was open for 0% of the time, Pallas kernels for 21%

profile of v6, /device:TPU:1, one launch (start us, length us, event | category | flops | bytes accessed | tf_op | source)
XLA Modules:
  0.0 79.3 jit_solution(414377522209172613)
XLA Ops:
  0.6 11.2 %left_product.1 = (bf16[1024,7168]{1,0:T(8,128)(2,1)S(1)}, f32[128,512]{1,0:T(8,128)S(1)}, f32[128,512]{1,0:T(8,128)S(1)}) custom-call(s32[1]{0:T(128)} %bitcast.dp, s32[1]{0:T(128)} %bitcast.1.mp, bf16[1024,7168]{1,0:T(8,128)(2,1)} %bitcast.6, bf16[1024,7168]{1,0:T(8,128)(2,1)} %bitcast.7, bf16[7168,128]{1,0:T(8,128)(2,1)} %init.1), custom_call_target="tpu_custom_call" | custom-call | bytes 42000000 | tf_op jit(solution)/shard_map/left_product/pallas_call | solution.py:106
  11.9 0.1 collective-permute-start
  12.0 1.5 %collective-permute-done = f32[128,512]{1,0:T(8,128)S(1)} collective-permute-done((f32[128,512]{1,0:T(8,128)S(1)}, f32[128,512]{1,0:T(8,128)S(1)}, u32[]{:S(2)}, u32[]{:S(2)}) %collective-permute-start) | collective-permute-done | bytes 262176 | tf_op jit(solution)/shard_map/ppermute | solution.py:363
  13.5 3.5 %collective-permute-start.1 = (bf16[128,512]{1,0:T(8,128)(2,1)S(1)}, bf16[128,512]{1,0:T(8,128)(2,1)S(1)}, u32[]{:S(2)}, u32[]{:S(2)}) collective-permute-start(bf16[128,512]{1,0:T(8,128)(2,1)S(1)} %fusion.1), channel_id=1, source_target_pairs={{0,8},{1,9},{2,10},{3,11},{4,20},{5,21},{6,22},{7,23},{8,0},{9,1},... | collective-permute-start | bytes 393224 | tf_op jit(solution)/shard_map/ppermute | solution.py:363
  17.0 3.7 %collective-permute-done.1 = bf16[128,512]{1,0:T(8,128)(2,1)S(1)} collective-permute-done((bf16[128,512]{1,0:T(8,128)(2,1)S(1)}, bf16[128,512]{1,0:T(8,128)(2,1)S(1)}, u32[]{:S(2)}, u32[]{:S(2)}) %collective-permute-start.1) | collective-permute-done | bytes 131104 | tf_op jit(solution)/shard_map/ppermute | solution.py:363
  20.7 0.1 fusion
  20.8 0.7 collective-permute-start.2
  21.5 3.4 %collective-permute-done.2 = bf16[128,512]{1,0:T(8,128)(2,1)S(1)} collective-permute-done((bf16[128,512]{1,0:T(8,128)(2,1)S(1)}, bf16[128,512]{1,0:T(8,128)(2,1)S(1)}, u32[]{:S(2)}, u32[]{:S(2)}) %collective-permute-start.2) | collective-permute-done | bytes 131104 | tf_op jit(solution)/shard_map/ppermute | solution.py:363
  25.0 0.1 add_convert_fusion.near
  25.1 1.9 %collective-permute-start.3 = (bf16[128,512]{1,0:T(8,128)(2,1)S(1)}, bf16[128,512]{1,0:T(8,128)(2,1)S(1)}, u32[]{:S(2)}, u32[]{:S(2)}) collective-permute-start(bf16[128,512]{1,0:T(8,128)(2,1)S(1)} %add_convert_fusion.near), channel_id=1, source_target_pairs={{0,4},{1,5},{2,6},{3,7},{4,0},{5,1},{6,2},{7,3},{8,12},{9,13},{10,... | collective-permute-start | bytes 393224 | tf_op jit(solution)/shard_map/ppermute | solution.py:363
  26.9 1.0 %collective-permute-done.3.far = bf16[128,512]{1,0:T(8,128)(2,1)S(1)} collective-permute-done((bf16[128,512]{1,0:T(8,128)(2,1)S(1)}, bf16[128,512]{1,0:T(8,128)(2,1)S(1)}, u32[]{:S(2)}, u32[]{:S(2)}) %collective-permute-start.3) | collective-permute-done | bytes 131104 | tf_op jit(solution)/shard_map/ppermute | solution.py:363
  27.9 0.5 right_product.9
  28.4 0.4 collective-permute-start.4
  28.9 0.5 right_product.11
  29.3 0.2 collective-permute-start.5
  29.5 0.5 right_product.8.one
  30.0 0.0 collective-permute-done.4.other
  30.0 0.1 first_sum.2
  30.1 2.4 %collective-permute-start.6 = (bf16[7,128,128]{2,1,0:T(8,128)(2,1)S(1)}, bf16[7,128,128]{2,1,0:T(8,128)(2,1)S(1)}, u32[]{:S(2)}, u32[]{:S(2)}) collective-permute-start(bf16[7,128,128]{2,1,0:T(8,128)(2,1)S(1)} %first_sum.2), channel_id=1, source_target_pairs={{0,1},{1,0},{2,3},{3,2},{4,6},{5,7},{6,4},{7,5},{8,9},{9,8},{10,11... | collective-permute-start | bytes 688136 | tf_op jit(solution)/shard_map/ppermute | solution.py:363
  32.6 0.5 right_product.10.part
  33.0 0.0 collective-permute-done.5.across
  33.0 0.2 first_sum.3
  33.3 0.5 right_product.15
  33.8 0.7 collective-permute-start.9
  34.5 1.2 %collective-permute-start.8 = (bf16[9,128,128]{2,1,0:T(8,128)(2,1)S(1)}, bf16[9,128,128]{2,1,0:T(8,128)(2,1)S(1)}, u32[]{:S(2)}, u32[]{:S(2)}) collective-permute-start(bf16[9,128,128]{2,1,0:T(8,128)(2,1)S(1)} %get-tuple-element.46), channel_id=1, source_target_pairs={{0,1},{1,0},{2,3},{3,2},{4,6},{5,7},{6,4},{7,5},{8,9},{9,8},{10,11... | collective-permute-start | bytes 884744 | tf_op jit(solution)/shard_map/ppermute | solution.py:363
  35.7 0.5 right_product.14.part
  36.2 0.0 collective-permute-done.6.arrived
  36.3 0.5 right_product.13
  36.8 1.0 %collective-permute-start.7 = (bf16[7,128,128]{2,1,0:T(8,128)(2,1)S(1)}, bf16[7,128,128]{2,1,0:T(8,128)(2,1)S(1)}, u32[]{:S(2)}, u32[]{:S(2)}) collective-permute-start(bf16[7,128,128]{2,1,0:T(8,128)(2,1)S(1)} %right_product.13), channel_id=1, source_target_pairs={{0,4},{1,5},{2,6},{3,7},{4,0},{5,1},{6,2},{7,3},{8,12},{9,13},{10,... | collective-permute-start | bytes 688136 | tf_op jit(solution)/shard_map/ppermute | solution.py:363
  37.7 0.0 collective-permute-done.9.across
  37.7 0.1 second_sum.3
  37.8 1.8 %collective-permute-start.10 = (bf16[7,128,128]{2,1,0:T(8,128)(2,1)S(1)}, bf16[7,128,128]{2,1,0:T(8,128)(2,1)S(1)}, u32[]{:S(2)}, u32[]{:S(2)}) collective-permute-start(bf16[7,128,128]{2,1,0:T(8,128)(2,1)S(1)} %second_sum.3), channel_id=1, source_target_pairs={{0,2},{1,3},{2,0},{3,1},{4,5},{5,4},{6,7},{7,6},{8,10},{9,11},{10,... | collective-permute-start | bytes 688136 | tf_op jit(solution)/shard_map/ppermute | solution.py:363
  39.6 0.5 right_product.12.part
  40.1 0.2 collective-permute-done.8.arrived
  40.3 0.0 collective-permute-done.7.across
  40.3 0.1 second_sum.2
  40.4 2.9 %collective-permute-done.10.other = bf16[7,128,128]{2,1,0:T(8,128)(2,1)S(1)} collective-permute-done((bf16[7,128,128]{2,1,0:T(8,128)(2,1)S(1)}, bf16[7,128,128]{2,1,0:T(8,128)(2,1)S(1)}, u32[]{:S(2)}, u32[]{:S(2)}) %collective-permute-start.10) | collective-permute-done | bytes 229408 | tf_op jit(solution)/shard_map/ppermute | solution.py:363
  43.4 1.3 %collective-permute-start.11 = (bf16[7,128,128]{2,1,0:T(8,128)(2,1)S(1)}, bf16[7,128,128]{2,1,0:T(8,128)(2,1)S(1)}, u32[]{:S(2)}, u32[]{:S(2)}) collective-permute-start(bf16[7,128,128]{2,1,0:T(8,128)(2,1)S(1)} %third_sum.1.one), channel_id=1, source_target_pairs={{0,8},{1,9},{2,10},{3,11},{4,20},{5,21},{6,22},{7,23},{8,0},{9,1},... | collective-permute-start | bytes 688136 | tf_op jit(solution)/shard_map/ppermute | solution.py:363
  44.7 1.2 %collective-permute-start.12 = (f32[128,128]{1,0:T(8,128)S(1)}, f32[128,128]{1,0:T(8,128)S(1)}, u32[]{:S(2)}, u32[]{:S(2)}) collective-permute-start(f32[128,128]{1,0:T(8,128)S(1)} %get-tuple-element.50), channel_id=1, source_target_pairs={{0,2},{1,3},{2,0},{3,1},{4,5},{5,4},{6,7},{7,6},{8,10},{9,11},{10,... | collective-permute-start | bytes 196616 | tf_op jit(solution)/shard_map/ppermute | solution.py:363
  45.9 2.2 %collective-permute-done.12 = f32[128,128]{1,0:T(8,128)S(1)} collective-permute-done((f32[128,128]{1,0:T(8,128)S(1)}, f32[128,128]{1,0:T(8,128)S(1)}, u32[]{:S(2)}, u32[]{:S(2)}) %collective-permute-start.12) | collective-permute-done | bytes 65568 | tf_op jit(solution)/shard_map/ppermute | solution.py:363
  48.1 3.3 %collective-permute-done.11.other = bf16[7,128,128]{2,1,0:T(8,128)(2,1)S(1)} collective-permute-done((bf16[7,128,128]{2,1,0:T(8,128)(2,1)S(1)}, bf16[7,128,128]{2,1,0:T(8,128)(2,1)S(1)}, u32[]{:S(2)}, u32[]{:S(2)}) %collective-permute-start.11) | collective-permute-done | bytes 229408 | tf_op jit(solution)/shard_map/ppermute | solution.py:363
  51.4 0.1 pair_sum.1.own
  51.5 0.8 %collective-permute-start.13 = (bf16[7,128,128]{2,1,0:T(8,128)(2,1)S(1)}, bf16[7,128,128]{2,1,0:T(8,128)(2,1)S(1)}, u32[]{:S(2)}, u32[]{:S(2)}) collective-permute-start(bf16[7,128,128]{2,1,0:T(8,128)(2,1)S(1)} %pair_sum.1.own), channel_id=1, source_target_pairs={{0,16},{1,17},{2,18},{3,19},{4,12},{5,13},{6,14},{7,15},{8,24},{9,... | collective-permute-start | bytes 688136 | tf_op jit(solution)/shard_map/ppermute | solution.py:363
  52.3 4.9 %inverse.1.state = f32[128,256]{1,0:T(8,128)S(1)} custom-call(f32[128,128]{1,0:T(8,128)S(1)} %add.15.gram), custom_call_target="tpu_custom_call" | custom-call | bytes 15750000 | tf_op jit(solution)/shard_map/inverse/pallas_call | solution.py:277
  57.2 0.8 collective-permute-done.13.arrived
  58.0 0.3 factor.1.after.rest_0_.own
  58.3 1.6 %collective-permute-start.14 = (bf16[7,128,128]{2,1,0:T(8,128)(2,1)S(1)}, bf16[7,128,128]{2,1,0:T(8,128)(2,1)S(1)}, u32[]{:S(2)}, u32[]{:S(2)}) collective-permute-start(bf16[7,128,128]{2,1,0:T(8,128)(2,1)S(1)} %factor.1.after.rest_0_.own), channel_id=1, source_target_pairs={{0,2},{1,3},{2,0},{3,1},{4,5},{5,4},{6,7},{7,6},{8,10},{9,11},{10,... | collective-permute-start | bytes 688136 | tf_op jit(solution)/shard_map/ppermute | solution.py:363
  59.8 0.4 base.1
  60.2 1.3 %collective-permute-start.18 = (bf16[7,128,128]{2,1,0:T(8,128)(2,1)S(1)}, bf16[7,128,128]{2,1,0:T(8,128)(2,1)S(1)}, u32[]{:S(2)}, u32[]{:S(2)}) collective-permute-start(bf16[7,128,128]{2,1,0:T(8,128)(2,1)S(1)} %factor.1.after.rest_0_.own), channel_id=1, source_target_pairs={{0,1},{1,0},{2,3},{3,2},{4,6},{5,7},{6,4},{7,5},{8,9},{9,8},{10,11... | collective-permute-start | bytes 688136 | tf_op jit(solution)/shard_map/ppermute | solution.py:363
  61.5 1.6 %new_error.4.rest_3_ = bf16[1024,7168]{1,0:T(8,128)(2,1)} custom-call(s32[1]{0:T(128)} %bitcast.dp, s32[1]{0:T(128)} %bitcast.1.mp, bf16[1024,7168]{1,0:T(8,128)(2,1)S(1)} %get-tuple-element.35.comp, bf16[512,128]{1,0:T(8,128)(2,1)S(1)} %get-tuple-element.57.near, bf16[512,128]{1,0:T(8,128)(2,1)S(1)} %get-tuple-element.58.far, ...), custom_call_target="tpu_custom_call" | custom-call | bytes 4900000 | tf_op jit(solution)/shard_map/new_error/pallas_call | solution.py:180
  63.1 4.5 %collective-permute-start.16 = (bf16[7,128,128]{2,1,0:T(8,128)(2,1)S(1)}, bf16[7,128,128]{2,1,0:T(8,128)(2,1)S(1)}, u32[]{:S(2)}, u32[]{:S(2)}) collective-permute-start(bf16[7,128,128]{2,1,0:T(8,128)(2,1)S(1)} %factor.1.after.rest_0_.own), channel_id=1, source_target_pairs={{0,4},{1,5},{2,6},{3,7},{4,0},{5,1},{6,2},{7,3},{8,12},{9,13},{10,... | collective-permute-start | bytes 688136 | tf_op jit(solution)/shard_map/ppermute | solution.py:363
  67.6 0.0 collective-permute-done.14.rest_1_
  67.6 0.7 collective-permute-start.17
  68.3 1.4 %collective-permute-start.15 = (bf16[7,128,128]{2,1,0:T(8,128)(2,1)S(1)}, bf16[7,128,128]{2,1,0:T(8,128)(2,1)S(1)}, u32[]{:S(2)}, u32[]{:S(2)}) collective-permute-start(bf16[7,128,128]{2,1,0:T(8,128)(2,1)S(1)} %collective-permute-done.14.rest_1_), channel_id=1, source_target_pairs={{0,1},{1,0},{2,3},{3,2},{4,6},{5,7},{6,4},{7,5},{8,9},{9,8},{10,11... | collective-permute-start | bytes 688136 | tf_op jit(solution)/shard_map/ppermute | solution.py:363
  69.7 0.0 collective-permute-done.18.rest_0_
  69.7 0.7 collective-permute-start.20
  70.4 0.0 collective-permute-done.16.rest_0_.other
  70.4 0.9 %factor_rows.1 = bf16[1792,128]{1,0:T(8,128)(2,1)} custom-call(s32[1]{0:T(128)} %bitcast.dp, s32[1]{0:T(128)} %bitcast.1.mp, bf16[7,128,128]{2,1,0:T(8,128)(2,1)S(1)} %factor.1.after.rest_0_.own, bf16[7,128,128]{2,1,0:T(8,128)(2,1)S(1)} %collective-permute-done.16.rest_0_.other), custom_call_target="tpu_custom_call" | custom-call | bytes 3500000 | tf_op jit(solution)/shard_map/factor_rows/pallas_call | solution.py:438
  71.4 0.0 collective-permute-done.17.rest_2_
  71.4 3.0 %new_error.5.rest_2_ = bf16[1024,7168]{1,0:T(8,128)(2,1)} custom-call(s32[1]{0:T(128)} %bitcast.dp, s32[1]{0:T(128)} %bitcast.1.mp, bf16[1024,7168]{1,0:T(8,128)(2,1)S(1)} %get-tuple-element.35.comp, bf16[512,128]{1,0:T(8,128)(2,1)S(1)} %get-tuple-element.57.near, bf16[512,128]{1,0:T(8,128)(2,1)S(1)} %get-tuple-element.58.far, ...), custom_call_target="tpu_custom_call", output_to_operand_aliasing={{}: (8, {})} | custom-call | bytes 10500000 | tf_op jit(solution)/shard_map/new_error/pallas_call | solution.py:180
  74.4 0.1 collective-permute-start.19
  74.5 0.0 collective-permute-done.20.rest_1_
  74.5 2.3 %new_error.6.rest_2_ = bf16[1024,7168]{1,0:T(8,128)(2,1)} custom-call(s32[1]{0:T(128)} %bitcast.dp, s32[1]{0:T(128)} %bitcast.1.mp, bf16[1024,7168]{1,0:T(8,128)(2,1)S(1)} %get-tuple-element.35.comp, bf16[512,128]{1,0:T(8,128)(2,1)S(1)} %get-tuple-element.57.near, bf16[512,128]{1,0:T(8,128)(2,1)S(1)} %get-tuple-element.58.far, ...), custom_call_target="tpu_custom_call", output_to_operand_aliasing={{}: (7, {})} | custom-call | bytes 7700000 | tf_op jit(solution)/shard_map/new_error/pallas_call | solution.py:180
  76.8 2.3 %new_error.7 = bf16[1024,7168]{1,0:T(8,128)(2,1)} custom-call(s32[1]{0:T(128)} %bitcast.dp, s32[1]{0:T(128)} %bitcast.1.mp, bf16[1024,7168]{1,0:T(8,128)(2,1)S(1)} %get-tuple-element.35.comp, bf16[512,128]{1,0:T(8,128)(2,1)S(1)} %get-tuple-element.57.near, bf16[512,128]{1,0:T(8,128)(2,1)S(1)} %get-tuple-element.58.far, ...), custom_call_target="tpu_custom_call", output_to_operand_aliasing={{}: (7, {})} | custom-call | bytes 7700000 | tf_op jit(solution)/shard_map/new_error/pallas_call | solution.py:180
  (5 shorter events, 0.1 us)
Async XLA Ops:
  11.9 1.6 %collective-permute-start = (f32[128,512]{1,0:T(8,128)S(1)}, f32[128,512]{1,0:T(8,128)S(1)}, u32[]{:S(2)}, u32[]{:S(2)}) collective-permute-start(f32[128,512]{1,0:T(8,128)S(1)} %get-tuple-element.37), channel_id=1, source_target_pairs={{0,4},{1,5},{2,6},{3,7},{4,0},{5,1},{6,2},{7,3},{8,12},{9,13},{10,... | collective-permute-start | bytes 786440 | tf_op jit(solution)/shard_map/ppermute | solution.py:363
  13.5 7.2 %collective-permute-start.1 = (bf16[128,512]{1,0:T(8,128)(2,1)S(1)}, bf16[128,512]{1,0:T(8,128)(2,1)S(1)}, u32[]{:S(2)}, u32[]{:S(2)}) collective-permute-start(bf16[128,512]{1,0:T(8,128)(2,1)S(1)} %fusion.1), channel_id=1, source_target_pairs={{0,8},{1,9},{2,10},{3,11},{4,20},{5,21},{6,22},{7,23},{8,0},{9,1},... | collective-permute-start | bytes 393224 | tf_op jit(solution)/shard_map/ppermute | solution.py:363
  20.8 4.2 %collective-permute-start.2 = (bf16[128,512]{1,0:T(8,128)(2,1)S(1)}, bf16[128,512]{1,0:T(8,128)(2,1)S(1)}, u32[]{:S(2)}, u32[]{:S(2)}) collective-permute-start(bf16[128,512]{1,0:T(8,128)(2,1)S(1)} %fusion), channel_id=1, source_target_pairs={{0,16},{1,17},{2,18},{3,19},{4,12},{5,13},{6,14},{7,15},{8,24},{9,... | collective-permute-start | bytes 393224 | tf_op jit(solution)/shard_map/ppermute | solution.py:363
  25.1 2.8 %collective-permute-start.3 = (bf16[128,512]{1,0:T(8,128)(2,1)S(1)}, bf16[128,512]{1,0:T(8,128)(2,1)S(1)}, u32[]{:S(2)}, u32[]{:S(2)}) collective-permute-start(bf16[128,512]{1,0:T(8,128)(2,1)S(1)} %add_convert_fusion.near), channel_id=1, source_target_pairs={{0,4},{1,5},{2,6},{3,7},{4,0},{5,1},{6,2},{7,3},{8,12},{9,13},{10,... | collective-permute-start | bytes 393224 | tf_op jit(solution)/shard_map/ppermute | solution.py:363
  28.4 1.6 %collective-permute-start.4 = (bf16[7,128,128]{2,1,0:T(8,128)(2,1)S(1)}, bf16[7,128,128]{2,1,0:T(8,128)(2,1)S(1)}, u32[]{:S(2)}, u32[]{:S(2)}) collective-permute-start(bf16[7,128,128]{2,1,0:T(8,128)(2,1)S(1)} %right_product.9), channel_id=1, source_target_pairs={{0,4},{1,5},{2,6},{3,7},{4,0},{5,1},{6,2},{7,3},{8,12},{9,13},{10,... | collective-permute-start | bytes 688136 | tf_op jit(solution)/shard_map/ppermute | solution.py:363
  29.3 3.7 %collective-permute-start.5 = (bf16[7,128,128]{2,1,0:T(8,128)(2,1)S(1)}, bf16[7,128,128]{2,1,0:T(8,128)(2,1)S(1)}, u32[]{:S(2)}, u32[]{:S(2)}) collective-permute-start(bf16[7,128,128]{2,1,0:T(8,128)(2,1)S(1)} %right_product.11), channel_id=1, source_target_pairs={{0,4},{1,5},{2,6},{3,7},{4,0},{5,1},{6,2},{7,3},{8,12},{9,13},{10,... | collective-permute-start | bytes 688136 | tf_op jit(solution)/shard_map/ppermute | solution.py:363
  30.1 6.2 %collective-permute-start.6 = (bf16[7,128,128]{2,1,0:T(8,128)(2,1)S(1)}, bf16[7,128,128]{2,1,0:T(8,128)(2,1)S(1)}, u32[]{:S(2)}, u32[]{:S(2)}) collective-permute-start(bf16[7,128,128]{2,1,0:T(8,128)(2,1)S(1)} %first_sum.2), channel_id=1, source_target_pairs={{0,1},{1,0},{2,3},{3,2},{4,6},{5,7},{6,4},{7,5},{8,9},{9,8},{10,11... | collective-permute-start | bytes 688136 | tf_op jit(solution)/shard_map/ppermute | solution.py:363
  33.8 3.9 %collective-permute-start.9 = (bf16[7,128,128]{2,1,0:T(8,128)(2,1)S(1)}, bf16[7,128,128]{2,1,0:T(8,128)(2,1)S(1)}, u32[]{:S(2)}, u32[]{:S(2)}) collective-permute-start(bf16[7,128,128]{2,1,0:T(8,128)(2,1)S(1)} %right_product.15), channel_id=1, source_target_pairs={{0,4},{1,5},{2,6},{3,7},{4,0},{5,1},{6,2},{7,3},{8,12},{9,13},{10,... | collective-permute-start | bytes 688136 | tf_op jit(solution)/shard_map/ppermute | solution.py:363
  34.5 5.9 %collective-permute-start.8 = (bf16[9,128,128]{2,1,0:T(8,128)(2,1)S(1)}, bf16[9,128,128]{2,1,0:T(8,128)(2,1)S(1)}, u32[]{:S(2)}, u32[]{:S(2)}) collective-permute-start(bf16[9,128,128]{2,1,0:T(8,128)(2,1)S(1)} %get-tuple-element.46), channel_id=1, source_target_pairs={{0,1},{1,0},{2,3},{3,2},{4,6},{5,7},{6,4},{7,5},{8,9},{9,8},{10,11... | collective-permute-start | bytes 884744 | tf_op jit(solution)/shard_map/ppermute | solution.py:363
  36.8 3.6 %collective-permute-start.7 = (bf16[7,128,128]{2,1,0:T(8,128)(2,1)S(1)}, bf16[7,128,128]{2,1,0:T(8,128)(2,1)S(1)}, u32[]{:S(2)}, u32[]{:S(2)}) collective-permute-start(bf16[7,128,128]{2,1,0:T(8,128)(2,1)S(1)} %right_product.13), channel_id=1, source_target_pairs={{0,4},{1,5},{2,6},{3,7},{4,0},{5,1},{6,2},{7,3},{8,12},{9,13},{10,... | collective-permute-start | bytes 688136 | tf_op jit(solution)/shard_map/ppermute | solution.py:363
  37.8 5.5 %collective-permute-start.10 = (bf16[7,128,128]{2,1,0:T(8,128)(2,1)S(1)}, bf16[7,128,128]{2,1,0:T(8,128)(2,1)S(1)}, u32[]{:S(2)}, u32[]{:S(2)}) collective-permute-start(bf16[7,128,128]{2,1,0:T(8,128)(2,1)S(1)} %second_sum.3), channel_id=1, source_target_pairs={{0,2},{1,3},{2,0},{3,1},{4,5},{5,4},{6,7},{7,6},{8,10},{9,11},{10,... | collective-permute-start | bytes 688136 | tf_op jit(solution)/shard_map/ppermute | solution.py:363
  43.4 8.1 %collective-permute-start.11 = (bf16[7,128,128]{2,1,0:T(8,128)(2,1)S(1)}, bf16[7,128,128]{2,1,0:T(8,128)(2,1)S(1)}, u32[]{:S(2)}, u32[]{:S(2)}) collective-permute-start(bf16[7,128,128]{2,1,0:T(8,128)(2,1)S(1)} %third_sum.1.one), channel_id=1, source_target_pairs={{0,8},{1,9},{2,10},{3,11},{4,20},{5,21},{6,22},{7,23},{8,0},{9,1},... | collective-permute-start | bytes 688136 | tf_op jit(solution)/shard_map/ppermute | solution.py:363
  44.7 3.4 %collective-permute-start.12 = (f32[128,128]{1,0:T(8,128)S(1)}, f32[128,128]{1,0:T(8,128)S(1)}, u32[]{:S(2)}, u32[]{:S(2)}) collective-permute-start(f32[128,128]{1,0:T(8,128)S(1)} %get-tuple-element.50), channel_id=1, source_target_pairs={{0,2},{1,3},{2,0},{3,1},{4,5},{5,4},{6,7},{7,6},{8,10},{9,11},{10,... | collective-permute-start | bytes 196616 | tf_op jit(solution)/shard_map/ppermute | solution.py:363
  51.5 6.5 %collective-permute-start.13 = (bf16[7,128,128]{2,1,0:T(8,128)(2,1)S(1)}, bf16[7,128,128]{2,1,0:T(8,128)(2,1)S(1)}, u32[]{:S(2)}, u32[]{:S(2)}) collective-permute-start(bf16[7,128,128]{2,1,0:T(8,128)(2,1)S(1)} %pair_sum.1.own), channel_id=1, source_target_pairs={{0,16},{1,17},{2,18},{3,19},{4,12},{5,13},{6,14},{7,15},{8,24},{9,... | collective-permute-start | bytes 688136 | tf_op jit(solution)/shard_map/ppermute | solution.py:363
  58.3 9.3 %collective-permute-start.14 = (bf16[7,128,128]{2,1,0:T(8,128)(2,1)S(1)}, bf16[7,128,128]{2,1,0:T(8,128)(2,1)S(1)}, u32[]{:S(2)}, u32[]{:S(2)}) collective-permute-start(bf16[7,128,128]{2,1,0:T(8,128)(2,1)S(1)} %factor.1.after.rest_0_.own), channel_id=1, source_target_pairs={{0,2},{1,3},{2,0},{3,1},{4,5},{5,4},{6,7},{7,6},{8,10},{9,11},{10,... | collective-permute-start | bytes 688136 | tf_op jit(solution)/shard_map/ppermute | solution.py:363
  60.2 9.5 %collective-permute-start.18 = (bf16[7,128,128]{2,1,0:T(8,128)(2,1)S(1)}, bf16[7,128,128]{2,1,0:T(8,128)(2,1)S(1)}, u32[]{:S(2)}, u32[]{:S(2)}) collective-permute-start(bf16[7,128,128]{2,1,0:T(8,128)(2,1)S(1)} %factor.1.after.rest_0_.own), channel_id=1, source_target_pairs={{0,1},{1,0},{2,3},{3,2},{4,6},{5,7},{6,4},{7,5},{8,9},{9,8},{10,11... | collective-permute-start | bytes 688136 | tf_op jit(solution)/shard_map/ppermute | solution.py:363
  63.1 7.3 %collective-permute-start.16 = (bf16[7,128,128]{2,1,0:T(8,128)(2,1)S(1)}, bf16[7,128,128]{2,1,0:T(8,128)(2,1)S(1)}, u32[]{:S(2)}, u32[]{:S(2)}) collective-permute-start(bf16[7,128,128]{2,1,0:T(8,128)(2,1)S(1)} %factor.1.after.rest_0_.own), channel_id=1, source_target_pairs={{0,4},{1,5},{2,6},{3,7},{4,0},{5,1},{6,2},{7,3},{8,12},{9,13},{10,... | collective-permute-start | bytes 688136 | tf_op jit(solution)/shard_map/ppermute | solution.py:363
  67.6 3.8 %collective-permute-start.17 = (bf16[7,128,128]{2,1,0:T(8,128)(2,1)S(1)}, bf16[7,128,128]{2,1,0:T(8,128)(2,1)S(1)}, u32[]{:S(2)}, u32[]{:S(2)}) collective-permute-start(bf16[7,128,128]{2,1,0:T(8,128)(2,1)S(1)} %collective-permute-done.14.rest_1_), channel_id=1, source_target_pairs={{0,4},{1,5},{2,6},{3,7},{4,0},{5,1},{6,2},{7,3},{8,12},{9,13},{10,... | collective-permute-start | bytes 688136 | tf_op jit(solution)/shard_map/ppermute | solution.py:363
  68.3 6.1 %collective-permute-start.15 = (bf16[7,128,128]{2,1,0:T(8,128)(2,1)S(1)}, bf16[7,128,128]{2,1,0:T(8,128)(2,1)S(1)}, u32[]{:S(2)}, u32[]{:S(2)}) collective-permute-start(bf16[7,128,128]{2,1,0:T(8,128)(2,1)S(1)} %collective-permute-done.14.rest_1_), channel_id=1, source_target_pairs={{0,1},{1,0},{2,3},{3,2},{4,6},{5,7},{6,4},{7,5},{8,9},{9,8},{10,11... | collective-permute-start | bytes 688136 | tf_op jit(solution)/shard_map/ppermute | solution.py:363
  69.7 4.7 %collective-permute-start.20 = (bf16[7,128,128]{2,1,0:T(8,128)(2,1)S(1)}, bf16[7,128,128]{2,1,0:T(8,128)(2,1)S(1)}, u32[]{:S(2)}, u32[]{:S(2)}) collective-permute-start(bf16[7,128,128]{2,1,0:T(8,128)(2,1)S(1)} %collective-permute-done.18.rest_0_), channel_id=1, source_target_pairs={{0,4},{1,5},{2,6},{3,7},{4,0},{5,1},{6,2},{7,3},{8,12},{9,13},{10,... | collective-permute-start | bytes 688136 | tf_op jit(solution)/shard_map/ppermute | solution.py:363
  74.4 2.4 %collective-permute-start.19 = (bf16[7,128,128]{2,1,0:T(8,128)(2,1)S(1)}, bf16[7,128,128]{2,1,0:T(8,128)(2,1)S(1)}, u32[]{:S(2)}, u32[]{:S(2)}) collective-permute-start(bf16[7,128,128]{2,1,0:T(8,128)(2,1)S(1)} %collective-permute-done.15.rest_0_), channel_id=1, source_target_pairs={{0,4},{1,5},{2,6},{3,7},{4,0},{5,1},{6,2},{7,3},{8,12},{9,13},{10,... | collective-permute-start | bytes 688136 | tf_op jit(solution)/shard_map/ppermute | solution.py:363

commit v7 on v6

--- a/solution.py
+++ b/solution.py
@@ -147,11 +147,22 @@
     )(*place, in_vmem(comp), near, far)
 
 
-def new_error_kernel(net, units, blocks, dp, mp, comp, near, far, *rest):
+def new_error_kernel(net, units, blocks, rows_too, dp, mp, comp, near, far, *rest):
     place = Place(net, (dp, mp))
-    rights, (out, buf, sems) = rest[: len(blocks)], rest[-3:]
+    rights, rest = rest[: len(blocks)], rest[len(blocks) :]
     count = comp.shape[0] // 2
     copies = []
+    if rows_too:
+        own, _, out, factor_rows, buf, sems, rows_buf, rows_sem = rest
+        for side, source in ((NEAR, own), (FAR, rights[0])):
+            start = place.half(side) * (units * LANES)
+            for i in range(units):
+                rows_buf[pl.ds(pl.multiple_of(start + i * LANES, LANES), LANES), :] = source[i].T
+        copies.append(pltpu.make_async_copy(rows_buf, factor_rows, rows_sem))
+        copies[0].start()
+    else:
+        out, buf, sems = rest[-3:]
+    step = min(128, count)
     for j, ((side, k), right) in enumerate(zip(blocks, rights)):
         start = place.block(side, k) * (units * LANES)
         for half, base in enumerate((near, far)):
@@ -160,11 +171,12 @@
                 wide = min(2, units - unit)
                 factor = [right[unit + i] for i in range(wide)]
                 factor = jnp.concatenate(factor, axis=1) if wide > 1 else factor[0]
-                product = jnp.dot(base[...], factor, preferred_element_type=F32)
                 at = pl.ds(pl.multiple_of(start + unit * LANES, LANES), wide * LANES)
-                kept = comp[half * count : (half + 1) * count, at].astype(F32)
                 here = pl.ds(unit * LANES, wide * LANES)
-                buf[half, j, :, here] = (kept - product).astype(BF16)
+                for row in range(0, count, step):
+                    product = jnp.dot(base[row : row + step], factor, preferred_element_type=F32)
+                    kept = comp[half * count + row : half * count + row + step, at].astype(F32)
+                    buf[half, j, row : row + step, here] = (kept - product).astype(BF16)
                 copy = pltpu.make_async_copy(
                     buf.at[half, j, :, here], out.at[rows, at], sems.at[half, j, unit // 2]
                 )
@@ -174,23 +186,30 @@
         copy.wait()
 
 
-def new_error(net, place, blocks, rights, units, comp, near, far, held=None):
+def new_error(net, place, blocks, rights, units, comp, near, far, held=None, own=None):
     rows, cols = comp.shape
-    extra = [] if held is None else [in_hbm(held)]
-    return call(
-        functools.partial(new_error_kernel, net, units, blocks),
+    rank = near.shape[1]
+    extra = [] if own is None else [own]
+    outs, scratch = [shaped((rows, cols), BF16)], [
+        pltpu.VMEM((2, len(blocks), rows // 2, units * LANES), BF16),
+        pltpu.SemaphoreType.DMA((2, len(blocks), (units + 1) // 2)),
+    ]
+    if own is not None:
+        outs.append(shaped((2 * units * LANES, rank), BF16))
+        scratch += [pltpu.VMEM((2 * units * LANES, rank), BF16), pltpu.SemaphoreType.DMA]
+    held = [] if held is None else [in_hbm(held)]
+    out = call(
+        functools.partial(new_error_kernel, net, units, blocks, own is not None),
         "new_error",
-        shaped((rows, cols), BF16),
-        [SMEM] * 2 + [VMEM] * (3 + len(blocks)) + [HBM] * len(extra),
+        outs,
+        [SMEM] * 2 + [VMEM] * (3 + len(blocks) + len(extra)) + [HBM] * len(held),
         12,
         0.6 + 0.8 * len(blocks),
-        out_specs=HBM,
-        scratch_shapes=[
-            pltpu.VMEM((2, len(blocks), rows // 2, units * LANES), BF16),
-            pltpu.SemaphoreType.DMA((2, len(blocks), (units + 1) // 2)),
-        ],
-        input_output_aliases={5 + len(blocks): 0} if extra else {},
-    )(*place, in_vmem(comp), near, far, *rights, *extra)
+        out_specs=[HBM] * len(outs),
+        scratch_shapes=scratch,
+        input_output_aliases={5 + len(blocks) + len(extra): 0} if held else {},
+    )(*place, in_vmem(comp), near, far, *rights, *extra, *held)
+    return out[0] if own is None else out
 
 
 def leaf_steps(state, leaf):
@@ -323,21 +342,12 @@
             out[k] = product[:, (k - i) * LANES : (k - i + 1) * LANES].astype(BF16)
 
 
-def base_kernel(near, far, state, after, near_out, far_out):
-    del after
+def base_kernel(near, far, state, near_out, far_out):
     rank = near.shape[0]
     lhs = jnp.concatenate(split2(state[:, rank:]), axis=0)
     for source, out in ((near, near_out), (far, far_out)):
         product = jnp.dot(lhs, source[...], preferred_element_type=F32)
         out[...] = (product[:rank] + product[rank:]).T.astype(BF16)
-
-
-def rows_kernel(net, units, dp, mp, own, other, out):
-    place = Place(net, (dp, mp))
-    for side, source in ((NEAR, own), (FAR, other)):
-        start = place.half(side) * (units * LANES)
-        for i in range(units):
-            out[pl.ds(pl.multiple_of(start + i * LANES, LANES), LANES), :] = source[i].T
 
 
 class Exchange:
@@ -421,31 +431,29 @@
         sent = small(add_kernel, "pair_sum", block, sent, arrived)
     arrived = net.send(sent, net.rest[-1])
     sent, gram = lax.optimization_barrier((sent, gram))
-    arrived, state = lax.optimization_barrier((arrived, inverse_of(gram)))
+    state = inverse_of(gram)
+    base_near, base_far = small(base_kernel, "base", [shaped((rows // 2, rank), BF16)] * 2, near, far, state)
+    arrived, state, base_near, base_far = lax.optimization_barrier((arrived, state, base_near, base_far))
     own = small(functools.partial(factor_kernel, dp), "factor", block, sent, arrived, state)
 
     blocks = [own, net.send(own, net.scatter[1]), net.send(own, net.scatter[0]), None]
-    base_near, base_far = small(
-        base_kernel, "base", [shaped((rows // 2, rank), BF16)] * 2, near, far, state, own
-    )
     write = functools.partial(new_error, net, place, units=units, comp=comp, near=base_near, far=base_far)
     out = write([(NEAR, 0)], [own])
     own, out = lax.optimization_barrier((own, out))
     others = [net.core(own)]
-    share, width = cols // mp, units * LANES
-    right_factor = None
-    if share == 2 * width:
-        right_factor = call(
-            functools.partial(rows_kernel, net, units), "factor_rows", shaped((share, rank), BF16),
-            [SMEM, SMEM, VMEM, VMEM], 4, 1, out_specs=VMEM,
-        )(*place, own, others[0])
     blocks[1], out = lax.optimization_barrier((blocks[1], out))
     blocks[3] = net.send(blocks[1], net.scatter[0])
     others.append(net.core(blocks[1]))
     blocks[2], out = lax.optimization_barrier((blocks[2], out))
     others.append(net.core(blocks[2]))
-    out = write([(FAR, 0), (NEAR, 1), (FAR, 1)], [others[0], blocks[1], others[1]], held=out)
-    blocks[3], out, right_factor = lax.optimization_barrier((blocks[3], out, right_factor))
+    share, width = cols // mp, units * LANES
+    right_factor = None
+    some = [(FAR, 0), (NEAR, 1), (FAR, 1)], [others[0], blocks[1], others[1]]
+    if share == 2 * width:
+        out, right_factor = write(*some, held=out, own=own)
+    else:
+        out = write(*some, held=out)
+    blocks[3], out = lax.optimization_barrier((blocks[3], out))
     others.append(net.core(blocks[3]))
     out = write([(NEAR, 2), (FAR, 2)], [blocks[2], others[2]], held=out)
     out = write([(NEAR, 3), (FAR, 3)], [blocks[3], others[3]], held=out)

time: 79.8 us -> 79 us (0.990)
  Pallas kernels: 31.4 us -> 30 us
  starting transfers between devices: 27.6 us -> 28.4 us
    pallas_call x5 -> x4, Pallas kernels: 10.2 us -> 8.87 us  [new_error(): call(functools.partial(new_error_kernel, net, units, blocks, own is not N...]
    ppermute x21, starting transfers between devices: 27.6 us -> 28.4 us  [send(): return lax.ppermute(x, AXES, pairs)]
  transfers between devices with their start and end apart: 21 -> 21, of which waited for: 9 -> 10; matrix products, arithmetic and copies ran while one was open for 0% -> 0% of each run, Pallas kernels for 21% -> 20%
where the time goes in v7:
time: 79 us; the launch traced here: 78.9 us
  Pallas kernels  30 us (38%)
  starting transfers between devices  28.4 us (36%)
  waiting for transfers between devices  19.2 us (24%)
  between operations  0.98 us (1%)
    ppermute x21, starting transfers between devices, send(): return lax.ppermute(x, AXES, pairs)  28.4 us
    ppermute x21, waiting for transfers between devices, send(): return lax.ppermute(x, AXES, pairs)  19.2 us
    pallas_call x1, Pallas kernels, left_product(): call(functools.partial(left_kernel, net, PIECES), 'left_product', [pltpu....  11.2 us
    pallas_call x4, Pallas kernels, new_error(): call(functools.partial(new_error_kernel, net, units, blocks, own is not N...  8.87 us
    pallas_call x1, Pallas kernels, inverse_of(): call(inverse_kernel, 'inverse', shaped((n, 2 * n), F32), [VMEM], 4, 4.5,...  4.86 us
    pallas_call x8, Pallas kernels, right_product(): call(functools.partial(right_kernel, net, units, side, places), 'right_pr...  3.86 us
  transfers between devices with their start and end apart: 21, of which 10 were waited for; matrix products, arithmetic and copies ran while one was open for 0% of the time, Pallas kernels for 20%

profile of v7, /device:TPU:1, one launch (start us, length us, event | category | flops | bytes accessed | tf_op | source)
XLA Modules:
  0.0 78.9 jit_solution(15176738079633626252)
XLA Ops:
  0.6 11.2 %left_product.1 = (bf16[1024,7168]{1,0:T(8,128)(2,1)S(1)}, f32[128,512]{1,0:T(8,128)S(1)}, f32[128,512]{1,0:T(8,128)S(1)}) custom-call(s32[1]{0:T(128)} %bitcast.dp, s32[1]{0:T(128)} %bitcast.1.mp, bf16[1024,7168]{1,0:T(8,128)(2,1)} %bitcast.6, bf16[1024,7168]{1,0:T(8,128)(2,1)} %bitcast.7, bf16[7168,128]{1,0:T(8,128)(2,1)} %init.1), custom_call_target="tpu_custom_call" | custom-call | bytes 42000000 | tf_op jit(solution)/shard_map/left_product/pallas_call | solution.py:106
  11.9 0.1 collective-permute-start
  12.0 1.5 %collective-permute-done = f32[128,512]{1,0:T(8,128)S(1)} collective-permute-done((f32[128,512]{1,0:T(8,128)S(1)}, f32[128,512]{1,0:T(8,128)S(1)}, u32[]{:S(2)}, u32[]{:S(2)}) %collective-permute-start) | collective-permute-done | bytes 262176 | tf_op jit(solution)/shard_map/ppermute | solution.py:373
  13.5 3.5 %collective-permute-start.1 = (bf16[128,512]{1,0:T(8,128)(2,1)S(1)}, bf16[128,512]{1,0:T(8,128)(2,1)S(1)}, u32[]{:S(2)}, u32[]{:S(2)}) collective-permute-start(bf16[128,512]{1,0:T(8,128)(2,1)S(1)} %fusion.1), channel_id=1, source_target_pairs={{0,8},{1,9},{2,10},{3,11},{4,20},{5,21},{6,22},{7,23},{8,0},{9,1},... | collective-permute-start | bytes 393224 | tf_op jit(solution)/shard_map/ppermute | solution.py:373
  17.0 3.7 %collective-permute-done.1 = bf16[128,512]{1,0:T(8,128)(2,1)S(1)} collective-permute-done((bf16[128,512]{1,0:T(8,128)(2,1)S(1)}, bf16[128,512]{1,0:T(8,128)(2,1)S(1)}, u32[]{:S(2)}, u32[]{:S(2)}) %collective-permute-start.1) | collective-permute-done | bytes 131104 | tf_op jit(solution)/shard_map/ppermute | solution.py:373
  20.7 0.1 fusion
  20.8 0.7 collective-permute-start.2
  21.5 3.4 %collective-permute-done.2 = bf16[128,512]{1,0:T(8,128)(2,1)S(1)} collective-permute-done((bf16[128,512]{1,0:T(8,128)(2,1)S(1)}, bf16[128,512]{1,0:T(8,128)(2,1)S(1)}, u32[]{:S(2)}, u32[]{:S(2)}) %collective-permute-start.2) | collective-permute-done | bytes 131104 | tf_op jit(solution)/shard_map/ppermute | solution.py:373
  25.0 0.1 add_convert_fusion.near
  25.1 1.9 %collective-permute-start.3 = (bf16[128,512]{1,0:T(8,128)(2,1)S(1)}, bf16[128,512]{1,0:T(8,128)(2,1)S(1)}, u32[]{:S(2)}, u32[]{:S(2)}) collective-permute-start(bf16[128,512]{1,0:T(8,128)(2,1)S(1)} %add_convert_fusion.near), channel_id=1, source_target_pairs={{0,4},{1,5},{2,6},{3,7},{4,0},{5,1},{6,2},{7,3},{8,12},{9,13},{10,... | collective-permute-start | bytes 393224 | tf_op jit(solution)/shard_map/ppermute | solution.py:373
  26.9 1.0 %collective-permute-done.3.far = bf16[128,512]{1,0:T(8,128)(2,1)S(1)} collective-permute-done((bf16[128,512]{1,0:T(8,128)(2,1)S(1)}, bf16[128,512]{1,0:T(8,128)(2,1)S(1)}, u32[]{:S(2)}, u32[]{:S(2)}) %collective-permute-start.3) | collective-permute-done | bytes 131104 | tf_op jit(solution)/shard_map/ppermute | solution.py:373
  27.9 0.5 right_product.9
  28.4 0.4 collective-permute-start.4
  28.9 0.5 right_product.11
  29.3 0.2 collective-permute-start.5
  29.5 0.5 right_product.8.one
  30.0 0.0 collective-permute-done.4.other
  30.0 0.1 first_sum.2
  30.1 2.4 %collective-permute-start.6 = (bf16[7,128,128]{2,1,0:T(8,128)(2,1)S(1)}, bf16[7,128,128]{2,1,0:T(8,128)(2,1)S(1)}, u32[]{:S(2)}, u32[]{:S(2)}) collective-permute-start(bf16[7,128,128]{2,1,0:T(8,128)(2,1)S(1)} %first_sum.2), channel_id=1, source_target_pairs={{0,1},{1,0},{2,3},{3,2},{4,6},{5,7},{6,4},{7,5},{8,9},{9,8},{10,11... | collective-permute-start | bytes 688136 | tf_op jit(solution)/shard_map/ppermute | solution.py:373
  32.6 0.5 right_product.10.part
  33.0 0.0 collective-permute-done.5.across
  33.0 0.2 first_sum.3
  33.3 0.5 right_product.15
  33.8 0.7 collective-permute-start.9
  34.5 1.2 %collective-permute-start.8 = (bf16[9,128,128]{2,1,0:T(8,128)(2,1)S(1)}, bf16[9,128,128]{2,1,0:T(8,128)(2,1)S(1)}, u32[]{:S(2)}, u32[]{:S(2)}) collective-permute-start(bf16[9,128,128]{2,1,0:T(8,128)(2,1)S(1)} %get-tuple-element.49), channel_id=1, source_target_pairs={{0,1},{1,0},{2,3},{3,2},{4,6},{5,7},{6,4},{7,5},{8,9},{9,8},{10,11... | collective-permute-start | bytes 884744 | tf_op jit(solution)/shard_map/ppermute | solution.py:373
  35.7 0.5 right_product.14.part
  36.2 0.0 collective-permute-done.6.arrived
  36.3 0.5 right_product.13
  36.8 1.0 %collective-permute-start.7 = (bf16[7,128,128]{2,1,0:T(8,128)(2,1)S(1)}, bf16[7,128,128]{2,1,0:T(8,128)(2,1)S(1)}, u32[]{:S(2)}, u32[]{:S(2)}) collective-permute-start(bf16[7,128,128]{2,1,0:T(8,128)(2,1)S(1)} %right_product.13), channel_id=1, source_target_pairs={{0,4},{1,5},{2,6},{3,7},{4,0},{5,1},{6,2},{7,3},{8,12},{9,13},{10,... | collective-permute-start | bytes 688136 | tf_op jit(solution)/shard_map/ppermute | solution.py:373
  37.7 0.0 collective-permute-done.9.across
  37.7 0.1 second_sum.3
  37.8 1.8 %collective-permute-start.10 = (bf16[7,128,128]{2,1,0:T(8,128)(2,1)S(1)}, bf16[7,128,128]{2,1,0:T(8,128)(2,1)S(1)}, u32[]{:S(2)}, u32[]{:S(2)}) collective-permute-start(bf16[7,128,128]{2,1,0:T(8,128)(2,1)S(1)} %second_sum.3), channel_id=1, source_target_pairs={{0,2},{1,3},{2,0},{3,1},{4,5},{5,4},{6,7},{7,6},{8,10},{9,11},{10,... | collective-permute-start | bytes 688136 | tf_op jit(solution)/shard_map/ppermute | solution.py:373
  39.6 0.5 right_product.12.part
  40.1 0.2 collective-permute-done.8.arrived
  40.3 0.0 collective-permute-done.7.across
  40.3 0.1 second_sum.2
  40.4 2.9 %collective-permute-done.10.other = bf16[7,128,128]{2,1,0:T(8,128)(2,1)S(1)} collective-permute-done((bf16[7,128,128]{2,1,0:T(8,128)(2,1)S(1)}, bf16[7,128,128]{2,1,0:T(8,128)(2,1)S(1)}, u32[]{:S(2)}, u32[]{:S(2)}) %collective-permute-start.10) | collective-permute-done | bytes 229408 | tf_op jit(solution)/shard_map/ppermute | solution.py:373
  43.4 1.3 %collective-permute-start.11 = (bf16[7,128,128]{2,1,0:T(8,128)(2,1)S(1)}, bf16[7,128,128]{2,1,0:T(8,128)(2,1)S(1)}, u32[]{:S(2)}, u32[]{:S(2)}) collective-permute-start(bf16[7,128,128]{2,1,0:T(8,128)(2,1)S(1)} %third_sum.1.one), channel_id=1, source_target_pairs={{0,8},{1,9},{2,10},{3,11},{4,20},{5,21},{6,22},{7,23},{8,0},{9,1},... | collective-permute-start | bytes 688136 | tf_op jit(solution)/shard_map/ppermute | solution.py:373
  44.7 1.2 %collective-permute-start.12 = (f32[128,128]{1,0:T(8,128)S(1)}, f32[128,128]{1,0:T(8,128)S(1)}, u32[]{:S(2)}, u32[]{:S(2)}) collective-permute-start(f32[128,128]{1,0:T(8,128)S(1)} %get-tuple-element.53), channel_id=1, source_target_pairs={{0,2},{1,3},{2,0},{3,1},{4,5},{5,4},{6,7},{7,6},{8,10},{9,11},{10,... | collective-permute-start | bytes 196616 | tf_op jit(solution)/shard_map/ppermute | solution.py:373
  45.9 2.2 %collective-permute-done.12 = f32[128,128]{1,0:T(8,128)S(1)} collective-permute-done((f32[128,128]{1,0:T(8,128)S(1)}, f32[128,128]{1,0:T(8,128)S(1)}, u32[]{:S(2)}, u32[]{:S(2)}) %collective-permute-start.12) | collective-permute-done | bytes 65568 | tf_op jit(solution)/shard_map/ppermute | solution.py:373
  48.1 3.3 %collective-permute-done.11.other = bf16[7,128,128]{2,1,0:T(8,128)(2,1)S(1)} collective-permute-done((bf16[7,128,128]{2,1,0:T(8,128)(2,1)S(1)}, bf16[7,128,128]{2,1,0:T(8,128)(2,1)S(1)}, u32[]{:S(2)}, u32[]{:S(2)}) %collective-permute-start.11) | collective-permute-done | bytes 229408 | tf_op jit(solution)/shard_map/ppermute | solution.py:373
  51.4 0.1 pair_sum.1.own
  51.5 0.8 %collective-permute-start.13 = (bf16[7,128,128]{2,1,0:T(8,128)(2,1)S(1)}, bf16[7,128,128]{2,1,0:T(8,128)(2,1)S(1)}, u32[]{:S(2)}, u32[]{:S(2)}) collective-permute-start(bf16[7,128,128]{2,1,0:T(8,128)(2,1)S(1)} %pair_sum.1.own), channel_id=1, source_target_pairs={{0,16},{1,17},{2,18},{3,19},{4,12},{5,13},{6,14},{7,15},{8,24},{9,... | collective-permute-start | bytes 688136 | tf_op jit(solution)/shard_map/ppermute | solution.py:373
  52.3 4.9 %inverse.1.state = f32[128,256]{1,0:T(8,128)S(1)} custom-call(f32[128,128]{1,0:T(8,128)S(1)} %add.15.gram), custom_call_target="tpu_custom_call" | custom-call | bytes 15750000 | tf_op jit(solution)/shard_map/inverse/pallas_call | solution.py:296
  57.2 0.3 base.1
  57.5 0.4 collective-permute-done.13.arrived
  58.0 0.3 factor.1.rest_0_.rest_3_
  58.3 1.6 %collective-permute-start.14 = (bf16[7,128,128]{2,1,0:T(8,128)(2,1)S(1)}, bf16[7,128,128]{2,1,0:T(8,128)(2,1)S(1)}, u32[]{:S(2)}, u32[]{:S(2)}) collective-permute-start(bf16[7,128,128]{2,1,0:T(8,128)(2,1)S(1)} %factor.1.rest_0_.rest_3_), channel_id=1, source_target_pairs={{0,2},{1,3},{2,0},{3,1},{4,5},{5,4},{6,7},{7,6},{8,10},{9,11},{10,... | collective-permute-start | bytes 688136 | tf_op jit(solution)/shard_map/ppermute | solution.py:373
  59.8 1.2 %collective-permute-start.18 = (bf16[7,128,128]{2,1,0:T(8,128)(2,1)S(1)}, bf16[7,128,128]{2,1,0:T(8,128)(2,1)S(1)}, u32[]{:S(2)}, u32[]{:S(2)}) collective-permute-start(bf16[7,128,128]{2,1,0:T(8,128)(2,1)S(1)} %factor.1.rest_0_.rest_3_), channel_id=1, source_target_pairs={{0,1},{1,0},{2,3},{3,2},{4,6},{5,7},{6,4},{7,5},{8,9},{9,8},{10,11... | collective-permute-start | bytes 688136 | tf_op jit(solution)/shard_map/ppermute | solution.py:373
  61.1 1.5 %new_error.4.rest_4_ = bf16[1024,7168]{1,0:T(8,128)(2,1)} custom-call(s32[1]{0:T(128)} %bitcast.dp, s32[1]{0:T(128)} %bitcast.1.mp, bf16[1024,7168]{1,0:T(8,128)(2,1)S(1)} %get-tuple-element.38.comp, bf16[512,128]{1,0:T(8,128)(2,1)S(1)} %get-tuple-element.59.near, bf16[512,128]{1,0:T(8,128)(2,1)S(1)} %get-tuple-element.60.far, ...), custom_call_target="tpu_custom_call" | custom-call | bytes 4900000 | tf_op jit(solution)/shard_map/new_error/pallas_call | solution.py:201
  62.6 4.5 %collective-permute-start.16 = (bf16[7,128,128]{2,1,0:T(8,128)(2,1)S(1)}, bf16[7,128,128]{2,1,0:T(8,128)(2,1)S(1)}, u32[]{:S(2)}, u32[]{:S(2)}) collective-permute-start(bf16[7,128,128]{2,1,0:T(8,128)(2,1)S(1)} %factor.1.rest_0_.rest_3_), channel_id=1, source_target_pairs={{0,4},{1,5},{2,6},{3,7},{4,0},{5,1},{6,2},{7,3},{8,12},{9,13},{10,... | collective-permute-start | bytes 688136 | tf_op jit(solution)/shard_map/ppermute | solution.py:373
  67.0 0.0 collective-permute-done.14.rest_1_
  67.1 1.2 %collective-permute-start.17 = (bf16[7,128,128]{2,1,0:T(8,128)(2,1)S(1)}, bf16[7,128,128]{2,1,0:T(8,128)(2,1)S(1)}, u32[]{:S(2)}, u32[]{:S(2)}) collective-permute-start(bf16[7,128,128]{2,1,0:T(8,128)(2,1)S(1)} %collective-permute-done.14.rest_1_), channel_id=1, source_target_pairs={{0,4},{1,5},{2,6},{3,7},{4,0},{5,1},{6,2},{7,3},{8,12},{9,13},{10,... | collective-permute-start | bytes 688136 | tf_op jit(solution)/shard_map/ppermute | solution.py:373
  68.3 1.4 %collective-permute-start.15 = (bf16[7,128,128]{2,1,0:T(8,128)(2,1)S(1)}, bf16[7,128,128]{2,1,0:T(8,128)(2,1)S(1)}, u32[]{:S(2)}, u32[]{:S(2)}) collective-permute-start(bf16[7,128,128]{2,1,0:T(8,128)(2,1)S(1)} %collective-permute-done.14.rest_1_), channel_id=1, source_target_pairs={{0,1},{1,0},{2,3},{3,2},{4,6},{5,7},{6,4},{7,5},{8,9},{9,8},{10,11... | collective-permute-start | bytes 688136 | tf_op jit(solution)/shard_map/ppermute | solution.py:373
  69.7 0.0 collective-permute-done.18.rest_0_
  69.7 0.3 collective-permute-start.20
  70.0 0.0 collective-permute-done.16.rest_0_
  70.0 0.0 collective-permute-done.17.rest_2_
  70.0 3.0 %new_error.5 = (bf16[1024,7168]{1,0:T(8,128)(2,1)}, bf16[1792,128]{1,0:T(8,128)(2,1)}) custom-call(s32[1]{0:T(128)} %bitcast.dp, s32[1]{0:T(128)} %bitcast.1.mp, bf16[1024,7168]{1,0:T(8,128)(2,1)S(1)} %get-tuple-element.38.comp, bf16[512,128]{1,0:T(8,128)(2,1)S(1)} %get-tuple-element.59.near, ...), custom_call_target="tpu_custom_call", output_to_operand_aliasing={{0}: (9, {})} | custom-call | bytes 10500000 | tf_op jit(solution)/shard_map/new_error/pallas_call | solution.py:201
  73.0 0.4 collective-permute-done.15.rest_0_
  73.5 0.9 %collective-permute-start.19 = (bf16[7,128,128]{2,1,0:T(8,128)(2,1)S(1)}, bf16[7,128,128]{2,1,0:T(8,128)(2,1)S(1)}, u32[]{:S(2)}, u32[]{:S(2)}) collective-permute-start(bf16[7,128,128]{2,1,0:T(8,128)(2,1)S(1)} %collective-permute-done.15.rest_0_), channel_id=1, source_target_pairs={{0,4},{1,5},{2,6},{3,7},{4,0},{5,1},{6,2},{7,3},{8,12},{9,13},{10,... | collective-permute-start | bytes 688136 | tf_op jit(solution)/shard_map/ppermute | solution.py:373
  74.3 0.0 collective-permute-done.20.rest_1_
  74.3 2.2 %new_error.6.rest_2_ = bf16[1024,7168]{1,0:T(8,128)(2,1)} custom-call(s32[1]{0:T(128)} %bitcast.dp, s32[1]{0:T(128)} %bitcast.1.mp, bf16[1024,7168]{1,0:T(8,128)(2,1)S(1)} %get-tuple-element.38.comp, bf16[512,128]{1,0:T(8,128)(2,1)S(1)} %get-tuple-element.59.near, bf16[512,128]{1,0:T(8,128)(2,1)S(1)} %get-tuple-element.60.far, ...), custom_call_target="tpu_custom_call", output_to_operand_aliasing={{}: (7, {})} | custom-call | bytes 7700000 | tf_op jit(solution)/shard_map/new_error/pallas_call | solution.py:201
  76.5 2.2 %new_error.7 = bf16[1024,7168]{1,0:T(8,128)(2,1)} custom-call(s32[1]{0:T(128)} %bitcast.dp, s32[1]{0:T(128)} %bitcast.1.mp, bf16[1024,7168]{1,0:T(8,128)(2,1)S(1)} %get-tuple-element.38.comp, bf16[512,128]{1,0:T(8,128)(2,1)S(1)} %get-tuple-element.59.near, bf16[512,128]{1,0:T(8,128)(2,1)S(1)} %get-tuple-element.60.far, ...), custom_call_target="tpu_custom_call", output_to_operand_aliasing={{}: (7, {})} | custom-call | bytes 7700000 | tf_op jit(solution)/shard_map/new_error/pallas_call | solution.py:201
  (4 shorter events, 0.1 us)
Async XLA Ops:
  11.9 1.6 %collective-permute-start = (f32[128,512]{1,0:T(8,128)S(1)}, f32[128,512]{1,0:T(8,128)S(1)}, u32[]{:S(2)}, u32[]{:S(2)}) collective-permute-start(f32[128,512]{1,0:T(8,128)S(1)} %get-tuple-element.40), channel_id=1, source_target_pairs={{0,4},{1,5},{2,6},{3,7},{4,0},{5,1},{6,2},{7,3},{8,12},{9,13},{10,... | collective-permute-start | bytes 786440 | tf_op jit(solution)/shard_map/ppermute | solution.py:373
  13.5 7.2 %collective-permute-start.1 = (bf16[128,512]{1,0:T(8,128)(2,1)S(1)}, bf16[128,512]{1,0:T(8,128)(2,1)S(1)}, u32[]{:S(2)}, u32[]{:S(2)}) collective-permute-start(bf16[128,512]{1,0:T(8,128)(2,1)S(1)} %fusion.1), channel_id=1, source_target_pairs={{0,8},{1,9},{2,10},{3,11},{4,20},{5,21},{6,22},{7,23},{8,0},{9,1},... | collective-permute-start | bytes 393224 | tf_op jit(solution)/shard_map/ppermute | solution.py:373
  20.8 4.2 %collective-permute-start.2 = (bf16[128,512]{1,0:T(8,128)(2,1)S(1)}, bf16[128,512]{1,0:T(8,128)(2,1)S(1)}, u32[]{:S(2)}, u32[]{:S(2)}) collective-permute-start(bf16[128,512]{1,0:T(8,128)(2,1)S(1)} %fusion), channel_id=1, source_target_pairs={{0,16},{1,17},{2,18},{3,19},{4,12},{5,13},{6,14},{7,15},{8,24},{9,... | collective-permute-start | bytes 393224 | tf_op jit(solution)/shard_map/ppermute | solution.py:373
  25.1 2.8 %collective-permute-start.3 = (bf16[128,512]{1,0:T(8,128)(2,1)S(1)}, bf16[128,512]{1,0:T(8,128)(2,1)S(1)}, u32[]{:S(2)}, u32[]{:S(2)}) collective-permute-start(bf16[128,512]{1,0:T(8,128)(2,1)S(1)} %add_convert_fusion.near), channel_id=1, source_target_pairs={{0,4},{1,5},{2,6},{3,7},{4,0},{5,1},{6,2},{7,3},{8,12},{9,13},{10,... | collective-permute-start | bytes 393224 | tf_op jit(solution)/shard_map/ppermute | solution.py:373
  28.4 1.6 %collective-permute-start.4 = (bf16[7,128,128]{2,1,0:T(8,128)(2,1)S(1)}, bf16[7,128,128]{2,1,0:T(8,128)(2,1)S(1)}, u32[]{:S(2)}, u32[]{:S(2)}) collective-permute-start(bf16[7,128,128]{2,1,0:T(8,128)(2,1)S(1)} %right_product.9), channel_id=1, source_target_pairs={{0,4},{1,5},{2,6},{3,7},{4,0},{5,1},{6,2},{7,3},{8,12},{9,13},{10,... | collective-permute-start | bytes 688136 | tf_op jit(solution)/shard_map/ppermute | solution.py:373
  29.3 3.7 %collective-permute-start.5 = (bf16[7,128,128]{2,1,0:T(8,128)(2,1)S(1)}, bf16[7,128,128]{2,1,0:T(8,128)(2,1)S(1)}, u32[]{:S(2)}, u32[]{:S(2)}) collective-permute-start(bf16[7,128,128]{2,1,0:T(8,128)(2,1)S(1)} %right_product.11), channel_id=1, source_target_pairs={{0,4},{1,5},{2,6},{3,7},{4,0},{5,1},{6,2},{7,3},{8,12},{9,13},{10,... | collective-permute-start | bytes 688136 | tf_op jit(solution)/shard_map/ppermute | solution.py:373
  30.1 6.2 %collective-permute-start.6 = (bf16[7,128,128]{2,1,0:T(8,128)(2,1)S(1)}, bf16[7,128,128]{2,1,0:T(8,128)(2,1)S(1)}, u32[]{:S(2)}, u32[]{:S(2)}) collective-permute-start(bf16[7,128,128]{2,1,0:T(8,128)(2,1)S(1)} %first_sum.2), channel_id=1, source_target_pairs={{0,1},{1,0},{2,3},{3,2},{4,6},{5,7},{6,4},{7,5},{8,9},{9,8},{10,11... | collective-permute-start | bytes 688136 | tf_op jit(solution)/shard_map/ppermute | solution.py:373
  33.8 3.9 %collective-permute-start.9 = (bf16[7,128,128]{2,1,0:T(8,128)(2,1)S(1)}, bf16[7,128,128]{2,1,0:T(8,128)(2,1)S(1)}, u32[]{:S(2)}, u32[]{:S(2)}) collective-permute-start(bf16[7,128,128]{2,1,0:T(8,128)(2,1)S(1)} %right_product.15), channel_id=1, source_target_pairs={{0,4},{1,5},{2,6},{3,7},{4,0},{5,1},{6,2},{7,3},{8,12},{9,13},{10,... | collective-permute-start | bytes 688136 | tf_op jit(solution)/shard_map/ppermute | solution.py:373
  34.5 5.9 %collective-permute-start.8 = (bf16[9,128,128]{2,1,0:T(8,128)(2,1)S(1)}, bf16[9,128,128]{2,1,0:T(8,128)(2,1)S(1)}, u32[]{:S(2)}, u32[]{:S(2)}) collective-permute-start(bf16[9,128,128]{2,1,0:T(8,128)(2,1)S(1)} %get-tuple-element.49), channel_id=1, source_target_pairs={{0,1},{1,0},{2,3},{3,2},{4,6},{5,7},{6,4},{7,5},{8,9},{9,8},{10,11... | collective-permute-start | bytes 884744 | tf_op jit(solution)/shard_map/ppermute | solution.py:373
  36.8 3.6 %collective-permute-start.7 = (bf16[7,128,128]{2,1,0:T(8,128)(2,1)S(1)}, bf16[7,128,128]{2,1,0:T(8,128)(2,1)S(1)}, u32[]{:S(2)}, u32[]{:S(2)}) collective-permute-start(bf16[7,128,128]{2,1,0:T(8,128)(2,1)S(1)} %right_product.13), channel_id=1, source_target_pairs={{0,4},{1,5},{2,6},{3,7},{4,0},{5,1},{6,2},{7,3},{8,12},{9,13},{10,... | collective-permute-start | bytes 688136 | tf_op jit(solution)/shard_map/ppermute | solution.py:373
  37.8 5.5 %collective-permute-start.10 = (bf16[7,128,128]{2,1,0:T(8,128)(2,1)S(1)}, bf16[7,128,128]{2,1,0:T(8,128)(2,1)S(1)}, u32[]{:S(2)}, u32[]{:S(2)}) collective-permute-start(bf16[7,128,128]{2,1,0:T(8,128)(2,1)S(1)} %second_sum.3), channel_id=1, source_target_pairs={{0,2},{1,3},{2,0},{3,1},{4,5},{5,4},{6,7},{7,6},{8,10},{9,11},{10,... | collective-permute-start | bytes 688136 | tf_op jit(solution)/shard_map/ppermute | solution.py:373
  43.4 8.1 %collective-permute-start.11 = (bf16[7,128,128]{2,1,0:T(8,128)(2,1)S(1)}, bf16[7,128,128]{2,1,0:T(8,128)(2,1)S(1)}, u32[]{:S(2)}, u32[]{:S(2)}) collective-permute-start(bf16[7,128,128]{2,1,0:T(8,128)(2,1)S(1)} %third_sum.1.one), channel_id=1, source_target_pairs={{0,8},{1,9},{2,10},{3,11},{4,20},{5,21},{6,22},{7,23},{8,0},{9,1},... | collective-permute-start | bytes 688136 | tf_op jit(solution)/shard_map/ppermute | solution.py:373
  44.7 3.4 %collective-permute-start.12 = (f32[128,128]{1,0:T(8,128)S(1)}, f32[128,128]{1,0:T(8,128)S(1)}, u32[]{:S(2)}, u32[]{:S(2)}) collective-permute-start(f32[128,128]{1,0:T(8,128)S(1)} %get-tuple-element.53), channel_id=1, source_target_pairs={{0,2},{1,3},{2,0},{3,1},{4,5},{5,4},{6,7},{7,6},{8,10},{9,11},{10,... | collective-permute-start | bytes 196616 | tf_op jit(solution)/shard_map/ppermute | solution.py:373
  51.5 6.5 %collective-permute-start.13 = (bf16[7,128,128]{2,1,0:T(8,128)(2,1)S(1)}, bf16[7,128,128]{2,1,0:T(8,128)(2,1)S(1)}, u32[]{:S(2)}, u32[]{:S(2)}) collective-permute-start(bf16[7,128,128]{2,1,0:T(8,128)(2,1)S(1)} %pair_sum.1.own), channel_id=1, source_target_pairs={{0,16},{1,17},{2,18},{3,19},{4,12},{5,13},{6,14},{7,15},{8,24},{9,... | collective-permute-start | bytes 688136 | tf_op jit(solution)/shard_map/ppermute | solution.py:373
  58.3 8.8 %collective-permute-start.14 = (bf16[7,128,128]{2,1,0:T(8,128)(2,1)S(1)}, bf16[7,128,128]{2,1,0:T(8,128)(2,1)S(1)}, u32[]{:S(2)}, u32[]{:S(2)}) collective-permute-start(bf16[7,128,128]{2,1,0:T(8,128)(2,1)S(1)} %factor.1.rest_0_.rest_3_), channel_id=1, source_target_pairs={{0,2},{1,3},{2,0},{3,1},{4,5},{5,4},{6,7},{7,6},{8,10},{9,11},{10,... | collective-permute-start | bytes 688136 | tf_op jit(solution)/shard_map/ppermute | solution.py:373
  59.8 9.9 %collective-permute-start.18 = (bf16[7,128,128]{2,1,0:T(8,128)(2,1)S(1)}, bf16[7,128,128]{2,1,0:T(8,128)(2,1)S(1)}, u32[]{:S(2)}, u32[]{:S(2)}) collective-permute-start(bf16[7,128,128]{2,1,0:T(8,128)(2,1)S(1)} %factor.1.rest_0_.rest_3_), channel_id=1, source_target_pairs={{0,1},{1,0},{2,3},{3,2},{4,6},{5,7},{6,4},{7,5},{8,9},{9,8},{10,11... | collective-permute-start | bytes 688136 | tf_op jit(solution)/shard_map/ppermute | solution.py:373
  62.6 7.4 %collective-permute-start.16 = (bf16[7,128,128]{2,1,0:T(8,128)(2,1)S(1)}, bf16[7,128,128]{2,1,0:T(8,128)(2,1)S(1)}, u32[]{:S(2)}, u32[]{:S(2)}) collective-permute-start(bf16[7,128,128]{2,1,0:T(8,128)(2,1)S(1)} %factor.1.rest_0_.rest_3_), channel_id=1, source_target_pairs={{0,4},{1,5},{2,6},{3,7},{4,0},{5,1},{6,2},{7,3},{8,12},{9,13},{10,... | collective-permute-start | bytes 688136 | tf_op jit(solution)/shard_map/ppermute | solution.py:373
  67.1 2.9 %collective-permute-start.17 = (bf16[7,128,128]{2,1,0:T(8,128)(2,1)S(1)}, bf16[7,128,128]{2,1,0:T(8,128)(2,1)S(1)}, u32[]{:S(2)}, u32[]{:S(2)}) collective-permute-start(bf16[7,128,128]{2,1,0:T(8,128)(2,1)S(1)} %collective-permute-done.14.rest_1_), channel_id=1, source_target_pairs={{0,4},{1,5},{2,6},{3,7},{4,0},{5,1},{6,2},{7,3},{8,12},{9,13},{10,... | collective-permute-start | bytes 688136 | tf_op jit(solution)/shard_map/ppermute | solution.py:373
  68.3 5.2 %collective-permute-start.15 = (bf16[7,128,128]{2,1,0:T(8,128)(2,1)S(1)}, bf16[7,128,128]{2,1,0:T(8,128)(2,1)S(1)}, u32[]{:S(2)}, u32[]{:S(2)}) collective-permute-start(bf16[7,128,128]{2,1,0:T(8,128)(2,1)S(1)} %collective-permute-done.14.rest_1_), channel_id=1, source_target_pairs={{0,1},{1,0},{2,3},{3,2},{4,6},{5,7},{6,4},{7,5},{8,9},{9,8},{10,11... | collective-permute-start | bytes 688136 | tf_op jit(solution)/shard_map/ppermute | solution.py:373
  69.7 4.6 %collective-permute-start.20 = (bf16[7,128,128]{2,1,0:T(8,128)(2,1)S(1)}, bf16[7,128,128]{2,1,0:T(8,128)(2,1)S(1)}, u32[]{:S(2)}, u32[]{:S(2)}) collective-permute-start(bf16[7,128,128]{2,1,0:T(8,128)(2,1)S(1)} %collective-permute-done.18.rest_0_), channel_id=1, source_target_pairs={{0,4},{1,5},{2,6},{3,7},{4,0},{5,1},{6,2},{7,3},{8,12},{9,13},{10,... | collective-permute-start | bytes 688136 | tf_op jit(solution)/shard_map/ppermute | solution.py:373
  73.5 3.0 %collective-permute-start.19 = (bf16[7,128,128]{2,1,0:T(8,128)(2,1)S(1)}, bf16[7,128,128]{2,1,0:T(8,128)(2,1)S(1)}, u32[]{:S(2)}, u32[]{:S(2)}) collective-permute-start(bf16[7,128,128]{2,1,0:T(8,128)(2,1)S(1)} %collective-permute-done.15.rest_0_), channel_id=1, source_target_pairs={{0,4},{1,5},{2,6},{3,7},{4,0},{5,1},{6,2},{7,3},{8,12},{9,13},{10,... | collective-permute-start | bytes 688136 | tf_op jit(solution)/shard_map/ppermute | solution.py:373

commit v8 on v7

--- a/solution.py
+++ b/solution.py
@@ -153,8 +153,8 @@
     count = comp.shape[0] // 2
     copies = []
     if rows_too:
-        own, _, out, factor_rows, buf, sems, rows_buf, rows_sem = rest
-        for side, source in ((NEAR, own), (FAR, rights[0])):
+        own, other, _, out, factor_rows, buf, sems, rows_buf, rows_sem = rest
+        for side, source in ((NEAR, own), (FAR, other)):
             start = place.half(side) * (units * LANES)
             for i in range(units):
                 rows_buf[pl.ds(pl.multiple_of(start + i * LANES, LANES), LANES), :] = source[i].T
@@ -186,30 +186,29 @@
         copy.wait()
 
 
-def new_error(net, place, blocks, rights, units, comp, near, far, held=None, own=None):
+def new_error(net, place, blocks, rights, units, comp, near, far, held=None, block_0=()):
     rows, cols = comp.shape
     rank = near.shape[1]
-    extra = [] if own is None else [own]
     outs, scratch = [shaped((rows, cols), BF16)], [
         pltpu.VMEM((2, len(blocks), rows // 2, units * LANES), BF16),
         pltpu.SemaphoreType.DMA((2, len(blocks), (units + 1) // 2)),
     ]
-    if own is not None:
+    if block_0:
         outs.append(shaped((2 * units * LANES, rank), BF16))
         scratch += [pltpu.VMEM((2 * units * LANES, rank), BF16), pltpu.SemaphoreType.DMA]
     held = [] if held is None else [in_hbm(held)]
     out = call(
-        functools.partial(new_error_kernel, net, units, blocks, own is not None),
+        functools.partial(new_error_kernel, net, units, blocks, len(block_0)),
         "new_error",
         outs,
-        [SMEM] * 2 + [VMEM] * (3 + len(blocks) + len(extra)) + [HBM] * len(held),
+        [SMEM] * 2 + [VMEM] * (3 + len(blocks) + len(block_0)) + [HBM] * len(held),
         12,
         0.6 + 0.8 * len(blocks),
         out_specs=[HBM] * len(outs),
         scratch_shapes=scratch,
-        input_output_aliases={5 + len(blocks) + len(extra): 0} if held else {},
-    )(*place, in_vmem(comp), near, far, *rights, *extra, *held)
-    return out[0] if own is None else out
+        input_output_aliases={5 + len(blocks) + len(block_0): 0} if held else {},
+    )(*place, in_vmem(comp), near, far, *rights, *block_0, *held)
+    return out if block_0 else out[0]
 
 
 def leaf_steps(state, leaf):
@@ -448,15 +447,15 @@
     others.append(net.core(blocks[2]))
     share, width = cols // mp, units * LANES
     right_factor = None
-    some = [(FAR, 0), (NEAR, 1), (FAR, 1)], [others[0], blocks[1], others[1]]
+    some = [(FAR, 0), (NEAR, 1), (FAR, 1), (NEAR, 2)], [others[0], blocks[1], others[1], blocks[2]]
     if share == 2 * width:
-        out, right_factor = write(*some, held=out, own=own)
+        out, right_factor = write(*some, held=out, block_0=(own, others[0]))
     else:
         out = write(*some, held=out)
     blocks[3], out = lax.optimization_barrier((blocks[3], out))
     others.append(net.core(blocks[3]))
-    out = write([(NEAR, 2), (FAR, 2)], [blocks[2], others[2]], held=out)
-    out = write([(NEAR, 3), (FAR, 3)], [blocks[3], others[3]], held=out)
+    out = write([(FAR, 2), (NEAR, 3)], [others[2], blocks[3]], held=out)
+    out = write([(FAR, 3)], [others[3]], held=out)
     if right_factor is None:
         everything = jnp.concatenate(blocks + others, axis=0)
         here = Place(net, place)

time: 79 us -> 78.3 us (level)
  transfers between devices with their start and end apart: 21 -> 21, of which waited for: 10 -> 9; matrix products, arithmetic and copies ran while one was open for 0% -> 0% of each run, Pallas kernels for 20% -> 21%
where the time goes in v8:
time: 78.3 us; the launch traced here: 78.2 us
  Pallas kernels  30 us (38%)
  starting transfers between devices  28.2 us (36%)
  waiting for transfers between devices  18.8 us (24%)
  between operations  0.99 us (1%)
    ppermute x21, starting transfers between devices, send(): return lax.ppermute(x, AXES, pairs)  28.2 us
    ppermute x21, waiting for transfers between devices, send(): return lax.ppermute(x, AXES, pairs)  18.8 us
    pallas_call x1, Pallas kernels, left_product(): call(functools.partial(left_kernel, net, PIECES), 'left_product', [pltpu....  11.2 us
    pallas_call x4, Pallas kernels, new_error(): call(functools.partial(new_error_kernel, net, units, blocks, len(block_0)...  8.82 us
    pallas_call x1, Pallas kernels, inverse_of(): call(inverse_kernel, 'inverse', shaped((n, 2 * n), F32), [VMEM], 4, 4.5,...  4.86 us
    pallas_call x8, Pallas kernels, right_product(): call(functools.partial(right_kernel, net, units, side, places), 'right_pr...  3.86 us
  transfers between devices with their start and end apart: 21, of which 9 were waited for; matrix products, arithmetic and copies ran while one was open for 0% of the time, Pallas kernels for 21%

profile of v8, /device:TPU:1, one launch (start us, length us, event | category | flops | bytes accessed | tf_op | source)
XLA Modules:
  0.0 78.2 jit_solution(11735749302640105870)
XLA Ops:
  0.6 11.2 %left_product.1 = (bf16[1024,7168]{1,0:T(8,128)(2,1)S(1)}, f32[128,512]{1,0:T(8,128)S(1)}, f32[128,512]{1,0:T(8,128)S(1)}) custom-call(s32[1]{0:T(128)} %bitcast.dp, s32[1]{0:T(128)} %bitcast.1.mp, bf16[1024,7168]{1,0:T(8,128)(2,1)} %bitcast.6, bf16[1024,7168]{1,0:T(8,128)(2,1)} %bitcast.7, bf16[7168,128]{1,0:T(8,128)(2,1)} %init.1), custom_call_target="tpu_custom_call" | custom-call | bytes 42000000 | tf_op jit(solution)/shard_map/left_product/pallas_call | solution.py:106
  11.9 0.1 collective-permute-start
  12.0 1.5 %collective-permute-done = f32[128,512]{1,0:T(8,128)S(1)} collective-permute-done((f32[128,512]{1,0:T(8,128)S(1)}, f32[128,512]{1,0:T(8,128)S(1)}, u32[]{:S(2)}, u32[]{:S(2)}) %collective-permute-start) | collective-permute-done | bytes 262176 | tf_op jit(solution)/shard_map/ppermute | solution.py:372
  13.5 3.5 %collective-permute-start.1 = (bf16[128,512]{1,0:T(8,128)(2,1)S(1)}, bf16[128,512]{1,0:T(8,128)(2,1)S(1)}, u32[]{:S(2)}, u32[]{:S(2)}) collective-permute-start(bf16[128,512]{1,0:T(8,128)(2,1)S(1)} %fusion.1), channel_id=1, source_target_pairs={{0,8},{1,9},{2,10},{3,11},{4,20},{5,21},{6,22},{7,23},{8,0},{9,1},... | collective-permute-start | bytes 393224 | tf_op jit(solution)/shard_map/ppermute | solution.py:372
  17.0 3.7 %collective-permute-done.1 = bf16[128,512]{1,0:T(8,128)(2,1)S(1)} collective-permute-done((bf16[128,512]{1,0:T(8,128)(2,1)S(1)}, bf16[128,512]{1,0:T(8,128)(2,1)S(1)}, u32[]{:S(2)}, u32[]{:S(2)}) %collective-permute-start.1) | collective-permute-done | bytes 131104 | tf_op jit(solution)/shard_map/ppermute | solution.py:372
  20.7 0.1 fusion
  20.8 0.7 collective-permute-start.2
  21.5 3.4 %collective-permute-done.2 = bf16[128,512]{1,0:T(8,128)(2,1)S(1)} collective-permute-done((bf16[128,512]{1,0:T(8,128)(2,1)S(1)}, bf16[128,512]{1,0:T(8,128)(2,1)S(1)}, u32[]{:S(2)}, u32[]{:S(2)}) %collective-permute-start.2) | collective-permute-done | bytes 131104 | tf_op jit(solution)/shard_map/ppermute | solution.py:372
  25.0 0.1 add_convert_fusion.near
  25.1 1.9 %collective-permute-start.3 = (bf16[128,512]{1,0:T(8,128)(2,1)S(1)}, bf16[128,512]{1,0:T(8,128)(2,1)S(1)}, u32[]{:S(2)}, u32[]{:S(2)}) collective-permute-start(bf16[128,512]{1,0:T(8,128)(2,1)S(1)} %add_convert_fusion.near), channel_id=1, source_target_pairs={{0,4},{1,5},{2,6},{3,7},{4,0},{5,1},{6,2},{7,3},{8,12},{9,13},{10,... | collective-permute-start | bytes 393224 | tf_op jit(solution)/shard_map/ppermute | solution.py:372
  26.9 1.0 %collective-permute-done.3.far = bf16[128,512]{1,0:T(8,128)(2,1)S(1)} collective-permute-done((bf16[128,512]{1,0:T(8,128)(2,1)S(1)}, bf16[128,512]{1,0:T(8,128)(2,1)S(1)}, u32[]{:S(2)}, u32[]{:S(2)}) %collective-permute-start.3) | collective-permute-done | bytes 131104 | tf_op jit(solution)/shard_map/ppermute | solution.py:372
  27.9 0.5 right_product.9
  28.4 0.4 collective-permute-start.4
  28.9 0.5 right_product.11
  29.3 0.2 collective-permute-start.5
  29.5 0.5 right_product.8.one
  30.0 0.0 collective-permute-done.4.other
  30.0 0.1 first_sum.2
  30.1 2.4 %collective-permute-start.6 = (bf16[7,128,128]{2,1,0:T(8,128)(2,1)S(1)}, bf16[7,128,128]{2,1,0:T(8,128)(2,1)S(1)}, u32[]{:S(2)}, u32[]{:S(2)}) collective-permute-start(bf16[7,128,128]{2,1,0:T(8,128)(2,1)S(1)} %first_sum.2), channel_id=1, source_target_pairs={{0,1},{1,0},{2,3},{3,2},{4,6},{5,7},{6,4},{7,5},{8,9},{9,8},{10,11... | collective-permute-start | bytes 688136 | tf_op jit(solution)/shard_map/ppermute | solution.py:372
  32.6 0.5 right_product.10.part
  33.0 0.0 collective-permute-done.5.across
  33.0 0.2 first_sum.3
  33.3 0.5 right_product.15
  33.8 0.7 collective-permute-start.9
  34.5 1.2 %collective-permute-start.8 = (bf16[9,128,128]{2,1,0:T(8,128)(2,1)S(1)}, bf16[9,128,128]{2,1,0:T(8,128)(2,1)S(1)}, u32[]{:S(2)}, u32[]{:S(2)}) collective-permute-start(bf16[9,128,128]{2,1,0:T(8,128)(2,1)S(1)} %get-tuple-element.49), channel_id=1, source_target_pairs={{0,1},{1,0},{2,3},{3,2},{4,6},{5,7},{6,4},{7,5},{8,9},{9,8},{10,11... | collective-permute-start | bytes 884744 | tf_op jit(solution)/shard_map/ppermute | solution.py:372
  35.7 0.5 right_product.14.part
  36.2 0.0 collective-permute-done.6.arrived
  36.3 0.5 right_product.13
  36.8 1.0 %collective-permute-start.7 = (bf16[7,128,128]{2,1,0:T(8,128)(2,1)S(1)}, bf16[7,128,128]{2,1,0:T(8,128)(2,1)S(1)}, u32[]{:S(2)}, u32[]{:S(2)}) collective-permute-start(bf16[7,128,128]{2,1,0:T(8,128)(2,1)S(1)} %right_product.13), channel_id=1, source_target_pairs={{0,4},{1,5},{2,6},{3,7},{4,0},{5,1},{6,2},{7,3},{8,12},{9,13},{10,... | collective-permute-start | bytes 688136 | tf_op jit(solution)/shard_map/ppermute | solution.py:372
  37.7 0.0 collective-permute-done.9.across
  37.7 0.1 second_sum.3
  37.8 1.8 %collective-permute-start.10 = (bf16[7,128,128]{2,1,0:T(8,128)(2,1)S(1)}, bf16[7,128,128]{2,1,0:T(8,128)(2,1)S(1)}, u32[]{:S(2)}, u32[]{:S(2)}) collective-permute-start(bf16[7,128,128]{2,1,0:T(8,128)(2,1)S(1)} %second_sum.3), channel_id=1, source_target_pairs={{0,2},{1,3},{2,0},{3,1},{4,5},{5,4},{6,7},{7,6},{8,10},{9,11},{10,... | collective-permute-start | bytes 688136 | tf_op jit(solution)/shard_map/ppermute | solution.py:372
  39.6 0.5 right_product.12.part
  40.1 0.2 collective-permute-done.8.arrived
  40.3 0.0 collective-permute-done.7.across
  40.3 0.1 second_sum.2
  40.4 2.9 %collective-permute-done.10.other = bf16[7,128,128]{2,1,0:T(8,128)(2,1)S(1)} collective-permute-done((bf16[7,128,128]{2,1,0:T(8,128)(2,1)S(1)}, bf16[7,128,128]{2,1,0:T(8,128)(2,1)S(1)}, u32[]{:S(2)}, u32[]{:S(2)}) %collective-permute-start.10) | collective-permute-done | bytes 229408 | tf_op jit(solution)/shard_map/ppermute | solution.py:372
  43.4 1.3 %collective-permute-start.11 = (bf16[7,128,128]{2,1,0:T(8,128)(2,1)S(1)}, bf16[7,128,128]{2,1,0:T(8,128)(2,1)S(1)}, u32[]{:S(2)}, u32[]{:S(2)}) collective-permute-start(bf16[7,128,128]{2,1,0:T(8,128)(2,1)S(1)} %third_sum.1.one), channel_id=1, source_target_pairs={{0,8},{1,9},{2,10},{3,11},{4,20},{5,21},{6,22},{7,23},{8,0},{9,1},... | collective-permute-start | bytes 688136 | tf_op jit(solution)/shard_map/ppermute | solution.py:372
  44.7 1.2 %collective-permute-start.12 = (f32[128,128]{1,0:T(8,128)S(1)}, f32[128,128]{1,0:T(8,128)S(1)}, u32[]{:S(2)}, u32[]{:S(2)}) collective-permute-start(f32[128,128]{1,0:T(8,128)S(1)} %get-tuple-element.53), channel_id=1, source_target_pairs={{0,2},{1,3},{2,0},{3,1},{4,5},{5,4},{6,7},{7,6},{8,10},{9,11},{10,... | collective-permute-start | bytes 196616 | tf_op jit(solution)/shard_map/ppermute | solution.py:372
  45.9 2.2 %collective-permute-done.12 = f32[128,128]{1,0:T(8,128)S(1)} collective-permute-done((f32[128,128]{1,0:T(8,128)S(1)}, f32[128,128]{1,0:T(8,128)S(1)}, u32[]{:S(2)}, u32[]{:S(2)}) %collective-permute-start.12) | collective-permute-done | bytes 65568 | tf_op jit(solution)/shard_map/ppermute | solution.py:372
  48.1 3.3 %collective-permute-done.11.other = bf16[7,128,128]{2,1,0:T(8,128)(2,1)S(1)} collective-permute-done((bf16[7,128,128]{2,1,0:T(8,128)(2,1)S(1)}, bf16[7,128,128]{2,1,0:T(8,128)(2,1)S(1)}, u32[]{:S(2)}, u32[]{:S(2)}) %collective-permute-start.11) | collective-permute-done | bytes 229408 | tf_op jit(solution)/shard_map/ppermute | solution.py:372
  51.4 0.1 pair_sum.1.own
  51.5 0.8 %collective-permute-start.13 = (bf16[7,128,128]{2,1,0:T(8,128)(2,1)S(1)}, bf16[7,128,128]{2,1,0:T(8,128)(2,1)S(1)}, u32[]{:S(2)}, u32[]{:S(2)}) collective-permute-start(bf16[7,128,128]{2,1,0:T(8,128)(2,1)S(1)} %pair_sum.1.own), channel_id=1, source_target_pairs={{0,16},{1,17},{2,18},{3,19},{4,12},{5,13},{6,14},{7,15},{8,24},{9,... | collective-permute-start | bytes 688136 | tf_op jit(solution)/shard_map/ppermute | solution.py:372
  52.3 4.9 %inverse.1.state = f32[128,256]{1,0:T(8,128)S(1)} custom-call(f32[128,128]{1,0:T(8,128)S(1)} %add.15.gram), custom_call_target="tpu_custom_call" | custom-call | bytes 15750000 | tf_op jit(solution)/shard_map/inverse/pallas_call | solution.py:295
  57.2 0.3 base.1
  57.5 0.4 collective-permute-done.13.arrived
  58.0 0.3 factor.1.rest_0_.rest_4_
  58.3 1.6 %collective-permute-start.14 = (bf16[7,128,128]{2,1,0:T(8,128)(2,1)S(1)}, bf16[7,128,128]{2,1,0:T(8,128)(2,1)S(1)}, u32[]{:S(2)}, u32[]{:S(2)}) collective-permute-start(bf16[7,128,128]{2,1,0:T(8,128)(2,1)S(1)} %factor.1.rest_0_.rest_4_), channel_id=1, source_target_pairs={{0,2},{1,3},{2,0},{3,1},{4,5},{5,4},{6,7},{7,6},{8,10},{9,11},{10,... | collective-permute-start | bytes 688136 | tf_op jit(solution)/shard_map/ppermute | solution.py:372
  59.8 1.2 %collective-permute-start.18 = (bf16[7,128,128]{2,1,0:T(8,128)(2,1)S(1)}, bf16[7,128,128]{2,1,0:T(8,128)(2,1)S(1)}, u32[]{:S(2)}, u32[]{:S(2)}) collective-permute-start(bf16[7,128,128]{2,1,0:T(8,128)(2,1)S(1)} %factor.1.rest_0_.rest_4_), channel_id=1, source_target_pairs={{0,1},{1,0},{2,3},{3,2},{4,6},{5,7},{6,4},{7,5},{8,9},{9,8},{10,11... | collective-permute-start | bytes 688136 | tf_op jit(solution)/shard_map/ppermute | solution.py:372
  61.1 1.5 %new_error.4.rest_6_ = bf16[1024,7168]{1,0:T(8,128)(2,1)} custom-call(s32[1]{0:T(128)} %bitcast.dp, s32[1]{0:T(128)} %bitcast.1.mp, bf16[1024,7168]{1,0:T(8,128)(2,1)S(1)} %get-tuple-element.38.comp, bf16[512,128]{1,0:T(8,128)(2,1)S(1)} %get-tuple-element.59.near, bf16[512,128]{1,0:T(8,128)(2,1)S(1)} %get-tuple-element.60.far, ...), custom_call_target="tpu_custom_call" | custom-call | bytes 4900000 | tf_op jit(solution)/shard_map/new_error/pallas_call | solution.py:200
  62.6 4.5 %collective-permute-start.16 = (bf16[7,128,128]{2,1,0:T(8,128)(2,1)S(1)}, bf16[7,128,128]{2,1,0:T(8,128)(2,1)S(1)}, u32[]{:S(2)}, u32[]{:S(2)}) collective-permute-start(bf16[7,128,128]{2,1,0:T(8,128)(2,1)S(1)} %factor.1.rest_0_.rest_4_), channel_id=1, source_target_pairs={{0,4},{1,5},{2,6},{3,7},{4,0},{5,1},{6,2},{7,3},{8,12},{9,13},{10,... | collective-permute-start | bytes 688136 | tf_op jit(solution)/shard_map/ppermute | solution.py:372
  67.0 0.0 collective-permute-done.14.rest_1_
  67.1 1.2 %collective-permute-start.17 = (bf16[7,128,128]{2,1,0:T(8,128)(2,1)S(1)}, bf16[7,128,128]{2,1,0:T(8,128)(2,1)S(1)}, u32[]{:S(2)}, u32[]{:S(2)}) collective-permute-start(bf16[7,128,128]{2,1,0:T(8,128)(2,1)S(1)} %collective-permute-done.14.rest_1_), channel_id=1, source_target_pairs={{0,4},{1,5},{2,6},{3,7},{4,0},{5,1},{6,2},{7,3},{8,12},{9,13},{10,... | collective-permute-start | bytes 688136 | tf_op jit(solution)/shard_map/ppermute | solution.py:372
  68.3 1.4 %collective-permute-start.15 = (bf16[7,128,128]{2,1,0:T(8,128)(2,1)S(1)}, bf16[7,128,128]{2,1,0:T(8,128)(2,1)S(1)}, u32[]{:S(2)}, u32[]{:S(2)}) collective-permute-start(bf16[7,128,128]{2,1,0:T(8,128)(2,1)S(1)} %collective-permute-done.14.rest_1_), channel_id=1, source_target_pairs={{0,1},{1,0},{2,3},{3,2},{4,6},{5,7},{6,4},{7,5},{8,9},{9,8},{10,11... | collective-permute-start | bytes 688136 | tf_op jit(solution)/shard_map/ppermute | solution.py:372
  69.7 0.0 collective-permute-done.18.rest_3_
  69.7 0.3 collective-permute-start.20
  70.0 0.0 collective-permute-done.16.rest_0_.rest_5_
  70.0 0.0 collective-permute-done.17.rest_2_
  70.0 3.6 %new_error.5 = (bf16[1024,7168]{1,0:T(8,128)(2,1)}, bf16[1792,128]{1,0:T(8,128)(2,1)}) custom-call(s32[1]{0:T(128)} %bitcast.dp, s32[1]{0:T(128)} %bitcast.1.mp, bf16[1024,7168]{1,0:T(8,128)(2,1)S(1)} %get-tuple-element.38.comp, bf16[512,128]{1,0:T(8,128)(2,1)S(1)} %get-tuple-element.59.near, ...), custom_call_target="tpu_custom_call", output_to_operand_aliasing={{0}: (11, {})} | custom-call | bytes 13300000 | tf_op jit(solution)/shard_map/new_error/pallas_call | solution.py:200
  73.7 0.7 collective-permute-start.19
  74.3 0.0 collective-permute-done.20.rest_0_
  74.3 2.2 %new_error.6.rest_1_ = bf16[1024,7168]{1,0:T(8,128)(2,1)} custom-call(s32[1]{0:T(128)} %bitcast.dp, s32[1]{0:T(128)} %bitcast.1.mp, bf16[1024,7168]{1,0:T(8,128)(2,1)S(1)} %get-tuple-element.38.comp, bf16[512,128]{1,0:T(8,128)(2,1)S(1)} %get-tuple-element.59.near, bf16[512,128]{1,0:T(8,128)(2,1)S(1)} %get-tuple-element.60.far, ...), custom_call_target="tpu_custom_call", output_to_operand_aliasing={{}: (7, {})} | custom-call | bytes 7700000 | tf_op jit(solution)/shard_map/new_error/pallas_call | solution.py:200
  76.5 0.0 collective-permute-done.19.rest_0_
  76.5 1.5 %new_error.7 = bf16[1024,7168]{1,0:T(8,128)(2,1)} custom-call(s32[1]{0:T(128)} %bitcast.dp, s32[1]{0:T(128)} %bitcast.1.mp, bf16[1024,7168]{1,0:T(8,128)(2,1)S(1)} %get-tuple-element.38.comp, bf16[512,128]{1,0:T(8,128)(2,1)S(1)} %get-tuple-element.59.near, bf16[512,128]{1,0:T(8,128)(2,1)S(1)} %get-tuple-element.60.far, ...), custom_call_target="tpu_custom_call", output_to_operand_aliasing={{}: (6, {})} | custom-call | bytes 4900000 | tf_op jit(solution)/shard_map/new_error/pallas_call | solution.py:200
  (4 shorter events, 0.1 us)
Async XLA Ops:
  11.9 1.6 %collective-permute-start = (f32[128,512]{1,0:T(8,128)S(1)}, f32[128,512]{1,0:T(8,128)S(1)}, u32[]{:S(2)}, u32[]{:S(2)}) collective-permute-start(f32[128,512]{1,0:T(8,128)S(1)} %get-tuple-element.40), channel_id=1, source_target_pairs={{0,4},{1,5},{2,6},{3,7},{4,0},{5,1},{6,2},{7,3},{8,12},{9,13},{10,... | collective-permute-start | bytes 786440 | tf_op jit(solution)/shard_map/ppermute | solution.py:372
  13.5 7.2 %collective-permute-start.1 = (bf16[128,512]{1,0:T(8,128)(2,1)S(1)}, bf16[128,512]{1,0:T(8,128)(2,1)S(1)}, u32[]{:S(2)}, u32[]{:S(2)}) collective-permute-start(bf16[128,512]{1,0:T(8,128)(2,1)S(1)} %fusion.1), channel_id=1, source_target_pairs={{0,8},{1,9},{2,10},{3,11},{4,20},{5,21},{6,22},{7,23},{8,0},{9,1},... | collective-permute-start | bytes 393224 | tf_op jit(solution)/shard_map/ppermute | solution.py:372
  20.8 4.2 %collective-permute-start.2 = (bf16[128,512]{1,0:T(8,128)(2,1)S(1)}, bf16[128,512]{1,0:T(8,128)(2,1)S(1)}, u32[]{:S(2)}, u32[]{:S(2)}) collective-permute-start(bf16[128,512]{1,0:T(8,128)(2,1)S(1)} %fusion), channel_id=1, source_target_pairs={{0,16},{1,17},{2,18},{3,19},{4,12},{5,13},{6,14},{7,15},{8,24},{9,... | collective-permute-start | bytes 393224 | tf_op jit(solution)/shard_map/ppermute | solution.py:372
  25.1 2.8 %collective-permute-start.3 = (bf16[128,512]{1,0:T(8,128)(2,1)S(1)}, bf16[128,512]{1,0:T(8,128)(2,1)S(1)}, u32[]{:S(2)}, u32[]{:S(2)}) collective-permute-start(bf16[128,512]{1,0:T(8,128)(2,1)S(1)} %add_convert_fusion.near), channel_id=1, source_target_pairs={{0,4},{1,5},{2,6},{3,7},{4,0},{5,1},{6,2},{7,3},{8,12},{9,13},{10,... | collective-permute-start | bytes 393224 | tf_op jit(solution)/shard_map/ppermute | solution.py:372
  28.4 1.6 %collective-permute-start.4 = (bf16[7,128,128]{2,1,0:T(8,128)(2,1)S(1)}, bf16[7,128,128]{2,1,0:T(8,128)(2,1)S(1)}, u32[]{:S(2)}, u32[]{:S(2)}) collective-permute-start(bf16[7,128,128]{2,1,0:T(8,128)(2,1)S(1)} %right_product.9), channel_id=1, source_target_pairs={{0,4},{1,5},{2,6},{3,7},{4,0},{5,1},{6,2},{7,3},{8,12},{9,13},{10,... | collective-permute-start | bytes 688136 | tf_op jit(solution)/shard_map/ppermute | solution.py:372
  29.3 3.7 %collective-permute-start.5 = (bf16[7,128,128]{2,1,0:T(8,128)(2,1)S(1)}, bf16[7,128,128]{2,1,0:T(8,128)(2,1)S(1)}, u32[]{:S(2)}, u32[]{:S(2)}) collective-permute-start(bf16[7,128,128]{2,1,0:T(8,128)(2,1)S(1)} %right_product.11), channel_id=1, source_target_pairs={{0,4},{1,5},{2,6},{3,7},{4,0},{5,1},{6,2},{7,3},{8,12},{9,13},{10,... | collective-permute-start | bytes 688136 | tf_op jit(solution)/shard_map/ppermute | solution.py:372
  30.1 6.2 %collective-permute-start.6 = (bf16[7,128,128]{2,1,0:T(8,128)(2,1)S(1)}, bf16[7,128,128]{2,1,0:T(8,128)(2,1)S(1)}, u32[]{:S(2)}, u32[]{:S(2)}) collective-permute-start(bf16[7,128,128]{2,1,0:T(8,128)(2,1)S(1)} %first_sum.2), channel_id=1, source_target_pairs={{0,1},{1,0},{2,3},{3,2},{4,6},{5,7},{6,4},{7,5},{8,9},{9,8},{10,11... | collective-permute-start | bytes 688136 | tf_op jit(solution)/shard_map/ppermute | solution.py:372
  33.8 3.9 %collective-permute-start.9 = (bf16[7,128,128]{2,1,0:T(8,128)(2,1)S(1)}, bf16[7,128,128]{2,1,0:T(8,128)(2,1)S(1)}, u32[]{:S(2)}, u32[]{:S(2)}) collective-permute-start(bf16[7,128,128]{2,1,0:T(8,128)(2,1)S(1)} %right_product.15), channel_id=1, source_target_pairs={{0,4},{1,5},{2,6},{3,7},{4,0},{5,1},{6,2},{7,3},{8,12},{9,13},{10,... | collective-permute-start | bytes 688136 | tf_op jit(solution)/shard_map/ppermute | solution.py:372
  34.5 5.9 %collective-permute-start.8 = (bf16[9,128,128]{2,1,0:T(8,128)(2,1)S(1)}, bf16[9,128,128]{2,1,0:T(8,128)(2,1)S(1)}, u32[]{:S(2)}, u32[]{:S(2)}) collective-permute-start(bf16[9,128,128]{2,1,0:T(8,128)(2,1)S(1)} %get-tuple-element.49), channel_id=1, source_target_pairs={{0,1},{1,0},{2,3},{3,2},{4,6},{5,7},{6,4},{7,5},{8,9},{9,8},{10,11... | collective-permute-start | bytes 884744 | tf_op jit(solution)/shard_map/ppermute | solution.py:372
  36.8 3.6 %collective-permute-start.7 = (bf16[7,128,128]{2,1,0:T(8,128)(2,1)S(1)}, bf16[7,128,128]{2,1,0:T(8,128)(2,1)S(1)}, u32[]{:S(2)}, u32[]{:S(2)}) collective-permute-start(bf16[7,128,128]{2,1,0:T(8,128)(2,1)S(1)} %right_product.13), channel_id=1, source_target_pairs={{0,4},{1,5},{2,6},{3,7},{4,0},{5,1},{6,2},{7,3},{8,12},{9,13},{10,... | collective-permute-start | bytes 688136 | tf_op jit(solution)/shard_map/ppermute | solution.py:372
  37.8 5.5 %collective-permute-start.10 = (bf16[7,128,128]{2,1,0:T(8,128)(2,1)S(1)}, bf16[7,128,128]{2,1,0:T(8,128)(2,1)S(1)}, u32[]{:S(2)}, u32[]{:S(2)}) collective-permute-start(bf16[7,128,128]{2,1,0:T(8,128)(2,1)S(1)} %second_sum.3), channel_id=1, source_target_pairs={{0,2},{1,3},{2,0},{3,1},{4,5},{5,4},{6,7},{7,6},{8,10},{9,11},{10,... | collective-permute-start | bytes 688136 | tf_op jit(solution)/shard_map/ppermute | solution.py:372
  43.4 8.1 %collective-permute-start.11 = (bf16[7,128,128]{2,1,0:T(8,128)(2,1)S(1)}, bf16[7,128,128]{2,1,0:T(8,128)(2,1)S(1)}, u32[]{:S(2)}, u32[]{:S(2)}) collective-permute-start(bf16[7,128,128]{2,1,0:T(8,128)(2,1)S(1)} %third_sum.1.one), channel_id=1, source_target_pairs={{0,8},{1,9},{2,10},{3,11},{4,20},{5,21},{6,22},{7,23},{8,0},{9,1},... | collective-permute-start | bytes 688136 | tf_op jit(solution)/shard_map/ppermute | solution.py:372
  44.7 3.4 %collective-permute-start.12 = (f32[128,128]{1,0:T(8,128)S(1)}, f32[128,128]{1,0:T(8,128)S(1)}, u32[]{:S(2)}, u32[]{:S(2)}) collective-permute-start(f32[128,128]{1,0:T(8,128)S(1)} %get-tuple-element.53), channel_id=1, source_target_pairs={{0,2},{1,3},{2,0},{3,1},{4,5},{5,4},{6,7},{7,6},{8,10},{9,11},{10,... | collective-permute-start | bytes 196616 | tf_op jit(solution)/shard_map/ppermute | solution.py:372
  51.5 6.5 %collective-permute-start.13 = (bf16[7,128,128]{2,1,0:T(8,128)(2,1)S(1)}, bf16[7,128,128]{2,1,0:T(8,128)(2,1)S(1)}, u32[]{:S(2)}, u32[]{:S(2)}) collective-permute-start(bf16[7,128,128]{2,1,0:T(8,128)(2,1)S(1)} %pair_sum.1.own), channel_id=1, source_target_pairs={{0,16},{1,17},{2,18},{3,19},{4,12},{5,13},{6,14},{7,15},{8,24},{9,... | collective-permute-start | bytes 688136 | tf_op jit(solution)/shard_map/ppermute | solution.py:372
  58.3 8.8 %collective-permute-start.14 = (bf16[7,128,128]{2,1,0:T(8,128)(2,1)S(1)}, bf16[7,128,128]{2,1,0:T(8,128)(2,1)S(1)}, u32[]{:S(2)}, u32[]{:S(2)}) collective-permute-start(bf16[7,128,128]{2,1,0:T(8,128)(2,1)S(1)} %factor.1.rest_0_.rest_4_), channel_id=1, source_target_pairs={{0,2},{1,3},{2,0},{3,1},{4,5},{5,4},{6,7},{7,6},{8,10},{9,11},{10,... | collective-permute-start | bytes 688136 | tf_op jit(solution)/shard_map/ppermute | solution.py:372
  59.8 9.9 %collective-permute-start.18 = (bf16[7,128,128]{2,1,0:T(8,128)(2,1)S(1)}, bf16[7,128,128]{2,1,0:T(8,128)(2,1)S(1)}, u32[]{:S(2)}, u32[]{:S(2)}) collective-permute-start(bf16[7,128,128]{2,1,0:T(8,128)(2,1)S(1)} %factor.1.rest_0_.rest_4_), channel_id=1, source_target_pairs={{0,1},{1,0},{2,3},{3,2},{4,6},{5,7},{6,4},{7,5},{8,9},{9,8},{10,11... | collective-permute-start | bytes 688136 | tf_op jit(solution)/shard_map/ppermute | solution.py:372
  62.6 7.4 %collective-permute-start.16 = (bf16[7,128,128]{2,1,0:T(8,128)(2,1)S(1)}, bf16[7,128,128]{2,1,0:T(8,128)(2,1)S(1)}, u32[]{:S(2)}, u32[]{:S(2)}) collective-permute-start(bf16[7,128,128]{2,1,0:T(8,128)(2,1)S(1)} %factor.1.rest_0_.rest_4_), channel_id=1, source_target_pairs={{0,4},{1,5},{2,6},{3,7},{4,0},{5,1},{6,2},{7,3},{8,12},{9,13},{10,... | collective-permute-start | bytes 688136 | tf_op jit(solution)/shard_map/ppermute | solution.py:372
  67.1 2.9 %collective-permute-start.17 = (bf16[7,128,128]{2,1,0:T(8,128)(2,1)S(1)}, bf16[7,128,128]{2,1,0:T(8,128)(2,1)S(1)}, u32[]{:S(2)}, u32[]{:S(2)}) collective-permute-start(bf16[7,128,128]{2,1,0:T(8,128)(2,1)S(1)} %collective-permute-done.14.rest_1_), channel_id=1, source_target_pairs={{0,4},{1,5},{2,6},{3,7},{4,0},{5,1},{6,2},{7,3},{8,12},{9,13},{10,... | collective-permute-start | bytes 688136 | tf_op jit(solution)/shard_map/ppermute | solution.py:372
  68.3 5.4 %collective-permute-start.15 = (bf16[7,128,128]{2,1,0:T(8,128)(2,1)S(1)}, bf16[7,128,128]{2,1,0:T(8,128)(2,1)S(1)}, u32[]{:S(2)}, u32[]{:S(2)}) collective-permute-start(bf16[7,128,128]{2,1,0:T(8,128)(2,1)S(1)} %collective-permute-done.14.rest_1_), channel_id=1, source_target_pairs={{0,1},{1,0},{2,3},{3,2},{4,6},{5,7},{6,4},{7,5},{8,9},{9,8},{10,11... | collective-permute-start | bytes 688136 | tf_op jit(solution)/shard_map/ppermute | solution.py:372
  69.7 4.6 %collective-permute-start.20 = (bf16[7,128,128]{2,1,0:T(8,128)(2,1)S(1)}, bf16[7,128,128]{2,1,0:T(8,128)(2,1)S(1)}, u32[]{:S(2)}, u32[]{:S(2)}) collective-permute-start(bf16[7,128,128]{2,1,0:T(8,128)(2,1)S(1)} %collective-permute-done.18.rest_3_), channel_id=1, source_target_pairs={{0,4},{1,5},{2,6},{3,7},{4,0},{5,1},{6,2},{7,3},{8,12},{9,13},{10,... | collective-permute-start | bytes 688136 | tf_op jit(solution)/shard_map/ppermute | solution.py:372
  73.7 2.8 %collective-permute-start.19 = (bf16[7,128,128]{2,1,0:T(8,128)(2,1)S(1)}, bf16[7,128,128]{2,1,0:T(8,128)(2,1)S(1)}, u32[]{:S(2)}, u32[]{:S(2)}) collective-permute-start(bf16[7,128,128]{2,1,0:T(8,128)(2,1)S(1)} %collective-permute-done.15.rest_1_), channel_id=1, source_target_pairs={{0,4},{1,5},{2,6},{3,7},{4,0},{5,1},{6,2},{7,3},{8,12},{9,13},{10,... | collective-permute-start | bytes 688136 | tf_op jit(solution)/shard_map/ppermute | solution.py:372

commit v9 on v8

--- a/solution.py
+++ b/solution.py
@@ -300,15 +300,10 @@
     return high, (x - high.astype(F32)).astype(BF16)
 
 
-def first_kernel(part, across, near, far, out, gram):
-    units = part.shape[0]
+def gram_kernel(near, far, gram):
     contract = (((1,), (1,)), ((), ()))
     total = lax.dot_general(near[...], near[...], contract, preferred_element_type=F32)
-    total += lax.dot_general(far[...], far[...], contract, preferred_element_type=F32)
-    out[units], out[units + 1] = split2(total)
-    gram[...] = out[units].astype(F32) + out[units + 1].astype(F32)
-    for i in range(units):
-        out[i] = (part[i] + across[i].astype(F32)).astype(BF16)
+    gram[...] = total + lax.dot_general(far[...], far[...], contract, preferred_element_type=F32)
 
 
 def second_kernel(part, across, arrived, out):
@@ -316,10 +311,8 @@
         out[i] = (part[i] + across[i].astype(F32) + arrived[i].astype(F32)).astype(BF16)
 
 
-def kept_kernel(part, across, arrived, gram_in, out, gram):
-    units = out.shape[0]
-    gram[...] = gram_in[...] + (arrived[units].astype(F32) + arrived[units + 1].astype(F32))
-    for i in range(units):
+def kept_kernel(part, across, arrived, out):
+    for i in range(out.shape[0]):
         out[i] = part[i] + across[i].astype(F32) + arrived[i].astype(F32)
 
 
@@ -328,25 +321,19 @@
         out[i] = (one[i].astype(F32) + other[i].astype(F32)).astype(BF16)
 
 
-def factor_kernel(replicas, own, arrived, state, out):
-    units, rank = own.shape[:2]
-    lhs = jnp.concatenate(split2(state[:, rank:]), axis=0)
-    for i in range(0, units, 2):
-        some = range(i, min(i + 2, units))
-        summed = [(own[k].astype(F32) + arrived[k].astype(F32)).astype(BF16) for k in some]
-        summed = jnp.concatenate(summed, axis=1) if len(summed) > 1 else summed[0]
-        product = jnp.dot(lhs, summed, preferred_element_type=F32)
-        product = (product[:rank] + product[rank:]) / replicas
-        for k in some:
-            out[k] = product[:, (k - i) * LANES : (k - i + 1) * LANES].astype(BF16)
-
-
-def base_kernel(near, far, state, near_out, far_out):
+def factor_kernel(replicas, one, other, out):
+    for i in range(out.shape[0]):
+        out[i] = ((one[i].astype(F32) + other[i].astype(F32)) / replicas).astype(BF16)
+
+
+def base_kernel(near, far, state, near_out, far_out, near_rows, far_rows):
     rank = near.shape[0]
     lhs = jnp.concatenate(split2(state[:, rank:]), axis=0)
-    for source, out in ((near, near_out), (far, far_out)):
+    for source, out, rows in ((near, near_out, near_rows), (far, far_out, far_rows)):
         product = jnp.dot(lhs, source[...], preferred_element_type=F32)
-        out[...] = (product[:rank] + product[rank:]).T.astype(BF16)
+        product = product[:rank] + product[rank:]
+        out[...] = product.astype(BF16)
+        rows[...] = product.T.astype(BF16)
 
 
 class Exchange:
@@ -355,9 +342,10 @@
         mp_bits = [("mp", 1 << k) for k in range(mp.bit_length() - 1)]
         z_bits = [("dp", 2 << k) for k in range(dp.bit_length() - 2)]
         low, high = mp_bits[0], mp_bits[len(mp_bits) // 2]
-        self.other = [bit for bit in mp_bits if bit not in (low, high)]
+        other = [bit for bit in mp_bits if bit not in (low, high)]
+        self.mp_bits = mp_bits
         self.scatter = [(low, high), (high, low)]
-        rest = self.other + z_bits
+        rest = other + z_bits
         self.rest = list(zip(rest, rest[::-1]))
         self.replicas = list(zip(z_bits, z_bits[::-1]))
         self.low, self.high = low, high
@@ -392,22 +380,27 @@
     near = near.astype(BF16)
     far = net.core(near)
 
+    def small(kernel, name, outs, *ins):
+        return call(kernel, name, outs, [VMEM] * len(ins), 4, 0.3, out_specs=jax.tree.map(lambda _: VMEM, outs))(*ins)
+
+    gram = small(gram_kernel, "gram", shaped((rank, rank), F32), near, far)
+    for bit in net.mp_bits:
+        gram = gram + net.send(gram, (bit, bit))
+    near, far, base_near, base_far = small(
+        base_kernel, "base", [shaped((rank, rows // 2), BF16)] * 2 + [shaped((rows // 2, rank), BF16)] * 2,
+        near, far, inverse_of(gram),
+    )
+
     def right(side, places, dtype):
         return right_product(net, place, side, places, units, comp, near, far, dtype)
 
-    def small(kernel, name, outs, *ins):
-        return call(kernel, name, outs, [VMEM] * len(ins), 4, 0.3, out_specs=jax.tree.map(lambda _: VMEM, outs))(*ins)
-
-    block, square_f32 = shaped((units, *square), BF16), shaped((rank, rank), F32)
+    block = shaped((units, *square), BF16)
     across_3 = net.core(right(FAR, (3,), BF16))
     across_2 = net.core(right(FAR, (2,), BF16))
     sent = small(add_kernel, "first_sum", block, right(NEAR, (3,), F32), across_3)
     near, far, sent = lax.optimization_barrier((near, far, sent))
     arrived_1 = net.send(sent, net.scatter[0])
-    sent, gram = small(
-        first_kernel, "first_sum", [shaped((units + 2, *square), BF16), square_f32],
-        right(NEAR, (2,), F32), across_2, near, far,
-    )
+    sent = small(add_kernel, "first_sum", block, right(NEAR, (2,), F32), across_2)
     near, far, sent = lax.optimization_barrier((near, far, sent))
     arrived_0 = net.send(sent, net.scatter[0])
     across = net.core(right(FAR, (1,), BF16))
@@ -417,23 +410,13 @@
     across = net.core(right(FAR, (0,), BF16))
     part = right(NEAR, (0,), F32)
     arrived = net.send(sent, net.scatter[1])
-    kept, gram = small(
-        kept_kernel, "second_sum", [shaped((units, *square), F32), square_f32], part, across, arrived_0, gram
-    )
-    gram = gram + net.send(gram, net.scatter[1])
-    for bit in net.other:
-        gram = gram + net.send(gram, (bit, bit))
+    kept = small(kept_kernel, "second_sum", shaped((units, *square), F32), part, across, arrived_0)
     sent = small(add_kernel, "third_sum", block, kept, arrived)
 
     for step in net.rest[:-1]:
-        arrived, gram = lax.optimization_barrier((net.send(sent, step), gram))
-        sent = small(add_kernel, "pair_sum", block, sent, arrived)
+        sent = small(add_kernel, "pair_sum", block, sent, net.send(sent, step))
     arrived = net.send(sent, net.rest[-1])
-    sent, gram = lax.optimization_barrier((sent, gram))
-    state = inverse_of(gram)
-    base_near, base_far = small(base_kernel, "base", [shaped((rows // 2, rank), BF16)] * 2, near, far, state)
-    arrived, state, base_near, base_far = lax.optimization_barrier((arrived, state, base_near, base_far))
-    own = small(functools.partial(factor_kernel, dp), "factor", block, sent, arrived, state)
+    own = small(functools.partial(factor_kernel, dp), "factor", block, sent, arrived)
 
     blocks = [own, net.send(own, net.scatter[1]), net.send(own, net.scatter[0]), None]
     write = functools.partial(new_error, net, place, units=units, comp=comp, near=base_near, far=base_far)

time: 78.3 us -> 92 us (1.17)
  waiting for transfers between devices: 18.8 us -> 29.5 us
  starting transfers between devices: 28.2 us -> 31.6 us
    ppermute x21 -> x22, waiting for transfers between devices: 18.8 us -> 29.5 us  [send(): return lax.ppermute(x, AXES, pairs)]
    ppermute x21 -> x22, starting transfers between devices: 28.2 us -> 31.6 us  [send(): return lax.ppermute(x, AXES, pairs)]
  transfers between devices with their start and end apart: 21 -> 22, of which waited for: 9 -> 9; matrix products, arithmetic and copies ran while one was open for 0% -> 0% of each run, Pallas kernels for 21% -> 12%
where the time goes in v9:
time: 92 us; the launch traced here: 91.9 us
  starting transfers between devices  31.6 us (34%)
  Pallas kernels  29.6 us (32%)
  waiting for transfers between devices  29.5 us (32%)
  between operations  0.99 us (1%)
    ppermute x22, starting transfers between devices, send(): return lax.ppermute(x, AXES, pairs)  31.6 us
    ppermute x22, waiting for transfers between devices, send(): return lax.ppermute(x, AXES, pairs)  29.5 us
    pallas_call x1, Pallas kernels, left_product(): call(functools.partial(left_kernel, net, PIECES), 'left_product', [pltpu....  11.2 us
    pallas_call x4, Pallas kernels, new_error(): call(functools.partial(new_error_kernel, net, units, blocks, len(block_0)...  8.83 us
    pallas_call x1, Pallas kernels, inverse_of(): call(inverse_kernel, 'inverse', shaped((n, 2 * n), F32), [VMEM], 4, 4.5,...  4.67 us
    pallas_call x8, Pallas kernels, right_product(): call(functools.partial(right_kernel, net, units, side, places), 'right_pr...  3.88 us
  transfers between devices with their start and end apart: 22, of which 9 were waited for; matrix products, arithmetic and copies ran while one was open for 0% of the time, Pallas kernels for 12%

profile of v9, /device:TPU:1, one launch (start us, length us, event | category | flops | bytes accessed | tf_op | source)
XLA Modules:
  0.0 91.9 jit_solution(17797210518131782467)
XLA Ops:
  0.6 11.2 %left_product.1 = (bf16[1024,7168]{1,0:T(8,128)(2,1)S(1)}, f32[128,512]{1,0:T(8,128)S(1)}, f32[128,512]{1,0:T(8,128)S(1)}) custom-call(s32[1]{0:T(128)} %bitcast.dp, s32[1]{0:T(128)} %bitcast.1.mp, bf16[1024,7168]{1,0:T(8,128)(2,1)} %bitcast.6, bf16[1024,7168]{1,0:T(8,128)(2,1)} %bitcast.7, bf16[7168,128]{1,0:T(8,128)(2,1)} %init.1), custom_call_target="tpu_custom_call" | custom-call | bytes 42000000 | tf_op jit(solution)/shard_map/left_product/pallas_call | solution.py:106
  11.9 0.1 collective-permute-start
  12.0 1.5 %collective-permute-done = f32[128,512]{1,0:T(8,128)S(1)} collective-permute-done((f32[128,512]{1,0:T(8,128)S(1)}, f32[128,512]{1,0:T(8,128)S(1)}, u32[]{:S(2)}, u32[]{:S(2)}) %collective-permute-start) | collective-permute-done | bytes 262176 | tf_op jit(solution)/shard_map/ppermute | solution.py:360
  13.5 3.5 %collective-permute-start.1 = (bf16[128,512]{1,0:T(8,128)(2,1)S(1)}, bf16[128,512]{1,0:T(8,128)(2,1)S(1)}, u32[]{:S(2)}, u32[]{:S(2)}) collective-permute-start(bf16[128,512]{1,0:T(8,128)(2,1)S(1)} %fusion.1), channel_id=1, source_target_pairs={{0,8},{1,9},{2,10},{3,11},{4,20},{5,21},{6,22},{7,23},{8,0},{9,1},... | collective-permute-start | bytes 393224 | tf_op jit(solution)/shard_map/ppermute | solution.py:360
  17.0 3.7 %collective-permute-done.1 = bf16[128,512]{1,0:T(8,128)(2,1)S(1)} collective-permute-done((bf16[128,512]{1,0:T(8,128)(2,1)S(1)}, bf16[128,512]{1,0:T(8,128)(2,1)S(1)}, u32[]{:S(2)}, u32[]{:S(2)}) %collective-permute-start.1) | collective-permute-done | bytes 131104 | tf_op jit(solution)/shard_map/ppermute | solution.py:360
  20.7 0.1 fusion
  20.8 0.7 collective-permute-start.2
  21.5 3.4 %collective-permute-done.2 = bf16[128,512]{1,0:T(8,128)(2,1)S(1)} collective-permute-done((bf16[128,512]{1,0:T(8,128)(2,1)S(1)}, bf16[128,512]{1,0:T(8,128)(2,1)S(1)}, u32[]{:S(2)}, u32[]{:S(2)}) %collective-permute-start.2) | collective-permute-done | bytes 131104 | tf_op jit(solution)/shard_map/ppermute | solution.py:360
  25.0 0.1 add_convert_fusion.near
  25.1 1.9 %collective-permute-start.3 = (bf16[128,512]{1,0:T(8,128)(2,1)S(1)}, bf16[128,512]{1,0:T(8,128)(2,1)S(1)}, u32[]{:S(2)}, u32[]{:S(2)}) collective-permute-start(bf16[128,512]{1,0:T(8,128)(2,1)S(1)} %add_convert_fusion.near), channel_id=1, source_target_pairs={{0,4},{1,5},{2,6},{3,7},{4,0},{5,1},{6,2},{7,3},{8,12},{9,13},{10,... | collective-permute-start | bytes 393224 | tf_op jit(solution)/shard_map/ppermute | solution.py:360
  26.9 1.0 %collective-permute-done.3.far = bf16[128,512]{1,0:T(8,128)(2,1)S(1)} collective-permute-done((bf16[128,512]{1,0:T(8,128)(2,1)S(1)}, bf16[128,512]{1,0:T(8,128)(2,1)S(1)}, u32[]{:S(2)}, u32[]{:S(2)}) %collective-permute-start.3) | collective-permute-done | bytes 131104 | tf_op jit(solution)/shard_map/ppermute | solution.py:360
  27.9 0.2 gram.1
  28.1 2.4 %collective-permute-start.4 = (f32[128,128]{1,0:T(8,128)S(1)}, f32[128,128]{1,0:T(8,128)S(1)}, u32[]{:S(2)}, u32[]{:S(2)}) collective-permute-start(f32[128,128]{1,0:T(8,128)S(1)} %gram.1), channel_id=1, source_target_pairs={{0,1},{1,0},{2,3},{3,2},{4,5},{5,4},{6,7},{7,6},{8,9},{9,8},{10,11... | collective-permute-start | bytes 196616 | tf_op jit(solution)/shard_map/ppermute | solution.py:360
  30.6 2.2 %collective-permute-done.4 = f32[128,128]{1,0:T(8,128)S(1)} collective-permute-done((f32[128,128]{1,0:T(8,128)S(1)}, f32[128,128]{1,0:T(8,128)S(1)}, u32[]{:S(2)}, u32[]{:S(2)}) %collective-permute-start.4) | collective-permute-done | bytes 65568 | tf_op jit(solution)/shard_map/ppermute | solution.py:360
  32.7 1.0 %collective-permute-start.5 = (f32[128,128]{1,0:T(8,128)S(1)}, f32[128,128]{1,0:T(8,128)S(1)}, u32[]{:S(2)}, u32[]{:S(2)}) collective-permute-start(f32[128,128]{1,0:T(8,128)S(1)} %add.18), channel_id=1, source_target_pairs={{0,2},{1,3},{2,0},{3,1},{4,6},{5,7},{6,4},{7,5},{8,10},{9,11},{10,... | collective-permute-start | bytes 196616 | tf_op jit(solution)/shard_map/ppermute | solution.py:360
  33.8 2.1 %collective-permute-done.5 = f32[128,128]{1,0:T(8,128)S(1)} collective-permute-done((f32[128,128]{1,0:T(8,128)S(1)}, f32[128,128]{1,0:T(8,128)S(1)}, u32[]{:S(2)}, u32[]{:S(2)}) %collective-permute-start.5) | collective-permute-done | bytes 65568 | tf_op jit(solution)/shard_map/ppermute | solution.py:360
  35.9 4.7 %inverse.1.state = f32[128,256]{1,0:T(8,128)S(1)} custom-call(f32[128,128]{1,0:T(8,128)S(1)} %add.19.gram), custom_call_target="tpu_custom_call" | custom-call | bytes 15750000 | tf_op jit(solution)/shard_map/inverse/pallas_call | solution.py:295
  40.6 0.4 base.1
  41.0 0.5 right_product.9
  41.5 2.1 %collective-permute-start.6 = (bf16[7,128,128]{2,1,0:T(8,128)(2,1)S(1)}, bf16[7,128,128]{2,1,0:T(8,128)(2,1)S(1)}, u32[]{:S(2)}, u32[]{:S(2)}) collective-permute-start(bf16[7,128,128]{2,1,0:T(8,128)(2,1)S(1)} %right_product.9), channel_id=1, source_target_pairs={{0,4},{1,5},{2,6},{3,7},{4,0},{5,1},{6,2},{7,3},{8,12},{9,13},{10,... | collective-permute-start | bytes 688136 | tf_op jit(solution)/shard_map/ppermute | solution.py:360
  43.5 0.5 right_product.11
  44.0 0.1 collective-permute-start.7
  44.1 0.5 right_product.8.one
  44.6 0.0 collective-permute-done.6.other
  44.7 1.7 %collective-permute-start.8 = (bf16[7,128,128]{2,1,0:T(8,128)(2,1)S(1)}, bf16[7,128,128]{2,1,0:T(8,128)(2,1)S(1)}, u32[]{:S(2)}, u32[]{:S(2)}) collective-permute-start(bf16[7,128,128]{2,1,0:T(8,128)(2,1)S(1)} %first_sum.2), channel_id=1, source_target_pairs={{0,1},{1,0},{2,3},{3,2},{4,6},{5,7},{6,4},{7,5},{8,9},{9,8},{10,11... | collective-permute-start | bytes 688136 | tf_op jit(solution)/shard_map/ppermute | solution.py:360
  46.4 0.5 right_product.10.one
  47.0 0.5 right_product.15
  47.4 0.9 %collective-permute-start.11 = (bf16[7,128,128]{2,1,0:T(8,128)(2,1)S(1)}, bf16[7,128,128]{2,1,0:T(8,128)(2,1)S(1)}, u32[]{:S(2)}, u32[]{:S(2)}) collective-permute-start(bf16[7,128,128]{2,1,0:T(8,128)(2,1)S(1)} %right_product.15), channel_id=1, source_target_pairs={{0,4},{1,5},{2,6},{3,7},{4,0},{5,1},{6,2},{7,3},{8,12},{9,13},{10,... | collective-permute-start | bytes 688136 | tf_op jit(solution)/shard_map/ppermute | solution.py:360
  48.4 0.5 right_product.14.part
  48.9 1.3 %collective-permute-start.10 = (bf16[7,128,128]{2,1,0:T(8,128)(2,1)S(1)}, bf16[7,128,128]{2,1,0:T(8,128)(2,1)S(1)}, u32[]{:S(2)}, u32[]{:S(2)}) collective-permute-start(bf16[7,128,128]{2,1,0:T(8,128)(2,1)S(1)} %first_sum.3), channel_id=1, source_target_pairs={{0,1},{1,0},{2,3},{3,2},{4,6},{5,7},{6,4},{7,5},{8,9},{9,8},{10,11... | collective-permute-start | bytes 688136 | tf_op jit(solution)/shard_map/ppermute | solution.py:360
  50.2 0.0 collective-permute-done.8.arrived
  50.2 0.5 right_product.13
  50.7 1.2 %collective-permute-start.9 = (bf16[7,128,128]{2,1,0:T(8,128)(2,1)S(1)}, bf16[7,128,128]{2,1,0:T(8,128)(2,1)S(1)}, u32[]{:S(2)}, u32[]{:S(2)}) collective-permute-start(bf16[7,128,128]{2,1,0:T(8,128)(2,1)S(1)} %right_product.13), channel_id=1, source_target_pairs={{0,4},{1,5},{2,6},{3,7},{4,0},{5,1},{6,2},{7,3},{8,12},{9,13},{10,... | collective-permute-start | bytes 688136 | tf_op jit(solution)/shard_map/ppermute | solution.py:360
  51.8 0.0 collective-permute-done.11.across
  51.8 0.1 second_sum.3
  51.9 1.6 %collective-permute-start.12 = (bf16[7,128,128]{2,1,0:T(8,128)(2,1)S(1)}, bf16[7,128,128]{2,1,0:T(8,128)(2,1)S(1)}, u32[]{:S(2)}, u32[]{:S(2)}) collective-permute-start(bf16[7,128,128]{2,1,0:T(8,128)(2,1)S(1)} %second_sum.3), channel_id=1, source_target_pairs={{0,2},{1,3},{2,0},{3,1},{4,5},{5,4},{6,7},{7,6},{8,10},{9,11},{10,... | collective-permute-start | bytes 688136 | tf_op jit(solution)/shard_map/ppermute | solution.py:360
  53.6 0.5 right_product.12.part
  54.1 0.0 collective-permute-done.10.arrived
  54.1 0.0 collective-permute-done.9.across
  54.1 0.1 second_sum.2.one
  54.2 3.1 %collective-permute-done.12.other = bf16[7,128,128]{2,1,0:T(8,128)(2,1)S(1)} collective-permute-done((bf16[7,128,128]{2,1,0:T(8,128)(2,1)S(1)}, bf16[7,128,128]{2,1,0:T(8,128)(2,1)S(1)}, u32[]{:S(2)}, u32[]{:S(2)}) %collective-permute-start.12) | collective-permute-done | bytes 229408 | tf_op jit(solution)/shard_map/ppermute | solution.py:360
  57.3 1.3 %collective-permute-start.13 = (bf16[7,128,128]{2,1,0:T(8,128)(2,1)S(1)}, bf16[7,128,128]{2,1,0:T(8,128)(2,1)S(1)}, u32[]{:S(2)}, u32[]{:S(2)}) collective-permute-start(bf16[7,128,128]{2,1,0:T(8,128)(2,1)S(1)} %third_sum.1.one), channel_id=1, source_target_pairs={{0,8},{1,9},{2,10},{3,11},{4,20},{5,21},{6,22},{7,23},{8,0},{9,1},... | collective-permute-start | bytes 688136 | tf_op jit(solution)/shard_map/ppermute | solution.py:360
  58.6 6.7 %collective-permute-done.13.other = bf16[7,128,128]{2,1,0:T(8,128)(2,1)S(1)} collective-permute-done((bf16[7,128,128]{2,1,0:T(8,128)(2,1)S(1)}, bf16[7,128,128]{2,1,0:T(8,128)(2,1)S(1)}, u32[]{:S(2)}, u32[]{:S(2)}) %collective-permute-start.13) | collective-permute-done | bytes 229408 | tf_op jit(solution)/shard_map/ppermute | solution.py:360
  65.3 0.1 pair_sum.1.one
  65.4 0.8 collective-permute-start.14
  66.2 5.6 %collective-permute-done.14.other = bf16[7,128,128]{2,1,0:T(8,128)(2,1)S(1)} collective-permute-done((bf16[7,128,128]{2,1,0:T(8,128)(2,1)S(1)}, bf16[7,128,128]{2,1,0:T(8,128)(2,1)S(1)}, u32[]{:S(2)}, u32[]{:S(2)}) %collective-permute-start.14) | collective-permute-done | bytes 229408 | tf_op jit(solution)/shard_map/ppermute | solution.py:360
  71.9 0.1 factor.1.rest_0_.rest_4_
  72.0 1.6 %collective-permute-start.15 = (bf16[7,128,128]{2,1,0:T(8,128)(2,1)S(1)}, bf16[7,128,128]{2,1,0:T(8,128)(2,1)S(1)}, u32[]{:S(2)}, u32[]{:S(2)}) collective-permute-start(bf16[7,128,128]{2,1,0:T(8,128)(2,1)S(1)} %factor.1.rest_0_.rest_4_), channel_id=1, source_target_pairs={{0,2},{1,3},{2,0},{3,1},{4,5},{5,4},{6,7},{7,6},{8,10},{9,11},{10,... | collective-permute-start | bytes 688136 | tf_op jit(solution)/shard_map/ppermute | solution.py:360
  73.5 1.2 %collective-permute-start.19 = (bf16[7,128,128]{2,1,0:T(8,128)(2,1)S(1)}, bf16[7,128,128]{2,1,0:T(8,128)(2,1)S(1)}, u32[]{:S(2)}, u32[]{:S(2)}) collective-permute-start(bf16[7,128,128]{2,1,0:T(8,128)(2,1)S(1)} %factor.1.rest_0_.rest_4_), channel_id=1, source_target_pairs={{0,1},{1,0},{2,3},{3,2},{4,6},{5,7},{6,4},{7,5},{8,9},{9,8},{10,11... | collective-permute-start | bytes 688136 | tf_op jit(solution)/shard_map/ppermute | solution.py:360
  74.8 1.5 %new_error.4.rest_6_ = bf16[1024,7168]{1,0:T(8,128)(2,1)} custom-call(s32[1]{0:T(128)} %bitcast.dp, s32[1]{0:T(128)} %bitcast.1.mp, bf16[1024,7168]{1,0:T(8,128)(2,1)S(1)} %get-tuple-element.28.comp, bf16[512,128]{1,0:T(8,128)(2,1)S(1)} %get-tuple-element.31.near, bf16[512,128]{1,0:T(8,128)(2,1)S(1)} %get-tuple-element.32.far, ...), custom_call_target="tpu_custom_call" | custom-call | bytes 4900000 | tf_op jit(solution)/shard_map/new_error/pallas_call | solution.py:200
  76.3 4.5 %collective-permute-start.17 = (bf16[7,128,128]{2,1,0:T(8,128)(2,1)S(1)}, bf16[7,128,128]{2,1,0:T(8,128)(2,1)S(1)}, u32[]{:S(2)}, u32[]{:S(2)}) collective-permute-start(bf16[7,128,128]{2,1,0:T(8,128)(2,1)S(1)} %factor.1.rest_0_.rest_4_), channel_id=1, source_target_pairs={{0,4},{1,5},{2,6},{3,7},{4,0},{5,1},{6,2},{7,3},{8,12},{9,13},{10,... | collective-permute-start | bytes 688136 | tf_op jit(solution)/shard_map/ppermute | solution.py:360
  80.8 0.0 collective-permute-done.15.rest_1_
  80.8 1.2 %collective-permute-start.18 = (bf16[7,128,128]{2,1,0:T(8,128)(2,1)S(1)}, bf16[7,128,128]{2,1,0:T(8,128)(2,1)S(1)}, u32[]{:S(2)}, u32[]{:S(2)}) collective-permute-start(bf16[7,128,128]{2,1,0:T(8,128)(2,1)S(1)} %collective-permute-done.15.rest_1_), channel_id=1, source_target_pairs={{0,4},{1,5},{2,6},{3,7},{4,0},{5,1},{6,2},{7,3},{8,12},{9,13},{10,... | collective-permute-start | bytes 688136 | tf_op jit(solution)/shard_map/ppermute | solution.py:360
  82.0 1.4 %collective-permute-start.16 = (bf16[7,128,128]{2,1,0:T(8,128)(2,1)S(1)}, bf16[7,128,128]{2,1,0:T(8,128)(2,1)S(1)}, u32[]{:S(2)}, u32[]{:S(2)}) collective-permute-start(bf16[7,128,128]{2,1,0:T(8,128)(2,1)S(1)} %collective-permute-done.15.rest_1_), channel_id=1, source_target_pairs={{0,1},{1,0},{2,3},{3,2},{4,6},{5,7},{6,4},{7,5},{8,9},{9,8},{10,11... | collective-permute-start | bytes 688136 | tf_op jit(solution)/shard_map/ppermute | solution.py:360
  83.4 0.0 collective-permute-done.19.rest_3_
  83.4 0.3 collective-permute-start.21
  83.7 0.0 collective-permute-done.17.rest_0_.rest_5_
  83.7 0.0 collective-permute-done.18.rest_2_
  83.7 3.6 %new_error.5 = (bf16[1024,7168]{1,0:T(8,128)(2,1)}, bf16[1792,128]{1,0:T(8,128)(2,1)}) custom-call(s32[1]{0:T(128)} %bitcast.dp, s32[1]{0:T(128)} %bitcast.1.mp, bf16[1024,7168]{1,0:T(8,128)(2,1)S(1)} %get-tuple-element.28.comp, bf16[512,128]{1,0:T(8,128)(2,1)S(1)} %get-tuple-element.31.near, ...), custom_call_target="tpu_custom_call", output_to_operand_aliasing={{0}: (11, {})} | custom-call | bytes 13300000 | tf_op jit(solution)/shard_map/new_error/pallas_call | solution.py:200
  87.4 0.6 collective-permute-start.20
  88.0 0.0 collective-permute-done.21.rest_0_
  88.0 2.2 %new_error.6.rest_1_ = bf16[1024,7168]{1,0:T(8,128)(2,1)} custom-call(s32[1]{0:T(128)} %bitcast.dp, s32[1]{0:T(128)} %bitcast.1.mp, bf16[1024,7168]{1,0:T(8,128)(2,1)S(1)} %get-tuple-element.28.comp, bf16[512,128]{1,0:T(8,128)(2,1)S(1)} %get-tuple-element.31.near, bf16[512,128]{1,0:T(8,128)(2,1)S(1)} %get-tuple-element.32.far, ...), custom_call_target="tpu_custom_call", output_to_operand_aliasing={{}: (7, {})} | custom-call | bytes 7700000 | tf_op jit(solution)/shard_map/new_error/pallas_call | solution.py:200
  90.2 0.0 collective-permute-done.20.rest_0_
  90.2 1.5 %new_error.7 = bf16[1024,7168]{1,0:T(8,128)(2,1)} custom-call(s32[1]{0:T(128)} %bitcast.dp, s32[1]{0:T(128)} %bitcast.1.mp, bf16[1024,7168]{1,0:T(8,128)(2,1)S(1)} %get-tuple-element.28.comp, bf16[512,128]{1,0:T(8,128)(2,1)S(1)} %get-tuple-element.31.near, bf16[512,128]{1,0:T(8,128)(2,1)S(1)} %get-tuple-element.32.far, ...), custom_call_target="tpu_custom_call", output_to_operand_aliasing={{}: (6, {})} | custom-call | bytes 4900000 | tf_op jit(solution)/shard_map/new_error/pallas_call | solution.py:200
  (8 shorter events, 0.2 us)
Async XLA Ops:
  11.9 1.6 %collective-permute-start = (f32[128,512]{1,0:T(8,128)S(1)}, f32[128,512]{1,0:T(8,128)S(1)}, u32[]{:S(2)}, u32[]{:S(2)}) collective-permute-start(f32[128,512]{1,0:T(8,128)S(1)} %get-tuple-element.30), channel_id=1, source_target_pairs={{0,4},{1,5},{2,6},{3,7},{4,0},{5,1},{6,2},{7,3},{8,12},{9,13},{10,... | collective-permute-start | bytes 786440 | tf_op jit(solution)/shard_map/ppermute | solution.py:360
  13.5 7.2 %collective-permute-start.1 = (bf16[128,512]{1,0:T(8,128)(2,1)S(1)}, bf16[128,512]{1,0:T(8,128)(2,1)S(1)}, u32[]{:S(2)}, u32[]{:S(2)}) collective-permute-start(bf16[128,512]{1,0:T(8,128)(2,1)S(1)} %fusion.1), channel_id=1, source_target_pairs={{0,8},{1,9},{2,10},{3,11},{4,20},{5,21},{6,22},{7,23},{8,0},{9,1},... | collective-permute-start | bytes 393224 | tf_op jit(solution)/shard_map/ppermute | solution.py:360
  20.8 4.2 %collective-permute-start.2 = (bf16[128,512]{1,0:T(8,128)(2,1)S(1)}, bf16[128,512]{1,0:T(8,128)(2,1)S(1)}, u32[]{:S(2)}, u32[]{:S(2)}) collective-permute-start(bf16[128,512]{1,0:T(8,128)(2,1)S(1)} %fusion), channel_id=1, source_target_pairs={{0,16},{1,17},{2,18},{3,19},{4,12},{5,13},{6,14},{7,15},{8,24},{9,... | collective-permute-start | bytes 393224 | tf_op jit(solution)/shard_map/ppermute | solution.py:360
  25.1 2.8 %collective-permute-start.3 = (bf16[128,512]{1,0:T(8,128)(2,1)S(1)}, bf16[128,512]{1,0:T(8,128)(2,1)S(1)}, u32[]{:S(2)}, u32[]{:S(2)}) collective-permute-start(bf16[128,512]{1,0:T(8,128)(2,1)S(1)} %add_convert_fusion.near), channel_id=1, source_target_pairs={{0,4},{1,5},{2,6},{3,7},{4,0},{5,1},{6,2},{7,3},{8,12},{9,13},{10,... | collective-permute-start | bytes 393224 | tf_op jit(solution)/shard_map/ppermute | solution.py:360
  28.1 4.6 %collective-permute-start.4 = (f32[128,128]{1,0:T(8,128)S(1)}, f32[128,128]{1,0:T(8,128)S(1)}, u32[]{:S(2)}, u32[]{:S(2)}) collective-permute-start(f32[128,128]{1,0:T(8,128)S(1)} %gram.1), channel_id=1, source_target_pairs={{0,1},{1,0},{2,3},{3,2},{4,5},{5,4},{6,7},{7,6},{8,9},{9,8},{10,11... | collective-permute-start | bytes 196616 | tf_op jit(solution)/shard_map/ppermute | solution.py:360
  32.7 3.2 %collective-permute-start.5 = (f32[128,128]{1,0:T(8,128)S(1)}, f32[128,128]{1,0:T(8,128)S(1)}, u32[]{:S(2)}, u32[]{:S(2)}) collective-permute-start(f32[128,128]{1,0:T(8,128)S(1)} %add.18), channel_id=1, source_target_pairs={{0,2},{1,3},{2,0},{3,1},{4,6},{5,7},{6,4},{7,5},{8,10},{9,11},{10,... | collective-permute-start | bytes 196616 | tf_op jit(solution)/shard_map/ppermute | solution.py:360
  41.5 3.2 %collective-permute-start.6 = (bf16[7,128,128]{2,1,0:T(8,128)(2,1)S(1)}, bf16[7,128,128]{2,1,0:T(8,128)(2,1)S(1)}, u32[]{:S(2)}, u32[]{:S(2)}) collective-permute-start(bf16[7,128,128]{2,1,0:T(8,128)(2,1)S(1)} %right_product.9), channel_id=1, source_target_pairs={{0,4},{1,5},{2,6},{3,7},{4,0},{5,1},{6,2},{7,3},{8,12},{9,13},{10,... | collective-permute-start | bytes 688136 | tf_op jit(solution)/shard_map/ppermute | solution.py:360
  44.0 2.9 %collective-permute-start.7 = (bf16[7,128,128]{2,1,0:T(8,128)(2,1)S(1)}, bf16[7,128,128]{2,1,0:T(8,128)(2,1)S(1)}, u32[]{:S(2)}, u32[]{:S(2)}) collective-permute-start(bf16[7,128,128]{2,1,0:T(8,128)(2,1)S(1)} %right_product.11), channel_id=1, source_target_pairs={{0,4},{1,5},{2,6},{3,7},{4,0},{5,1},{6,2},{7,3},{8,12},{9,13},{10,... | collective-permute-start | bytes 688136 | tf_op jit(solution)/shard_map/ppermute | solution.py:360
  44.7 5.5 %collective-permute-start.8 = (bf16[7,128,128]{2,1,0:T(8,128)(2,1)S(1)}, bf16[7,128,128]{2,1,0:T(8,128)(2,1)S(1)}, u32[]{:S(2)}, u32[]{:S(2)}) collective-permute-start(bf16[7,128,128]{2,1,0:T(8,128)(2,1)S(1)} %first_sum.2), channel_id=1, source_target_pairs={{0,1},{1,0},{2,3},{3,2},{4,6},{5,7},{6,4},{7,5},{8,9},{9,8},{10,11... | collective-permute-start | bytes 688136 | tf_op jit(solution)/shard_map/ppermute | solution.py:360
  47.4 4.4 %collective-permute-start.11 = (bf16[7,128,128]{2,1,0:T(8,128)(2,1)S(1)}, bf16[7,128,128]{2,1,0:T(8,128)(2,1)S(1)}, u32[]{:S(2)}, u32[]{:S(2)}) collective-permute-start(bf16[7,128,128]{2,1,0:T(8,128)(2,1)S(1)} %right_product.15), channel_id=1, source_target_pairs={{0,4},{1,5},{2,6},{3,7},{4,0},{5,1},{6,2},{7,3},{8,12},{9,13},{10,... | collective-permute-start | bytes 688136 | tf_op jit(solution)/shard_map/ppermute | solution.py:360
  48.9 5.2 %collective-permute-start.10 = (bf16[7,128,128]{2,1,0:T(8,128)(2,1)S(1)}, bf16[7,128,128]{2,1,0:T(8,128)(2,1)S(1)}, u32[]{:S(2)}, u32[]{:S(2)}) collective-permute-start(bf16[7,128,128]{2,1,0:T(8,128)(2,1)S(1)} %first_sum.3), channel_id=1, source_target_pairs={{0,1},{1,0},{2,3},{3,2},{4,6},{5,7},{6,4},{7,5},{8,9},{9,8},{10,11... | collective-permute-start | bytes 688136 | tf_op jit(solution)/shard_map/ppermute | solution.py:360
  50.7 3.4 %collective-permute-start.9 = (bf16[7,128,128]{2,1,0:T(8,128)(2,1)S(1)}, bf16[7,128,128]{2,1,0:T(8,128)(2,1)S(1)}, u32[]{:S(2)}, u32[]{:S(2)}) collective-permute-start(bf16[7,128,128]{2,1,0:T(8,128)(2,1)S(1)} %right_product.13), channel_id=1, source_target_pairs={{0,4},{1,5},{2,6},{3,7},{4,0},{5,1},{6,2},{7,3},{8,12},{9,13},{10,... | collective-permute-start | bytes 688136 | tf_op jit(solution)/shard_map/ppermute | solution.py:360
  51.9 5.3 %collective-permute-start.12 = (bf16[7,128,128]{2,1,0:T(8,128)(2,1)S(1)}, bf16[7,128,128]{2,1,0:T(8,128)(2,1)S(1)}, u32[]{:S(2)}, u32[]{:S(2)}) collective-permute-start(bf16[7,128,128]{2,1,0:T(8,128)(2,1)S(1)} %second_sum.3), channel_id=1, source_target_pairs={{0,2},{1,3},{2,0},{3,1},{4,5},{5,4},{6,7},{7,6},{8,10},{9,11},{10,... | collective-permute-start | bytes 688136 | tf_op jit(solution)/shard_map/ppermute | solution.py:360
  57.3 8.0 %collective-permute-start.13 = (bf16[7,128,128]{2,1,0:T(8,128)(2,1)S(1)}, bf16[7,128,128]{2,1,0:T(8,128)(2,1)S(1)}, u32[]{:S(2)}, u32[]{:S(2)}) collective-permute-start(bf16[7,128,128]{2,1,0:T(8,128)(2,1)S(1)} %third_sum.1.one), channel_id=1, source_target_pairs={{0,8},{1,9},{2,10},{3,11},{4,20},{5,21},{6,22},{7,23},{8,0},{9,1},... | collective-permute-start | bytes 688136 | tf_op jit(solution)/shard_map/ppermute | solution.py:360
  65.4 6.5 %collective-permute-start.14 = (bf16[7,128,128]{2,1,0:T(8,128)(2,1)S(1)}, bf16[7,128,128]{2,1,0:T(8,128)(2,1)S(1)}, u32[]{:S(2)}, u32[]{:S(2)}) collective-permute-start(bf16[7,128,128]{2,1,0:T(8,128)(2,1)S(1)} %pair_sum.1.one), channel_id=1, source_target_pairs={{0,16},{1,17},{2,18},{3,19},{4,12},{5,13},{6,14},{7,15},{8,24},{9,... | collective-permute-start | bytes 688136 | tf_op jit(solution)/shard_map/ppermute | solution.py:360
  72.0 8.8 %collective-permute-start.15 = (bf16[7,128,128]{2,1,0:T(8,128)(2,1)S(1)}, bf16[7,128,128]{2,1,0:T(8,128)(2,1)S(1)}, u32[]{:S(2)}, u32[]{:S(2)}) collective-permute-start(bf16[7,128,128]{2,1,0:T(8,128)(2,1)S(1)} %factor.1.rest_0_.rest_4_), channel_id=1, source_target_pairs={{0,2},{1,3},{2,0},{3,1},{4,5},{5,4},{6,7},{7,6},{8,10},{9,11},{10,... | collective-permute-start | bytes 688136 | tf_op jit(solution)/shard_map/ppermute | solution.py:360
  73.5 9.9 %collective-permute-start.19 = (bf16[7,128,128]{2,1,0:T(8,128)(2,1)S(1)}, bf16[7,128,128]{2,1,0:T(8,128)(2,1)S(1)}, u32[]{:S(2)}, u32[]{:S(2)}) collective-permute-start(bf16[7,128,128]{2,1,0:T(8,128)(2,1)S(1)} %factor.1.rest_0_.rest_4_), channel_id=1, source_target_pairs={{0,1},{1,0},{2,3},{3,2},{4,6},{5,7},{6,4},{7,5},{8,9},{9,8},{10,11... | collective-permute-start | bytes 688136 | tf_op jit(solution)/shard_map/ppermute | solution.py:360
  76.3 7.4 %collective-permute-start.17 = (bf16[7,128,128]{2,1,0:T(8,128)(2,1)S(1)}, bf16[7,128,128]{2,1,0:T(8,128)(2,1)S(1)}, u32[]{:S(2)}, u32[]{:S(2)}) collective-permute-start(bf16[7,128,128]{2,1,0:T(8,128)(2,1)S(1)} %factor.1.rest_0_.rest_4_), channel_id=1, source_target_pairs={{0,4},{1,5},{2,6},{3,7},{4,0},{5,1},{6,2},{7,3},{8,12},{9,13},{10,... | collective-permute-start | bytes 688136 | tf_op jit(solution)/shard_map/ppermute | solution.py:360
  80.8 3.0 %collective-permute-start.18 = (bf16[7,128,128]{2,1,0:T(8,128)(2,1)S(1)}, bf16[7,128,128]{2,1,0:T(8,128)(2,1)S(1)}, u32[]{:S(2)}, u32[]{:S(2)}) collective-permute-start(bf16[7,128,128]{2,1,0:T(8,128)(2,1)S(1)} %collective-permute-done.15.rest_1_), channel_id=1, source_target_pairs={{0,4},{1,5},{2,6},{3,7},{4,0},{5,1},{6,2},{7,3},{8,12},{9,13},{10,... | collective-permute-start | bytes 688136 | tf_op jit(solution)/shard_map/ppermute | solution.py:360
  82.0 5.4 %collective-permute-start.16 = (bf16[7,128,128]{2,1,0:T(8,128)(2,1)S(1)}, bf16[7,128,128]{2,1,0:T(8,128)(2,1)S(1)}, u32[]{:S(2)}, u32[]{:S(2)}) collective-permute-start(bf16[7,128,128]{2,1,0:T(8,128)(2,1)S(1)} %collective-permute-done.15.rest_1_), channel_id=1, source_target_pairs={{0,1},{1,0},{2,3},{3,2},{4,6},{5,7},{6,4},{7,5},{8,9},{9,8},{10,11... | collective-permute-start | bytes 688136 | tf_op jit(solution)/shard_map/ppermute | solution.py:360
  83.4 4.6 %collective-permute-start.21 = (bf16[7,128,128]{2,1,0:T(8,128)(2,1)S(1)}, bf16[7,128,128]{2,1,0:T(8,128)(2,1)S(1)}, u32[]{:S(2)}, u32[]{:S(2)}) collective-permute-start(bf16[7,128,128]{2,1,0:T(8,128)(2,1)S(1)} %collective-permute-done.19.rest_3_), channel_id=1, source_target_pairs={{0,4},{1,5},{2,6},{3,7},{4,0},{5,1},{6,2},{7,3},{8,12},{9,13},{10,... | collective-permute-start | bytes 688136 | tf_op jit(solution)/shard_map/ppermute | solution.py:360
  87.4 2.8 %collective-permute-start.20 = (bf16[7,128,128]{2,1,0:T(8,128)(2,1)S(1)}, bf16[7,128,128]{2,1,0:T(8,128)(2,1)S(1)}, u32[]{:S(2)}, u32[]{:S(2)}) collective-permute-start(bf16[7,128,128]{2,1,0:T(8,128)(2,1)S(1)} %collective-permute-done.16.rest_1_), channel_id=1, source_target_pairs={{0,4},{1,5},{2,6},{3,7},{4,0},{5,1},{6,2},{7,3},{8,12},{9,13},{10,... | collective-permute-start | bytes 688136 | tf_op jit(solution)/shard_map/ppermute | solution.py:360

commit v10 on v8

--- a/solution.py
+++ b/solution.py
@@ -12,7 +12,7 @@
 LANES = 128
 MIB = 1024 * 1024
 AXES = ("dp", "mp")
-PIECES = 14
+PIECES = 7
 LEAF = 8
 
 VMEM = pl.BlockSpec(memory_space=pltpu.VMEM)
@@ -358,7 +358,7 @@
         self.other = [bit for bit in mp_bits if bit not in (low, high)]
         self.scatter = [(low, high), (high, low)]
         rest = self.other + z_bits
-        self.rest = list(zip(rest, rest[::-1]))
+        self.rest = list(zip(rest[::-1], rest))
         self.replicas = list(zip(z_bits, z_bits[::-1]))
         self.low, self.high = low, high
 

time: 78.3 us -> 78 us (level)
  transfers between devices with their start and end apart: 21 -> 21, of which waited for: 9 -> 10; matrix products, arithmetic and copies ran while one was open for 0% -> 0% of each run, Pallas kernels for 21% -> 21%
where the time goes in v10:
time: 78 us; the launch traced here: 77.9 us
  Pallas kernels  29.9 us (38%)
  starting transfers between devices  27.7 us (36%)
  waiting for transfers between devices  19.1 us (24%)
  between operations  0.99 us (1%)
    ppermute x21, starting transfers between devices, send(): return lax.ppermute(x, AXES, pairs)  27.7 us
    ppermute x21, waiting for transfers between devices, send(): return lax.ppermute(x, AXES, pairs)  19.1 us
    pallas_call x1, Pallas kernels, left_product(): call(functools.partial(left_kernel, net, PIECES), 'left_product', [pltpu....  11.2 us
    pallas_call x4, Pallas kernels, new_error(): call(functools.partial(new_error_kernel, net, units, blocks, len(block_0)...  8.82 us
    pallas_call x1, Pallas kernels, inverse_of(): call(inverse_kernel, 'inverse', shaped((n, 2 * n), F32), [VMEM], 4, 4.5,...  4.83 us
    pallas_call x8, Pallas kernels, right_product(): call(functools.partial(right_kernel, net, units, side, places), 'right_pr...  3.86 us
  transfers between devices with their start and end apart: 21, of which 10 were waited for; matrix products, arithmetic and copies ran while one was open for 0% of the time, Pallas kernels for 21%

profile of v10, /device:TPU:1, one launch (start us, length us, event | category | flops | bytes accessed | tf_op | source)
XLA Modules:
  0.0 77.9 jit_solution(18249289138517691413)
XLA Ops:
  0.6 11.2 %left_product.1 = (bf16[1024,7168]{1,0:T(8,128)(2,1)S(1)}, f32[128,512]{1,0:T(8,128)S(1)}, f32[128,512]{1,0:T(8,128)S(1)}) custom-call(s32[1]{0:T(128)} %bitcast.dp, s32[1]{0:T(128)} %bitcast.1.mp, bf16[1024,7168]{1,0:T(8,128)(2,1)} %bitcast.6, bf16[1024,7168]{1,0:T(8,128)(2,1)} %bitcast.7, bf16[7168,128]{1,0:T(8,128)(2,1)} %init.1), custom_call_target="tpu_custom_call" | custom-call | bytes 42000000 | tf_op jit(solution)/shard_map/left_product/pallas_call | solution.py:106
  11.8 0.1 collective-permute-start
  11.9 1.5 %collective-permute-done = f32[128,512]{1,0:T(8,128)S(1)} collective-permute-done((f32[128,512]{1,0:T(8,128)S(1)}, f32[128,512]{1,0:T(8,128)S(1)}, u32[]{:S(2)}, u32[]{:S(2)}) %collective-permute-start) | collective-permute-done | bytes 262176 | tf_op jit(solution)/shard_map/ppermute | solution.py:372
  13.5 3.5 %collective-permute-start.1 = (bf16[128,512]{1,0:T(8,128)(2,1)S(1)}, bf16[128,512]{1,0:T(8,128)(2,1)S(1)}, u32[]{:S(2)}, u32[]{:S(2)}) collective-permute-start(bf16[128,512]{1,0:T(8,128)(2,1)S(1)} %fusion.1), channel_id=1, source_target_pairs={{0,8},{1,9},{2,10},{3,11},{4,20},{5,21},{6,22},{7,23},{8,0},{9,1},... | collective-permute-start | bytes 393224 | tf_op jit(solution)/shard_map/ppermute | solution.py:372
  17.0 3.7 %collective-permute-done.1 = bf16[128,512]{1,0:T(8,128)(2,1)S(1)} collective-permute-done((bf16[128,512]{1,0:T(8,128)(2,1)S(1)}, bf16[128,512]{1,0:T(8,128)(2,1)S(1)}, u32[]{:S(2)}, u32[]{:S(2)}) %collective-permute-start.1) | collective-permute-done | bytes 131104 | tf_op jit(solution)/shard_map/ppermute | solution.py:372
  20.7 0.1 fusion
  20.7 0.7 collective-permute-start.2
  21.5 3.4 %collective-permute-done.2 = bf16[128,512]{1,0:T(8,128)(2,1)S(1)} collective-permute-done((bf16[128,512]{1,0:T(8,128)(2,1)S(1)}, bf16[128,512]{1,0:T(8,128)(2,1)S(1)}, u32[]{:S(2)}, u32[]{:S(2)}) %collective-permute-start.2) | collective-permute-done | bytes 131104 | tf_op jit(solution)/shard_map/ppermute | solution.py:372
  24.9 0.1 add_convert_fusion.near
  25.0 1.9 %collective-permute-start.3 = (bf16[128,512]{1,0:T(8,128)(2,1)S(1)}, bf16[128,512]{1,0:T(8,128)(2,1)S(1)}, u32[]{:S(2)}, u32[]{:S(2)}) collective-permute-start(bf16[128,512]{1,0:T(8,128)(2,1)S(1)} %add_convert_fusion.near), channel_id=1, source_target_pairs={{0,4},{1,5},{2,6},{3,7},{4,0},{5,1},{6,2},{7,3},{8,12},{9,13},{10,... | collective-permute-start | bytes 393224 | tf_op jit(solution)/shard_map/ppermute | solution.py:372
  26.9 1.0 %collective-permute-done.3.far = bf16[128,512]{1,0:T(8,128)(2,1)S(1)} collective-permute-done((bf16[128,512]{1,0:T(8,128)(2,1)S(1)}, bf16[128,512]{1,0:T(8,128)(2,1)S(1)}, u32[]{:S(2)}, u32[]{:S(2)}) %collective-permute-start.3) | collective-permute-done | bytes 131104 | tf_op jit(solution)/shard_map/ppermute | solution.py:372
  27.9 0.5 right_product.9
  28.3 0.4 collective-permute-start.4
  28.8 0.5 right_product.11
  29.3 0.2 collective-permute-start.5
  29.5 0.5 right_product.8.one
  30.0 0.0 collective-permute-done.4.other
  30.0 0.1 first_sum.2
  30.0 2.5 %collective-permute-start.6 = (bf16[7,128,128]{2,1,0:T(8,128)(2,1)S(1)}, bf16[7,128,128]{2,1,0:T(8,128)(2,1)S(1)}, u32[]{:S(2)}, u32[]{:S(2)}) collective-permute-start(bf16[7,128,128]{2,1,0:T(8,128)(2,1)S(1)} %first_sum.2), channel_id=1, source_target_pairs={{0,1},{1,0},{2,3},{3,2},{4,6},{5,7},{6,4},{7,5},{8,9},{9,8},{10,11... | collective-permute-start | bytes 688136 | tf_op jit(solution)/shard_map/ppermute | solution.py:372
  32.5 0.5 right_product.10.part
  33.0 0.0 collective-permute-done.5.across
  33.0 0.2 first_sum.3
  33.2 0.5 right_product.15
  33.7 0.7 collective-permute-start.9
  34.4 1.2 %collective-permute-start.8 = (bf16[9,128,128]{2,1,0:T(8,128)(2,1)S(1)}, bf16[9,128,128]{2,1,0:T(8,128)(2,1)S(1)}, u32[]{:S(2)}, u32[]{:S(2)}) collective-permute-start(bf16[9,128,128]{2,1,0:T(8,128)(2,1)S(1)} %get-tuple-element.49), channel_id=1, source_target_pairs={{0,1},{1,0},{2,3},{3,2},{4,6},{5,7},{6,4},{7,5},{8,9},{9,8},{10,11... | collective-permute-start | bytes 884744 | tf_op jit(solution)/shard_map/ppermute | solution.py:372
  35.6 0.5 right_product.14.part
  36.1 0.0 collective-permute-done.6.arrived
  36.2 0.5 right_product.13
  36.7 1.0 %collective-permute-start.7 = (bf16[7,128,128]{2,1,0:T(8,128)(2,1)S(1)}, bf16[7,128,128]{2,1,0:T(8,128)(2,1)S(1)}, u32[]{:S(2)}, u32[]{:S(2)}) collective-permute-start(bf16[7,128,128]{2,1,0:T(8,128)(2,1)S(1)} %right_product.13), channel_id=1, source_target_pairs={{0,4},{1,5},{2,6},{3,7},{4,0},{5,1},{6,2},{7,3},{8,12},{9,13},{10,... | collective-permute-start | bytes 688136 | tf_op jit(solution)/shard_map/ppermute | solution.py:372
  37.6 0.0 collective-permute-done.9.across
  37.7 0.1 second_sum.3
  37.7 1.8 %collective-permute-start.10 = (bf16[7,128,128]{2,1,0:T(8,128)(2,1)S(1)}, bf16[7,128,128]{2,1,0:T(8,128)(2,1)S(1)}, u32[]{:S(2)}, u32[]{:S(2)}) collective-permute-start(bf16[7,128,128]{2,1,0:T(8,128)(2,1)S(1)} %second_sum.3), channel_id=1, source_target_pairs={{0,2},{1,3},{2,0},{3,1},{4,5},{5,4},{6,7},{7,6},{8,10},{9,11},{10,... | collective-permute-start | bytes 688136 | tf_op jit(solution)/shard_map/ppermute | solution.py:372
  39.6 0.5 right_product.12.part
  40.0 0.2 collective-permute-done.8.arrived
  40.3 0.0 collective-permute-done.7.across
  40.3 0.1 second_sum.2
  40.4 2.9 %collective-permute-done.10.other = bf16[7,128,128]{2,1,0:T(8,128)(2,1)S(1)} collective-permute-done((bf16[7,128,128]{2,1,0:T(8,128)(2,1)S(1)}, bf16[7,128,128]{2,1,0:T(8,128)(2,1)S(1)}, u32[]{:S(2)}, u32[]{:S(2)}) %collective-permute-start.10) | collective-permute-done | bytes 229408 | tf_op jit(solution)/shard_map/ppermute | solution.py:372
  43.3 1.5 %collective-permute-start.11 = (bf16[7,128,128]{2,1,0:T(8,128)(2,1)S(1)}, bf16[7,128,128]{2,1,0:T(8,128)(2,1)S(1)}, u32[]{:S(2)}, u32[]{:S(2)}) collective-permute-start(bf16[7,128,128]{2,1,0:T(8,128)(2,1)S(1)} %third_sum.1.one), channel_id=1, source_target_pairs={{0,16},{1,17},{2,18},{3,19},{4,12},{5,13},{6,14},{7,15},{8,24},{9,... | collective-permute-start | bytes 688136 | tf_op jit(solution)/shard_map/ppermute | solution.py:372
  44.8 1.2 %collective-permute-start.12 = (f32[128,128]{1,0:T(8,128)S(1)}, f32[128,128]{1,0:T(8,128)S(1)}, u32[]{:S(2)}, u32[]{:S(2)}) collective-permute-start(f32[128,128]{1,0:T(8,128)S(1)} %get-tuple-element.53), channel_id=1, source_target_pairs={{0,2},{1,3},{2,0},{3,1},{4,5},{5,4},{6,7},{7,6},{8,10},{9,11},{10,... | collective-permute-start | bytes 196616 | tf_op jit(solution)/shard_map/ppermute | solution.py:372
  46.0 2.2 %collective-permute-done.12 = f32[128,128]{1,0:T(8,128)S(1)} collective-permute-done((f32[128,128]{1,0:T(8,128)S(1)}, f32[128,128]{1,0:T(8,128)S(1)}, u32[]{:S(2)}, u32[]{:S(2)}) %collective-permute-start.12) | collective-permute-done | bytes 65568 | tf_op jit(solution)/shard_map/ppermute | solution.py:372
  48.2 2.1 %collective-permute-done.11.other = bf16[7,128,128]{2,1,0:T(8,128)(2,1)S(1)} collective-permute-done((bf16[7,128,128]{2,1,0:T(8,128)(2,1)S(1)}, bf16[7,128,128]{2,1,0:T(8,128)(2,1)S(1)}, u32[]{:S(2)}, u32[]{:S(2)}) %collective-permute-start.11) | collective-permute-done | bytes 229408 | tf_op jit(solution)/shard_map/ppermute | solution.py:372
  50.4 0.1 pair_sum.1.own
  50.4 1.5 %collective-permute-start.13 = (bf16[7,128,128]{2,1,0:T(8,128)(2,1)S(1)}, bf16[7,128,128]{2,1,0:T(8,128)(2,1)S(1)}, u32[]{:S(2)}, u32[]{:S(2)}) collective-permute-start(bf16[7,128,128]{2,1,0:T(8,128)(2,1)S(1)} %pair_sum.1.own), channel_id=1, source_target_pairs={{0,8},{1,9},{2,10},{3,11},{4,20},{5,21},{6,22},{7,23},{8,0},{9,1},... | collective-permute-start | bytes 688136 | tf_op jit(solution)/shard_map/ppermute | solution.py:372
  52.0 4.8 %inverse.1.state = f32[128,256]{1,0:T(8,128)S(1)} custom-call(f32[128,128]{1,0:T(8,128)S(1)} %add.15.gram), custom_call_target="tpu_custom_call" | custom-call | bytes 15750000 | tf_op jit(solution)/shard_map/inverse/pallas_call | solution.py:295
  56.8 0.3 base.1
  57.2 1.7 %collective-permute-done.13.arrived = bf16[7,128,128]{2,1,0:T(8,128)(2,1)S(1)} collective-permute-done((bf16[7,128,128]{2,1,0:T(8,128)(2,1)S(1)}, bf16[7,128,128]{2,1,0:T(8,128)(2,1)S(1)}, u32[]{:S(2)}, u32[]{:S(2)}) %collective-permute-start.13) | collective-permute-done | bytes 229408 | tf_op jit(solution)/shard_map/ppermute | solution.py:372
  58.8 0.3 factor.1.rest_0_.rest_4_
  59.1 0.8 %collective-permute-start.14 = (bf16[7,128,128]{2,1,0:T(8,128)(2,1)S(1)}, bf16[7,128,128]{2,1,0:T(8,128)(2,1)S(1)}, u32[]{:S(2)}, u32[]{:S(2)}) collective-permute-start(bf16[7,128,128]{2,1,0:T(8,128)(2,1)S(1)} %factor.1.rest_0_.rest_4_), channel_id=1, source_target_pairs={{0,2},{1,3},{2,0},{3,1},{4,5},{5,4},{6,7},{7,6},{8,10},{9,11},{10,... | collective-permute-start | bytes 688136 | tf_op jit(solution)/shard_map/ppermute | solution.py:372
  60.0 1.2 %collective-permute-start.18 = (bf16[7,128,128]{2,1,0:T(8,128)(2,1)S(1)}, bf16[7,128,128]{2,1,0:T(8,128)(2,1)S(1)}, u32[]{:S(2)}, u32[]{:S(2)}) collective-permute-start(bf16[7,128,128]{2,1,0:T(8,128)(2,1)S(1)} %factor.1.rest_0_.rest_4_), channel_id=1, source_target_pairs={{0,1},{1,0},{2,3},{3,2},{4,6},{5,7},{6,4},{7,5},{8,9},{9,8},{10,11... | collective-permute-start | bytes 688136 | tf_op jit(solution)/shard_map/ppermute | solution.py:372
  61.2 1.5 %new_error.4.rest_6_ = bf16[1024,7168]{1,0:T(8,128)(2,1)} custom-call(s32[1]{0:T(128)} %bitcast.dp, s32[1]{0:T(128)} %bitcast.1.mp, bf16[1024,7168]{1,0:T(8,128)(2,1)S(1)} %get-tuple-element.38.comp, bf16[512,128]{1,0:T(8,128)(2,1)S(1)} %get-tuple-element.59.near, bf16[512,128]{1,0:T(8,128)(2,1)S(1)} %get-tuple-element.60.far, ...), custom_call_target="tpu_custom_call" | custom-call | bytes 4900000 | tf_op jit(solution)/shard_map/new_error/pallas_call | solution.py:200
  62.7 3.5 %collective-permute-start.16 = (bf16[7,128,128]{2,1,0:T(8,128)(2,1)S(1)}, bf16[7,128,128]{2,1,0:T(8,128)(2,1)S(1)}, u32[]{:S(2)}, u32[]{:S(2)}) collective-permute-start(bf16[7,128,128]{2,1,0:T(8,128)(2,1)S(1)} %factor.1.rest_0_.rest_4_), channel_id=1, source_target_pairs={{0,4},{1,5},{2,6},{3,7},{4,0},{5,1},{6,2},{7,3},{8,12},{9,13},{10,... | collective-permute-start | bytes 688136 | tf_op jit(solution)/shard_map/ppermute | solution.py:372
  66.2 0.0 collective-permute-done.14.rest_1_
  66.2 1.7 %collective-permute-start.17 = (bf16[7,128,128]{2,1,0:T(8,128)(2,1)S(1)}, bf16[7,128,128]{2,1,0:T(8,128)(2,1)S(1)}, u32[]{:S(2)}, u32[]{:S(2)}) collective-permute-start(bf16[7,128,128]{2,1,0:T(8,128)(2,1)S(1)} %collective-permute-done.14.rest_1_), channel_id=1, source_target_pairs={{0,4},{1,5},{2,6},{3,7},{4,0},{5,1},{6,2},{7,3},{8,12},{9,13},{10,... | collective-permute-start | bytes 688136 | tf_op jit(solution)/shard_map/ppermute | solution.py:372
  68.0 1.2 %collective-permute-start.15 = (bf16[7,128,128]{2,1,0:T(8,128)(2,1)S(1)}, bf16[7,128,128]{2,1,0:T(8,128)(2,1)S(1)}, u32[]{:S(2)}, u32[]{:S(2)}) collective-permute-start(bf16[7,128,128]{2,1,0:T(8,128)(2,1)S(1)} %collective-permute-done.14.rest_1_), channel_id=1, source_target_pairs={{0,1},{1,0},{2,3},{3,2},{4,6},{5,7},{6,4},{7,5},{8,9},{9,8},{10,11... | collective-permute-start | bytes 688136 | tf_op jit(solution)/shard_map/ppermute | solution.py:372
  69.2 0.0 collective-permute-done.18.rest_3_
  69.2 0.0 collective-permute-start.20
  69.2 0.0 collective-permute-done.16.rest_0_.rest_5_
  69.2 3.6 %new_error.5 = (bf16[1024,7168]{1,0:T(8,128)(2,1)}, bf16[1792,128]{1,0:T(8,128)(2,1)}) custom-call(s32[1]{0:T(128)} %bitcast.dp, s32[1]{0:T(128)} %bitcast.1.mp, bf16[1024,7168]{1,0:T(8,128)(2,1)S(1)} %get-tuple-element.38.comp, bf16[512,128]{1,0:T(8,128)(2,1)S(1)} %get-tuple-element.59.near, ...), custom_call_target="tpu_custom_call", output_to_operand_aliasing={{0}: (11, {})} | custom-call | bytes 13300000 | tf_op jit(solution)/shard_map/new_error/pallas_call | solution.py:200
  72.9 0.3 collective-permute-done.15.rest_1_
  73.1 0.9 %collective-permute-start.19 = (bf16[7,128,128]{2,1,0:T(8,128)(2,1)S(1)}, bf16[7,128,128]{2,1,0:T(8,128)(2,1)S(1)}, u32[]{:S(2)}, u32[]{:S(2)}) collective-permute-start(bf16[7,128,128]{2,1,0:T(8,128)(2,1)S(1)} %collective-permute-done.15.rest_1_), channel_id=1, source_target_pairs={{0,4},{1,5},{2,6},{3,7},{4,0},{5,1},{6,2},{7,3},{8,12},{9,13},{10,... | collective-permute-start | bytes 688136 | tf_op jit(solution)/shard_map/ppermute | solution.py:372
  74.0 0.0 collective-permute-done.20.rest_0_
  74.0 2.2 %new_error.6.rest_1_ = bf16[1024,7168]{1,0:T(8,128)(2,1)} custom-call(s32[1]{0:T(128)} %bitcast.dp, s32[1]{0:T(128)} %bitcast.1.mp, bf16[1024,7168]{1,0:T(8,128)(2,1)S(1)} %get-tuple-element.38.comp, bf16[512,128]{1,0:T(8,128)(2,1)S(1)} %get-tuple-element.59.near, bf16[512,128]{1,0:T(8,128)(2,1)S(1)} %get-tuple-element.60.far, ...), custom_call_target="tpu_custom_call", output_to_operand_aliasing={{}: (7, {})} | custom-call | bytes 7700000 | tf_op jit(solution)/shard_map/new_error/pallas_call | solution.py:200
  76.2 0.0 collective-permute-done.19.rest_0_
  76.2 1.5 %new_error.7 = bf16[1024,7168]{1,0:T(8,128)(2,1)} custom-call(s32[1]{0:T(128)} %bitcast.dp, s32[1]{0:T(128)} %bitcast.1.mp, bf16[1024,7168]{1,0:T(8,128)(2,1)S(1)} %get-tuple-element.38.comp, bf16[512,128]{1,0:T(8,128)(2,1)S(1)} %get-tuple-element.59.near, bf16[512,128]{1,0:T(8,128)(2,1)S(1)} %get-tuple-element.60.far, ...), custom_call_target="tpu_custom_call", output_to_operand_aliasing={{}: (6, {})} | custom-call | bytes 4900000 | tf_op jit(solution)/shard_map/new_error/pallas_call | solution.py:200
  (4 shorter events, 0.1 us)
Async XLA Ops:
  11.8 1.6 %collective-permute-start = (f32[128,512]{1,0:T(8,128)S(1)}, f32[128,512]{1,0:T(8,128)S(1)}, u32[]{:S(2)}, u32[]{:S(2)}) collective-permute-start(f32[128,512]{1,0:T(8,128)S(1)} %get-tuple-element.40), channel_id=1, source_target_pairs={{0,4},{1,5},{2,6},{3,7},{4,0},{5,1},{6,2},{7,3},{8,12},{9,13},{10,... | collective-permute-start | bytes 786440 | tf_op jit(solution)/shard_map/ppermute | solution.py:372
  13.5 7.2 %collective-permute-start.1 = (bf16[128,512]{1,0:T(8,128)(2,1)S(1)}, bf16[128,512]{1,0:T(8,128)(2,1)S(1)}, u32[]{:S(2)}, u32[]{:S(2)}) collective-permute-start(bf16[128,512]{1,0:T(8,128)(2,1)S(1)} %fusion.1), channel_id=1, source_target_pairs={{0,8},{1,9},{2,10},{3,11},{4,20},{5,21},{6,22},{7,23},{8,0},{9,1},... | collective-permute-start | bytes 393224 | tf_op jit(solution)/shard_map/ppermute | solution.py:372
  20.7 4.2 %collective-permute-start.2 = (bf16[128,512]{1,0:T(8,128)(2,1)S(1)}, bf16[128,512]{1,0:T(8,128)(2,1)S(1)}, u32[]{:S(2)}, u32[]{:S(2)}) collective-permute-start(bf16[128,512]{1,0:T(8,128)(2,1)S(1)} %fusion), channel_id=1, source_target_pairs={{0,16},{1,17},{2,18},{3,19},{4,12},{5,13},{6,14},{7,15},{8,24},{9,... | collective-permute-start | bytes 393224 | tf_op jit(solution)/shard_map/ppermute | solution.py:372
  25.0 2.8 %collective-permute-start.3 = (bf16[128,512]{1,0:T(8,128)(2,1)S(1)}, bf16[128,512]{1,0:T(8,128)(2,1)S(1)}, u32[]{:S(2)}, u32[]{:S(2)}) collective-permute-start(bf16[128,512]{1,0:T(8,128)(2,1)S(1)} %add_convert_fusion.near), channel_id=1, source_target_pairs={{0,4},{1,5},{2,6},{3,7},{4,0},{5,1},{6,2},{7,3},{8,12},{9,13},{10,... | collective-permute-start | bytes 393224 | tf_op jit(solution)/shard_map/ppermute | solution.py:372
  28.3 1.6 %collective-permute-start.4 = (bf16[7,128,128]{2,1,0:T(8,128)(2,1)S(1)}, bf16[7,128,128]{2,1,0:T(8,128)(2,1)S(1)}, u32[]{:S(2)}, u32[]{:S(2)}) collective-permute-start(bf16[7,128,128]{2,1,0:T(8,128)(2,1)S(1)} %right_product.9), channel_id=1, source_target_pairs={{0,4},{1,5},{2,6},{3,7},{4,0},{5,1},{6,2},{7,3},{8,12},{9,13},{10,... | collective-permute-start | bytes 688136 | tf_op jit(solution)/shard_map/ppermute | solution.py:372
  29.3 3.7 %collective-permute-start.5 = (bf16[7,128,128]{2,1,0:T(8,128)(2,1)S(1)}, bf16[7,128,128]{2,1,0:T(8,128)(2,1)S(1)}, u32[]{:S(2)}, u32[]{:S(2)}) collective-permute-start(bf16[7,128,128]{2,1,0:T(8,128)(2,1)S(1)} %right_product.11), channel_id=1, source_target_pairs={{0,4},{1,5},{2,6},{3,7},{4,0},{5,1},{6,2},{7,3},{8,12},{9,13},{10,... | collective-permute-start | bytes 688136 | tf_op jit(solution)/shard_map/ppermute | solution.py:372
  30.0 6.2 %collective-permute-start.6 = (bf16[7,128,128]{2,1,0:T(8,128)(2,1)S(1)}, bf16[7,128,128]{2,1,0:T(8,128)(2,1)S(1)}, u32[]{:S(2)}, u32[]{:S(2)}) collective-permute-start(bf16[7,128,128]{2,1,0:T(8,128)(2,1)S(1)} %first_sum.2), channel_id=1, source_target_pairs={{0,1},{1,0},{2,3},{3,2},{4,6},{5,7},{6,4},{7,5},{8,9},{9,8},{10,11... | collective-permute-start | bytes 688136 | tf_op jit(solution)/shard_map/ppermute | solution.py:372
  33.7 3.9 %collective-permute-start.9 = (bf16[7,128,128]{2,1,0:T(8,128)(2,1)S(1)}, bf16[7,128,128]{2,1,0:T(8,128)(2,1)S(1)}, u32[]{:S(2)}, u32[]{:S(2)}) collective-permute-start(bf16[7,128,128]{2,1,0:T(8,128)(2,1)S(1)} %right_product.15), channel_id=1, source_target_pairs={{0,4},{1,5},{2,6},{3,7},{4,0},{5,1},{6,2},{7,3},{8,12},{9,13},{10,... | collective-permute-start | bytes 688136 | tf_op jit(solution)/shard_map/ppermute | solution.py:372
  34.4 5.9 %collective-permute-start.8 = (bf16[9,128,128]{2,1,0:T(8,128)(2,1)S(1)}, bf16[9,128,128]{2,1,0:T(8,128)(2,1)S(1)}, u32[]{:S(2)}, u32[]{:S(2)}) collective-permute-start(bf16[9,128,128]{2,1,0:T(8,128)(2,1)S(1)} %get-tuple-element.49), channel_id=1, source_target_pairs={{0,1},{1,0},{2,3},{3,2},{4,6},{5,7},{6,4},{7,5},{8,9},{9,8},{10,11... | collective-permute-start | bytes 884744 | tf_op jit(solution)/shard_map/ppermute | solution.py:372
  36.7 3.6 %collective-permute-start.7 = (bf16[7,128,128]{2,1,0:T(8,128)(2,1)S(1)}, bf16[7,128,128]{2,1,0:T(8,128)(2,1)S(1)}, u32[]{:S(2)}, u32[]{:S(2)}) collective-permute-start(bf16[7,128,128]{2,1,0:T(8,128)(2,1)S(1)} %right_product.13), channel_id=1, source_target_pairs={{0,4},{1,5},{2,6},{3,7},{4,0},{5,1},{6,2},{7,3},{8,12},{9,13},{10,... | collective-permute-start | bytes 688136 | tf_op jit(solution)/shard_map/ppermute | solution.py:372
  37.7 5.5 %collective-permute-start.10 = (bf16[7,128,128]{2,1,0:T(8,128)(2,1)S(1)}, bf16[7,128,128]{2,1,0:T(8,128)(2,1)S(1)}, u32[]{:S(2)}, u32[]{:S(2)}) collective-permute-start(bf16[7,128,128]{2,1,0:T(8,128)(2,1)S(1)} %second_sum.3), channel_id=1, source_target_pairs={{0,2},{1,3},{2,0},{3,1},{4,5},{5,4},{6,7},{7,6},{8,10},{9,11},{10,... | collective-permute-start | bytes 688136 | tf_op jit(solution)/shard_map/ppermute | solution.py:372
  43.3 7.1 %collective-permute-start.11 = (bf16[7,128,128]{2,1,0:T(8,128)(2,1)S(1)}, bf16[7,128,128]{2,1,0:T(8,128)(2,1)S(1)}, u32[]{:S(2)}, u32[]{:S(2)}) collective-permute-start(bf16[7,128,128]{2,1,0:T(8,128)(2,1)S(1)} %third_sum.1.one), channel_id=1, source_target_pairs={{0,16},{1,17},{2,18},{3,19},{4,12},{5,13},{6,14},{7,15},{8,24},{9,... | collective-permute-start | bytes 688136 | tf_op jit(solution)/shard_map/ppermute | solution.py:372
  44.8 3.4 %collective-permute-start.12 = (f32[128,128]{1,0:T(8,128)S(1)}, f32[128,128]{1,0:T(8,128)S(1)}, u32[]{:S(2)}, u32[]{:S(2)}) collective-permute-start(f32[128,128]{1,0:T(8,128)S(1)} %get-tuple-element.53), channel_id=1, source_target_pairs={{0,2},{1,3},{2,0},{3,1},{4,5},{5,4},{6,7},{7,6},{8,10},{9,11},{10,... | collective-permute-start | bytes 196616 | tf_op jit(solution)/shard_map/ppermute | solution.py:372
  50.4 8.4 %collective-permute-start.13 = (bf16[7,128,128]{2,1,0:T(8,128)(2,1)S(1)}, bf16[7,128,128]{2,1,0:T(8,128)(2,1)S(1)}, u32[]{:S(2)}, u32[]{:S(2)}) collective-permute-start(bf16[7,128,128]{2,1,0:T(8,128)(2,1)S(1)} %pair_sum.1.own), channel_id=1, source_target_pairs={{0,8},{1,9},{2,10},{3,11},{4,20},{5,21},{6,22},{7,23},{8,0},{9,1},... | collective-permute-start | bytes 688136 | tf_op jit(solution)/shard_map/ppermute | solution.py:372
  59.1 7.1 %collective-permute-start.14 = (bf16[7,128,128]{2,1,0:T(8,128)(2,1)S(1)}, bf16[7,128,128]{2,1,0:T(8,128)(2,1)S(1)}, u32[]{:S(2)}, u32[]{:S(2)}) collective-permute-start(bf16[7,128,128]{2,1,0:T(8,128)(2,1)S(1)} %factor.1.rest_0_.rest_4_), channel_id=1, source_target_pairs={{0,2},{1,3},{2,0},{3,1},{4,5},{5,4},{6,7},{7,6},{8,10},{9,11},{10,... | collective-permute-start | bytes 688136 | tf_op jit(solution)/shard_map/ppermute | solution.py:372
  60.0 9.3 %collective-permute-start.18 = (bf16[7,128,128]{2,1,0:T(8,128)(2,1)S(1)}, bf16[7,128,128]{2,1,0:T(8,128)(2,1)S(1)}, u32[]{:S(2)}, u32[]{:S(2)}) collective-permute-start(bf16[7,128,128]{2,1,0:T(8,128)(2,1)S(1)} %factor.1.rest_0_.rest_4_), channel_id=1, source_target_pairs={{0,1},{1,0},{2,3},{3,2},{4,6},{5,7},{6,4},{7,5},{8,9},{9,8},{10,11... | collective-permute-start | bytes 688136 | tf_op jit(solution)/shard_map/ppermute | solution.py:372
  62.7 6.5 %collective-permute-start.16 = (bf16[7,128,128]{2,1,0:T(8,128)(2,1)S(1)}, bf16[7,128,128]{2,1,0:T(8,128)(2,1)S(1)}, u32[]{:S(2)}, u32[]{:S(2)}) collective-permute-start(bf16[7,128,128]{2,1,0:T(8,128)(2,1)S(1)} %factor.1.rest_0_.rest_4_), channel_id=1, source_target_pairs={{0,4},{1,5},{2,6},{3,7},{4,0},{5,1},{6,2},{7,3},{8,12},{9,13},{10,... | collective-permute-start | bytes 688136 | tf_op jit(solution)/shard_map/ppermute | solution.py:372
  66.2 3.0 %collective-permute-start.17 = (bf16[7,128,128]{2,1,0:T(8,128)(2,1)S(1)}, bf16[7,128,128]{2,1,0:T(8,128)(2,1)S(1)}, u32[]{:S(2)}, u32[]{:S(2)}) collective-permute-start(bf16[7,128,128]{2,1,0:T(8,128)(2,1)S(1)} %collective-permute-done.14.rest_1_), channel_id=1, source_target_pairs={{0,4},{1,5},{2,6},{3,7},{4,0},{5,1},{6,2},{7,3},{8,12},{9,13},{10,... | collective-permute-start | bytes 688136 | tf_op jit(solution)/shard_map/ppermute | solution.py:372
  68.0 5.2 %collective-permute-start.15 = (bf16[7,128,128]{2,1,0:T(8,128)(2,1)S(1)}, bf16[7,128,128]{2,1,0:T(8,128)(2,1)S(1)}, u32[]{:S(2)}, u32[]{:S(2)}) collective-permute-start(bf16[7,128,128]{2,1,0:T(8,128)(2,1)S(1)} %collective-permute-done.14.rest_1_), channel_id=1, source_target_pairs={{0,1},{1,0},{2,3},{3,2},{4,6},{5,7},{6,4},{7,5},{8,9},{9,8},{10,11... | collective-permute-start | bytes 688136 | tf_op jit(solution)/shard_map/ppermute | solution.py:372
  69.2 4.8 %collective-permute-start.20 = (bf16[7,128,128]{2,1,0:T(8,128)(2,1)S(1)}, bf16[7,128,128]{2,1,0:T(8,128)(2,1)S(1)}, u32[]{:S(2)}, u32[]{:S(2)}) collective-permute-start(bf16[7,128,128]{2,1,0:T(8,128)(2,1)S(1)} %collective-permute-done.18.rest_3_), channel_id=1, source_target_pairs={{0,4},{1,5},{2,6},{3,7},{4,0},{5,1},{6,2},{7,3},{8,12},{9,13},{10,... | collective-permute-start | bytes 688136 | tf_op jit(solution)/shard_map/ppermute | solution.py:372
  73.1 3.0 %collective-permute-start.19 = (bf16[7,128,128]{2,1,0:T(8,128)(2,1)S(1)}, bf16[7,128,128]{2,1,0:T(8,128)(2,1)S(1)}, u32[]{:S(2)}, u32[]{:S(2)}) collective-permute-start(bf16[7,128,128]{2,1,0:T(8,128)(2,1)S(1)} %collective-permute-done.15.rest_1_), channel_id=1, source_target_pairs={{0,4},{1,5},{2,6},{3,7},{4,0},{5,1},{6,2},{7,3},{8,12},{9,13},{10,... | collective-permute-start | bytes 688136 | tf_op jit(solution)/shard_map/ppermute | solution.py:372
